TPU v7x, 32 devices: a whole 2x2x4 slice. The times are simulated.
32 devices in a mesh: gx: 8 (over y, x, core), gy: 4 (over z).
Axes of the slice: x: 2, y: 2, z: 4, core: 2. Of those that a mesh axis runs over, the one named last changes fastest.
Arguments:
- wave_fields: float32 [9, 32, 32, 1024], P(None, None, 'gy', 'gx'), may hold values from -6 to 6
- lame_lambda: float32 [32, 32, 1024], P(None, 'gy', 'gx'), may hold values from 0.5 to 1
- shear_modulus: float32 [32, 32, 1024], P(None, 'gy', 'gx'), may hold values from 0.3 to 0.7
- buoyancy: float32 [32, 32, 1024], P(None, 'gy', 'gx'), may hold values from 0.5 to 1
- ocean_state: float32 [3, 32, 1024], P(None, 'gy', 'gx'), may hold values from -6 to 6
- water_depth: float32 [32, 1024], P('gy', 'gx'), may hold values from 0.5 to 2
- seafloor_index: int32 [32, 1024], P('gy', 'gx'), may hold values from 0 to 15
- wet_mask: int32 [32, 1024], P('gy', 'gx'), may hold values 0 or 1
Outputs:
- wave_out: float32 [9, 32, 32, 1024], P(None, None, 'gy', 'gx')
- ocean_out: float32 [3, 32, 1024], P(None, 'gy', 'gx')
All inputs are finite; a program needn't handle non-finite values. No bound on the sum of `wet_mask` on one device may be relied on, other than what follows from the above.
Results may differ from a plain program's by a relative error of at most 0.0001.
Values sent between devices are 32-bit elements; how exact they have to be, the bound alone decides.
No kernel may reach another device: no remote copies, remote signals or barrier semaphores. Data moves between devices by JAX's collectives and lax.ppermute only.
A program may use at most 64 MiB of HBM per device.

v0:
```python
import jax
import jax.numpy as jnp
from jax import lax
from jax.sharding import PartitionSpec as P

STEPS = 2


coef_near = 9.0 / 8.0
coef_far = -1.0 / 24.0
courant = 0.3
ocean_rate = 0.3
uplift = 0.5
loading = 0.5
viscous = 0.1


def extended(block, sides, width):
    for axis, dim in sides:
        count = lax.axis_size(axis)
        forward = [(i, i + 1) for i in range(count - 1)]
        backward = [(target, source) for source, target in forward]
        low = lax.ppermute(
            lax.slice_in_dim(block, block.shape[dim] - width, None, axis=dim), axis, forward
        )
        high = lax.ppermute(lax.slice_in_dim(block, 0, width, axis=dim), axis, backward)
        block = jnp.concatenate([low, block, high], axis=dim)
    return block


def differ(padded, direction, margins, forward):
    extent = padded.shape

    def sample(offset):
        selector = []
        for dimension in range(3):
            margin = margins[dimension]
            if dimension == direction:
                selector.append(slice(margin + offset, extent[dimension] - margin + offset))
            else:
                selector.append(slice(margin, extent[dimension] - margin))
        return padded[tuple(selector)]

    if forward:
        return coef_near * (sample(1) - sample(0)) + coef_far * (sample(2) - sample(-1))
    return coef_near * (sample(0) - sample(-1)) + coef_far * (sample(1) - sample(-2))


def advance_velocity(velocity, stress_pad, buoyancy, margins):
    stress_xx, stress_yy, stress_zz = (stress_pad[0], stress_pad[1], stress_pad[2])
    stress_xy, stress_xz, stress_yz = (stress_pad[3], stress_pad[4], stress_pad[5])
    accel_x = (
        differ(stress_xx, 2, margins, True)
        + differ(stress_xy, 1, margins, False)
        + differ(stress_xz, 0, margins, False)
    )
    accel_y = (
        differ(stress_xy, 2, margins, False)
        + differ(stress_yy, 1, margins, True)
        + differ(stress_yz, 0, margins, False)
    )
    accel_z = (
        differ(stress_xz, 2, margins, False)
        + differ(stress_yz, 1, margins, False)
        + differ(stress_zz, 0, margins, True)
    )
    return jnp.stack(
        [
            velocity[0] + courant * buoyancy * accel_x,
            velocity[1] + courant * buoyancy * accel_y,
            velocity[2] + courant * buoyancy * accel_z,
        ]
    )


def advance_stress(stress, velocity_pad, lame, shear, margins):
    speed_x, speed_y, speed_z = (velocity_pad[0], velocity_pad[1], velocity_pad[2])
    strain_x = differ(speed_x, 2, margins, False)
    strain_y = differ(speed_y, 1, margins, False)
    strain_z = differ(speed_z, 0, margins, False)
    trace = strain_x + strain_y + strain_z
    shear_xy = differ(speed_x, 1, margins, True) + differ(speed_y, 2, margins, True)
    shear_xz = differ(speed_x, 0, margins, True) + differ(speed_z, 2, margins, True)
    shear_yz = differ(speed_y, 0, margins, True) + differ(speed_z, 1, margins, True)
    return jnp.stack(
        [
            stress[0] + courant * (lame * trace + 2.0 * shear * strain_x),
            stress[1] + courant * (lame * trace + 2.0 * shear * strain_y),
            stress[2] + courant * (lame * trace + 2.0 * shear * strain_z),
            stress[3] + courant * shear * shear_xy,
            stress[4] + courant * shear * shear_xz,
            stress[5] + courant * shear * shear_yz,
        ]
    )


def ocean_level(level, flux_pad, vertical, onehot, wet):
    seafloor = jnp.sum(vertical * onehot, axis=0)
    east = flux_pad[0]
    north = flux_pad[1]
    spread = 0.5 * (east[1:-1, 2:] - east[1:-1, :-2]) + 0.5 * (north[2:, 1:-1] - north[:-2, 1:-1])
    return level + wet * (uplift * seafloor - ocean_rate * spread)


def ocean_flux(fluxes, flux_pad, level_pad, depth, wet):
    slope_x = 0.5 * (level_pad[1:-1, 2:] - level_pad[1:-1, :-2])
    slope_y = 0.5 * (level_pad[2:, 1:-1] - level_pad[:-2, 1:-1])
    laplace = (
        flux_pad[:, 1:-1, 2:]
        + flux_pad[:, 1:-1, :-2]
        + flux_pad[:, 2:, 1:-1]
        + flux_pad[:, :-2, 1:-1]
        - 4.0 * fluxes
    )
    east = wet * (fluxes[0] - ocean_rate * depth * slope_x + viscous * laplace[0])
    north = wet * (fluxes[1] - ocean_rate * depth * slope_y + viscous * laplace[1])
    return jnp.stack([east, north])


def pad_both(field):
    return jnp.pad(field, ((0, 0), (2, 2), (2, 2)))


def pad_rows(field):
    return jnp.pad(field, ((0, 0), (2, 2), (0, 0)))


def pad_columns(field):
    return jnp.pad(field, ((0, 0), (0, 0), (2, 2)))


def local(
    wave_fields,
    lame_lambda,
    shear_modulus,
    buoyancy,
    ocean_state,
    water_depth,
    seafloor_index,
    wet_mask,
):
    wet = wet_mask.astype(jnp.float32)
    layers = jnp.arange(wave_fields.shape[1], dtype=jnp.int32)
    onehot = (layers[:, None, None] == seafloor_index[None, :, :]).astype(jnp.float32)
    depth_pad = ((0, 0), (2, 2), (0, 0), (0, 0))
    fields = wave_fields
    ocean = ocean_state
    for number in range(STEPS):
        flux_pad = extended(ocean[1:3], (("gx", 2), ("gy", 1)), 1)
        stress = fields[3:9]
        along = jnp.stack([stress[0], stress[3], stress[4]])
        across = jnp.stack([stress[1], stress[3], stress[5]])
        along_pad = extended(along, (("gx", 3),), 2)
        across_pad = extended(across, (("gy", 2),), 2)
        mixed_xy = jnp.concatenate(
            [
                pad_columns(across_pad[1, :, 0:2, :]),
                along_pad[1],
                pad_columns(across_pad[1, :, -2:, :]),
            ],
            axis=1,
        )
        stress_pad = jnp.stack(
            [
                pad_rows(along_pad[0]),
                pad_columns(across_pad[0]),
                pad_both(stress[2]),
                mixed_xy,
                pad_rows(along_pad[2]),
                pad_columns(across_pad[2]),
            ]
        )
        stress_pad = jnp.pad(stress_pad, depth_pad)
        velocity = advance_velocity(fields[0:3], stress_pad, buoyancy, (2, 2, 2))
        velocity_pad = extended(velocity, (("gx", 3), ("gy", 2)), 2)
        velocity_pad = jnp.pad(velocity_pad, depth_pad)
        stress = advance_stress(stress, velocity_pad, lame_lambda, shear_modulus, (2, 2, 2))
        level = ocean_level(ocean[0], flux_pad, velocity[2], onehot, wet)
        level_pad = extended(level, (("gx", 1), ("gy", 0)), 1)
        fluxes = ocean_flux(ocean[1:3], flux_pad, level_pad, water_depth, wet)
        pressed = stress[2] - loading * onehot * (wet * level)[None, :, :]
        stress = jnp.concatenate([stress[0:2], pressed[None], stress[3:6]], axis=0)
        fields = jnp.concatenate([velocity, stress], axis=0)
        ocean = jnp.concatenate([level[None], fluxes], axis=0)
    return (fields, ocean)


def solution(mesh):
    in_specs = (
        P(None, None, "gy", "gx"),
        P(None, "gy", "gx"),
        P(None, "gy", "gx"),
        P(None, "gy", "gx"),
        P(None, "gy", "gx"),
        P("gy", "gx"),
        P("gy", "gx"),
        P("gy", "gx"),
    )
    out_specs = (P(None, None, "gy", "gx"), P(None, "gy", "gx"))
    return jax.shard_map(local, mesh=mesh, in_specs=in_specs, out_specs=out_specs, check_vma=False)
```

profile of v0, /device:TPU:10, one launch (start us, length us, event | category | flops | bytes accessed | tf_op | source)
XLA Modules:
  0.0 157.9 jit_solution(9801731998918394110)
XLA Ops:
  3.5 3.6 %collective-permute-start.13 = (f32[2,8,1]{2,1,0:T(8,128)S(1)}, f32[2,8,1]{2,1,0:T(8,128)S(1)}, u32[]{:S(2)}, u32[]{:S(2)}) collective-permute-start(f32[2,8,1]{2,1,0:T(8,128)S(1)} %get-tuple-element.95), channel_id=1, source_target_pairs={{4,0},{8,4},{12,8},{16,12},{20,16},{24,20},{28,24},{5,1},{9,5},{13... | collective-permute-start | bytes 200 | tf_op jit(solution)/shard_map/ppermute | solution.py:26
  8.4 3.5 %collective-permute-start.2 = (f32[3,32,2,128]{3,2,1,0:T(2,128)S(1)}, f32[3,32,2,128]{3,2,1,0:T(2,128)S(1)}, u32[]{:S(2)}, u32[]{:S(2)}) collective-permute-start(f32[3,32,2,128]{3,2,1,0:T(2,128)S(1)} %get-tuple-element.72), channel_id=1, source_target_pairs={{0,1},{1,2},{2,3},{4,5},{5,6},{6,7},{8,9},{9,10},{10,11},{12,13},{... | collective-permute-start | bytes 294920 | tf_op jit(solution)/shard_map/ppermute | solution.py:23
  11.9 2.4 %collective-permute-start.3 = (f32[3,32,2,128]{3,2,1,0:T(2,128)S(1)}, f32[3,32,2,128]{3,2,1,0:T(2,128)S(1)}, u32[]{:S(2)}, u32[]{:S(2)}) collective-permute-start(f32[3,32,2,128]{3,2,1,0:T(2,128)S(1)} %get-tuple-element.73), channel_id=1, source_target_pairs={{1,0},{2,1},{3,2},{5,4},{6,5},{7,6},{9,8},{10,9},{11,10},{13,12},{... | collective-permute-start | bytes 294920 | tf_op jit(solution)/shard_map/ppermute | solution.py:26
  14.4 3.5 %collective-permute-start.14 = (f32[2,1,130]{2,1,0:T(1,128)S(1)}, f32[2,1,130]{2,1,0:T(1,128)S(1)}, u32[]{:S(2)}, u32[]{:S(2)}) collective-permute-start(f32[2,1,130]{2,1,0:T(1,128)S(1)} %get-tuple-element.88), channel_id=1, source_target_pairs={{0,1},{1,2},{2,3},{4,5},{5,6},{6,7},{8,9},{9,10},{10,11},{12,13},{... | collective-permute-start | bytes 3128 | tf_op jit(solution)/shard_map/ppermute | solution.py:23
  17.9 2.4 %collective-permute-start.15 = (f32[2,1,130]{2,1,0:T(1,128)S(1)}, f32[2,1,130]{2,1,0:T(1,128)S(1)}, u32[]{:S(2)}, u32[]{:S(2)}) collective-permute-start(f32[2,1,130]{2,1,0:T(1,128)S(1)} %get-tuple-element.89), channel_id=1, source_target_pairs={{1,0},{2,1},{3,2},{5,4},{6,5},{7,6},{9,8},{10,9},{11,10},{13,12},{... | collective-permute-start | bytes 3128 | tf_op jit(solution)/shard_map/ppermute | solution.py:26
  22.4 3.6 %collective-permute-start.1 = (f32[3,32,8,2]{3,2,1,0:T(8,128)S(1)}, f32[3,32,8,2]{3,2,1,0:T(8,128)S(1)}, u32[]{:S(2)}, u32[]{:S(2)}) collective-permute-start(f32[3,32,8,2]{3,2,1,0:T(8,128)S(1)} %get-tuple-element.75), channel_id=1, source_target_pairs={{4,0},{8,4},{12,8},{16,12},{20,16},{24,20},{28,24},{5,1},{9,5},{13... | collective-permute-start | bytes 18440 | tf_op jit(solution)/shard_map/ppermute | solution.py:26
  26.2 3.3 %collective-permute-done = f32[3,32,8,2]{3,2,1,0:T(8,128)S(1)} collective-permute-done((f32[3,32,8,2]{3,2,1,0:T(8,128)S(1)}, f32[3,32,8,2]{3,2,1,0:T(8,128)S(1)}, u32[]{:S(2)}, u32[]{:S(2)}) %collective-permute-start) | collective-permute-done | bytes 6176 | tf_op jit(solution)/shard_map/ppermute | solution.py:23
  29.5 4.1 %collective-permute-done.1 = f32[3,32,8,2]{3,2,1,0:T(8,128)S(1)} collective-permute-done((f32[3,32,8,2]{3,2,1,0:T(8,128)S(1)}, f32[3,32,8,2]{3,2,1,0:T(8,128)S(1)}, u32[]{:S(2)}, u32[]{:S(2)}) %collective-permute-start.1) | collective-permute-done | bytes 6176 | tf_op jit(solution)/shard_map/ppermute | solution.py:26
  37.7 3.8 %collective-permute-start.20 = (f32[8,1]{1,0:T(8,128)S(1)}, f32[8,1]{1,0:T(8,128)S(1)}, u32[]{:S(2)}, u32[]{:S(2)}) collective-permute-start(f32[8,1]{1,0:T(8,128)S(1)} %get-tuple-element.100), channel_id=1, source_target_pairs={{4,0},{8,4},{12,8},{16,12},{20,16},{24,20},{28,24},{5,1},{9,5},{13... | collective-permute-start | bytes 104 | tf_op jit(solution)/shard_map/ppermute | solution.py:26
  43.5 3.0 %collective-permute-done.21 = f32[8,1]{1,0:T(8,128)S(1)} collective-permute-done((f32[8,1]{1,0:T(8,128)S(1)}, f32[8,1]{1,0:T(8,128)S(1)}, u32[]{:S(2)}, u32[]{:S(2)}) %collective-permute-start.21) | collective-permute-done | bytes 64 | tf_op jit(solution)/shard_map/ppermute | solution.py:23
  48.5 3.9 %collective-permute-start.23 = (f32[1,130]{1,0:T(1,128)S(1)}, f32[1,130]{1,0:T(1,128)S(1)}, u32[]{:S(2)}, u32[]{:S(2)}) collective-permute-start(f32[1,130]{1,0:T(1,128)S(1)} %get-tuple-element.93), channel_id=1, source_target_pairs={{0,1},{1,2},{2,3},{4,5},{5,6},{6,7},{8,9},{9,10},{10,11},{12,13},{... | collective-permute-start | bytes 1568 | tf_op jit(solution)/shard_map/ppermute | solution.py:23
  56.0 3.6 %collective-permute-start.25 = (f32[2,8,1]{2,1,0:T(8,128)S(1)}, f32[2,8,1]{2,1,0:T(8,128)S(1)}, u32[]{:S(2)}, u32[]{:S(2)}) collective-permute-start(f32[2,8,1]{2,1,0:T(8,128)S(1)} %get-tuple-element.97), channel_id=1, source_target_pairs={{4,0},{8,4},{12,8},{16,12},{20,16},{24,20},{28,24},{5,1},{9,5},{13... | collective-permute-start | bytes 200 | tf_op jit(solution)/shard_map/ppermute | solution.py:26
  61.5 3.9 %collective-permute-start.26 = (f32[2,1,130]{2,1,0:T(1,128)S(1)}, f32[2,1,130]{2,1,0:T(1,128)S(1)}, u32[]{:S(2)}, u32[]{:S(2)}) collective-permute-start(f32[2,1,130]{2,1,0:T(1,128)S(1)} %get-tuple-element.86), channel_id=1, source_target_pairs={{0,1},{1,2},{2,3},{4,5},{5,6},{6,7},{8,9},{9,10},{10,11},{12,13},{... | collective-permute-start | bytes 3128 | tf_op jit(solution)/shard_map/ppermute | solution.py:23
  67.5 4.9 %collective-permute-start.4 = (f32[3,32,8,2]{3,2,1,0:T(8,128)S(1)}, f32[3,32,8,2]{3,2,1,0:T(8,128)S(1)}, u32[]{:S(2)}, u32[]{:S(2)}) collective-permute-start(f32[3,32,8,2]{3,2,1,0:T(8,128)S(1)} %get-tuple-element.70), channel_id=1, source_target_pairs={{0,4},{4,8},{8,12},{12,16},{16,20},{20,24},{24,28},{1,5},{5,9},{9,... | collective-permute-start | bytes 18440 | tf_op jit(solution)/shard_map/ppermute | solution.py:23
  74.5 2.1 %collective-permute-done.4 = f32[3,32,8,2]{3,2,1,0:T(8,128)S(1)} collective-permute-done((f32[3,32,8,2]{3,2,1,0:T(8,128)S(1)}, f32[3,32,8,2]{3,2,1,0:T(8,128)S(1)}, u32[]{:S(2)}, u32[]{:S(2)}) %collective-permute-start.4) | collective-permute-done | bytes 6176 | tf_op jit(solution)/shard_map/ppermute | solution.py:23
  76.6 5.0 %collective-permute-done.5 = f32[3,32,8,2]{3,2,1,0:T(8,128)S(1)} collective-permute-done((f32[3,32,8,2]{3,2,1,0:T(8,128)S(1)}, f32[3,32,8,2]{3,2,1,0:T(8,128)S(1)}, u32[]{:S(2)}, u32[]{:S(2)}) %collective-permute-start.5) | collective-permute-done | bytes 6176 | tf_op jit(solution)/shard_map/ppermute | solution.py:26
  82.3 3.9 %collective-permute-start.6 = (f32[3,32,2,132]{3,2,1,0:T(2,128)S(1)}, f32[3,32,2,132]{3,2,1,0:T(2,128)S(1)}, u32[]{:S(2)}, u32[]{:S(2)}) collective-permute-start(f32[3,32,2,132]{3,2,1,0:T(2,128)S(1)} %get-tuple-element.47), channel_id=1, source_target_pairs={{0,1},{1,2},{2,3},{4,5},{5,6},{6,7},{8,9},{9,10},{10,11},{12,13},{... | collective-permute-start | bytes 304136 | tf_op jit(solution)/shard_map/ppermute | solution.py:23
  88.2 3.5 %collective-permute-done.6 = f32[3,32,2,132]{3,2,1,0:T(2,128)S(1)} collective-permute-done((f32[3,32,2,132]{3,2,1,0:T(2,128)S(1)}, f32[3,32,2,132]{3,2,1,0:T(2,128)S(1)}, u32[]{:S(2)}, u32[]{:S(2)}) %collective-permute-start.6) | collective-permute-done | bytes 101408 | tf_op jit(solution)/shard_map/ppermute | solution.py:23
  91.7 4.1 %collective-permute-done.7 = f32[3,32,2,132]{3,2,1,0:T(2,128)S(1)} collective-permute-done((f32[3,32,2,132]{3,2,1,0:T(2,128)S(1)}, f32[3,32,2,132]{3,2,1,0:T(2,128)S(1)}, u32[]{:S(2)}, u32[]{:S(2)}) %collective-permute-start.7) | collective-permute-done | bytes 101408 | tf_op jit(solution)/shard_map/ppermute | solution.py:26
  101.1 3.6 %collective-permute-start.9 = (f32[3,32,8,2]{3,2,1,0:T(8,128)S(1)}, f32[3,32,8,2]{3,2,1,0:T(8,128)S(1)}, u32[]{:S(2)}, u32[]{:S(2)}) collective-permute-start(f32[3,32,8,2]{3,2,1,0:T(8,128)S(1)} %get-tuple-element.69), channel_id=1, source_target_pairs={{4,0},{8,4},{12,8},{16,12},{20,16},{24,20},{28,24},{5,1},{9,5},{13... | collective-permute-start | bytes 18440 | tf_op jit(solution)/shard_map/ppermute | solution.py:26
  104.8 3.5 %collective-permute-start.10 = (f32[3,32,2,128]{3,2,1,0:T(2,128)S(1)}, f32[3,32,2,128]{3,2,1,0:T(2,128)S(1)}, u32[]{:S(2)}, u32[]{:S(2)}) collective-permute-start(f32[3,32,2,128]{3,2,1,0:T(2,128)S(1)} %get-tuple-element.66), channel_id=1, source_target_pairs={{0,1},{1,2},{2,3},{4,5},{5,6},{6,7},{8,9},{9,10},{10,11},{12,13},{... | collective-permute-start | bytes 294920 | tf_op jit(solution)/shard_map/ppermute | solution.py:23
  108.3 2.4 %collective-permute-start.11 = (f32[3,32,2,128]{3,2,1,0:T(2,128)S(1)}, f32[3,32,2,128]{3,2,1,0:T(2,128)S(1)}, u32[]{:S(2)}, u32[]{:S(2)}) collective-permute-start(f32[3,32,2,128]{3,2,1,0:T(2,128)S(1)} %get-tuple-element.67), channel_id=1, source_target_pairs={{1,0},{2,1},{3,2},{5,4},{6,5},{7,6},{9,8},{10,9},{11,10},{13,12},{... | collective-permute-start | bytes 294920 | tf_op jit(solution)/shard_map/ppermute | solution.py:26
  111.3 3.5 %collective-permute-done.11 = f32[3,32,2,128]{3,2,1,0:T(2,128)S(1)} collective-permute-done((f32[3,32,2,128]{3,2,1,0:T(2,128)S(1)}, f32[3,32,2,128]{3,2,1,0:T(2,128)S(1)}, u32[]{:S(2)}, u32[]{:S(2)}) %collective-permute-start.11) | collective-permute-done | bytes 98336 | tf_op jit(solution)/shard_map/ppermute | solution.py:26
  118.8 3.8 %collective-permute-start.28 = (f32[8,1]{1,0:T(8,128)S(1)}, f32[8,1]{1,0:T(8,128)S(1)}, u32[]{:S(2)}, u32[]{:S(2)}) collective-permute-start(f32[8,1]{1,0:T(8,128)S(1)} %get-tuple-element.99), channel_id=1, source_target_pairs={{4,0},{8,4},{12,8},{16,12},{20,16},{24,20},{28,24},{5,1},{9,5},{13... | collective-permute-start | bytes 104 | tf_op jit(solution)/shard_map/ppermute | solution.py:26
  123.8 2.4 %collective-permute-start.30 = (f32[1,130]{1,0:T(1,128)S(1)}, f32[1,130]{1,0:T(1,128)S(1)}, u32[]{:S(2)}, u32[]{:S(2)}) collective-permute-start(f32[1,130]{1,0:T(1,128)S(1)} %get-tuple-element.90), channel_id=1, source_target_pairs={{1,0},{2,1},{3,2},{5,4},{6,5},{7,6},{9,8},{10,9},{11,10},{13,12},{... | collective-permute-start | bytes 1568 | tf_op jit(solution)/shard_map/ppermute | solution.py:26
  126.2 3.5 %collective-permute-start.31 = (f32[1,130]{1,0:T(1,128)S(1)}, f32[1,130]{1,0:T(1,128)S(1)}, u32[]{:S(2)}, u32[]{:S(2)}) collective-permute-start(f32[1,130]{1,0:T(1,128)S(1)} %get-tuple-element.91), channel_id=1, source_target_pairs={{0,1},{1,2},{2,3},{4,5},{5,6},{6,7},{8,9},{9,10},{10,11},{12,13},{... | collective-permute-start | bytes 1568 | tf_op jit(solution)/shard_map/ppermute | solution.py:23
  129.7 3.1 %collective-permute-start.16 = (f32[3,32,8,2]{3,2,1,0:T(8,128)S(1)}, f32[3,32,8,2]{3,2,1,0:T(8,128)S(1)}, u32[]{:S(2)}, u32[]{:S(2)}) collective-permute-start(f32[3,32,8,2]{3,2,1,0:T(8,128)S(1)} %get-tuple-element.64), channel_id=1, source_target_pairs={{0,4},{4,8},{8,12},{12,16},{16,20},{20,24},{24,28},{1,5},{5,9},{9,... | collective-permute-start | bytes 18440 | tf_op jit(solution)/shard_map/ppermute | solution.py:23
  132.8 2.4 %collective-permute-start.17 = (f32[3,32,8,2]{3,2,1,0:T(8,128)S(1)}, f32[3,32,8,2]{3,2,1,0:T(8,128)S(1)}, u32[]{:S(2)}, u32[]{:S(2)}) collective-permute-start(f32[3,32,8,2]{3,2,1,0:T(8,128)S(1)} %get-tuple-element.65), channel_id=1, source_target_pairs={{4,0},{8,4},{12,8},{16,12},{20,16},{24,20},{28,24},{5,1},{9,5},{13... | collective-permute-start | bytes 18440 | tf_op jit(solution)/shard_map/ppermute | solution.py:26
  135.4 3.4 %collective-permute-done.16 = f32[3,32,8,2]{3,2,1,0:T(8,128)S(1)} collective-permute-done((f32[3,32,8,2]{3,2,1,0:T(8,128)S(1)}, f32[3,32,8,2]{3,2,1,0:T(8,128)S(1)}, u32[]{:S(2)}, u32[]{:S(2)}) %collective-permute-start.16) | collective-permute-done | bytes 6176 | tf_op jit(solution)/shard_map/ppermute | solution.py:23
  138.8 3.5 %collective-permute-done.17 = f32[3,32,8,2]{3,2,1,0:T(8,128)S(1)} collective-permute-done((f32[3,32,8,2]{3,2,1,0:T(8,128)S(1)}, f32[3,32,8,2]{3,2,1,0:T(8,128)S(1)}, u32[]{:S(2)}, u32[]{:S(2)}) %collective-permute-start.17) | collective-permute-done | bytes 6176 | tf_op jit(solution)/shard_map/ppermute | solution.py:26
  144.9 3.9 %collective-permute-start.19 = (f32[3,32,2,132]{3,2,1,0:T(2,128)S(1)}, f32[3,32,2,132]{3,2,1,0:T(2,128)S(1)}, u32[]{:S(2)}, u32[]{:S(2)}) collective-permute-start(f32[3,32,2,132]{3,2,1,0:T(2,128)S(1)} %get-tuple-element.46), channel_id=1, source_target_pairs={{1,0},{2,1},{3,2},{5,4},{6,5},{7,6},{9,8},{10,9},{11,10},{13,12},{... | collective-permute-start | bytes 304136 | tf_op jit(solution)/shard_map/ppermute | solution.py:26
  149.4 3.0 %collective-permute-done.18 = f32[3,32,2,132]{3,2,1,0:T(2,128)S(1)} collective-permute-done((f32[3,32,2,132]{3,2,1,0:T(2,128)S(1)}, f32[3,32,2,132]{3,2,1,0:T(2,128)S(1)}, u32[]{:S(2)}, u32[]{:S(2)}) %collective-permute-start.18) | collective-permute-done | bytes 101408 | tf_op jit(solution)/shard_map/ppermute | solution.py:23
  (127 shorter events, 46.3 us)
Async XLA Ops:
  1.5 12.8 %collective-permute-start.12 = (f32[2,8,1]{2,1,0:T(8,128)S(1)}, f32[2,8,1]{2,1,0:T(8,128)S(1)}, u32[]{:S(2)}, u32[]{:S(2)}) collective-permute-start(f32[2,8,1]{2,1,0:T(8,128)S(1)} %get-tuple-element.94), channel_id=1, source_target_pairs={{0,4},{4,8},{8,12},{12,16},{16,20},{20,24},{24,28},{1,5},{5,9},{9,... | collective-permute-start | bytes 200 | tf_op jit(solution)/shard_map/ppermute | solution.py:23
  3.5 10.9 %collective-permute-start.13 = (f32[2,8,1]{2,1,0:T(8,128)S(1)}, f32[2,8,1]{2,1,0:T(8,128)S(1)}, u32[]{:S(2)}, u32[]{:S(2)}) collective-permute-start(f32[2,8,1]{2,1,0:T(8,128)S(1)} %get-tuple-element.95), channel_id=1, source_target_pairs={{4,0},{8,4},{12,8},{16,12},{20,16},{24,20},{28,24},{5,1},{9,5},{13... | collective-permute-start | bytes 200 | tf_op jit(solution)/shard_map/ppermute | solution.py:26
  8.4 25.8 %collective-permute-start.2 = (f32[3,32,2,128]{3,2,1,0:T(2,128)S(1)}, f32[3,32,2,128]{3,2,1,0:T(2,128)S(1)}, u32[]{:S(2)}, u32[]{:S(2)}) collective-permute-start(f32[3,32,2,128]{3,2,1,0:T(2,128)S(1)} %get-tuple-element.72), channel_id=1, source_target_pairs={{0,1},{1,2},{2,3},{4,5},{5,6},{6,7},{8,9},{9,10},{10,11},{12,13},{... | collective-permute-start | bytes 294920 | tf_op jit(solution)/shard_map/ppermute | solution.py:23
  11.9 22.3 %collective-permute-start.3 = (f32[3,32,2,128]{3,2,1,0:T(2,128)S(1)}, f32[3,32,2,128]{3,2,1,0:T(2,128)S(1)}, u32[]{:S(2)}, u32[]{:S(2)}) collective-permute-start(f32[3,32,2,128]{3,2,1,0:T(2,128)S(1)} %get-tuple-element.73), channel_id=1, source_target_pairs={{1,0},{2,1},{3,2},{5,4},{6,5},{7,6},{9,8},{10,9},{11,10},{13,12},{... | collective-permute-start | bytes 294920 | tf_op jit(solution)/shard_map/ppermute | solution.py:26
  14.4 8.0 %collective-permute-start.14 = (f32[2,1,130]{2,1,0:T(1,128)S(1)}, f32[2,1,130]{2,1,0:T(1,128)S(1)}, u32[]{:S(2)}, u32[]{:S(2)}) collective-permute-start(f32[2,1,130]{2,1,0:T(1,128)S(1)} %get-tuple-element.88), channel_id=1, source_target_pairs={{0,1},{1,2},{2,3},{4,5},{5,6},{6,7},{8,9},{9,10},{10,11},{12,13},{... | collective-permute-start | bytes 3128 | tf_op jit(solution)/shard_map/ppermute | solution.py:23
  17.9 8.1 %collective-permute-start.15 = (f32[2,1,130]{2,1,0:T(1,128)S(1)}, f32[2,1,130]{2,1,0:T(1,128)S(1)}, u32[]{:S(2)}, u32[]{:S(2)}) collective-permute-start(f32[2,1,130]{2,1,0:T(1,128)S(1)} %get-tuple-element.89), channel_id=1, source_target_pairs={{1,0},{2,1},{3,2},{5,4},{6,5},{7,6},{9,8},{10,9},{11,10},{13,12},{... | collective-permute-start | bytes 3128 | tf_op jit(solution)/shard_map/ppermute | solution.py:26
  20.4 9.1 %collective-permute-start = (f32[3,32,8,2]{3,2,1,0:T(8,128)S(1)}, f32[3,32,8,2]{3,2,1,0:T(8,128)S(1)}, u32[]{:S(2)}, u32[]{:S(2)}) collective-permute-start(f32[3,32,8,2]{3,2,1,0:T(8,128)S(1)} %get-tuple-element.74), channel_id=1, source_target_pairs={{0,4},{4,8},{8,12},{12,16},{16,20},{20,24},{24,28},{1,5},{5,9},{9,... | collective-permute-start | bytes 18440 | tf_op jit(solution)/shard_map/ppermute | solution.py:23
  22.4 11.3 %collective-permute-start.1 = (f32[3,32,8,2]{3,2,1,0:T(8,128)S(1)}, f32[3,32,8,2]{3,2,1,0:T(8,128)S(1)}, u32[]{:S(2)}, u32[]{:S(2)}) collective-permute-start(f32[3,32,8,2]{3,2,1,0:T(8,128)S(1)} %get-tuple-element.75), channel_id=1, source_target_pairs={{4,0},{8,4},{12,8},{16,12},{20,16},{24,20},{28,24},{5,1},{9,5},{13... | collective-permute-start | bytes 18440 | tf_op jit(solution)/shard_map/ppermute | solution.py:26
  37.7 5.7 %collective-permute-start.20 = (f32[8,1]{1,0:T(8,128)S(1)}, f32[8,1]{1,0:T(8,128)S(1)}, u32[]{:S(2)}, u32[]{:S(2)}) collective-permute-start(f32[8,1]{1,0:T(8,128)S(1)} %get-tuple-element.100), channel_id=1, source_target_pairs={{4,0},{8,4},{12,8},{16,12},{20,16},{24,20},{28,24},{5,1},{9,5},{13... | collective-permute-start | bytes 104 | tf_op jit(solution)/shard_map/ppermute | solution.py:26
  41.5 4.9 %collective-permute-start.21 = (f32[8,1]{1,0:T(8,128)S(1)}, f32[8,1]{1,0:T(8,128)S(1)}, u32[]{:S(2)}, u32[]{:S(2)}) collective-permute-start(f32[8,1]{1,0:T(8,128)S(1)} %get-tuple-element.101), channel_id=1, source_target_pairs={{0,4},{4,8},{8,12},{12,16},{16,20},{20,24},{24,28},{1,5},{5,9},{9,... | collective-permute-start | bytes 104 | tf_op jit(solution)/shard_map/ppermute | solution.py:23
  46.5 5.9 %collective-permute-start.22 = (f32[1,130]{1,0:T(1,128)S(1)}, f32[1,130]{1,0:T(1,128)S(1)}, u32[]{:S(2)}, u32[]{:S(2)}) collective-permute-start(f32[1,130]{1,0:T(1,128)S(1)} %get-tuple-element.92), channel_id=1, source_target_pairs={{1,0},{2,1},{3,2},{5,4},{6,5},{7,6},{9,8},{10,9},{11,10},{13,12},{... | collective-permute-start | bytes 1568 | tf_op jit(solution)/shard_map/ppermute | solution.py:26
  48.5 5.5 %collective-permute-start.23 = (f32[1,130]{1,0:T(1,128)S(1)}, f32[1,130]{1,0:T(1,128)S(1)}, u32[]{:S(2)}, u32[]{:S(2)}) collective-permute-start(f32[1,130]{1,0:T(1,128)S(1)} %get-tuple-element.93), channel_id=1, source_target_pairs={{0,1},{1,2},{2,3},{4,5},{5,6},{6,7},{8,9},{9,10},{10,11},{12,13},{... | collective-permute-start | bytes 1568 | tf_op jit(solution)/shard_map/ppermute | solution.py:23
  54.1 5.6 %collective-permute-start.24 = (f32[2,8,1]{2,1,0:T(8,128)S(1)}, f32[2,8,1]{2,1,0:T(8,128)S(1)}, u32[]{:S(2)}, u32[]{:S(2)}) collective-permute-start(f32[2,8,1]{2,1,0:T(8,128)S(1)} %get-tuple-element.96), channel_id=1, source_target_pairs={{0,4},{4,8},{8,12},{12,16},{16,20},{20,24},{24,28},{1,5},{5,9},{9,... | collective-permute-start | bytes 200 | tf_op jit(solution)/shard_map/ppermute | solution.py:23
  56.0 5.4 %collective-permute-start.25 = (f32[2,8,1]{2,1,0:T(8,128)S(1)}, f32[2,8,1]{2,1,0:T(8,128)S(1)}, u32[]{:S(2)}, u32[]{:S(2)}) collective-permute-start(f32[2,8,1]{2,1,0:T(8,128)S(1)} %get-tuple-element.97), channel_id=1, source_target_pairs={{4,0},{8,4},{12,8},{16,12},{20,16},{24,20},{28,24},{5,1},{9,5},{13... | collective-permute-start | bytes 200 | tf_op jit(solution)/shard_map/ppermute | solution.py:26
  61.5 12.9 %collective-permute-start.26 = (f32[2,1,130]{2,1,0:T(1,128)S(1)}, f32[2,1,130]{2,1,0:T(1,128)S(1)}, u32[]{:S(2)}, u32[]{:S(2)}) collective-permute-start(f32[2,1,130]{2,1,0:T(1,128)S(1)} %get-tuple-element.86), channel_id=1, source_target_pairs={{0,1},{1,2},{2,3},{4,5},{5,6},{6,7},{8,9},{9,10},{10,11},{12,13},{... | collective-permute-start | bytes 3128 | tf_op jit(solution)/shard_map/ppermute | solution.py:23
  65.4 9.0 %collective-permute-start.27 = (f32[2,1,130]{2,1,0:T(1,128)S(1)}, f32[2,1,130]{2,1,0:T(1,128)S(1)}, u32[]{:S(2)}, u32[]{:S(2)}) collective-permute-start(f32[2,1,130]{2,1,0:T(1,128)S(1)} %get-tuple-element.87), channel_id=1, source_target_pairs={{1,0},{2,1},{3,2},{5,4},{6,5},{7,6},{9,8},{10,9},{11,10},{13,12},{... | collective-permute-start | bytes 3128 | tf_op jit(solution)/shard_map/ppermute | solution.py:26
  67.5 9.1 %collective-permute-start.4 = (f32[3,32,8,2]{3,2,1,0:T(8,128)S(1)}, f32[3,32,8,2]{3,2,1,0:T(8,128)S(1)}, u32[]{:S(2)}, u32[]{:S(2)}) collective-permute-start(f32[3,32,8,2]{3,2,1,0:T(8,128)S(1)} %get-tuple-element.70), channel_id=1, source_target_pairs={{0,4},{4,8},{8,12},{12,16},{16,20},{20,24},{24,28},{1,5},{5,9},{9,... | collective-permute-start | bytes 18440 | tf_op jit(solution)/shard_map/ppermute | solution.py:23
  72.5 9.1 %collective-permute-start.5 = (f32[3,32,8,2]{3,2,1,0:T(8,128)S(1)}, f32[3,32,8,2]{3,2,1,0:T(8,128)S(1)}, u32[]{:S(2)}, u32[]{:S(2)}) collective-permute-start(f32[3,32,8,2]{3,2,1,0:T(8,128)S(1)} %get-tuple-element.71), channel_id=1, source_target_pairs={{4,0},{8,4},{12,8},{16,12},{20,16},{24,20},{28,24},{5,1},{9,5},{13... | collective-permute-start | bytes 18440 | tf_op jit(solution)/shard_map/ppermute | solution.py:26
  82.3 9.4 %collective-permute-start.6 = (f32[3,32,2,132]{3,2,1,0:T(2,128)S(1)}, f32[3,32,2,132]{3,2,1,0:T(2,128)S(1)}, u32[]{:S(2)}, u32[]{:S(2)}) collective-permute-start(f32[3,32,2,132]{3,2,1,0:T(2,128)S(1)} %get-tuple-element.47), channel_id=1, source_target_pairs={{0,1},{1,2},{2,3},{4,5},{5,6},{6,7},{8,9},{9,10},{10,11},{12,13},{... | collective-permute-start | bytes 304136 | tf_op jit(solution)/shard_map/ppermute | solution.py:23
  86.2 9.6 %collective-permute-start.7 = (f32[3,32,2,132]{3,2,1,0:T(2,128)S(1)}, f32[3,32,2,132]{3,2,1,0:T(2,128)S(1)}, u32[]{:S(2)}, u32[]{:S(2)}) collective-permute-start(f32[3,32,2,132]{3,2,1,0:T(2,128)S(1)} %get-tuple-element.48), channel_id=1, source_target_pairs={{1,0},{2,1},{3,2},{5,4},{6,5},{7,6},{9,8},{10,9},{11,10},{13,12},{... | collective-permute-start | bytes 304136 | tf_op jit(solution)/shard_map/ppermute | solution.py:26
  99.2 11.5 %collective-permute-start.8 = (f32[3,32,8,2]{3,2,1,0:T(8,128)S(1)}, f32[3,32,8,2]{3,2,1,0:T(8,128)S(1)}, u32[]{:S(2)}, u32[]{:S(2)}) collective-permute-start(f32[3,32,8,2]{3,2,1,0:T(8,128)S(1)} %get-tuple-element.68), channel_id=1, source_target_pairs={{0,4},{4,8},{8,12},{12,16},{16,20},{20,24},{24,28},{1,5},{5,9},{9,... | collective-permute-start | bytes 18440 | tf_op jit(solution)/shard_map/ppermute | solution.py:23
  101.1 9.5 %collective-permute-start.9 = (f32[3,32,8,2]{3,2,1,0:T(8,128)S(1)}, f32[3,32,8,2]{3,2,1,0:T(8,128)S(1)}, u32[]{:S(2)}, u32[]{:S(2)}) collective-permute-start(f32[3,32,8,2]{3,2,1,0:T(8,128)S(1)} %get-tuple-element.69), channel_id=1, source_target_pairs={{4,0},{8,4},{12,8},{16,12},{20,16},{24,20},{28,24},{5,1},{9,5},{13... | collective-permute-start | bytes 18440 | tf_op jit(solution)/shard_map/ppermute | solution.py:26
  104.8 6.5 %collective-permute-start.10 = (f32[3,32,2,128]{3,2,1,0:T(2,128)S(1)}, f32[3,32,2,128]{3,2,1,0:T(2,128)S(1)}, u32[]{:S(2)}, u32[]{:S(2)}) collective-permute-start(f32[3,32,2,128]{3,2,1,0:T(2,128)S(1)} %get-tuple-element.66), channel_id=1, source_target_pairs={{0,1},{1,2},{2,3},{4,5},{5,6},{6,7},{8,9},{9,10},{10,11},{12,13},{... | collective-permute-start | bytes 294920 | tf_op jit(solution)/shard_map/ppermute | solution.py:23
  108.3 6.5 %collective-permute-start.11 = (f32[3,32,2,128]{3,2,1,0:T(2,128)S(1)}, f32[3,32,2,128]{3,2,1,0:T(2,128)S(1)}, u32[]{:S(2)}, u32[]{:S(2)}) collective-permute-start(f32[3,32,2,128]{3,2,1,0:T(2,128)S(1)} %get-tuple-element.67), channel_id=1, source_target_pairs={{1,0},{2,1},{3,2},{5,4},{6,5},{7,6},{9,8},{10,9},{11,10},{13,12},{... | collective-permute-start | bytes 294920 | tf_op jit(solution)/shard_map/ppermute | solution.py:26
  116.8 6.9 %collective-permute-start.29 = (f32[8,1]{1,0:T(8,128)S(1)}, f32[8,1]{1,0:T(8,128)S(1)}, u32[]{:S(2)}, u32[]{:S(2)}) collective-permute-start(f32[8,1]{1,0:T(8,128)S(1)} %get-tuple-element.98), channel_id=1, source_target_pairs={{0,4},{4,8},{8,12},{12,16},{16,20},{20,24},{24,28},{1,5},{5,9},{9,... | collective-permute-start | bytes 104 | tf_op jit(solution)/shard_map/ppermute | solution.py:23
  118.8 5.0 %collective-permute-start.28 = (f32[8,1]{1,0:T(8,128)S(1)}, f32[8,1]{1,0:T(8,128)S(1)}, u32[]{:S(2)}, u32[]{:S(2)}) collective-permute-start(f32[8,1]{1,0:T(8,128)S(1)} %get-tuple-element.99), channel_id=1, source_target_pairs={{4,0},{8,4},{12,8},{16,12},{20,16},{24,20},{28,24},{5,1},{9,5},{13... | collective-permute-start | bytes 104 | tf_op jit(solution)/shard_map/ppermute | solution.py:26
  123.8 11.4 %collective-permute-start.30 = (f32[1,130]{1,0:T(1,128)S(1)}, f32[1,130]{1,0:T(1,128)S(1)}, u32[]{:S(2)}, u32[]{:S(2)}) collective-permute-start(f32[1,130]{1,0:T(1,128)S(1)} %get-tuple-element.90), channel_id=1, source_target_pairs={{1,0},{2,1},{3,2},{5,4},{6,5},{7,6},{9,8},{10,9},{11,10},{13,12},{... | collective-permute-start | bytes 1568 | tf_op jit(solution)/shard_map/ppermute | solution.py:26
  126.2 9.1 %collective-permute-start.31 = (f32[1,130]{1,0:T(1,128)S(1)}, f32[1,130]{1,0:T(1,128)S(1)}, u32[]{:S(2)}, u32[]{:S(2)}) collective-permute-start(f32[1,130]{1,0:T(1,128)S(1)} %get-tuple-element.91), channel_id=1, source_target_pairs={{0,1},{1,2},{2,3},{4,5},{5,6},{6,7},{8,9},{9,10},{10,11},{12,13},{... | collective-permute-start | bytes 1568 | tf_op jit(solution)/shard_map/ppermute | solution.py:23
  129.7 9.1 %collective-permute-start.16 = (f32[3,32,8,2]{3,2,1,0:T(8,128)S(1)}, f32[3,32,8,2]{3,2,1,0:T(8,128)S(1)}, u32[]{:S(2)}, u32[]{:S(2)}) collective-permute-start(f32[3,32,8,2]{3,2,1,0:T(8,128)S(1)} %get-tuple-element.64), channel_id=1, source_target_pairs={{0,4},{4,8},{8,12},{12,16},{16,20},{20,24},{24,28},{1,5},{5,9},{9,... | collective-permute-start | bytes 18440 | tf_op jit(solution)/shard_map/ppermute | solution.py:23
  132.8 9.4 %collective-permute-start.17 = (f32[3,32,8,2]{3,2,1,0:T(8,128)S(1)}, f32[3,32,8,2]{3,2,1,0:T(8,128)S(1)}, u32[]{:S(2)}, u32[]{:S(2)}) collective-permute-start(f32[3,32,8,2]{3,2,1,0:T(8,128)S(1)} %get-tuple-element.65), channel_id=1, source_target_pairs={{4,0},{8,4},{12,8},{16,12},{20,16},{24,20},{28,24},{5,1},{9,5},{13... | collective-permute-start | bytes 18440 | tf_op jit(solution)/shard_map/ppermute | solution.py:26
  143.0 9.4 %collective-permute-start.18 = (f32[3,32,2,132]{3,2,1,0:T(2,128)S(1)}, f32[3,32,2,132]{3,2,1,0:T(2,128)S(1)}, u32[]{:S(2)}, u32[]{:S(2)}) collective-permute-start(f32[3,32,2,132]{3,2,1,0:T(2,128)S(1)} %get-tuple-element.45), channel_id=1, source_target_pairs={{0,1},{1,2},{2,3},{4,5},{5,6},{6,7},{8,9},{9,10},{10,11},{12,13},{... | collective-permute-start | bytes 304136 | tf_op jit(solution)/shard_map/ppermute | solution.py:23
  144.9 9.4 %collective-permute-start.19 = (f32[3,32,2,132]{3,2,1,0:T(2,128)S(1)}, f32[3,32,2,132]{3,2,1,0:T(2,128)S(1)}, u32[]{:S(2)}, u32[]{:S(2)}) collective-permute-start(f32[3,32,2,132]{3,2,1,0:T(2,128)S(1)} %get-tuple-element.46), channel_id=1, source_target_pairs={{1,0},{2,1},{3,2},{5,4},{6,5},{7,6},{9,8},{10,9},{11,10},{13,12},{... | collective-permute-start | bytes 304136 | tf_op jit(solution)/shard_map/ppermute | solution.py:26
  (9 other events, 50.2 us)
where the time goes:
time: 161 us; the launch traced here: 158 us
  starting transfers between devices  92.8 us (58%)
  waiting for transfers between devices  43.8 us (27%)
  other arithmetic  12 us (7%)
  local copies, waits for them, and re-layouts  7.8 us (5%)
    ppermute x16, starting transfers between devices, extended(): lax.ppermute(lax.slice_in_dim(block, block.shape[dim] - width, None, axis...  47.2 us
    ppermute x16, starting transfers between devices, extended(): lax.ppermute(lax.slice_in_dim(block, 0, width, axis=dim), axis, backward)  45.6 us
    ppermute x16, waiting for transfers between devices, extended(): lax.ppermute(lax.slice_in_dim(block, 0, width, axis=dim), axis, backward)  23.9 us
    ppermute x16, waiting for transfers between devices, extended(): lax.ppermute(lax.slice_in_dim(block, block.shape[dim] - width, None, axis...  19.9 us
    unnamed x27, local copies, waits for them, and re-layouts  3.35 us
  transfers between devices with their start and end apart: 32, of which 15 were waited for; matrix products, arithmetic and copies ran while one was open for 3% of the time, Pallas kernels for 0%

commit v1 on v0

v1 whole, which is shorter than its diff:
```python
import jax
import jax.numpy as jnp
from jax import lax
from jax.experimental import pallas as pl
from jax.experimental.pallas import tpu as pltpu
from jax.sharding import PartitionSpec as P

RATE = 0.3 / 24.0
OCEAN_RATE = 0.3
UPLIFT = 0.5
LOADING = 0.5
VISCOUS = 0.1

ROWS = 8
LANES = 128
EDGE = 8
GROUP = 2 * EDGE
PACK = LANES // GROUP

LEVEL, FLUX_X, FLUX_Y, DEPTH, FLOOR, WET = range(6)
LAME, SHEAR, BUOY = 9, 10, 11
FIELDS = 12


def rolled(x, shift, axis):
    shift %= x.shape[axis]
    return x if shift == 0 else pltpu.roll(x, shift, axis)


def iotas():
    sub = lax.broadcasted_iota(jnp.int32, (ROWS, LANES), 0)
    lane = lax.broadcasted_iota(jnp.int32, (ROWS, LANES), 1)
    return sub, lane


def plane(ref, index):
    return ref[index * ROWS : (index + 1) * ROWS, :]


def row(ref, index):
    return ref[index : index + 1, :]


def store(ref, index, value):
    ref[index * ROWS : (index + 1) * ROWS, :] = value


def near_far(a, b, c, d):
    return 27.0 * (a - b) - (c - d)


class Grid:
    def __init__(self, depth):
        self.depth = depth
        self.per = depth // PACK
        self.planes = depth + 2 * self.per
        self.sub, self.lane = iotas()
        self.inner = self.lane % GROUP
        self.first = self.inner < EDGE
        self.group = self.lane // GROUP
        self.zero = jnp.zeros((ROWS, LANES), jnp.float32)

    def beside(self, field, which):
        left = field(self.depth + which)
        right = field(self.depth + self.per + which)
        return jnp.where(self.first, left, right)

    def besides(self, field):
        return [self.beside(field, which) for which in range(self.per)]

    def edge_of(self, besides, p):
        if p >= self.depth:
            return None
        return rolled(besides[p % self.per], LANES - EDGE - GROUP * (p // self.per), 1)

    def along(self, x, offset, edge):
        if edge is not None:
            lane = self.lane
            keep = {-1: lane == LANES - 1, -2: lane >= LANES - 2, 1: lane == 0, 2: lane <= 1}[offset]
            x = jnp.where(keep, edge, x)
        return rolled(x, -offset, 1)

    def across(self, x, offset, low=None, high=None):
        sub = self.sub
        out = rolled(x, -offset, 0)
        none = self.zero
        low = low or (none, none)
        high = high or (none, none)
        if offset == -1:
            return jnp.where(sub == 0, low[0], out)
        if offset == -2:
            return jnp.where(sub == 0, low[1], jnp.where(sub == 1, low[0], out))
        if offset == 1:
            return jnp.where(sub == ROWS - 1, high[0], out)
        return jnp.where(sub == ROWS - 1, high[1], jnp.where(sub == ROWS - 2, high[0], out))

    def down(self, field, p, offset):
        depth, per = self.depth, self.per
        if p < depth:
            q = p + offset
            return field(q) if 0 <= q < depth else self.zero
        side, which = divmod(p - depth, per)
        base = depth + side * per
        at = which + offset
        if 0 <= at < per:
            return field(base + at)
        if at >= per:
            x = rolled(field(base + at - per), -GROUP, 1)
            return jnp.where(self.lane < LANES - GROUP, x, 0.0)
        x = rolled(field(base + at + per), GROUP, 1)
        return jnp.where(self.lane >= GROUP, x, 0.0)

    def fx(self, x, edge):
        return near_far(self.along(x, 1, edge), x, self.along(x, 2, edge), self.along(x, -1, edge))

    def bx(self, x, edge):
        return near_far(x, self.along(x, -1, edge), self.along(x, 1, edge), self.along(x, -2, edge))

    def fy(self, x, low=None, high=None):
        return near_far(
            self.across(x, 1, low, high), x, self.across(x, 2, low, high), self.across(x, -1, low, high)
        )

    def by(self, x, low=None, high=None):
        return near_far(
            x, self.across(x, -1, low, high), self.across(x, 1, low, high), self.across(x, -2, low, high)
        )

    def fz(self, field, p):
        return near_far(
            self.down(field, p, 1), field(p), self.down(field, p, 2), self.down(field, p, -1)
        )

    def bz(self, field, p):
        return near_far(
            field(p), self.down(field, p, -1), self.down(field, p, 1), self.down(field, p, -2)
        )

    def every_group(self, x):
        shift = GROUP
        while shift < LANES:
            x = x + rolled(x, shift, 1)
            shift *= 2
        return x


def edges_kernel(depth, wave, lame, shear, buoy, ocean, deep, floor, wet, own, own_ocean, to_right, to_left):
    grid = Grid(depth)
    per = grid.per
    masks = [grid.group == g for g in range(PACK)]

    def collect(at):
        out = grid.zero
        for g in range(PACK):
            out = jnp.where(masks[g], rolled(at(g), EDGE + GROUP * g, 1), out)
        return out

    def both(index, one, two):
        store(to_right, index, jnp.where(grid.first, one, rolled(two, EDGE, 1)))
        store(to_left, index, jnp.where(grid.first, rolled(two, -EDGE, 1), one))

    sources = [(wave, f * depth) for f in range(9)] + [(lame, 0), (shear, 0), (buoy, 0)]
    for f in range(0, FIELDS, 2):
        for j in range(per):
            pair = []
            for h in (f, f + 1):
                ref, base = sources[h]
                pair.append(collect(lambda g: plane(ref, base + per * g + j)))
                store(own, h * per + j, pair[-1])
            both((f // 2) * per + j, *pair)
    flat = [plane(ocean, k) for k in range(3)] + [deep[...]]
    flat += [floor[...].astype(jnp.float32), wet[...].astype(jnp.float32)]
    for f in range(0, 6, 2):
        pair = []
        for h in (f, f + 1):
            pair.append(collect(lambda g: flat[h]))
            store(own_ocean, h, pair[-1])
        both((FIELDS // 2) * per + f // 2, *pair)


def partial_velocity(grid, stress, speed, buoy, out):
    sxx, syy, szz, sxy, sxz, syz = stress
    b_xx, b_xy, b_xz = grid.besides(sxx), grid.besides(sxy), grid.besides(sxz)
    for p in list(range(grid.depth, grid.planes)) + list(range(grid.depth)):
        rate = RATE * buoy(p)
        xy, yz, xz = sxy(p), syz(p), sxz(p)
        e_xy, e_xz = grid.edge_of(b_xy, p), grid.edge_of(b_xz, p)
        ax = grid.fx(sxx(p), grid.edge_of(b_xx, p)) + grid.by(xy) + grid.bz(sxz, p)
        store(out, p, speed[0](p) + rate * ax)
        ay = grid.bx(xy, e_xy) + grid.fy(syy(p)) + grid.bz(syz, p)
        store(out, grid.planes + p, speed[1](p) + rate * ay)
        az = grid.bx(xz, e_xz) + grid.by(yz) + grid.fz(szz, p)
        store(out, 2 * grid.planes + p, speed[2](p) + rate * az)


def partial_level(grid, flat, out):
    for k in range(3):
        x, y, wet = flat(FLUX_X, k), flat(FLUX_Y, k), flat(WET, k)
        edge = ocean_edge(grid, lambda q: flat(FLUX_X, q), k)
        spread = 0.5 * (grid.along(x, 1, edge) - grid.along(x, -1, edge))
        spread = spread + 0.5 * (grid.across(y, 1) - grid.across(y, -1))
        store(out, k, flat(LEVEL, k) - OCEAN_RATE * (wet * spread))


def ocean_edge(grid, at, k):
    if k:
        return None
    return rolled(jnp.where(grid.first, at(1), at(2)), LANES - EDGE, 1)


TO_HIGH = ((0, 7), (1, 6), (1, 7), (2, 7), (6, 6), (6, 7), (4, 7), (8, 6), (8, 7))
TO_LOW = ((0, 0), (0, 1), (1, 0), (2, 0), (2, 1), (6, 0), (4, 0), (4, 1), (8, 0))


def send_rows(grid, rows, take, level, flat, edge, out):
    at = 0
    for field, which in rows:
        for piece in take(field, which):
            out[at : at + piece.shape[0], :] = piece
            at += piece.shape[0]
    for which in (None, WET, FLOOR, FLUX_X, FLUX_Y):
        for k in range(3):
            source = level if which is None else flat[which]
            base = k * ROWS if which is None else flat[which, "at"] + k * ROWS
            out[at : at + 1, :] = row(source, base + edge)
            at += 1
    out[at : at + 1, :] = jnp.zeros((1, LANES), jnp.float32)


def start_kernel(
    depth, wave, buoy, own, own_ocean, ocean, deep, floor, wet, left, right,
    windows, flat, partial, level, high, low,
):
    grid = Grid(depth)
    per, planes = grid.per, grid.planes
    for f in range(FIELDS):
        for j in range(per):
            mine = plane(own, f * per + j)
            a = plane(left, (f // 2) * per + j)
            b = plane(right, (f // 2) * per + j)
            if f % 2:
                a, b = rolled(a, -EDGE, 1), rolled(b, EDGE, 1)
            store(windows, f * 2 * per + j, jnp.where(grid.first, a, mine))
            store(windows, f * 2 * per + per + j, jnp.where(grid.first, mine, b))
    whole = [plane(ocean, k) for k in range(3)] + [deep[...]]
    whole += [floor[...].astype(jnp.float32), wet[...].astype(jnp.float32)]
    for f in range(6):
        mine = plane(own_ocean, f)
        a = plane(left, (FIELDS // 2) * per + f // 2)
        b = plane(right, (FIELDS // 2) * per + f // 2)
        if f % 2:
            a, b = rolled(a, -EDGE, 1), rolled(b, EDGE, 1)
        store(flat, 3 * f, whole[f])
        store(flat, 3 * f + 1, jnp.where(grid.first, a, mine))
        store(flat, 3 * f + 2, jnp.where(grid.first, mine, b))

    def field(f):
        ref, base = (buoy, 0) if f == BUOY else (wave, f * depth)
        return lambda p: plane(ref, base + p) if p < depth else plane(windows, f * 2 * per + p - depth)

    partial_velocity(grid, [field(3 + f) for f in range(6)], [field(f) for f in range(3)], field(BUOY), partial)
    partial_level(grid, lambda f, k: plane(flat, 3 * f + k), level)

    def take(f, which):
        if f < 3:
            return [partial[pl.ds(f * planes * ROWS + which, planes, stride=ROWS), :]]
        ref, base = (buoy, 0) if f == BUOY else (wave, f * depth)
        return [
            ref[pl.ds(base * ROWS + which, depth, stride=ROWS), :],
            windows[pl.ds(f * 2 * per * ROWS + which, 2 * per, stride=ROWS), :],
        ]

    flats = {}
    for which in (WET, FLOOR, FLUX_X, FLUX_Y):
        flats[which] = flat
        flats[which, "at"] = 3 * which * ROWS
    send_rows(grid, TO_HIGH + ((BUOY, 6), (BUOY, 7)), take, level, flats, 7, high)
    send_rows(grid, TO_LOW + ((BUOY, 0), (BUOY, 1)), take, level, flats, 0, low)


def finish(grid, stress_rows, buoy, partial, level, now, fixed, low, high, low_buoy, high_buoy, halo, corr, speed, new):
    depth, per, planes = grid.depth, grid.per, grid.planes

    def piece(ref, index, part):
        start, size = part
        return ref[index * planes + start : index * planes + start + size, :]

    for part in ((0, depth), (depth, 2 * per)):
        start, size = part
        lo = lambda index: piece(low, index, part)
        hi = lambda index: piece(high, index, part)
        own = lambda f, which: stress_rows(f, which, part)

        def put(ref, index, value):
            ref[index * planes + start : index * planes + start + size, :] = value

        b1 = RATE * piece(low_buoy, 10, part)
        b2 = RATE * piece(low_buoy, 9, part)
        b8 = RATE * piece(high_buoy, 9, part)
        b9 = RATE * piece(high_buoy, 10, part)
        xy0, xy6, xy7 = own(6, 0), own(6, 6), own(6, 7)
        yz0, yz6, yz7 = own(8, 0), own(8, 6), own(8, 7)
        yy0, yy1, yy7 = own(4, 0), own(4, 1), own(4, 7)
        put(halo, 0, lo(0) - b1 * xy0)
        put(halo, 1, hi(0) + b8 * (xy6 - 27.0 * xy7))
        put(halo, 2, hi(1) + b9 * xy7)
        put(halo, 3, lo(2) + b1 * (27.0 * yy0 - yy1))
        put(halo, 4, lo(1) - b2 * yy0)
        put(halo, 5, hi(2) + b8 * yy7)
        put(halo, 6, lo(3) - b1 * yz0)
        put(halo, 7, hi(3) + b8 * (yz6 - 27.0 * yz7))
        put(halo, 8, hi(4) + b9 * yz7)
        put(corr, 0, lo(4) - 27.0 * lo(5))
        put(corr, 1, lo(5))
        put(corr, 2, -hi(5))
        put(corr, 3, lo(6))
        put(corr, 4, -hi(6))
        put(corr, 5, 27.0 * hi(6) - hi(7))
        put(corr, 6, lo(7) - 27.0 * lo(8))
        put(corr, 7, lo(8))
        put(corr, 8, -hi(8))

    sub = grid.sub
    floor = [fixed(FLOOR, k) for k in range(3)]
    sums = [grid.zero] * 3
    depths = grid.group.astype(jnp.float32) * per
    for p in range(planes):
        rate = RATE * buoy(p)
        c = [row(corr, index * planes + p) for index in range(9)]
        pick = lambda at, r0, r1, r2: jnp.where(
            sub == at[0], r0, jnp.where(sub == at[1], r1, jnp.where(sub == at[2], r2, 0.0))
        )
        store(speed, p, plane(partial, p) + rate * pick((0, 1, 7), c[0], c[1], c[2]))
        store(speed, planes + p, plane(partial, planes + p) + rate * pick((0, 6, 7), c[3], c[4], c[5]))
        vz = plane(partial, 2 * planes + p) + rate * pick((0, 1, 7), c[6], c[7], c[8])
        store(speed, 2 * planes + p, vz)
        if p < depth:
            k, at = 0, float(p)
        else:
            side, which = divmod(p - depth, per)
            k, at = 1 + side, depths + float(which)
        sums[k] = jnp.where(floor[k] == at, vz, sums[k])
    sums[1] = grid.every_group(sums[1])
    sums[2] = grid.every_group(sums[2])

    tail = low.shape[0] - 16
    tail_high = high.shape[0] - 16
    ends = []
    for message, base, index, own_row, sign in ((low, tail, 6, 0, -1.0), (high, tail_high, 7, 7, 1.0)):
        lines = lambda which, k, message=message, base=base: row(message, base + 3 * which + k)
        zs = lax.broadcasted_iota(jnp.int32, (depth, LANES), 0).astype(jnp.float32)
        main = halo[index * planes : index * planes + depth, :]
        floors = [jnp.sum(jnp.where(lines(2, 0) == zs, main, 0.0), axis=0, keepdims=True)]
        side = halo[index * planes + depth : (index + 1) * planes, :]
        half = lax.broadcasted_iota(jnp.int32, (2 * per, LANES), 0)
        group = (lax.broadcasted_iota(jnp.int32, (2 * per, LANES), 1) // GROUP) * per
        where = jnp.where(half < per, lines(2, 1), lines(2, 2))
        side = jnp.where(where == (group + half % per).astype(jnp.float32), side, 0.0)
        side = grid.every_group(side)
        floors.append(jnp.sum(jnp.where(half < per, side, 0.0), axis=0, keepdims=True))
        floors.append(jnp.sum(jnp.where(half < per, 0.0, side), axis=0, keepdims=True))
        end = []
        for k in range(3):
            mine = now(FLUX_Y, k)[own_row : own_row + 1, :]
            wet = lines(1, k)
            end.append(lines(0, k) + wet * (UPLIFT * floors[k] + (sign * 0.5 * OCEAN_RATE) * mine))
        ends.append((end, lines))
    (low_level, low_line), (high_level, high_line) = ends

    levels = []
    for k in range(3):
        wet = fixed(WET, k)
        beside = jnp.where(sub == 0, low_line(4, k), jnp.where(sub == ROWS - 1, -high_line(4, k), 0.0))
        levels.append(
            plane(level, k) + wet * (UPLIFT * sums[k] + (0.5 * OCEAN_RATE) * beside)
        )
        new(LEVEL, k, levels[k])
    for k in range(3):
        wet, deep = fixed(WET, k), fixed(DEPTH, k)
        edge = ocean_edge(grid, lambda q: levels[q], k)
        slope_x = 0.5 * (grid.along(levels[k], 1, edge) - grid.along(levels[k], -1, edge))
        lo, hi = (low_level[k],), (high_level[k],)
        slope_y = 0.5 * (grid.across(levels[k], 1, lo, hi) - grid.across(levels[k], -1, lo, hi))
        for which, line, slope in ((FLUX_X, 3, slope_x), (FLUX_Y, 4, slope_y)):
            x = now(which, k)
            edge = ocean_edge(grid, lambda q: now(which, q), k)
            lo, hi = (low_line(line, k),), (high_line(line, k),)
            laplace = grid.along(x, 1, edge) + grid.along(x, -1, edge)
            laplace = laplace + grid.across(x, 1, lo, hi) + grid.across(x, -1, lo, hi) - 4.0 * x
            new(which, k, wet * (x - OCEAN_RATE * deep * slope + VISCOUS * laplace))
    return levels


def new_stress(grid, todo, stress, lame, shear, speed, halo, levels, fixed, out):
    depth, per, planes = grid.depth, grid.per, grid.planes
    vx, vy, vz = [lambda p, f=f: plane(speed, f * planes + p) for f in range(3)]
    b_x, b_y, b_z = grid.besides(vx), grid.besides(vy), grid.besides(vz)
    press = [LOADING * fixed(WET, k) * levels[k] for k in range(3)]
    floor = [fixed(FLOOR, k) for k in range(3)]
    depths = grid.group.astype(jnp.float32) * per
    for p in todo:
        h = [row(halo, index * planes + p) for index in range(9)]
        x, y, z = vx(p), vy(p), vz(p)
        e_x, e_y, e_z = [grid.edge_of(b, p) for b in (b_x, b_y, b_z)]
        strain_x = grid.bx(x, e_x)
        strain_y = grid.by(y, (h[3], h[4]), (h[5], h[5]))
        strain_z = grid.bz(vz, p)
        mu = RATE * shear(p)
        spread = (RATE * lame(p)) * (strain_x + strain_y + strain_z)
        two = mu + mu
        if p < depth:
            k, at = 0, float(p)
        else:
            side, which = divmod(p - depth, per)
            k, at = 1 + side, depths + float(which)
        out(0, p, stress[0](p) + (spread + two * strain_x))
        out(1, p, stress[1](p) + (spread + two * strain_y))
        out(2, p, stress[2](p) + (spread + two * strain_z) - jnp.where(floor[k] == at, press[k], 0.0))
        xy = grid.fy(x, (h[0], h[0]), (h[1], h[2])) + grid.fx(y, e_y)
        out(3, p, stress[3](p) + mu * xy)
        xz = grid.fz(vx, p) + grid.fx(z, e_z)
        out(4, p, stress[4](p) + mu * xz)
        yz = grid.fz(vy, p) + grid.fy(z, (h[6], h[6]), (h[7], h[8]))
        out(5, p, stress[5](p) + mu * yz)


def middle_kernel(
    depth, wave, lame, shear, buoy, windows, flat, partial, level, from_low, from_high,
    stress_out, ocean_out, partial_out, level_out, high, low,
    halo, corr, speed,
):
    grid = Grid(depth)
    per, planes = grid.per, grid.planes

    def field(f):
        refs = {LAME: lame, SHEAR: shear, BUOY: buoy}
        ref, base = (refs[f], 0) if f in refs else (wave, f * depth)
        return lambda p: plane(ref, base + p) if p < depth else plane(windows, f * 2 * per + p - depth)

    def stress_rows(f, which, part):
        if part[0] == 0:
            return wave[pl.ds(f * depth * ROWS + which, depth, stride=ROWS), :]
        return windows[pl.ds(f * 2 * per * ROWS + which, 2 * per, stride=ROWS), :]

    flats = lambda f, k: plane(flat, 3 * f + k)
    levels = finish(
        grid, stress_rows, field(BUOY), partial, level, flats, flats, from_low, from_high, from_low, from_high,
        halo, corr, speed, lambda which, k, value: store(ocean_out, 3 * which + k, value),
    )
    order = list(range(depth, planes)) + list(range(depth))
    new_stress(
        grid, order, [field(3 + f) for f in range(6)], field(LAME), field(SHEAR), speed, halo, levels, flats,
        lambda f, p, value: store(stress_out, f * planes + p, value),
    )
    stress = [lambda p, f=f: plane(stress_out, f * planes + p) for f in range(6)]
    speeds = [lambda p, f=f: plane(speed, f * planes + p) for f in range(3)]
    partial_velocity(grid, stress, speeds, field(BUOY), partial_out)
    both = lambda f, k: plane(flat if f >= DEPTH else ocean_out, 3 * f + k)
    partial_level(grid, both, level_out)

    def take(f, which):
        ref, f = (partial_out, f) if f < 3 else (stress_out, f - 3)
        return [ref[pl.ds(f * planes * ROWS + which, planes, stride=ROWS), :]]

    rows_of = {}
    for which in (WET, FLOOR, FLUX_X, FLUX_Y):
        rows_of[which] = flat if which >= DEPTH else ocean_out
        rows_of[which, "at"] = 3 * which * ROWS
    send_rows(grid, TO_HIGH, take, level_out, rows_of, 7, high)
    send_rows(grid, TO_LOW, take, level_out, rows_of, 0, low)


def last_kernel(
    depth, lame, shear, buoy, windows, flat, stress_in, ocean, partial, level, low_buoy, high_buoy, from_low, from_high,
    wave_out, ocean_out,
    halo, corr, speed,
):
    grid = Grid(depth)
    per, planes = grid.per, grid.planes

    def field(f):
        ref = {LAME: lame, SHEAR: shear, BUOY: buoy}[f]
        return lambda p: plane(ref, p) if p < depth else plane(windows, f * 2 * per + p - depth)

    def stress_rows(f, which, part):
        start, size = part
        return stress_in[pl.ds(((f - 3) * planes + start) * ROWS + which, size, stride=ROWS), :]

    def new(which, k, value):
        if k == 0:
            store(ocean_out, which, value)

    fixed = lambda f, k: plane(flat, 3 * f + k)
    now = lambda f, k: plane(ocean, 3 * f + k)
    levels = finish(
        grid, stress_rows, field(BUOY), partial, level, now, fixed, from_low, from_high, low_buoy, high_buoy,
        halo, corr, speed, new,
    )
    stress = [lambda p, f=f: plane(stress_in, f * planes + p) for f in range(6)]
    new_stress(
        grid, list(range(depth)), stress, field(LAME), field(SHEAR), speed, halo, levels, fixed,
        lambda f, p, value: store(wave_out, (3 + f) * depth + p, value),
    )
    for f in range(3):
        for p in range(depth):
            store(wave_out, f * depth + p, plane(speed, f * planes + p))


def call(kernel, shapes, scratch, *arguments):
    vmem = pl.BlockSpec(memory_space=pltpu.VMEM)
    return pl.pallas_call(
        kernel,
        out_shape=[jax.ShapeDtypeStruct((n, LANES), jnp.float32) for n in shapes],
        in_specs=[vmem] * len(arguments),
        out_specs=[vmem] * len(shapes),
        scratch_shapes=[pltpu.VMEM((n, LANES), jnp.float32) for n in scratch],
        compiler_params=pltpu.CompilerParams(vmem_limit_bytes=24 * 1024 * 1024),
    )(*arguments)


def exchange(axis, forth, back):
    count = lax.axis_size(axis)
    forward = [(i, i + 1) for i in range(count - 1)]
    backward = [(i + 1, i) for i in range(count - 1)]
    return lax.ppermute(forth, axis, forward), lax.ppermute(back, axis, backward)


def local(wave_fields, lame_lambda, shear_modulus, buoyancy, ocean_state, water_depth, seafloor_index, wet_mask):
    depth = wave_fields.shape[1]
    per = depth // PACK
    planes = depth + 2 * per
    wave = wave_fields.reshape(-1, LANES)
    lame = lame_lambda.reshape(-1, LANES)
    shear = shear_modulus.reshape(-1, LANES)
    buoy = buoyancy.reshape(-1, LANES)
    ocean = ocean_state.reshape(-1, LANES)

    def bind(kernel):
        return lambda *refs: kernel(depth, *refs)

    edge = (FIELDS // 2 * per + 3) * ROWS
    own, own_ocean, to_right, to_left = call(
        bind(edges_kernel), [FIELDS * per * ROWS, 6 * ROWS, edge, edge], [],
        wave, lame, shear, buoy, ocean, water_depth, seafloor_index, wet_mask,
    )
    left, right = exchange("gx", to_right, to_left)
    first = 11 * planes + 16
    later = 9 * planes + 16
    windows, flat, partial, level, high, low = call(
        bind(start_kernel),
        [FIELDS * 2 * per * ROWS, 18 * ROWS, 3 * planes * ROWS, 3 * ROWS, first, first], [],
        wave, buoy, own, own_ocean, ocean, water_depth, seafloor_index, wet_mask, left, right,
    )
    low1, high1 = exchange("gy", high, low)
    scratch = [9 * planes, 9 * planes, 3 * planes * ROWS]
    stress, ocean1, partial, level, high, low = call(
        bind(middle_kernel),
        [6 * planes * ROWS, 9 * ROWS, 3 * planes * ROWS, 3 * ROWS, later, later], scratch,
        wave, lame, shear, buoy, windows, flat, partial, level, low1, high1,
    )
    low2, high2 = exchange("gy", high, low)
    wave_out, ocean_out = call(
        bind(last_kernel), [wave.shape[0], ocean.shape[0]], scratch,
        lame, shear, buoy, windows, flat, stress, ocean1, partial, level, low1, high1, low2, high2,
    )
    return wave_out.reshape(wave_fields.shape), ocean_out.reshape(ocean_state.shape)


def solution(mesh):
    in_specs = (
        P(None, None, "gy", "gx"),
        P(None, "gy", "gx"),
        P(None, "gy", "gx"),
        P(None, "gy", "gx"),
        P(None, "gy", "gx"),
        P("gy", "gx"),
        P("gy", "gx"),
        P("gy", "gx"),
    )
    out_specs = (P(None, None, "gy", "gx"), P(None, "gy", "gx"))
    return jax.shard_map(local, mesh=mesh, in_specs=in_specs, out_specs=out_specs, check_vma=False)
```

time: 161 us -> 54.4 us (0.34); the launches traced: 158 us -> 53.5 us
  starting transfers between devices: 92.8 us -> 17.4 us
  waiting for transfers between devices: 43.8 us -> 16.2 us
  Pallas kernels: 0 us -> 12.4 us
  other arithmetic: 12 us -> 0 us
    ppermute x32 -> x6, starting transfers between devices: 92.8 us -> 17.4 us  [the longest x3 9.02 us: exchange(): lax.ppermute(forth, axis, forward)]
    ppermute x32 -> x6, waiting for transfers between devices: 43.8 us -> 16.2 us  [the longest x3 9.35 us: exchange(): lax.ppermute(back, axis, backward)]
    pallas_call x0 -> x4, Pallas kernels: none -> 12.4 us  [call(): pl.pallas_call(kernel, out_shape=[jax.ShapeDtypeStruct((n, LANES), jnp.fl...]
    unnamed x27 -> x30, local copies, waits for them, and re-layouts: 3.35 us -> 6.78 us
    concatenate x8 -> x0, other arithmetic: 3.41 us -> none  [the longest x6 2.46 us: extended(): block = jnp.concatenate([low, block, high], axis=dim)]
    unnamed x9 -> x0, other arithmetic: 2.57 us -> none
    squeeze x13 -> x0, local copies, waits for them, and re-layouts: 2.4 us -> none  [the longest x1 1.21 us: local(): stress[2]]
    slice x7 -> x0, other arithmetic: 1.74 us -> none  [the longest x5 1.59 us: extended(): lax.slice_in_dim(block, block.shape[dim] - width, None, axis=dim)]
  transfers between devices with their start and end apart: 32 -> 6, of which waited for: 15 -> 6; matrix products, arithmetic and copies ran while one was open for 3% -> 0% of each run, Pallas kernels for 0% -> 0%
where the time goes in v1:
time: 54.4 us; the launch traced here: 53.5 us
  starting transfers between devices  17.4 us (32%)
  waiting for transfers between devices  16.2 us (30%)
  Pallas kernels  12.4 us (23%)
  local copies, waits for them, and re-layouts  6.78 us (12%)
  between operations  0.74 us (1%)
    pallas_call x4, Pallas kernels, call(): pl.pallas_call(kernel, out_shape=[jax.ShapeDtypeStruct((n, LANES), jnp.fl...  12.4 us
    ppermute x3, waiting for transfers between devices, exchange(): lax.ppermute(back, axis, backward)  9.35 us
    ppermute x3, starting transfers between devices, exchange(): lax.ppermute(forth, axis, forward)  9.02 us
    ppermute x3, starting transfers between devices, exchange(): lax.ppermute(back, axis, backward)  8.38 us
    ppermute x3, waiting for transfers between devices, exchange(): lax.ppermute(forth, axis, forward)  6.82 us
    unnamed x30, local copies, waits for them, and re-layouts  6.78 us
  transfers between devices with their start and end apart: 6, of which 6 were waited for; matrix products, arithmetic and copies ran while one was open for 0% of the time, Pallas kernels for 0%

profile of v1, /device:TPU:10, one launch (start us, length us, event | category | flops | bytes accessed | tf_op | source)
XLA Modules:
  0.0 53.5 jit_solution(9923903101023138236)
XLA Ops:
  0.6 0.0 copy-start.12
  0.6 0.0 copy-start.10
  0.7 0.0 copy-start
  0.7 1.3 %copy-done = f32[9,32,8,128]{3,2,1,0:T(8,128)S(1)} copy-done((f32[9,32,8,128]{3,2,1,0:T(8,128)S(1)}, f32[9,32,8,128]{3,2,1,0:T(8,128)}, u32[]{:S(2)}) %copy-start) | copy-done | bytes 1179672
  1.9 0.9 %copy-done.1 = f32[32,8,128]{2,1,0:T(8,128)S(1)} copy-done((f32[32,8,128]{2,1,0:T(8,128)S(1)}, f32[32,8,128]{2,1,0:T(8,128)}, u32[]{:S(2)}) %copy-start.1) | copy-done | bytes 131096
  2.8 0.9 %copy-done.3 = f32[32,8,128]{2,1,0:T(8,128)S(1)} copy-done((f32[32,8,128]{2,1,0:T(8,128)S(1)}, f32[32,8,128]{2,1,0:T(8,128)}, u32[]{:S(2)}) %copy-start.3) | copy-done | bytes 131096
  3.7 0.9 %copy-done.5 = f32[32,8,128]{2,1,0:T(8,128)S(1)} copy-done((f32[32,8,128]{2,1,0:T(8,128)S(1)}, f32[32,8,128]{2,1,0:T(8,128)}, u32[]{:S(2)}) %copy-start.5) | copy-done | bytes 131096
  4.7 0.7 %copy-done.7 = f32[3,8,128]{2,1,0:T(8,128)S(1)} copy-done((f32[3,8,128]{2,1,0:T(8,128)S(1)}, f32[3,8,128]{2,1,0:T(8,128)}, u32[]{:S(2)}) %copy-start.7) | copy-done | bytes 12312
  5.4 0.7 %copy-done.9 = f32[8,128]{1,0:T(8,128)S(1)} copy-done((f32[8,128]{1,0:T(8,128)S(1)}, f32[8,128]{1,0:T(8,128)}, u32[]{:S(2)}) %copy-start.9) | copy-done | bytes 4120
  6.0 0.7 %copy-done.11 = s32[8,128]{1,0:T(8,128)S(1)} copy-done((s32[8,128]{1,0:T(8,128)S(1)}, s32[8,128]{1,0:T(8,128)}, u32[]{:S(2)}) %copy-start.11) | copy-done | bytes 4120
  6.7 0.7 %copy-done.13 = s32[8,128]{1,0:T(8,128)S(1)} copy-done((s32[8,128]{1,0:T(8,128)S(1)}, s32[8,128]{1,0:T(8,128)}, u32[]{:S(2)}) %copy-start.13) | copy-done | bytes 4120
  7.4 1.9 %shard_map.95 = (f32[384,128]{1,0:T(8,128)S(1)}, f32[48,128]{1,0:T(8,128)S(1)}, f32[216,128]{1,0:T(8,128)S(1)}, f32[216,128]{1,0:T(8,128)S(1)}) custom-call(f32[2304,128]{1,0:T(8,128)S(1)} %bitcast.7, f32[256,128]{1,0:T(8,128)S(1)} %bitcast.14, f32[256,128]{1,0:T(8,128)S(1)} %bitcast.17, f32[256,128]{1,0:T(8,128)S(1)} %bitcast.10, f32[24,128]{1,0:T(8,128)S(1)} %bitcast.20, ...), custom_call_target="tpu_custom_call" | custom-call | tf_op jit(solution)/shard_map/pallas_call | solution.py:511
  9.3 2.0 %collective-permute-start = (f32[216,128]{1,0:T(8,128)S(1)}, f32[216,128]{1,0:T(8,128)S(1)}, u32[]{:S(2)}, u32[]{:S(2)}) collective-permute-start(f32[216,128]{1,0:T(8,128)S(1)} %get-tuple-element.22), channel_id=1, source_target_pairs={{0,4},{4,8},{8,12},{12,16},{16,20},{20,24},{24,28},{1,5},{5,9},{9,... | collective-permute-start | bytes 331784 | tf_op jit(solution)/shard_map/ppermute | solution.py:525
  11.4 3.6 %collective-permute-start.1 = (f32[216,128]{1,0:T(8,128)S(1)}, f32[216,128]{1,0:T(8,128)S(1)}, u32[]{:S(2)}, u32[]{:S(2)}) collective-permute-start(f32[216,128]{1,0:T(8,128)S(1)} %get-tuple-element.23), channel_id=1, source_target_pairs={{4,0},{8,4},{12,8},{16,12},{20,16},{24,20},{28,24},{5,1},{9,5},{13... | collective-permute-start | bytes 331784 | tf_op jit(solution)/shard_map/ppermute | solution.py:525
  15.1 0.5 collective-permute-done.refs_8_
  15.5 1.8 %collective-permute-done.1.refs_9_ = f32[216,128]{1,0:T(8,128)S(1)} collective-permute-done((f32[216,128]{1,0:T(8,128)S(1)}, f32[216,128]{1,0:T(8,128)S(1)}, u32[]{:S(2)}, u32[]{:S(2)}) %collective-permute-start.1) | collective-permute-done | bytes 110624 | tf_op jit(solution)/shard_map/ppermute | solution.py:525
  17.4 0.0 copy-done.12
  17.4 0.0 copy-done.10
  17.4 0.0 copy-done.2
  17.4 0.0 copy-done.8
  17.4 0.0 copy-done.14
  17.4 2.5 %shard_map.96 = (f32[768,128]{1,0:T(8,128)S(1)}, f32[144,128]{1,0:T(8,128)S(1)}, f32[960,128]{1,0:T(8,128)S(1)}, f32[24,128]{1,0:T(8,128)S(1)}, f32[456,128]{1,0:T(8,128)S(1)}, /*index=5*/f32[456,128]{1,0:T(8,128)S(1)}) custom-call(f32[2304,128]{1,0:T(8,128)S(1)} %bitcast.8, f32[256,128]{1,0:T(8,128)S(1)} %bitcast.11, ...), custom_call_target="tpu_custom_call" | custom-call | tf_op jit(solution)/shard_map/pallas_call | solution.py:511
  19.9 3.5 %collective-permute-start.2 = (f32[456,128]{1,0:T(8,128)S(1)}, f32[456,128]{1,0:T(8,128)S(1)}, u32[]{:S(2)}, u32[]{:S(2)}) collective-permute-start(f32[456,128]{1,0:T(8,128)S(1)} %get-tuple-element.28), channel_id=1, source_target_pairs={{0,1},{1,2},{2,3},{4,5},{5,6},{6,7},{8,9},{9,10},{10,11},{12,13},{... | collective-permute-start | bytes 700424 | tf_op jit(solution)/shard_map/ppermute | solution.py:525
  23.4 2.4 %collective-permute-start.3 = (f32[456,128]{1,0:T(8,128)S(1)}, f32[456,128]{1,0:T(8,128)S(1)}, u32[]{:S(2)}, u32[]{:S(2)}) collective-permute-start(f32[456,128]{1,0:T(8,128)S(1)} %get-tuple-element.29), channel_id=1, source_target_pairs={{1,0},{2,1},{3,2},{5,4},{6,5},{7,6},{9,8},{10,9},{11,10},{13,12},{... | collective-permute-start | bytes 700424 | tf_op jit(solution)/shard_map/ppermute | solution.py:525
  25.8 2.9 %collective-permute-done.2.refs_8_.refs_9_ = f32[456,128]{1,0:T(8,128)S(1)} collective-permute-done((f32[456,128]{1,0:T(8,128)S(1)}, f32[456,128]{1,0:T(8,128)S(1)}, u32[]{:S(2)}, u32[]{:S(2)}) %collective-permute-start.2) | collective-permute-done | bytes 233504 | tf_op jit(solution)/shard_map/ppermute | solution.py:525
  28.6 3.8 %collective-permute-done.3.refs_9_.refs_10_ = f32[456,128]{1,0:T(8,128)S(1)} collective-permute-done((f32[456,128]{1,0:T(8,128)S(1)}, f32[456,128]{1,0:T(8,128)S(1)}, u32[]{:S(2)}, u32[]{:S(2)}) %collective-permute-start.3) | collective-permute-done | bytes 233504 | tf_op jit(solution)/shard_map/ppermute | solution.py:525
  32.4 5.1 %shard_map.97 = (f32[1920,128]{1,0:T(8,128)S(1)}, f32[72,128]{1,0:T(8,128)S(1)}, f32[960,128]{1,0:T(8,128)S(1)}, f32[24,128]{1,0:T(8,128)S(1)}, f32[376,128]{1,0:T(8,128)S(1)}, /*index=5*/f32[376,128]{1,0:T(8,128)S(1)}) custom-call(f32[2304,128]{1,0:T(8,128)S(1)} %bitcast.9, f32[256,128]{1,0:T(8,128)S(1)} %bitcast.15, f32[256,128]{1,0:T(8,128)S(1)} %bitcast.18, ...), custom_call_target="tpu_custom_call" | custom-call | tf_op jit(solution)/shard_map/pallas_call | solution.py:511
  37.5 3.5 %collective-permute-start.4 = (f32[376,128]{1,0:T(8,128)S(1)}, f32[376,128]{1,0:T(8,128)S(1)}, u32[]{:S(2)}, u32[]{:S(2)}) collective-permute-start(f32[376,128]{1,0:T(8,128)S(1)} %get-tuple-element.34), channel_id=1, source_target_pairs={{0,1},{1,2},{2,3},{4,5},{5,6},{6,7},{8,9},{9,10},{10,11},{12,13},{... | collective-permute-start | bytes 577544 | tf_op jit(solution)/shard_map/ppermute | solution.py:525
  41.0 2.4 %collective-permute-start.5 = (f32[376,128]{1,0:T(8,128)S(1)}, f32[376,128]{1,0:T(8,128)S(1)}, u32[]{:S(2)}, u32[]{:S(2)}) collective-permute-start(f32[376,128]{1,0:T(8,128)S(1)} %get-tuple-element.35), channel_id=1, source_target_pairs={{1,0},{2,1},{3,2},{5,4},{6,5},{7,6},{9,8},{10,9},{11,10},{13,12},{... | collective-permute-start | bytes 577544 | tf_op jit(solution)/shard_map/ppermute | solution.py:525
  43.4 3.4 %collective-permute-done.4.refs_11_ = f32[376,128]{1,0:T(8,128)S(1)} collective-permute-done((f32[376,128]{1,0:T(8,128)S(1)}, f32[376,128]{1,0:T(8,128)S(1)}, u32[]{:S(2)}, u32[]{:S(2)}) %collective-permute-start.4) | collective-permute-done | bytes 192544 | tf_op jit(solution)/shard_map/ppermute | solution.py:525
  46.8 3.7 %collective-permute-done.5.refs_12_ = f32[376,128]{1,0:T(8,128)S(1)} collective-permute-done((f32[376,128]{1,0:T(8,128)S(1)}, f32[376,128]{1,0:T(8,128)S(1)}, u32[]{:S(2)}, u32[]{:S(2)}) %collective-permute-start.5) | collective-permute-done | bytes 192544 | tf_op jit(solution)/shard_map/ppermute | solution.py:525
  50.6 3.0 %shard_map.98 = (f32[2304,128]{1,0:T(8,128)}, f32[24,128]{1,0:T(8,128)}) custom-call(f32[256,128]{1,0:T(8,128)S(1)} %bitcast.16, f32[256,128]{1,0:T(8,128)S(1)} %bitcast.19, f32[256,128]{1,0:T(8,128)S(1)} %bitcast.13, f32[768,128]{1,0:T(8,128)S(1)} %get-tuple-element.24.refs_4_.refs_3_, f32[144,128]{1,0:T(8,128)S(1)} %get-tuple-element.25.refs_5_.refs_4_, ...), custom_call_target="tpu_custom_call" | custom-call | tf_op jit(solution)/shard_map/pallas_call | solution.py:511
  (14 shorter events, 0.0 us)
Async XLA Ops:
  0.6 16.7 %copy-start.12 = (s32[8,128]{1,0:T(8,128)S(1)}, s32[8,128]{1,0:T(8,128)}, u32[]{:S(2)}) copy-start(s32[8,128]{1,0:T(8,128)} %refs_6_.3) | copy-start | bytes 12292
  0.6 16.7 %copy-start.10 = (f32[8,128]{1,0:T(8,128)S(1)}, f32[8,128]{1,0:T(8,128)}, u32[]{:S(2)}) copy-start(f32[8,128]{1,0:T(8,128)} %refs_5_.3) | copy-start | bytes 12292
  0.7 1.3 %copy-start = (f32[9,32,8,128]{3,2,1,0:T(8,128)S(1)}, f32[9,32,8,128]{3,2,1,0:T(8,128)}, u32[]{:S(2)}) copy-start(f32[9,32,8,128]{3,2,1,0:T(8,128)} %param.8) | copy-start | bytes 3538948
  1.9 0.9 %copy-start.1 = (f32[32,8,128]{2,1,0:T(8,128)S(1)}, f32[32,8,128]{2,1,0:T(8,128)}, u32[]{:S(2)}) copy-start(f32[32,8,128]{2,1,0:T(8,128)} %param.11) | copy-start | bytes 393220
  2.8 0.9 %copy-start.3 = (f32[32,8,128]{2,1,0:T(8,128)S(1)}, f32[32,8,128]{2,1,0:T(8,128)}, u32[]{:S(2)}) copy-start(f32[32,8,128]{2,1,0:T(8,128)} %param.9) | copy-start | bytes 393220
  3.7 0.9 %copy-start.5 = (f32[32,8,128]{2,1,0:T(8,128)S(1)}, f32[32,8,128]{2,1,0:T(8,128)}, u32[]{:S(2)}) copy-start(f32[32,8,128]{2,1,0:T(8,128)} %param.10) | copy-start | bytes 393220
  4.6 0.7 %copy-start.7 = (f32[3,8,128]{2,1,0:T(8,128)S(1)}, f32[3,8,128]{2,1,0:T(8,128)}, u32[]{:S(2)}) copy-start(f32[3,8,128]{2,1,0:T(8,128)} %param.12) | copy-start | bytes 36868
  5.4 0.7 %copy-start.9 = (f32[8,128]{1,0:T(8,128)S(1)}, f32[8,128]{1,0:T(8,128)}, u32[]{:S(2)}) copy-start(f32[8,128]{1,0:T(8,128)} %refs_5_.3) | copy-start | bytes 12292
  6.0 0.7 %copy-start.11 = (s32[8,128]{1,0:T(8,128)S(1)}, s32[8,128]{1,0:T(8,128)}, u32[]{:S(2)}) copy-start(s32[8,128]{1,0:T(8,128)} %refs_6_.3) | copy-start | bytes 12292
  6.7 0.7 %copy-start.13 = (s32[8,128]{1,0:T(8,128)S(1)}, s32[8,128]{1,0:T(8,128)}, u32[]{:S(2)}) copy-start(s32[8,128]{1,0:T(8,128)} %refs_7_.3) | copy-start | bytes 12292
  7.4 10.0 %copy-start.2 = (f32[32,8,128]{2,1,0:T(8,128)S(1)}, f32[32,8,128]{2,1,0:T(8,128)}, u32[]{:S(2)}) copy-start(f32[32,8,128]{2,1,0:T(8,128)} %param.11) | copy-start | bytes 393220
  7.4 10.0 %copy-start.8 = (f32[3,8,128]{2,1,0:T(8,128)S(1)}, f32[3,8,128]{2,1,0:T(8,128)}, u32[]{:S(2)}) copy-start(f32[3,8,128]{2,1,0:T(8,128)} %param.12) | copy-start | bytes 36868
  7.4 10.0 %copy-start.14 = (s32[8,128]{1,0:T(8,128)S(1)}, s32[8,128]{1,0:T(8,128)}, u32[]{:S(2)}) copy-start(s32[8,128]{1,0:T(8,128)} %refs_7_.3) | copy-start | bytes 12292
  9.3 23.1 %copy-start.6 = (f32[32,8,128]{2,1,0:T(8,128)S(1)}, f32[32,8,128]{2,1,0:T(8,128)}, u32[]{:S(2)}) copy-start(f32[32,8,128]{2,1,0:T(8,128)} %param.10) | copy-start | bytes 393220
  9.3 6.2 %collective-permute-start = (f32[216,128]{1,0:T(8,128)S(1)}, f32[216,128]{1,0:T(8,128)S(1)}, u32[]{:S(2)}, u32[]{:S(2)}) collective-permute-start(f32[216,128]{1,0:T(8,128)S(1)} %get-tuple-element.22), channel_id=1, source_target_pairs={{0,4},{4,8},{8,12},{12,16},{16,20},{20,24},{24,28},{1,5},{5,9},{9,... | collective-permute-start | bytes 331784 | tf_op jit(solution)/shard_map/ppermute | solution.py:525
  11.4 6.0 %collective-permute-start.1 = (f32[216,128]{1,0:T(8,128)S(1)}, f32[216,128]{1,0:T(8,128)S(1)}, u32[]{:S(2)}, u32[]{:S(2)}) collective-permute-start(f32[216,128]{1,0:T(8,128)S(1)} %get-tuple-element.23), channel_id=1, source_target_pairs={{4,0},{8,4},{12,8},{16,12},{20,16},{24,20},{28,24},{5,1},{9,5},{13... | collective-permute-start | bytes 331784 | tf_op jit(solution)/shard_map/ppermute | solution.py:525
  19.9 8.7 %collective-permute-start.2 = (f32[456,128]{1,0:T(8,128)S(1)}, f32[456,128]{1,0:T(8,128)S(1)}, u32[]{:S(2)}, u32[]{:S(2)}) collective-permute-start(f32[456,128]{1,0:T(8,128)S(1)} %get-tuple-element.28), channel_id=1, source_target_pairs={{0,1},{1,2},{2,3},{4,5},{5,6},{6,7},{8,9},{9,10},{10,11},{12,13},{... | collective-permute-start | bytes 700424 | tf_op jit(solution)/shard_map/ppermute | solution.py:525
  23.4 9.0 %collective-permute-start.3 = (f32[456,128]{1,0:T(8,128)S(1)}, f32[456,128]{1,0:T(8,128)S(1)}, u32[]{:S(2)}, u32[]{:S(2)}) collective-permute-start(f32[456,128]{1,0:T(8,128)S(1)} %get-tuple-element.29), channel_id=1, source_target_pairs={{1,0},{2,1},{3,2},{5,4},{6,5},{7,6},{9,8},{10,9},{11,10},{13,12},{... | collective-permute-start | bytes 700424 | tf_op jit(solution)/shard_map/ppermute | solution.py:525
  32.4 18.1 %copy-start.4 = (f32[32,8,128]{2,1,0:T(8,128)S(1)}, f32[32,8,128]{2,1,0:T(8,128)}, u32[]{:S(2)}) copy-start(f32[32,8,128]{2,1,0:T(8,128)} %param.9) | copy-start | bytes 393220
  37.5 9.3 %collective-permute-start.4 = (f32[376,128]{1,0:T(8,128)S(1)}, f32[376,128]{1,0:T(8,128)S(1)}, u32[]{:S(2)}, u32[]{:S(2)}) collective-permute-start(f32[376,128]{1,0:T(8,128)S(1)} %get-tuple-element.34), channel_id=1, source_target_pairs={{0,1},{1,2},{2,3},{4,5},{5,6},{6,7},{8,9},{9,10},{10,11},{12,13},{... | collective-permute-start | bytes 577544 | tf_op jit(solution)/shard_map/ppermute | solution.py:525
  41.0 9.6 %collective-permute-start.5 = (f32[376,128]{1,0:T(8,128)S(1)}, f32[376,128]{1,0:T(8,128)S(1)}, u32[]{:S(2)}, u32[]{:S(2)}) collective-permute-start(f32[376,128]{1,0:T(8,128)S(1)} %get-tuple-element.35), channel_id=1, source_target_pairs={{1,0},{2,1},{3,2},{5,4},{6,5},{7,6},{9,8},{10,9},{11,10},{13,12},{... | collective-permute-start | bytes 577544 | tf_op jit(solution)/shard_map/ppermute | solution.py:525

commit v2 on v1

--- a/solution.py
+++ b/solution.py
@@ -33,11 +33,21 @@
     return sub, lane
 
 
+def either(which, take):
+    if not isinstance(which, tuple):
+        return take(which)
+    return jnp.where(which[0], take(which[1]), take(which[2]))
+
+
 def plane(ref, index):
+    if isinstance(ref, tuple):
+        return either(ref, lambda one: plane(one, index))
     return ref[index * ROWS : (index + 1) * ROWS, :]
 
 
 def row(ref, index):
+    if isinstance(ref, tuple):
+        return either(ref, lambda one: row(one, index))
     return ref[index : index + 1, :]
 
 
@@ -144,7 +154,24 @@
         return x
 
 
-def edges_kernel(depth, wave, lame, shear, buoy, ocean, deep, floor, wet, own, own_ocean, to_right, to_left):
+def edges_kernel(
+    depth, odd_ref, *refs,
+):
+    hbm, vmem, (own, own_ocean, even_way, odd_way), sem = refs[:8], refs[8:16], refs[16:20], refs[20]
+    copies = [
+        pltpu.make_async_copy(source, target, sem.at[k]) for k, (source, target) in enumerate(zip(hbm[1:], vmem[1:]))
+    ]
+    size = depth * ROWS
+    waves = [
+        pltpu.make_async_copy(
+            hbm[0].at[f * size : (f + 1) * size, :], vmem[0].at[f * size : (f + 1) * size, :], sem.at[7 + f]
+        )
+        for f in range(9)
+    ]
+    for copy in waves + copies:
+        copy.start()
+    wave, lame, shear, buoy, ocean, deep, floor, wet = vmem
+    odd = (odd_ref[0] & 1) == 1
     grid = Grid(depth)
     per = grid.per
     masks = [grid.group == g for g in range(PACK)]
@@ -156,11 +183,15 @@
         return out
 
     def both(index, one, two):
-        store(to_right, index, jnp.where(grid.first, one, rolled(two, EDGE, 1)))
-        store(to_left, index, jnp.where(grid.first, rolled(two, -EDGE, 1), one))
+        to_right = jnp.where(grid.first, one, rolled(two, EDGE, 1))
+        to_left = jnp.where(grid.first, rolled(two, -EDGE, 1), one)
+        store(even_way, index, jnp.where(odd, to_left, to_right))
+        store(odd_way, index, jnp.where(odd, to_right, to_left))
 
     sources = [(wave, f * depth) for f in range(9)] + [(lame, 0), (shear, 0), (buoy, 0)]
     for f in range(0, FIELDS, 2):
+        for h in (f, f + 1):
+            (waves[h] if h < 9 else copies[h - 9]).wait()
         for j in range(per):
             pair = []
             for h in (f, f + 1):
@@ -168,6 +199,8 @@
                 pair.append(collect(lambda g: plane(ref, base + per * g + j)))
                 store(own, h * per + j, pair[-1])
             both((f // 2) * per + j, *pair)
+    for copy in copies[3:]:
+        copy.wait()
     flat = [plane(ocean, k) for k in range(3)] + [deep[...]]
     flat += [floor[...].astype(jnp.float32), wet[...].astype(jnp.float32)]
     for f in range(0, 6, 2):
@@ -227,10 +260,25 @@
     out[at : at + 1, :] = jnp.zeros((1, LANES), jnp.float32)
 
 
+def send(grid, odd, more_high, more_low, take, level, flat, even_way, odd_way):
+    @pl.when(odd)
+    def _():
+        send_rows(grid, TO_HIGH + more_high, take, level, flat, ROWS - 1, odd_way)
+        send_rows(grid, TO_LOW + more_low, take, level, flat, 0, even_way)
+
+    @pl.when(jnp.logical_not(odd))
+    def _():
+        send_rows(grid, TO_HIGH + more_high, take, level, flat, ROWS - 1, even_way)
+        send_rows(grid, TO_LOW + more_low, take, level, flat, 0, odd_way)
+
+
 def start_kernel(
-    depth, wave, buoy, own, own_ocean, ocean, deep, floor, wet, left, right,
-    windows, flat, partial, level, high, low,
+    depth, odd_ref, wave, buoy, own, own_ocean, ocean, deep, floor, wet, even_in, odd_in,
+    windows, flat, partial, level, even_way, odd_way,
 ):
+    x_odd = (odd_ref[0] & 1) == 1
+    left = (x_odd, even_in, odd_in)
+    right = (x_odd, odd_in, even_in)
     grid = Grid(depth)
     per, planes = grid.per, grid.planes
     for f in range(FIELDS):
@@ -274,8 +322,7 @@
     for which in (WET, FLOOR, FLUX_X, FLUX_Y):
         flats[which] = flat
         flats[which, "at"] = 3 * which * ROWS
-    send_rows(grid, TO_HIGH + ((BUOY, 6), (BUOY, 7)), take, level, flats, 7, high)
-    send_rows(grid, TO_LOW + ((BUOY, 0), (BUOY, 1)), take, level, flats, 0, low)
+    send(grid, (odd_ref[1] & 1) == 1, ((BUOY, 6), (BUOY, 7)), ((BUOY, 0), (BUOY, 1)), take, level, flats, even_way, odd_way)
 
 
 def finish(grid, stress_rows, buoy, partial, level, now, fixed, low, high, low_buoy, high_buoy, halo, corr, speed, new):
@@ -283,7 +330,7 @@
 
     def piece(ref, index, part):
         start, size = part
-        return ref[index * planes + start : index * planes + start + size, :]
+        return either(ref, lambda one: one[index * planes + start : index * planes + start + size, :])
 
     for part in ((0, depth), (depth, 2 * per)):
         start, size = part
@@ -343,8 +390,7 @@
     sums[1] = grid.every_group(sums[1])
     sums[2] = grid.every_group(sums[2])
 
-    tail = low.shape[0] - 16
-    tail_high = high.shape[0] - 16
+    tail = tail_high = low[1].shape[0] - 16
     ends = []
     for message, base, index, own_row, sign in ((low, tail, 6, 0, -1.0), (high, tail_high, 7, 7, 1.0)):
         lines = lambda which, k, message=message, base=base: row(message, base + 3 * which + k)
@@ -425,10 +471,12 @@
 
 
 def middle_kernel(
-    depth, wave, lame, shear, buoy, windows, flat, partial, level, from_low, from_high,
-    stress_out, ocean_out, partial_out, level_out, high, low,
+    depth, odd_ref, wave, lame, shear, buoy, windows, flat, partial, level, even_in, odd_in,
+    stress_out, ocean_out, partial_out, level_out, even_way, odd_way,
     halo, corr, speed,
 ):
+    odd = (odd_ref[1] & 1) == 1
+    from_low, from_high = (odd, even_in, odd_in), (odd, odd_in, even_in)
     grid = Grid(depth)
     per, planes = grid.per, grid.planes
 
@@ -466,15 +514,18 @@
     for which in (WET, FLOOR, FLUX_X, FLUX_Y):
         rows_of[which] = flat if which >= DEPTH else ocean_out
         rows_of[which, "at"] = 3 * which * ROWS
-    send_rows(grid, TO_HIGH, take, level_out, rows_of, 7, high)
-    send_rows(grid, TO_LOW, take, level_out, rows_of, 0, low)
+    send(grid, (odd_ref[1] & 1) == 1, (), (), take, level_out, rows_of, even_way, odd_way)
 
 
 def last_kernel(
-    depth, lame, shear, buoy, windows, flat, stress_in, ocean, partial, level, low_buoy, high_buoy, from_low, from_high,
+    depth, odd_ref, lame, shear, buoy, windows, flat, stress_in, ocean, partial, level,
+    even_first, odd_first, even_in, odd_in,
     wave_out, ocean_out,
     halo, corr, speed,
 ):
+    odd = (odd_ref[1] & 1) == 1
+    low_buoy, high_buoy = (odd, even_first, odd_first), (odd, odd_first, even_first)
+    from_low, from_high = (odd, even_in, odd_in), (odd, odd_in, even_in)
     grid = Grid(depth)
     per, planes = grid.per, grid.planes
 
@@ -506,62 +557,73 @@
             store(wave_out, f * depth + p, plane(speed, f * planes + p))
 
 
-def call(kernel, shapes, scratch, *arguments):
-    vmem = pl.BlockSpec(memory_space=pltpu.VMEM)
+VMEM = pl.BlockSpec(memory_space=pltpu.VMEM)
+SMEM = pl.BlockSpec(memory_space=pltpu.SMEM)
+HBM = pl.BlockSpec(memory_space=pltpu.HBM)
+
+
+def call(kernel, shapes, scratch, flags, *arguments, place=VMEM):
     return pl.pallas_call(
         kernel,
-        out_shape=[jax.ShapeDtypeStruct((n, LANES), jnp.float32) for n in shapes],
-        in_specs=[vmem] * len(arguments),
-        out_specs=[vmem] * len(shapes),
-        scratch_shapes=[pltpu.VMEM((n, LANES), jnp.float32) for n in scratch],
+        out_shape=[s if hasattr(s, "dtype") else jax.ShapeDtypeStruct((s, LANES), jnp.float32) for s in shapes],
+        in_specs=[SMEM] + [place] * len(arguments),
+        out_specs=[VMEM] * len(shapes),
+        scratch_shapes=[pltpu.VMEM((s, LANES), jnp.float32) if isinstance(s, int) else s for s in scratch],
         compiler_params=pltpu.CompilerParams(vmem_limit_bytes=24 * 1024 * 1024),
-    )(*arguments)
-
-
-def exchange(axis, forth, back):
+    )(flags, *arguments)
+
+
+def exchange(axis, even_way, odd_way, odd_first):
     count = lax.axis_size(axis)
-    forward = [(i, i + 1) for i in range(count - 1)]
-    backward = [(i + 1, i) for i in range(count - 1)]
-    return lax.ppermute(forth, axis, forward), lax.ppermute(back, axis, backward)
+
+    def swap(x, start):
+        pairs = [(i, i + 1) for i in range(start, count - 1, 2)]
+        return lax.ppermute(x, axis, pairs + [(j, i) for i, j in pairs])
+
+    if odd_first:
+        odd_in = swap(odd_way, 1)
+        return swap(even_way, 0), odd_in
+    even_in = swap(even_way, 0)
+    return even_in, swap(odd_way, 1)
 
 
 def local(wave_fields, lame_lambda, shear_modulus, buoyancy, ocean_state, water_depth, seafloor_index, wet_mask):
     depth = wave_fields.shape[1]
     per = depth // PACK
     planes = depth + 2 * per
-    wave = wave_fields.reshape(-1, LANES)
-    lame = lame_lambda.reshape(-1, LANES)
-    shear = shear_modulus.reshape(-1, LANES)
-    buoy = buoyancy.reshape(-1, LANES)
-    ocean = ocean_state.reshape(-1, LANES)
+    inputs = [wave_fields, lame_lambda, shear_modulus, buoyancy, ocean_state, water_depth, seafloor_index, wet_mask]
+    inputs = [x.reshape(-1, LANES) for x in inputs]
+    flags = jnp.stack([lax.axis_index("gx"), lax.axis_index("gy")])
 
     def bind(kernel):
         return lambda *refs: kernel(depth, *refs)
 
     edge = (FIELDS // 2 * per + 3) * ROWS
-    own, own_ocean, to_right, to_left = call(
-        bind(edges_kernel), [FIELDS * per * ROWS, 6 * ROWS, edge, edge], [],
-        wave, lame, shear, buoy, ocean, water_depth, seafloor_index, wet_mask,
-    )
-    left, right = exchange("gx", to_right, to_left)
+    copies = [jax.ShapeDtypeStruct(x.shape, x.dtype) for x in inputs]
+    *inputs, own, own_ocean, even_way, odd_way = call(
+        bind(edges_kernel), copies + [FIELDS * per * ROWS, 6 * ROWS, edge, edge], [pltpu.SemaphoreType.DMA((16,))],
+        flags, *inputs, place=HBM,
+    )
+    wave, lame, shear, buoy, ocean, deep, floor, wet = inputs
+    x_in = exchange("gx", even_way, odd_way, True)
     first = 11 * planes + 16
     later = 9 * planes + 16
-    windows, flat, partial, level, high, low = call(
+    windows, flat, partial, level, even_way, odd_way = call(
         bind(start_kernel),
         [FIELDS * 2 * per * ROWS, 18 * ROWS, 3 * planes * ROWS, 3 * ROWS, first, first], [],
-        wave, buoy, own, own_ocean, ocean, water_depth, seafloor_index, wet_mask, left, right,
-    )
-    low1, high1 = exchange("gy", high, low)
+        flags, wave, buoy, own, own_ocean, ocean, deep, floor, wet, *x_in,
+    )
+    y_in = exchange("gy", even_way, odd_way, False)
     scratch = [9 * planes, 9 * planes, 3 * planes * ROWS]
-    stress, ocean1, partial, level, high, low = call(
+    stress, ocean1, partial, level, even_way, odd_way = call(
         bind(middle_kernel),
         [6 * planes * ROWS, 9 * ROWS, 3 * planes * ROWS, 3 * ROWS, later, later], scratch,
-        wave, lame, shear, buoy, windows, flat, partial, level, low1, high1,
-    )
-    low2, high2 = exchange("gy", high, low)
+        flags, wave, lame, shear, buoy, windows, flat, partial, level, *y_in,
+    )
+    y_in2 = exchange("gy", even_way, odd_way, False)
     wave_out, ocean_out = call(
         bind(last_kernel), [wave.shape[0], ocean.shape[0]], scratch,
-        lame, shear, buoy, windows, flat, stress, ocean1, partial, level, low1, high1, low2, high2,
+        flags, lame, shear, buoy, windows, flat, stress, ocean1, partial, level, *y_in, *y_in2,
     )
     return wave_out.reshape(wave_fields.shape), ocean_out.reshape(ocean_state.shape)
 

time: 54.4 us -> 51.4 us (0.945)
  starting transfers between devices: 17.4 us -> 12 us
  Pallas kernels: 12.4 us -> 16.8 us
  waiting for transfers between devices: 16.2 us -> 14.5 us
    ppermute x6, starting transfers between devices: 17.4 us -> 12 us  [swap(): return lax.ppermute(x, axis, pairs + [(j, i) for i, j in pairs])]
    pallas_call x4, Pallas kernels: 12.4 us -> 16.8 us  [call(): pl.pallas_call(kernel, out_shape=[s if hasattr(s, 'dtype') else jax.Shape...]
    ppermute x6, waiting for transfers between devices: 16.2 us -> 14.5 us  [swap(): return lax.ppermute(x, axis, pairs + [(j, i) for i, j in pairs])]
    unnamed x30 -> x16, local copies, waits for them, and re-layouts: 6.78 us -> 6.75 us
  transfers between devices with their start and end apart: 6 -> 6, of which waited for: 6 -> 5; matrix products, arithmetic and copies ran while one was open for 0% -> 0% of each run, Pallas kernels for 0% -> 0%
where the time goes in v2:
time: 51.4 us; the launch traced here: 50.8 us
  Pallas kernels  16.8 us (33%)
  waiting for transfers between devices  14.5 us (28%)
  starting transfers between devices  12 us (23%)
  local copies, waits for them, and re-layouts  6.75 us (13%)
  between operations  0.72 us (1%)
    pallas_call x4, Pallas kernels, call(): pl.pallas_call(kernel, out_shape=[s if hasattr(s, 'dtype') else jax.Shape...  16.8 us
    ppermute x6, waiting for transfers between devices, swap(): return lax.ppermute(x, axis, pairs + [(j, i) for i, j in pairs])  14.5 us
    ppermute x6, starting transfers between devices, swap(): return lax.ppermute(x, axis, pairs + [(j, i) for i, j in pairs])  12 us
    unnamed x16, local copies, waits for them, and re-layouts  6.75 us
  transfers between devices with their start and end apart: 6, of which 5 were waited for; matrix products, arithmetic and copies ran while one was open for 0% of the time, Pallas kernels for 0%

profile of v2, /device:TPU:10, one launch (start us, length us, event | category | flops | bytes accessed | tf_op | source)
XLA Modules:
  0.0 50.8 jit_solution(3909483227024543945)
XLA Ops:
  0.6 0.1 pad_add_fusion.refs_0_
  0.7 0.0 copy-start
  0.7 1.3 %copy-done = f32[9,32,8,128]{3,2,1,0:T(8,128)S(1)} copy-done((f32[9,32,8,128]{3,2,1,0:T(8,128)S(1)}, f32[9,32,8,128]{3,2,1,0:T(8,128)}, u32[]{:S(2)}) %copy-start) | copy-done | bytes 1179672
  2.0 0.0 copy-start.1
  2.0 0.9 %copy-done.1 = f32[32,8,128]{2,1,0:T(8,128)S(1)} copy-done((f32[32,8,128]{2,1,0:T(8,128)S(1)}, f32[32,8,128]{2,1,0:T(8,128)}, u32[]{:S(2)}) %copy-start.1) | copy-done | bytes 131096
  2.9 0.0 copy-start.2
  2.9 0.9 %copy-done.2 = f32[32,8,128]{2,1,0:T(8,128)S(1)} copy-done((f32[32,8,128]{2,1,0:T(8,128)S(1)}, f32[32,8,128]{2,1,0:T(8,128)}, u32[]{:S(2)}) %copy-start.2) | copy-done | bytes 131096
  3.8 0.0 copy-start.3
  3.8 0.9 %copy-done.3 = f32[32,8,128]{2,1,0:T(8,128)S(1)} copy-done((f32[32,8,128]{2,1,0:T(8,128)S(1)}, f32[32,8,128]{2,1,0:T(8,128)}, u32[]{:S(2)}) %copy-start.3) | copy-done | bytes 131096
  4.7 0.0 copy-start.4
  4.7 0.7 %copy-done.4 = f32[3,8,128]{2,1,0:T(8,128)S(1)} copy-done((f32[3,8,128]{2,1,0:T(8,128)S(1)}, f32[3,8,128]{2,1,0:T(8,128)}, u32[]{:S(2)}) %copy-start.4) | copy-done | bytes 12312
  5.4 0.0 copy-start.5
  5.4 0.7 %copy-done.5 = f32[8,128]{1,0:T(8,128)S(1)} copy-done((f32[8,128]{1,0:T(8,128)S(1)}, f32[8,128]{1,0:T(8,128)}, u32[]{:S(2)}) %copy-start.5) | copy-done | bytes 4120
  6.1 0.0 copy-start.6
  6.1 0.7 %copy-done.6 = s32[8,128]{1,0:T(8,128)S(1)} copy-done((s32[8,128]{1,0:T(8,128)S(1)}, s32[8,128]{1,0:T(8,128)}, u32[]{:S(2)}) %copy-start.6) | copy-done | bytes 4120
  6.8 0.7 %copy-done.7 = s32[8,128]{1,0:T(8,128)S(1)} copy-done((s32[8,128]{1,0:T(8,128)S(1)}, s32[8,128]{1,0:T(8,128)}, u32[]{:S(2)}) %copy-start.7) | copy-done | bytes 4120
  7.5 4.4 %shard_map.95 = (f32[2304,128]{1,0:T(8,128)S(1)}, f32[256,128]{1,0:T(8,128)S(1)}, f32[256,128]{1,0:T(8,128)S(1)}, f32[256,128]{1,0:T(8,128)S(1)}, f32[24,128]{1,...) custom-call(s32[2]{0:T(128)S(1)} %pad_add_fusion.refs_0_, ...), custom_call_target="tpu_custom_call" | custom-call | tf_op jit(solution)/shard_map/pallas_call | solution.py:566
  11.9 0.1 collective-permute-start
  12.0 2.5 %collective-permute-start.1 = (f32[216,128]{1,0:T(8,128)S(1)}, f32[216,128]{1,0:T(8,128)S(1)}, u32[]{:S(2)}, u32[]{:S(2)}) collective-permute-start(f32[216,128]{1,0:T(8,128)S(1)} %get-tuple-element.39), channel_id=1, source_target_pairs={{4,8},{12,16},{20,24},{8,4},{16,12},{24,20},{5,9},{13,17},{21,25},... | collective-permute-start | bytes 331784 | tf_op jit(solution)/shard_map/ppermute | solution.py:581
  14.5 0.0 collective-permute-done.refs_9_
  14.5 3.5 %collective-permute-done.1.refs_10_ = f32[216,128]{1,0:T(8,128)S(1)} collective-permute-done((f32[216,128]{1,0:T(8,128)S(1)}, f32[216,128]{1,0:T(8,128)S(1)}, u32[]{:S(2)}, u32[]{:S(2)}) %collective-permute-start.1) | collective-permute-done | bytes 110624 | tf_op jit(solution)/shard_map/ppermute | solution.py:581
  18.0 3.1 %shard_map.96 = (f32[768,128]{1,0:T(8,128)S(1)}, f32[144,128]{1,0:T(8,128)S(1)}, f32[960,128]{1,0:T(8,128)S(1)}, f32[24,128]{1,0:T(8,128)S(1)}, f32[456,128]{1,0:T(8,128)S(1)}, /*index=5*/f32[456,128]{1,0:T(8,128)S(1)}) custom-call(s32[2]{0:T(128)S(1)} %pad_add_fusion.refs_0_, f32[2304,128]{1,0:T(8,128)S(1)} %get-tuple-element.31.refs_1_, ...), custom_call_target="tpu_custom_call" | custom-call | tf_op jit(solution)/shard_map/pallas_call | solution.py:566
  21.2 0.5 %collective-permute-start.2 = (f32[456,128]{1,0:T(8,128)S(1)}, f32[456,128]{1,0:T(8,128)S(1)}, u32[]{:S(2)}, u32[]{:S(2)}) collective-permute-start(f32[456,128]{1,0:T(8,128)S(1)} %get-tuple-element.44), channel_id=1, source_target_pairs={{0,1},{2,3},{1,0},{3,2},{4,5},{6,7},{5,4},{7,6},{8,9},{10,11},{9,8... | collective-permute-start | bytes 700424 | tf_op jit(solution)/shard_map/ppermute | solution.py:581
  21.7 4.6 %collective-permute-start.3 = (f32[456,128]{1,0:T(8,128)S(1)}, f32[456,128]{1,0:T(8,128)S(1)}, u32[]{:S(2)}, u32[]{:S(2)}) collective-permute-start(f32[456,128]{1,0:T(8,128)S(1)} %get-tuple-element.45), channel_id=1, source_target_pairs={{1,2},{2,1},{5,6},{6,5},{9,10},{10,9},{13,14},{14,13},{17,18},{18,... | collective-permute-start | bytes 700424 | tf_op jit(solution)/shard_map/ppermute | solution.py:581
  26.3 2.5 %collective-permute-done.2.refs_9_.refs_10_ = f32[456,128]{1,0:T(8,128)S(1)} collective-permute-done((f32[456,128]{1,0:T(8,128)S(1)}, f32[456,128]{1,0:T(8,128)S(1)}, u32[]{:S(2)}, u32[]{:S(2)}) %collective-permute-start.2) | collective-permute-done | bytes 233504 | tf_op jit(solution)/shard_map/ppermute | solution.py:581
  28.8 3.0 %collective-permute-done.3.refs_10_.refs_11_ = f32[456,128]{1,0:T(8,128)S(1)} collective-permute-done((f32[456,128]{1,0:T(8,128)S(1)}, f32[456,128]{1,0:T(8,128)S(1)}, u32[]{:S(2)}, u32[]{:S(2)}) %collective-permute-start.3) | collective-permute-done | bytes 233504 | tf_op jit(solution)/shard_map/ppermute | solution.py:581
  31.8 5.7 %shard_map.97 = (f32[1920,128]{1,0:T(8,128)S(1)}, f32[72,128]{1,0:T(8,128)S(1)}, f32[960,128]{1,0:T(8,128)S(1)}, f32[24,128]{1,0:T(8,128)S(1)}, f32[376,128]{1,0:T(8,128)S(1)}, /*index=5*/f32[376,128]{1,0:T(8,128)S(1)}) custom-call(s32[2]{0:T(128)S(1)} %pad_add_fusion.refs_0_, f32[2304,128]{1,0:T(8,128)S(1)} %get-tuple-element.31.refs_1_, ...), custom_call_target="tpu_custom_call" | custom-call | tf_op jit(solution)/shard_map/pallas_call | solution.py:566
  37.5 0.1 collective-permute-start.4
  37.6 4.2 %collective-permute-start.5 = (f32[376,128]{1,0:T(8,128)S(1)}, f32[376,128]{1,0:T(8,128)S(1)}, u32[]{:S(2)}, u32[]{:S(2)}) collective-permute-start(f32[376,128]{1,0:T(8,128)S(1)} %get-tuple-element.51), channel_id=1, source_target_pairs={{1,2},{2,1},{5,6},{6,5},{9,10},{10,9},{13,14},{14,13},{17,18},{18,... | collective-permute-start | bytes 577544 | tf_op jit(solution)/shard_map/ppermute | solution.py:581
  41.9 3.3 %collective-permute-done.4.refs_12_ = f32[376,128]{1,0:T(8,128)S(1)} collective-permute-done((f32[376,128]{1,0:T(8,128)S(1)}, f32[376,128]{1,0:T(8,128)S(1)}, u32[]{:S(2)}, u32[]{:S(2)}) %collective-permute-start.4) | collective-permute-done | bytes 192544 | tf_op jit(solution)/shard_map/ppermute | solution.py:581
  45.1 2.2 %collective-permute-done.5.refs_13_ = f32[376,128]{1,0:T(8,128)S(1)} collective-permute-done((f32[376,128]{1,0:T(8,128)S(1)}, f32[376,128]{1,0:T(8,128)S(1)}, u32[]{:S(2)}, u32[]{:S(2)}) %collective-permute-start.5) | collective-permute-done | bytes 192544 | tf_op jit(solution)/shard_map/ppermute | solution.py:581
  47.3 3.5 %shard_map.98 = (f32[2304,128]{1,0:T(8,128)}, f32[24,128]{1,0:T(8,128)}) custom-call(s32[2]{0:T(128)S(1)} %pad_add_fusion.refs_0_, f32[256,128]{1,0:T(8,128)S(1)} %get-tuple-element.28.refs_2_.refs_1_, f32[256,128]{1,0:T(8,128)S(1)} %get-tuple-element.29.refs_3_.refs_2_, f32[256,128]{1,0:T(8,128)S(1)} %get-tuple-element.30.refs_2_.refs_4_.refs_3_, ...), custom_call_target="tpu_custom_call" | custom-call | tf_op jit(solution)/shard_map/pallas_call | solution.py:566
  (1 shorter events, 0.0 us)
Async XLA Ops:
  0.7 1.3 %copy-start = (f32[9,32,8,128]{3,2,1,0:T(8,128)S(1)}, f32[9,32,8,128]{3,2,1,0:T(8,128)}, u32[]{:S(2)}) copy-start(f32[9,32,8,128]{3,2,1,0:T(8,128)} %param.8) | copy-start | bytes 3538948
  2.0 0.9 %copy-start.1 = (f32[32,8,128]{2,1,0:T(8,128)S(1)}, f32[32,8,128]{2,1,0:T(8,128)}, u32[]{:S(2)}) copy-start(f32[32,8,128]{2,1,0:T(8,128)} %param.9) | copy-start | bytes 393220
  2.9 0.9 %copy-start.2 = (f32[32,8,128]{2,1,0:T(8,128)S(1)}, f32[32,8,128]{2,1,0:T(8,128)}, u32[]{:S(2)}) copy-start(f32[32,8,128]{2,1,0:T(8,128)} %param.10) | copy-start | bytes 393220
  3.8 0.9 %copy-start.3 = (f32[32,8,128]{2,1,0:T(8,128)S(1)}, f32[32,8,128]{2,1,0:T(8,128)}, u32[]{:S(2)}) copy-start(f32[32,8,128]{2,1,0:T(8,128)} %param.11) | copy-start | bytes 393220
  4.7 0.7 %copy-start.4 = (f32[3,8,128]{2,1,0:T(8,128)S(1)}, f32[3,8,128]{2,1,0:T(8,128)}, u32[]{:S(2)}) copy-start(f32[3,8,128]{2,1,0:T(8,128)} %param.12) | copy-start | bytes 36868
  5.4 0.7 %copy-start.5 = (f32[8,128]{1,0:T(8,128)S(1)}, f32[8,128]{1,0:T(8,128)}, u32[]{:S(2)}) copy-start(f32[8,128]{1,0:T(8,128)} %refs_6_.1) | copy-start | bytes 12292
  6.1 0.7 %copy-start.6 = (s32[8,128]{1,0:T(8,128)S(1)}, s32[8,128]{1,0:T(8,128)}, u32[]{:S(2)}) copy-start(s32[8,128]{1,0:T(8,128)} %refs_7_.1) | copy-start | bytes 12292
  6.8 0.7 %copy-start.7 = (s32[8,128]{1,0:T(8,128)S(1)}, s32[8,128]{1,0:T(8,128)}, u32[]{:S(2)}) copy-start(s32[8,128]{1,0:T(8,128)} %refs_8_.1) | copy-start | bytes 12292
  11.9 2.6 %collective-permute-start = (f32[216,128]{1,0:T(8,128)S(1)}, f32[216,128]{1,0:T(8,128)S(1)}, u32[]{:S(2)}, u32[]{:S(2)}) collective-permute-start(f32[216,128]{1,0:T(8,128)S(1)} %get-tuple-element.38), channel_id=1, source_target_pairs={{0,4},{8,12},{16,20},{24,28},{4,0},{12,8},{20,16},{28,24},{1,5},{9... | collective-permute-start | bytes 331784 | tf_op jit(solution)/shard_map/ppermute | solution.py:581
  12.0 6.1 %collective-permute-start.1 = (f32[216,128]{1,0:T(8,128)S(1)}, f32[216,128]{1,0:T(8,128)S(1)}, u32[]{:S(2)}, u32[]{:S(2)}) collective-permute-start(f32[216,128]{1,0:T(8,128)S(1)} %get-tuple-element.39), channel_id=1, source_target_pairs={{4,8},{12,16},{20,24},{8,4},{16,12},{24,20},{5,9},{13,17},{21,25},... | collective-permute-start | bytes 331784 | tf_op jit(solution)/shard_map/ppermute | solution.py:581
  21.2 7.6 %collective-permute-start.2 = (f32[456,128]{1,0:T(8,128)S(1)}, f32[456,128]{1,0:T(8,128)S(1)}, u32[]{:S(2)}, u32[]{:S(2)}) collective-permute-start(f32[456,128]{1,0:T(8,128)S(1)} %get-tuple-element.44), channel_id=1, source_target_pairs={{0,1},{2,3},{1,0},{3,2},{4,5},{6,7},{5,4},{7,6},{8,9},{10,11},{9,8... | collective-permute-start | bytes 700424 | tf_op jit(solution)/shard_map/ppermute | solution.py:581
  21.7 10.1 %collective-permute-start.3 = (f32[456,128]{1,0:T(8,128)S(1)}, f32[456,128]{1,0:T(8,128)S(1)}, u32[]{:S(2)}, u32[]{:S(2)}) collective-permute-start(f32[456,128]{1,0:T(8,128)S(1)} %get-tuple-element.45), channel_id=1, source_target_pairs={{1,2},{2,1},{5,6},{6,5},{9,10},{10,9},{13,14},{14,13},{17,18},{18,... | collective-permute-start | bytes 700424 | tf_op jit(solution)/shard_map/ppermute | solution.py:581
  37.5 7.6 %collective-permute-start.4 = (f32[376,128]{1,0:T(8,128)S(1)}, f32[376,128]{1,0:T(8,128)S(1)}, u32[]{:S(2)}, u32[]{:S(2)}) collective-permute-start(f32[376,128]{1,0:T(8,128)S(1)} %get-tuple-element.50), channel_id=1, source_target_pairs={{0,1},{2,3},{1,0},{3,2},{4,5},{6,7},{5,4},{7,6},{8,9},{10,11},{9,8... | collective-permute-start | bytes 577544 | tf_op jit(solution)/shard_map/ppermute | solution.py:581
  37.6 9.7 %collective-permute-start.5 = (f32[376,128]{1,0:T(8,128)S(1)}, f32[376,128]{1,0:T(8,128)S(1)}, u32[]{:S(2)}, u32[]{:S(2)}) collective-permute-start(f32[376,128]{1,0:T(8,128)S(1)} %get-tuple-element.51), channel_id=1, source_target_pairs={{1,2},{2,1},{5,6},{6,5},{9,10},{10,9},{13,14},{14,13},{17,18},{18,... | collective-permute-start | bytes 577544 | tf_op jit(solution)/shard_map/ppermute | solution.py:581

commit v3 on v0

v3 whole, which is shorter than its diff:
```python
import jax
import jax.numpy as jnp
from jax import lax
from jax.experimental import pallas as pl
from jax.experimental.pallas import tpu as pltpu
from jax.sharding import PartitionSpec as P

RATE = 0.3 / 24.0
OCEAN_RATE = 0.3
UPLIFT = 0.5
LOADING = 0.5
VISCOUS = 0.1

ROWS = 8
SUB = 8
LANES = 128
EDGE = 8
GROUP = 2 * EDGE
TILES = 4
HALF = TILES * GROUP
SPAN = TILES + 1
WINDOW = TILES

LEVEL, FLUX_X, FLUX_Y, DEPTH, FLOOR, WET = range(6)
VX, VY, VZ, SXX, SYY, SZZ, SXY, SXZ, SYZ, LAME, SHEAR, BUOY = range(12)
FIELDS = 12

OPEN = ((VX, 0), (VX, 1), (VX, 7), (VY, 0), (VY, 6), (VY, 7), (VZ, 0), (VZ, 1), (VZ, 7))
CLOSED = tuple((c, y) for y in range(ROWS) for c in (VX, VY, VZ) if (c, y) not in OPEN)
INNER = (3, 4)
OUTER = tuple(y for y in range(ROWS) if y not in INNER)

SPEED_HIGH = ((VX, 7), (VY, 6), (VY, 7), (VZ, 7))
SPEED_LOW = ((VX, 0), (VX, 1), (VY, 0), (VZ, 0), (VZ, 1))
STRESS_HIGH = ((SXY, 6), (SXY, 7), (SYY, 7), (SYZ, 6), (SYZ, 7))
STRESS_LOW = ((SXY, 0), (SYY, 0), (SYY, 1), (SYZ, 0))
BUOY_HIGH = ((BUOY, 6), (BUOY, 7))
BUOY_LOW = ((BUOY, 0), (BUOY, 1))
LINES = (None, WET, FLOOR, FLUX_X, FLUX_Y)


def rolled(x, shift, axis):
    shift %= x.shape[axis]
    return x if shift == 0 else pltpu.roll(x, shift, axis)


def tile(ref, index):
    return ref[index * SUB : (index + 1) * SUB, :]


def row(ref, index):
    return ref[index : index + 1, :]


def store(ref, index, value):
    ref[index * SUB : (index + 1) * SUB, :] = value


def minus(a, b):
    if b is None:
        return a
    return -b if a is None else a - b


def near_far(a, b, c, d):
    near, far = 27.0 * minus(a, b), minus(c, d)
    return near if c is None and d is None else near - far


class Grid:
    def __init__(self):
        self.sub = lax.broadcasted_iota(jnp.int32, (SUB, LANES), 0)
        self.lane = lax.broadcasted_iota(jnp.int32, (SUB, LANES), 1)
        self.first = self.lane % GROUP < EDGE
        self.left = self.lane < HALF
        self.group = self.lane // GROUP
        self.zero = jnp.zeros((SUB, LANES), jnp.float32)
        depth = [self.sub + SUB * t for t in range(TILES)] + [self.sub + SUB * (self.group % TILES)]
        self.depth = [d.astype(jnp.float32) for d in depth]

    def beside(self, window):
        return jnp.where(self.first, window, rolled(window, HALF, 1))

    def edge(self, beside, t):
        return None if t == WINDOW else rolled(beside, LANES - EDGE - GROUP * t, 1)

    def along(self, x, offset, edge):
        if edge is not None:
            lane = self.lane
            keep = {-1: lane == LANES - 1, -2: lane >= LANES - 2, 1: lane == 0, 2: lane <= 1}[offset]
            x = jnp.where(keep, edge, x)
        return rolled(x, -offset, 1)

    def fx(self, x, edge):
        return near_far(self.along(x, 1, edge), x, self.along(x, 2, edge), self.along(x, -1, edge))

    def bx(self, x, edge):
        return near_far(x, self.along(x, -1, edge), self.along(x, 1, edge), self.along(x, -2, edge))

    def around(self, field, y, t):
        if t == WINDOW:
            x, at = field(y, t), self.lane % HALF
            above = jnp.where(at >= GROUP, rolled(x, GROUP, 1), 0.0)
            return above, x, jnp.where(at < HALF - GROUP, rolled(x, -GROUP, 1), 0.0)
        above = field(y, t - 1) if t else self.zero
        return above, field(y, t), field(y, t + 1) if t + 1 < TILES else self.zero

    def down(self, three, offset):
        above, x, below = three
        sub = self.sub
        keep = {-1: sub == SUB - 1, -2: sub >= SUB - 2, 1: sub == 0, 2: sub <= 1}[offset]
        return rolled(jnp.where(keep, above if offset < 0 else below, x), -offset, 0)

    def fz(self, field, y, t):
        three = self.around(field, y, t)
        return near_far(self.down(three, 1), three[1], self.down(three, 2), self.down(three, -1))

    def bz(self, field, y, t):
        three = self.around(field, y, t)
        return near_far(three[1], self.down(three, -1), self.down(three, 1), self.down(three, -2))

    def fy(self, field, y, t):
        return near_far(field(y + 1, t), field(y, t), field(y + 2, t), field(y - 1, t))

    def by(self, field, y, t):
        return near_far(field(y, t), field(y - 1, t), field(y + 1, t), field(y - 2, t))

    def windows(self, own, from_left, from_right):
        return jnp.where(
            self.left, jnp.where(self.first, from_left, own), jnp.where(self.first, own, from_right)
        )

    def every_group(self, x):
        for shift in (GROUP, 2 * GROUP):
            x = x + jnp.where(self.lane % HALF >= shift, rolled(x, shift, 1), rolled(x, shift - HALF, 1))
        return x

    def across(self, x, offset, beside):
        end = 0 if offset < 0 else ROWS - 1
        return jnp.where(self.sub == end, beside, rolled(x, -offset, 0))


def inside(field):
    return lambda y, t: field(y, t) if 0 <= y < ROWS else None


def fields_of(main, windows):
    def field(f):
        return lambda y, t: tile(windows, f * ROWS + y) if t == WINDOW else tile(main, (f * ROWS + y) * TILES + t)

    return field


def pack(grid, items, odd, even_way, odd_way, index):
    a, b, c, d = items
    first, left = grid.first, grid.left
    right_way = jnp.where(
        left, jnp.where(first, a, rolled(b, EDGE, 1)), jnp.where(first, c, rolled(d, EDGE, 1))
    )
    left_way = jnp.where(
        left, jnp.where(first, rolled(b, -EDGE, 1), a), jnp.where(first, rolled(d, -EDGE, 1), c)
    )
    store(even_way, index, jnp.where(odd, left_way, right_way))
    store(odd_way, index, jnp.where(odd, right_way, left_way))


def unpack(grid, items, odd, even_in, odd_in, index):
    x, y = tile(even_in, index), tile(odd_in, index)
    before, after = jnp.where(odd, x, y), jnp.where(odd, y, x)
    befores = [before, rolled(before, -EDGE, 1), rolled(before, HALF, 1), rolled(before, HALF - EDGE, 1)]
    afters = [rolled(after, HALF, 1), rolled(after, HALF + EDGE, 1), after, rolled(after, EDGE, 1)]
    return [grid.windows(*three) for three in zip(items, befores, afters)]


def edges_kernel(flags, *refs):
    hbm, refs = refs[:8], refs[8:]
    (main, flat, own, own_flat, even_way, odd_way), (wave, lame, shear, buoy, ocean, deep, floor, wet), sem = (
        refs[:6], refs[6:14], refs[14],
    )
    size = wave.shape[0] // 9
    copies = []
    for f in range(9):
        part = slice(f * size, (f + 1) * size)
        copies.append(pltpu.make_async_copy(hbm[0].at[part, :], wave.at[part, :], sem.at[f]))
    for k, target in enumerate((lame, shear, buoy, ocean, deep, floor, wet)):
        copies.append(pltpu.make_async_copy(hbm[1 + k], target, sem.at[9 + k]))
    for copy in copies:
        copy.start()
    grid = Grid()
    odd = (flags[0] & 1) == 1
    sources = [(wave, f) for f in range(9)] + [(lame, 0), (shear, 0), (buoy, 0)]
    for f in range(0, FIELDS, 2):
        copies[f].wait()
        copies[f + 1].wait()
        for q in range(0, ROWS, 2):
            items = []
            for y in (q, q + 1):
                for h in (f, f + 1):
                    ref, base = sources[h]
                    out = grid.zero
                    for t in range(TILES):
                        x = ref[pl.ds(base * size + t * SUB * ROWS + y, SUB, stride=ROWS), :]
                        store(main, (h * ROWS + y) * TILES + t, x)
                        out = jnp.where(grid.group == t, rolled(x, EDGE + GROUP * t, 1), out)
                    out = jnp.where(grid.left, out, rolled(out, HALF, 1))
                    store(own, h * ROWS + y, out)
                    items.append(out)
            pack(grid, items, odd, even_way, odd_way, (f * ROWS // 2 + q) // 2)
    for copy in copies[FIELDS:]:
        copy.wait()
    planes = [tile(ocean, k) for k in range(3)] + [deep[...]]
    planes += [floor[...].astype(jnp.float32), wet[...].astype(jnp.float32)]
    items = []
    for k, x in enumerate(planes):
        store(flat, k, x)
        out = grid.zero
        for g in range(LANES // GROUP):
            out = jnp.where(grid.group == g, rolled(x, EDGE + GROUP * g, 1), out)
        store(own_flat, k, out)
        items.append(out)
    pack(grid, items[:4], odd, even_way, odd_way, FIELDS * ROWS // 4)
    pack(grid, items[4:] * 2, odd, even_way, odd_way, FIELDS * ROWS // 4 + 1)


def speeds(grid, stress, speed, buoy, todo, put):
    sxx, syy, szz, sxy, sxz, syz = stress
    for y in range(ROWS):
        parts = [c for c in (VX, VY, VZ) if (c, y) in todo]
        if not parts:
            continue
        need = {VX: (sxx,), VY: (sxy,), VZ: (sxz,)}
        beside = {c: grid.beside(need[c][0](y, WINDOW)) for c in parts}
        for t in range(SPAN):
            rate = RATE * buoy(y, t)
            for c in parts:
                edge = grid.edge(beside[c], t)
                if c == VX:
                    a = grid.fx(sxx(y, t), edge) + grid.by(sxy, y, t) + grid.bz(sxz, y, t)
                elif c == VY:
                    a = grid.bx(sxy(y, t), edge) + grid.fy(syy, y, t) + grid.bz(syz, y, t)
                else:
                    a = grid.bx(sxz(y, t), edge) + grid.by(syz, y, t) + grid.fz(szz, y, t)
                put(c, y, t, speed(c)(y, t) + rate * a)


def stresses(grid, rows, tiles, speed, stress, lame, shear, put):
    vx, vy, vz = [speed(c) for c in (VX, VY, VZ)]
    for y in rows:
        b_x, b_y, b_z = [grid.beside(v(y, WINDOW)) for v in (vx, vy, vz)]
        for t in range(tiles):
            e_x, e_y, e_z = [grid.edge(b, t) for b in (b_x, b_y, b_z)]
            strain_x = grid.bx(vx(y, t), e_x)
            strain_y = grid.by(vy, y, t)
            strain_z = grid.bz(vz, y, t)
            mu = RATE * shear(y, t)
            spread = (RATE * lame(y, t)) * (strain_x + strain_y + strain_z)
            two = mu + mu
            put(SXX, y, t, stress(SXX)(y, t) + (spread + two * strain_x))
            put(SYY, y, t, stress(SYY)(y, t) + (spread + two * strain_y))
            put(SZZ, y, t, stress(SZZ)(y, t) + (spread + two * strain_z))
            put(SXY, y, t, stress(SXY)(y, t) + mu * (grid.fy(vx, y, t) + grid.fx(vy(y, t), e_y)))
            put(SXZ, y, t, stress(SXZ)(y, t) + mu * (grid.fz(vx, y, t) + grid.fx(vz(y, t), e_z)))
            put(SYZ, y, t, stress(SYZ)(y, t) + mu * (grid.fz(vy, y, t) + grid.fy(vz, y, t)))


def flat_edge(grid, at, k):
    return grid.edge(grid.beside(at(1)), 0) if k == 0 else None


def partial_level(grid, flat, put):
    for k in range(2):
        x, y = flat(FLUX_X, k), flat(FLUX_Y, k)
        edge = flat_edge(grid, lambda q: flat(FLUX_X, q), k)
        spread = 0.5 * (grid.along(x, 1, edge) - grid.along(x, -1, edge))
        spread = spread + 0.5 * (grid.across(y, 1, 0.0) - grid.across(y, -1, 0.0))
        put(k, flat(LEVEL, k) - OCEAN_RATE * (flat(WET, k) * spread))


class Message:
    def __init__(self, rows, thin):
        self.at, size = [], 0
        for f, _ in rows:
            self.at.append(size)
            size += TILES if thin and f < 3 else SPAN
        self.tiles = self.at[1:] + [size]
        self.tiles = [b - a for a, b in zip(self.at, self.tiles)]
        self.rows = rows
        self.base = size * SUB
        self.size = self.base + 2 * SUB


def messages(first):
    high = SPEED_HIGH + STRESS_HIGH + (BUOY_HIGH if first else ())
    low = SPEED_LOW + STRESS_LOW + (BUOY_LOW if first else ())
    return Message(high, not first), Message(low, not first)


def message_size(first):
    return max(m.size for m in messages(first))


def send(first, odd, field, line, even_way, odd_way):
    high, low = messages(first)

    def fill(message, edge, out):
        for (f, y), at, tiles in zip(message.rows, message.at, message.tiles):
            for t in range(tiles):
                store(out, at + t, field(f)(y, t))
        at = message.base
        for which in LINES:
            for k in range(2):
                out[at : at + 1, :] = line(which, k, edge)
                at += 1
        out[at : at + 6, :] = jnp.zeros((6, LANES), jnp.float32)
        tail = out.shape[0]
        if message.size < tail:
            out[message.size : tail, :] = jnp.zeros((tail - message.size, LANES), jnp.float32)

    @pl.when(odd)
    def _():
        fill(high, ROWS - 1, odd_way)
        fill(low, 0, even_way)

    @pl.when(jnp.logical_not(odd))
    def _():
        fill(high, ROWS - 1, even_way)
        fill(low, 0, odd_way)


class Received:
    def __init__(self, message, odd, if_odd, if_even):
        self.message, self.odd, self.refs = message, odd, (if_odd, if_even)

    def pick(self, take):
        return jnp.where(self.odd, take(self.refs[0]), take(self.refs[1]))

    def __call__(self, index, t):
        return self.pick(lambda ref: tile(ref, self.message.at[index] + t))

    def line(self, which, k):
        at = self.message.base + 2 * LINES.index(which) + k
        return self.pick(lambda ref: row(ref, at))


def received(first, odd, even_in, odd_in):
    high, low = messages(first)
    return Received(high, odd, even_in, odd_in), Received(low, odd, odd_in, even_in)


AROUND = ROWS + 4


def finish(grid, tiles, partial, stress, buoy, lo, hi, lo_buoy, hi_buoy, speed):
    sxy, syy, syz = [stress(f) for f in (SXY, SYY, SYZ)]

    def put(c, y, t, value):
        store(speed, (c * AROUND + y + 2) * SPAN + t, value)

    for t in range(SPAN):
        sends = {"xy": (4, 5), "yz": (7, 8)}
        for c, key, at in ((VX, "xy", 5), (VZ, "yz", 8)):
            two, one = lo(sends[key][0], t), lo(sends[key][1], t)
            rate = [RATE * buoy(y, t) for y in (0, 1, 7)]
            put(c, 0, t, partial(c, 0, t) + rate[0] * (two - 27.0 * one))
            put(c, 1, t, partial(c, 1, t) + rate[1] * one)
            put(c, 7, t, partial(c, 7, t) - rate[2] * hi(at, t))
        h8, h9 = hi(6, t), hi(7, t)
        put(VY, 0, t, partial(VY, 0, t) + (RATE * buoy(0, t)) * lo(6, t))
        put(VY, 6, t, partial(VY, 6, t) - (RATE * buoy(6, t)) * h8)
        put(VY, 7, t, partial(VY, 7, t) + (RATE * buoy(7, t)) * (27.0 * h8 - h9))
    for t in range(tiles):
        b2, b1 = RATE * lo_buoy(9, t), RATE * lo_buoy(10, t)
        b8, b9 = RATE * hi_buoy(9, t), RATE * hi_buoy(10, t)
        put(VX, -1, t, lo(0, t) - b1 * sxy(0, t))
        put(VY, -2, t, lo(1, t) - b2 * syy(0, t))
        put(VY, -1, t, lo(2, t) + b1 * (27.0 * syy(0, t) - syy(1, t)))
        put(VZ, -1, t, lo(3, t) - b1 * syz(0, t))
        put(VX, 8, t, hi(0, t) + b8 * (sxy(6, t) - 27.0 * sxy(7, t)))
        put(VX, 9, t, hi(1, t) + b9 * sxy(7, t))
        put(VY, 8, t, hi(2, t) + b8 * syy(7, t))
        put(VZ, 8, t, hi(3, t) + b8 * (syz(6, t) - 27.0 * syz(7, t)))
        put(VZ, 9, t, hi(4, t) + b9 * syz(7, t))


def seafloor(grid, vz, y, floors, out, index):
    total = None
    for t in range(TILES):
        part = jnp.where(floors[0] == grid.depth[t], vz(y, t), 0.0)
        total = part if total is None else total + part
    out[index : index + 1, :] = jnp.sum(total, axis=0, keepdims=True)
    if len(floors) > 1:
        part = jnp.where(floors[1] == grid.depth[WINDOW], vz(y, WINDOW), 0.0)
        out[2 * SUB + index : 2 * SUB + index + 1, :] = jnp.sum(part, axis=0, keepdims=True)


def sea(grid, speed, level, now, fixed, line, lo, hi, sums, new, last):
    vz = speed(VZ)
    for y in range(ROWS):
        seafloor(grid, vz, y, [line(FLOOR, k, y) for k in range(2)], sums, y)
    ends = 1 if last else 2
    for y, side, at in ((-1, lo, ROWS), (ROWS, hi, ROWS + 1)):
        seafloor(grid, vz, y, [side.line(FLOOR, k) for k in range(ends)], sums, at)
    floors, beyond = [tile(sums, 0), grid.every_group(tile(sums, 2))], [tile(sums, 1), None]
    if not last:
        beyond[1] = grid.every_group(tile(sums, 3))
    sub = grid.sub
    levels, lows, highs = [], [], []
    for k in range(2):
        near = jnp.where(sub == 0, lo.line(FLUX_Y, k), jnp.where(sub == ROWS - 1, -hi.line(FLUX_Y, k), 0.0))
        levels.append(level(k) + fixed(WET, k) * (UPLIFT * floors[k] + (0.5 * OCEAN_RATE) * near))
        new(LEVEL, k, levels[k])
        if k < ends:
            for side, at, y, sign, out in ((lo, 0, 0, -1.0, lows), (hi, 1, ROWS - 1, 1.0, highs)):
                mine = (sign * 0.5 * OCEAN_RATE) * line(FLUX_Y, k, y)
                rest = UPLIFT * beyond[k][at : at + 1, :] + mine
                out.append(side.line(None, k) + side.line(WET, k) * rest)
    for k in range(ends):
        wet, deep = fixed(WET, k), fixed(DEPTH, k)
        edge = flat_edge(grid, lambda q: levels[q], k)
        slope_x = 0.5 * (grid.along(levels[k], 1, edge) - grid.along(levels[k], -1, edge))
        slope_y = 0.5 * (grid.across(levels[k], 1, highs[k]) - grid.across(levels[k], -1, lows[k]))
        for which, slope in ((FLUX_X, slope_x), (FLUX_Y, slope_y)):
            x = now(which, k)
            edge = flat_edge(grid, lambda q: now(which, q), k)
            laplace = grid.along(x, 1, edge) + grid.along(x, -1, edge) - 4.0 * x
            laplace = laplace + grid.across(x, 1, hi.line(which, k)) + grid.across(x, -1, lo.line(which, k))
            new(which, k, wet * (x - OCEAN_RATE * deep * slope + VISCOUS * laplace))
    return levels


def press(grid, levels, fixed, line, pressure):
    for k in range(2):
        store(pressure, k, LOADING * fixed(WET, k) * levels[k])

    def load(y, t):
        k = 1 if t == WINDOW else 0
        return jnp.where(line(FLOOR, k, y) == grid.depth[t], row(pressure, k * ROWS + y), 0.0)

    return load


def edge_index(c, y):
    return OPEN.index((c, y)) * SPAN


def block_index(c, y):
    return (c * ROWS + y) * SPAN


def start_kernel(
    flags, main, flat, own, own_flat, even_in, odd_in,
    windows, flat_windows, partial, level, even_way, odd_way,
):
    grid = Grid()
    odd = (flags[0] & 1) == 1
    for f in range(0, FIELDS, 2):
        for q in range(0, ROWS, 2):
            places = [h * ROWS + y for y in (q, q + 1) for h in (f, f + 1)]
            items = [tile(own, p) for p in places]
            for p, x in zip(places, unpack(grid, items, odd, even_in, odd_in, (f * ROWS // 2 + q) // 2)):
                store(windows, p, x)
    items = [tile(own_flat, k) for k in range(6)]
    base = FIELDS * ROWS // 4
    for k, x in enumerate(unpack(grid, items[:4], odd, even_in, odd_in, base)):
        store(flat_windows, k, x)
    for k, x in enumerate(unpack(grid, items[4:] * 2, odd, even_in, odd_in, base + 1)[:2]):
        store(flat_windows, 4 + k, x)

    field = fields_of(main, windows)
    speeds(
        grid, [inside(field(f)) for f in range(SXX, SYZ + 1)], field, field(BUOY), OPEN,
        lambda c, y, t, value: store(partial, edge_index(c, y) + t, value),
    )
    flats = (flat, flat_windows)
    partial_level(grid, lambda f, k: tile(flats[k], f), lambda k, value: store(level, k, value))

    def rows_of(f):
        return (lambda y, t: tile(partial, edge_index(f, y) + t)) if f < 3 else field(f)

    def line(which, k, y):
        return row(level, k * ROWS + y) if which is None else row(flats[k], which * ROWS + y)

    send(True, (flags[1] & 1) == 1, rows_of, line, even_way, odd_way)


def start_rest_kernel(main, windows, speed_out, stress_out):
    grid = Grid()
    field = fields_of(main, windows)
    speeds(
        grid, [inside(field(f)) for f in range(SXX, SYZ + 1)], field, field(BUOY), CLOSED,
        lambda c, y, t, value: store(speed_out, block_index(c, y) + t, value),
    )
    stresses(
        grid, INNER, SPAN, lambda c: lambda y, t: tile(speed_out, block_index(c, y) + t), field,
        field(LAME), field(SHEAR),
        lambda f, y, t, value: store(stress_out, block_index(f - SXX, y) + t, value),
    )


def speed_reader(around, block):
    def speed(c):
        def read(y, t):
            if (c, y) in CLOSED:
                return tile(block, block_index(c, y) + t)
            return tile(around, (c * AROUND + y + 2) * SPAN + t)

        return read

    return speed


def middle_kernel(
    flags, main, windows, flat, flat_windows, partial, level, speed_in, stress_in, even_in, odd_in,
    speed_out, stress_out, ocean, partial_out, level_out, even_way, odd_way,
    sums, pressure,
):
    grid = Grid()
    odd = (flags[1] & 1) == 1
    lo, hi = received(True, odd, even_in, odd_in)
    field = fields_of(main, windows)
    finish(
        grid, SPAN, lambda c, y, t: tile(partial, edge_index(c, y) + t), field, field(BUOY), lo, hi, lo, hi, speed_out
    )
    speed = speed_reader(speed_out, speed_in)
    flats = (flat, flat_windows)
    fixed = lambda f, k: tile(flats[k], f)
    line = lambda f, k, y: row(flats[k], f * ROWS + y)

    def new(f, k, value):
        store(ocean, 3 * k + f, value)

    levels = sea(grid, speed, lambda k: tile(level, k), fixed, fixed, line, lo, hi, sums, new, False)
    load = press(grid, levels, fixed, line, pressure)

    def put(f, y, t, value):
        store(stress_out, block_index(f - SXX, y) + t, value - load(y, t) if f == SZZ else value)

    stresses(grid, OUTER, SPAN, speed, field, field(LAME), field(SHEAR), put)
    for f in range(SXX, SYZ + 1):
        for y in INNER:
            for t in range(SPAN):
                put(f, y, t, tile(stress_in, block_index(f - SXX, y) + t))
    stress = lambda f: lambda y, t: tile(stress_out, block_index(f - SXX, y) + t)
    speeds(
        grid, [inside(stress(f)) for f in range(SXX, SYZ + 1)], speed, field(BUOY), OPEN,
        lambda c, y, t, value: store(partial_out, edge_index(c, y) + t, value),
    )
    moving = lambda f, k: tile(flats[k], f) if f >= DEPTH else tile(ocean, 3 * k + f)
    partial_level(grid, moving, lambda k, value: store(level_out, k, value))

    def rows_of(f):
        return (lambda y, t: tile(partial_out, edge_index(f, y) + t)) if f < 3 else stress(f)

    def line_out(which, k, y):
        if which is None:
            return row(level_out, k * ROWS + y)
        return line(which, k, y) if which >= DEPTH else row(ocean, (3 * k + which) * ROWS + y)

    send(False, odd, rows_of, line_out, even_way, odd_way)


def middle_rest_kernel(main, windows, around, speed_in, stress_in, speed_out, stress_out):
    grid = Grid()
    field = fields_of(main, windows)
    stress = lambda f: lambda y, t: tile(stress_in, block_index(f - SXX, y) + t)
    speeds(
        grid, [inside(stress(f)) for f in range(SXX, SYZ + 1)], speed_reader(around, speed_in), field(BUOY), CLOSED,
        lambda c, y, t, value: store(speed_out, block_index(c, y) + t, value),
    )
    stresses(
        grid, INNER, TILES, lambda c: lambda y, t: tile(speed_out, block_index(c, y) + t), stress,
        field(LAME), field(SHEAR),
        lambda f, y, t, value: store(stress_out, block_index(f - SXX, y) + t, value),
    )


def last_kernel(
    flags, main, windows, flat, flat_windows, stress_in, ocean_in, partial, level, speed_in, inner_in,
    even_first, odd_first, even_in, odd_in,
    wave_hbm, ocean_out,
    sums, pressure, around, wave, sem,
):
    grid = Grid()
    odd = (flags[1] & 1) == 1
    lo, hi = received(False, odd, even_in, odd_in)
    lo_buoy, hi_buoy = received(True, odd, even_first, odd_first)
    field = fields_of(main, windows)
    stress = lambda f: lambda y, t: tile(stress_in, block_index(f - SXX, y) + t)
    finish(
        grid, TILES, lambda c, y, t: tile(partial, edge_index(c, y) + t), stress, field(BUOY),
        lo, hi, lo_buoy, hi_buoy, around,
    )
    speed = speed_reader(around, speed_in)
    size = wave.shape[0] // 9

    def put_out(f, y, t, value):
        wave[pl.ds(f * size + t * SUB * ROWS + y, SUB, stride=ROWS), :] = value

    def copy(f):
        part = slice(f * size, (f + 1) * size)
        return pltpu.make_async_copy(wave.at[part, :], wave_hbm.at[part, :], sem.at[f])

    for c in (VX, VY, VZ):
        for y in range(ROWS):
            for t in range(TILES):
                put_out(c, y, t, speed(c)(y, t))
        copy(c).start()
    flats = (flat, flat_windows)
    fixed = lambda f, k: tile(flats[k], f)

    def line(f, k, y):
        return row(flats[k], f * ROWS + y) if f >= DEPTH else row(ocean_in, (3 * k + f) * ROWS + y)

    def new(f, k, value):
        if k == 0:
            store(ocean_out, f, value)

    levels = sea(
        grid, speed, lambda k: tile(level, k), lambda f, k: tile(ocean_in, 3 * k + f), fixed, line, lo, hi, sums, new, True
    )
    load = press(grid, levels, fixed, line, pressure)

    def put(f, y, t, value):
        put_out(f, y, t, value - load(y, t) if f == SZZ else value)

    stresses(grid, OUTER, TILES, speed, stress, field(LAME), field(SHEAR), put)
    for f in range(SXX, SYZ + 1):
        for y in INNER:
            for t in range(TILES):
                put(f, y, t, tile(inner_in, block_index(f - SXX, y) + t))
        copy(f).start()
    for f in range(9):
        copy(f).wait()


IN_VMEM = pl.BlockSpec(memory_space=pltpu.VMEM)
IN_SMEM = pl.BlockSpec(memory_space=pltpu.SMEM)
IN_HBM = pl.BlockSpec(memory_space=pltpu.HBM)


def call(kernel, tiles, scratch, *arguments, flags=None, place=IN_VMEM, out_places=None, work=1):
    specs = [place] * len(arguments)
    if flags is not None:
        arguments, specs = (flags, *arguments), [IN_SMEM] + specs
    moved = sum(x.size for x in arguments) + sum(tiles) * SUB * LANES
    return pl.pallas_call(
        kernel,
        out_shape=[jax.ShapeDtypeStruct((n * SUB, LANES), jnp.float32) for n in tiles],
        in_specs=specs,
        out_specs=out_places or [IN_VMEM] * len(tiles),
        scratch_shapes=scratch,
        cost_estimate=pl.CostEstimate(flops=work * 1000000, bytes_accessed=4 * moved, transcendentals=0),
        compiler_params=pltpu.CompilerParams(vmem_limit_bytes=24 * 1024 * 1024),
    )(*arguments)


def planes(n):
    return pltpu.VMEM((n * SUB, LANES), jnp.float32)


def exchange(axis, even_way, odd_way):
    count = lax.axis_size(axis)

    def swap(x, start):
        pairs = [(i, i + 1) for i in range(start, count - 1, 2)]
        return lax.ppermute(x, axis, pairs + [(j, i) for i, j in pairs])

    return swap(even_way, 0), swap(odd_way, 1)


def local(*arguments):
    wave_fields, ocean_state = arguments[0], arguments[4]
    inputs = [pltpu.with_memory_space_constraint(x.reshape(-1, LANES), pltpu.HBM) for x in arguments]
    flags = jnp.stack([lax.axis_index("gx"), lax.axis_index("gy")])

    message = FIELDS * ROWS // 4 + 2
    main, flat, own, own_flat, even_way, odd_way = call(
        edges_kernel, [FIELDS * ROWS * TILES, 6, FIELDS * ROWS, 6, message, message],
        [pltpu.VMEM(x.shape, x.dtype) for x in inputs] + [pltpu.SemaphoreType.DMA((16,))],
        *inputs, flags=flags, place=IN_HBM,
    )
    x_in = exchange("gx", even_way, odd_way)
    first, later = [message_size(which) // SUB for which in (True, False)]
    edges, block = len(OPEN) * SPAN, ROWS * SPAN
    windows, flat_windows, partial, level, even_way, odd_way = call(
        start_kernel, [FIELDS * ROWS, 6, edges, 2, first, first], [],
        main, flat, own, own_flat, *x_in, flags=flags,
    )
    y_in = exchange("gy", even_way, odd_way)
    speed, inner = call(start_rest_kernel, [3 * block, 6 * block], [], main, windows, work=4)
    around, stress, ocean, partial, level, even_way, odd_way = call(
        middle_kernel, [3 * AROUND * SPAN, 6 * block, 6, edges, 2, later, later], [planes(4), planes(2)],
        main, windows, flat, flat_windows, partial, level, speed, inner, *y_in, flags=flags,
    )
    y_in2 = exchange("gy", even_way, odd_way)
    speed, inner = call(
        middle_rest_kernel, [3 * block, 6 * block], [], main, windows, around, speed, stress, work=4
    )
    wave_out, ocean_out = call(
        last_kernel, [9 * ROWS * TILES, 3],
        [planes(4), planes(2), planes(3 * AROUND * SPAN), planes(9 * ROWS * TILES), pltpu.SemaphoreType.DMA((9,))],
        main, windows, flat, flat_windows, stress, ocean, partial, level, speed, inner, *y_in, *y_in2,
        flags=flags, out_places=[IN_HBM, IN_VMEM],
    )
    return wave_out.reshape(wave_fields.shape), ocean_out.reshape(ocean_state.shape)


def solution(mesh):
    in_specs = (
        P(None, None, "gy", "gx"),
        P(None, "gy", "gx"),
        P(None, "gy", "gx"),
        P(None, "gy", "gx"),
        P(None, "gy", "gx"),
        P("gy", "gx"),
        P("gy", "gx"),
        P("gy", "gx"),
    )
    out_specs = (P(None, None, "gy", "gx"), P(None, "gy", "gx"))
    return jax.shard_map(local, mesh=mesh, in_specs=in_specs, out_specs=out_specs, check_vma=False)
```

time: 161 us -> 40.6 us (0.25); the launches traced: 158 us -> 40.3 us
  starting transfers between devices: 92.8 us -> 12 us
  waiting for transfers between devices: 43.8 us -> 7.55 us
  Pallas kernels: 0 us -> 19.9 us
  other arithmetic: 12 us -> 0.08 us
  local copies, waits for them, and re-layouts: 7.8 us -> 0 us
    ppermute x32 -> x6, starting transfers between devices: 92.8 us -> 12 us  [swap(): return lax.ppermute(x, axis, pairs + [(j, i) for i, j in pairs])]
    ppermute x32 -> x6, waiting for transfers between devices: 43.8 us -> 7.55 us  [swap(): return lax.ppermute(x, axis, pairs + [(j, i) for i, j in pairs])]
    pallas_call x0 -> x6, Pallas kernels: none -> 19.9 us  [call(): pl.pallas_call(kernel, out_shape=[jax.ShapeDtypeStruct((n * SUB, LANES),...]
    concatenate x8 -> x0, other arithmetic: 3.41 us -> none  [the longest x6 2.46 us: extended(): block = jnp.concatenate([low, block, high], axis=dim)]
    unnamed x27 -> x0, local copies, waits for them, and re-layouts: 3.35 us -> none
    unnamed x9 -> x0, other arithmetic: 2.57 us -> none
    squeeze x13 -> x0, local copies, waits for them, and re-layouts: 2.4 us -> none  [the longest x1 1.21 us: local(): stress[2]]
    slice x7 -> x0, other arithmetic: 1.74 us -> none  [the longest x5 1.59 us: extended(): lax.slice_in_dim(block, block.shape[dim] - width, None, axis=dim)]
  transfers between devices with their start and end apart: 32 -> 6, of which waited for: 15 -> 3; matrix products, arithmetic and copies ran while one was open for 3% -> 0% of each run, Pallas kernels for 0% -> 16%
where the time goes in v3:
time: 40.6 us; the launch traced here: 40.3 us
  Pallas kernels  19.9 us (49%)
  starting transfers between devices  12 us (30%)
  waiting for transfers between devices  7.55 us (19%)
  between operations  0.73 us (2%)
    pallas_call x6, Pallas kernels, call(): pl.pallas_call(kernel, out_shape=[jax.ShapeDtypeStruct((n * SUB, LANES),...  19.9 us
    ppermute x6, starting transfers between devices, swap(): return lax.ppermute(x, axis, pairs + [(j, i) for i, j in pairs])  12 us
    ppermute x6, waiting for transfers between devices, swap(): return lax.ppermute(x, axis, pairs + [(j, i) for i, j in pairs])  7.55 us
  transfers between devices with their start and end apart: 6, of which 3 were waited for; matrix products, arithmetic and copies ran while one was open for 0% of the time, Pallas kernels for 16%

profile of v3, /device:TPU:10, one launch (start us, length us, event | category | flops | bytes accessed | tf_op | source)
XLA Modules:
  0.0 40.3 jit_solution(9524564379816140935)
XLA Ops:
  0.6 0.1 pad_add_fusion.flags
  0.7 3.3 %shard_map.95 = (f32[3072,128]{1,0:T(8,128)S(1)}, f32[48,128]{1,0:T(8,128)S(1)}, f32[768,128]{1,0:T(8,128)S(1)}, f32[48,128]{1,0:T(8,128)S(1)}, f32[208,128]{1,0:T(8,128)S(1)}, /*index=5*/f32[208,128]{1,0:T(8,128)S(1)}) custom-call(s32[2]{0:T(128)S(1)} %pad_add_fusion.flags, f32[2304,128]{1,0:T(8,128)} %bitcast.9, f32[256,128]{1,0:T(8,128)} %bitcast.10, ...), custom_call_target="tpu_custom_call" | custom-call | flops 1000000 | bytes 3825672 | tf_op jit(solution)/shard_map/pallas_call | solution.py:646
  4.0 0.1 collective-permute-start
  4.1 2.5 %collective-permute-start.1 = (f32[208,128]{1,0:T(8,128)S(1)}, f32[208,128]{1,0:T(8,128)S(1)}, u32[]{:S(2)}, u32[]{:S(2)}) collective-permute-start(f32[208,128]{1,0:T(8,128)S(1)} %get-tuple-element.32), channel_id=1, source_target_pairs={{4,8},{12,16},{20,24},{8,4},{16,12},{24,20},{5,9},{13,17},{21,25},... | collective-permute-start | bytes 319496 | tf_op jit(solution)/shard_map/ppermute | solution.py:666
  6.7 0.0 collective-permute-done.even_in
  6.7 3.5 %collective-permute-done.1.odd_in = f32[208,128]{1,0:T(8,128)S(1)} collective-permute-done((f32[208,128]{1,0:T(8,128)S(1)}, f32[208,128]{1,0:T(8,128)S(1)}, u32[]{:S(2)}, u32[]{:S(2)}) %collective-permute-start.1) | collective-permute-done | bytes 106528 | tf_op jit(solution)/shard_map/ppermute | solution.py:666
  10.1 2.1 %shard_map.96 = (f32[768,128]{1,0:T(8,128)S(1)}, f32[48,128]{1,0:T(8,128)S(1)}, f32[360,128]{1,0:T(8,128)S(1)}, f32[16,128]{1,0:T(8,128)S(1)}, f32[456,128]{1,0:T(8,128)S(1)}, /*index=5*/f32[456,128]{1,0:T(8,128)S(1)}) custom-call(s32[2]{0:T(128)S(1)} %pad_add_fusion.flags, f32[3072,128]{1,0:T(8,128)S(1)} %get-tuple-element.27.main, ...), custom_call_target="tpu_custom_call" | custom-call | flops 1000000 | bytes 3305480 | tf_op jit(solution)/shard_map/pallas_call | solution.py:646
  12.3 0.5 %collective-permute-start.2 = (f32[456,128]{1,0:T(8,128)S(1)}, f32[456,128]{1,0:T(8,128)S(1)}, u32[]{:S(2)}, u32[]{:S(2)}) collective-permute-start(f32[456,128]{1,0:T(8,128)S(1)} %get-tuple-element.39), channel_id=1, source_target_pairs={{0,1},{2,3},{1,0},{3,2},{4,5},{6,7},{5,4},{7,6},{8,9},{10,11},{9,8... | collective-permute-start | bytes 700424 | tf_op jit(solution)/shard_map/ppermute | solution.py:666
  12.8 4.6 %collective-permute-start.3 = (f32[456,128]{1,0:T(8,128)S(1)}, f32[456,128]{1,0:T(8,128)S(1)}, u32[]{:S(2)}, u32[]{:S(2)}) collective-permute-start(f32[456,128]{1,0:T(8,128)S(1)} %get-tuple-element.40), channel_id=1, source_target_pairs={{1,2},{2,1},{5,6},{6,5},{9,10},{10,9},{13,14},{14,13},{17,18},{18,... | collective-permute-start | bytes 700424 | tf_op jit(solution)/shard_map/ppermute | solution.py:666
  17.4 3.4 %shard_map.97 = (f32[960,128]{1,0:T(8,128)S(1)}, f32[1920,128]{1,0:T(8,128)S(1)}) custom-call(f32[3072,128]{1,0:T(8,128)S(1)} %get-tuple-element.27.main, f32[768,128]{1,0:T(8,128)S(1)} %get-tuple-element.33.windows), custom_call_target="tpu_custom_call" | custom-call | flops 4000000 | bytes 3440640 | tf_op jit(solution)/shard_map/pallas_call | solution.py:646
  20.7 0.0 collective-permute-done.2.even_in.even_first
  20.8 2.2 %collective-permute-done.3.odd_in.odd_first = f32[456,128]{1,0:T(8,128)S(1)} collective-permute-done((f32[456,128]{1,0:T(8,128)S(1)}, f32[456,128]{1,0:T(8,128)S(1)}, u32[]{:S(2)}, u32[]{:S(2)}) %collective-permute-start.3) | collective-permute-done | bytes 233504 | tf_op jit(solution)/shard_map/ppermute | solution.py:666
  23.0 4.6 %shard_map.98 = (f32[1440,128]{1,0:T(8,128)S(1)}, f32[1920,128]{1,0:T(8,128)S(1)}, f32[48,128]{1,0:T(8,128)S(1)}, f32[360,128]{1,0:T(8,128)S(1)}, f32[16,128]{1,...) custom-call(s32[2]{0:T(128)S(1)} %pad_add_fusion.flags, f32[3072,128]{1,0:T(8,128)S(1)} %get-tuple-element.27.main, ...), custom_call_target="tpu_custom_call" | custom-call | flops 1000000 | bytes 6438920 | tf_op jit(solution)/shard_map/pallas_call | solution.py:646
  27.6 0.1 collective-permute-start.4
  27.6 4.2 %collective-permute-start.5 = (f32[344,128]{1,0:T(8,128)S(1)}, f32[344,128]{1,0:T(8,128)S(1)}, u32[]{:S(2)}, u32[]{:S(2)}) collective-permute-start(f32[344,128]{1,0:T(8,128)S(1)} %get-tuple-element.49), channel_id=1, source_target_pairs={{1,2},{2,1},{5,6},{6,5},{9,10},{10,9},{13,14},{14,13},{17,18},{18,... | collective-permute-start | bytes 528392 | tf_op jit(solution)/shard_map/ppermute | solution.py:666
  31.9 3.2 %shard_map.99 = (f32[960,128]{1,0:T(8,128)S(1)}, f32[1920,128]{1,0:T(8,128)S(1)}) custom-call(f32[3072,128]{1,0:T(8,128)S(1)} %get-tuple-element.27.main, f32[768,128]{1,0:T(8,128)S(1)} %get-tuple-element.33.windows, f32[1440,128]{1,0:T(8,128)S(1)} %get-tuple-element.45.around, f32[960,128]{1,0:T(8,128)S(1)} %get-tuple-element.37.speed_in, ...), custom_call_target="tpu_custom_call" | custom-call | flops 4000000 | bytes 5652480 | tf_op jit(solution)/shard_map/pallas_call | solution.py:646
  35.1 0.0 collective-permute-done.4.even_in
  35.1 1.8 %collective-permute-done.5.odd_in = f32[344,128]{1,0:T(8,128)S(1)} collective-permute-done((f32[344,128]{1,0:T(8,128)S(1)}, f32[344,128]{1,0:T(8,128)S(1)}, u32[]{:S(2)}, u32[]{:S(2)}) %collective-permute-start.5) | collective-permute-done | bytes 176160 | tf_op jit(solution)/shard_map/ppermute | solution.py:666
  36.9 3.3 %shard_map.100 = (f32[2304,128]{1,0:T(8,128)}, f32[24,128]{1,0:T(8,128)}) custom-call(s32[2]{0:T(128)S(1)} %pad_add_fusion.flags, f32[3072,128]{1,0:T(8,128)S(1)} %get-tuple-element.27.main, f32[768,128]{1,0:T(8,128)S(1)} %get-tuple-element.33.windows, f32[48,128]{1,0:T(8,128)S(1)} %get-tuple-element.28.flat, f32[48,128]{1,0:T(8,128)S(1)} %get-tuple-element.34.flat_windows, ...), custom_call_target="tpu_custom_call" | custom-call | flops 1000000 | bytes 6701064 | tf_op jit(solution)/shard_map/pallas_call | solution.py:646
Async XLA Ops:
  4.0 2.6 %collective-permute-start = (f32[208,128]{1,0:T(8,128)S(1)}, f32[208,128]{1,0:T(8,128)S(1)}, u32[]{:S(2)}, u32[]{:S(2)}) collective-permute-start(f32[208,128]{1,0:T(8,128)S(1)} %get-tuple-element.31), channel_id=1, source_target_pairs={{0,4},{8,12},{16,20},{24,28},{4,0},{12,8},{20,16},{28,24},{1,5},{9... | collective-permute-start | bytes 319496 | tf_op jit(solution)/shard_map/ppermute | solution.py:666
  4.1 6.0 %collective-permute-start.1 = (f32[208,128]{1,0:T(8,128)S(1)}, f32[208,128]{1,0:T(8,128)S(1)}, u32[]{:S(2)}, u32[]{:S(2)}) collective-permute-start(f32[208,128]{1,0:T(8,128)S(1)} %get-tuple-element.32), channel_id=1, source_target_pairs={{4,8},{12,16},{20,24},{8,4},{16,12},{24,20},{5,9},{13,17},{21,25},... | collective-permute-start | bytes 319496 | tf_op jit(solution)/shard_map/ppermute | solution.py:666
  12.3 8.5 %collective-permute-start.2 = (f32[456,128]{1,0:T(8,128)S(1)}, f32[456,128]{1,0:T(8,128)S(1)}, u32[]{:S(2)}, u32[]{:S(2)}) collective-permute-start(f32[456,128]{1,0:T(8,128)S(1)} %get-tuple-element.39), channel_id=1, source_target_pairs={{0,1},{2,3},{1,0},{3,2},{4,5},{6,7},{5,4},{7,6},{8,9},{10,11},{9,8... | collective-permute-start | bytes 700424 | tf_op jit(solution)/shard_map/ppermute | solution.py:666
  12.8 10.2 %collective-permute-start.3 = (f32[456,128]{1,0:T(8,128)S(1)}, f32[456,128]{1,0:T(8,128)S(1)}, u32[]{:S(2)}, u32[]{:S(2)}) collective-permute-start(f32[456,128]{1,0:T(8,128)S(1)} %get-tuple-element.40), channel_id=1, source_target_pairs={{1,2},{2,1},{5,6},{6,5},{9,10},{10,9},{13,14},{14,13},{17,18},{18,... | collective-permute-start | bytes 700424 | tf_op jit(solution)/shard_map/ppermute | solution.py:666
  27.6 7.5 %collective-permute-start.4 = (f32[344,128]{1,0:T(8,128)S(1)}, f32[344,128]{1,0:T(8,128)S(1)}, u32[]{:S(2)}, u32[]{:S(2)}) collective-permute-start(f32[344,128]{1,0:T(8,128)S(1)} %get-tuple-element.48), channel_id=1, source_target_pairs={{0,1},{2,3},{1,0},{3,2},{4,5},{6,7},{5,4},{7,6},{8,9},{10,11},{9,8... | collective-permute-start | bytes 528392 | tf_op jit(solution)/shard_map/ppermute | solution.py:666
  27.6 9.3 %collective-permute-start.5 = (f32[344,128]{1,0:T(8,128)S(1)}, f32[344,128]{1,0:T(8,128)S(1)}, u32[]{:S(2)}, u32[]{:S(2)}) collective-permute-start(f32[344,128]{1,0:T(8,128)S(1)} %get-tuple-element.49), channel_id=1, source_target_pairs={{1,2},{2,1},{5,6},{6,5},{9,10},{10,9},{13,14},{14,13},{17,18},{18,... | collective-permute-start | bytes 528392 | tf_op jit(solution)/shard_map/ppermute | solution.py:666

commit v4 on v3

--- a/solution.py
+++ b/solution.py
@@ -44,8 +44,10 @@
     return x if shift == 0 else pltpu.roll(x, shift, axis)
 
 
-def tile(ref, index):
-    return ref[index * SUB : (index + 1) * SUB, :]
+def tile(ref, index, start=None):
+    if start is None:
+        return ref[index * SUB : (index + 1) * SUB, :]
+    return ref[pl.ds(start + index * SUB, SUB), :]
 
 
 def row(ref, index):
@@ -54,6 +56,15 @@
 
 def store(ref, index, value):
     ref[index * SUB : (index + 1) * SUB, :] = value
+
+
+def split(x, parts):
+    out = []
+    for part in range(parts):
+        out.append(x.astype(jnp.bfloat16))
+        if part + 1 < parts:
+            x = x - out[-1].astype(jnp.float32)
+    return jnp.concatenate(out, axis=1)
 
 
 def minus(a, b):
@@ -68,7 +79,8 @@
 
 
 class Grid:
-    def __init__(self):
+    def __init__(self, origin=None, before=None, after=None):
+        self.origin, self.before, self.after = origin, before, after
         self.sub = lax.broadcasted_iota(jnp.int32, (SUB, LANES), 0)
         self.lane = lax.broadcasted_iota(jnp.int32, (SUB, LANES), 1)
         self.first = self.lane % GROUP < EDGE
@@ -91,33 +103,44 @@
             x = jnp.where(keep, edge, x)
         return rolled(x, -offset, 1)
 
-    def fx(self, x, edge):
-        return near_far(self.along(x, 1, edge), x, self.along(x, 2, edge), self.along(x, -1, edge))
-
-    def bx(self, x, edge):
-        return near_far(x, self.along(x, -1, edge), self.along(x, 1, edge), self.along(x, -2, edge))
-
-    def around(self, field, y, t):
-        if t == WINDOW:
-            x, at = field(y, t), self.lane % HALF
-            above = jnp.where(at >= GROUP, rolled(x, GROUP, 1), 0.0)
-            return above, x, jnp.where(at < HALF - GROUP, rolled(x, -GROUP, 1), 0.0)
-        above = field(y, t - 1) if t else self.zero
-        return above, field(y, t), field(y, t + 1) if t + 1 < TILES else self.zero
-
-    def down(self, three, offset):
-        above, x, below = three
-        sub = self.sub
-        keep = {-1: sub == SUB - 1, -2: sub >= SUB - 2, 1: sub == 0, 2: sub <= 1}[offset]
-        return rolled(jnp.where(keep, above if offset < 0 else below, x), -offset, 0)
+    def down(self, field, y, t, offset):
+        if t < WINDOW:
+            x = field(y, t, self.origin + offset)
+            if t == 0 and offset < 0:
+                return jnp.where(self.sub >= -offset, x, 0.0)
+            if t == TILES - 1 and offset > 0:
+                return jnp.where(self.sub < SUB - offset, x, 0.0)
+            return x
+        x, at = field(y, t), self.lane % HALF
+        if offset < 0:
+            beyond, far = jnp.where(at >= GROUP, rolled(x, GROUP, 1), 0.0), self.sub >= SUB + offset
+        else:
+            beyond, far = jnp.where(at < HALF - GROUP, rolled(x, -GROUP, 1), 0.0), self.sub < offset
+        return rolled(jnp.where(far, beyond, x), -offset, 0)
 
     def fz(self, field, y, t):
-        three = self.around(field, y, t)
-        return near_far(self.down(three, 1), three[1], self.down(three, 2), self.down(three, -1))
+        down = lambda offset: self.down(field, y, t, offset)
+        return near_far(down(1), field(y, t), down(2), down(-1))
 
     def bz(self, field, y, t):
-        three = self.around(field, y, t)
-        return near_far(three[1], self.down(three, -1), self.down(three, 1), self.down(three, -2))
+        down = lambda offset: self.down(field, y, t, offset)
+        return near_far(field(y, t), down(-1), down(1), down(-2))
+
+    def along_rows(self, matrix, rows):
+        main = split(jnp.concatenate([f(y, t) for f, y in rows for t in range(TILES)], axis=0), 2)
+        sides = [f(y, WINDOW) for f, y in rows]
+        side = split(jnp.concatenate(sides + sides[: len(sides) % 2], axis=0), 2)
+        main = jnp.dot(main, matrix[:, :LANES], preferred_element_type=jnp.float32)
+        side = jnp.dot(side, matrix[...], preferred_element_type=jnp.float32)
+        out = []
+        for i in range(len(rows)):
+            part = side[i * SUB : (i + 1) * SUB, :]
+            parts = [part[:, t * LANES : (t + 1) * LANES] for t in range(SPAN)]
+            tiles = [
+                main[(i * TILES + t) * SUB : (i * TILES + t + 1) * SUB, :] + parts[1 + t] for t in range(TILES)
+            ]
+            out.append(tiles + parts[:1])
+        return out
 
     def fy(self, field, y, t):
         return near_far(field(y + 1, t), field(y, t), field(y + 2, t), field(y - 1, t))
@@ -141,12 +164,15 @@
 
 
 def inside(field):
-    return lambda y, t: field(y, t) if 0 <= y < ROWS else None
+    return lambda y, t, *start: field(y, t, *start) if 0 <= y < ROWS else None
 
 
 def fields_of(main, windows):
     def field(f):
-        return lambda y, t: tile(windows, f * ROWS + y) if t == WINDOW else tile(main, (f * ROWS + y) * TILES + t)
+        def read(y, t, *start):
+            return tile(windows, f * ROWS + y) if t == WINDOW else tile(main, (f * ROWS + y) * TILES + t, *start)
+
+        return read
 
     return field
 
@@ -172,11 +198,38 @@
     return [grid.windows(*three) for three in zip(items, befores, afters)]
 
 
+def difference_matrix(out, weights, offsets):
+    shape = (LANES, LANES)
+    k, n = [lax.broadcasted_iota(jnp.int32, shape, axis) for axis in range(2)]
+
+    def weight(apart):
+        total = jnp.zeros(shape, jnp.float32)
+        for w, offset in zip(weights, offsets):
+            total = jnp.where(apart == offset, w, total)
+        return total
+
+    inner, left = k % GROUP, k < HALF
+    column = jnp.where(left, inner - EDGE, LANES - EDGE + inner)
+    outside = (left & (inner < EDGE)) | (jnp.logical_not(left) & (inner >= EDGE))
+    beside = jnp.where(outside, weight(n - column), 0.0)
+    parts = [weight(n - k)]
+    parts += [jnp.where(k % HALF // GROUP == t, beside, 0.0) for t in range(TILES)]
+    for p, x in enumerate(parts):
+        for half in range(2):
+            out[half * LANES : (half + 1) * LANES, p * LANES : (p + 1) * LANES] = x.astype(jnp.bfloat16)
+
+
+def picker(t):
+    k, n = [lax.broadcasted_iota(jnp.int32, (LANES, LANES), axis) for axis in range(2)]
+    column = (n % GROUP - EDGE) % LANES
+    one = jnp.where((n % HALF // GROUP == t) & (k == column), 1.0, 0.0).astype(jnp.bfloat16)
+    return jnp.concatenate([one] * 3, axis=0)
+
+
 def edges_kernel(flags, *refs):
     hbm, refs = refs[:8], refs[8:]
-    (main, flat, own, own_flat, even_way, odd_way), (wave, lame, shear, buoy, ocean, deep, floor, wet), sem = (
-        refs[:6], refs[6:14], refs[14],
-    )
+    (before, after, main, flat, own, own_flat, even_way, odd_way), refs = refs[:8], refs[8:]
+    (wave, lame, shear, buoy, ocean, deep, floor, wet), sem = refs[:8], refs[8]
     size = wave.shape[0] // 9
     copies = []
     for f in range(9):
@@ -186,25 +239,32 @@
         copies.append(pltpu.make_async_copy(hbm[1 + k], target, sem.at[9 + k]))
     for copy in copies:
         copy.start()
+    difference_matrix(before, (27.0, -27.0, -1.0, 1.0), (0, 1, -1, 2))
+    difference_matrix(after, (27.0, -27.0, -1.0, 1.0), (-1, 0, -2, 1))
+    pickers = [picker(t) for t in range(TILES)]
     grid = Grid()
     odd = (flags[0] & 1) == 1
     sources = [(wave, f) for f in range(9)] + [(lame, 0), (shear, 0), (buoy, 0)]
     for f in range(0, FIELDS, 2):
         copies[f].wait()
         copies[f + 1].wait()
+        totals = []
+        for h in (f, f + 1):
+            ref, base = sources[h]
+            total = None
+            for t in range(TILES):
+                tiles = []
+                for y in range(ROWS):
+                    x = ref[pl.ds(base * size + t * SUB * ROWS + y, SUB, stride=ROWS), :]
+                    store(main, (h * ROWS + y) * TILES + t, x)
+                    tiles.append(x)
+                part = split(jnp.concatenate(tiles, axis=0), 3)
+                part = jnp.dot(part, pickers[t], preferred_element_type=jnp.float32)
+                total = part if total is None else total + part
+            own[h * ROWS * SUB : (h + 1) * ROWS * SUB, :] = total
+            totals.append(total)
         for q in range(0, ROWS, 2):
-            items = []
-            for y in (q, q + 1):
-                for h in (f, f + 1):
-                    ref, base = sources[h]
-                    out = grid.zero
-                    for t in range(TILES):
-                        x = ref[pl.ds(base * size + t * SUB * ROWS + y, SUB, stride=ROWS), :]
-                        store(main, (h * ROWS + y) * TILES + t, x)
-                        out = jnp.where(grid.group == t, rolled(x, EDGE + GROUP * t, 1), out)
-                    out = jnp.where(grid.left, out, rolled(out, HALF, 1))
-                    store(own, h * ROWS + y, out)
-                    items.append(out)
+            items = [total[y * SUB : (y + 1) * SUB, :] for y in (q, q + 1) for total in totals]
             pack(grid, items, odd, even_way, odd_way, (f * ROWS // 2 + q) // 2)
     for copy in copies[FIELDS:]:
         copy.wait()
@@ -224,32 +284,34 @@
 
 def speeds(grid, stress, speed, buoy, todo, put):
     sxx, syy, szz, sxy, sxz, syz = stress
+    forth = [(VX, y) for c, y in todo if c == VX]
+    back = [(c, y) for c, y in todo if c != VX]
+    change = dict(zip(forth, grid.along_rows(grid.after, [(sxx, y) for _, y in forth])))
+    change.update(zip(back, grid.along_rows(grid.before, [(sxy if c == VY else sxz, y) for c, y in back])))
     for y in range(ROWS):
         parts = [c for c in (VX, VY, VZ) if (c, y) in todo]
         if not parts:
             continue
-        need = {VX: (sxx,), VY: (sxy,), VZ: (sxz,)}
-        beside = {c: grid.beside(need[c][0](y, WINDOW)) for c in parts}
         for t in range(SPAN):
             rate = RATE * buoy(y, t)
             for c in parts:
-                edge = grid.edge(beside[c], t)
+                a = change[c, y][t]
                 if c == VX:
-                    a = grid.fx(sxx(y, t), edge) + grid.by(sxy, y, t) + grid.bz(sxz, y, t)
+                    a = a + grid.by(sxy, y, t) + grid.bz(sxz, y, t)
                 elif c == VY:
-                    a = grid.bx(sxy(y, t), edge) + grid.fy(syy, y, t) + grid.bz(syz, y, t)
+                    a = a + grid.fy(syy, y, t) + grid.bz(syz, y, t)
                 else:
-                    a = grid.bx(sxz(y, t), edge) + grid.by(syz, y, t) + grid.fz(szz, y, t)
+                    a = a + grid.by(syz, y, t) + grid.fz(szz, y, t)
                 put(c, y, t, speed(c)(y, t) + rate * a)
 
 
 def stresses(grid, rows, tiles, speed, stress, lame, shear, put):
     vx, vy, vz = [speed(c) for c in (VX, VY, VZ)]
-    for y in rows:
-        b_x, b_y, b_z = [grid.beside(v(y, WINDOW)) for v in (vx, vy, vz)]
+    back = grid.along_rows(grid.before, [(vx, y) for y in rows])
+    forth = grid.along_rows(grid.after, [(v, y) for v in (vy, vz) for y in rows])
+    for i, y in enumerate(rows):
         for t in range(tiles):
-            e_x, e_y, e_z = [grid.edge(b, t) for b in (b_x, b_y, b_z)]
-            strain_x = grid.bx(vx(y, t), e_x)
+            strain_x = back[i][t]
             strain_y = grid.by(vy, y, t)
             strain_z = grid.bz(vz, y, t)
             mu = RATE * shear(y, t)
@@ -258,8 +320,8 @@
             put(SXX, y, t, stress(SXX)(y, t) + (spread + two * strain_x))
             put(SYY, y, t, stress(SYY)(y, t) + (spread + two * strain_y))
             put(SZZ, y, t, stress(SZZ)(y, t) + (spread + two * strain_z))
-            put(SXY, y, t, stress(SXY)(y, t) + mu * (grid.fy(vx, y, t) + grid.fx(vy(y, t), e_y)))
-            put(SXZ, y, t, stress(SXZ)(y, t) + mu * (grid.fz(vx, y, t) + grid.fx(vz(y, t), e_z)))
+            put(SXY, y, t, stress(SXY)(y, t) + mu * (grid.fy(vx, y, t) + forth[i][t]))
+            put(SXZ, y, t, stress(SXZ)(y, t) + mu * (grid.fz(vx, y, t) + forth[len(rows) + i][t]))
             put(SYZ, y, t, stress(SYZ)(y, t) + mu * (grid.fz(vy, y, t) + grid.fy(vz, y, t)))
 
 
@@ -448,10 +510,10 @@
 
 
 def start_kernel(
-    flags, main, flat, own, own_flat, even_in, odd_in,
+    flags, before, after, main, flat, own, own_flat, even_in, odd_in,
     windows, flat_windows, partial, level, even_way, odd_way,
 ):
-    grid = Grid()
+    grid = Grid(flags[2], before, after)
     odd = (flags[0] & 1) == 1
     for f in range(0, FIELDS, 2):
         for q in range(0, ROWS, 2):
@@ -483,26 +545,30 @@
     send(True, (flags[1] & 1) == 1, rows_of, line, even_way, odd_way)
 
 
-def start_rest_kernel(main, windows, speed_out, stress_out):
-    grid = Grid()
+def start_rest_kernel(flags, before, after, main, windows, speed_out, stress_out):
+    grid = Grid(flags[2], before, after)
     field = fields_of(main, windows)
     speeds(
         grid, [inside(field(f)) for f in range(SXX, SYZ + 1)], field, field(BUOY), CLOSED,
         lambda c, y, t, value: store(speed_out, block_index(c, y) + t, value),
     )
     stresses(
-        grid, INNER, SPAN, lambda c: lambda y, t: tile(speed_out, block_index(c, y) + t), field,
+        grid, INNER, SPAN, block_reader(speed_out, VX), field,
         field(LAME), field(SHEAR),
         lambda f, y, t, value: store(stress_out, block_index(f - SXX, y) + t, value),
     )
 
 
+def block_reader(ref, least):
+    return lambda f: lambda y, t, *start: tile(ref, block_index(f - least, y) + t, *start)
+
+
 def speed_reader(around, block):
     def speed(c):
-        def read(y, t):
+        def read(y, t, *start):
             if (c, y) in CLOSED:
-                return tile(block, block_index(c, y) + t)
-            return tile(around, (c * AROUND + y + 2) * SPAN + t)
+                return tile(block, block_index(c, y) + t, *start)
+            return tile(around, (c * AROUND + y + 2) * SPAN + t, *start)
 
         return read
 
@@ -510,11 +576,11 @@
 
 
 def middle_kernel(
-    flags, main, windows, flat, flat_windows, partial, level, speed_in, stress_in, even_in, odd_in,
+    flags, before, after, main, windows, flat, flat_windows, partial, level, speed_in, stress_in, even_in, odd_in,
     speed_out, stress_out, ocean, partial_out, level_out, even_way, odd_way,
     sums, pressure,
 ):
-    grid = Grid()
+    grid = Grid(flags[2], before, after)
     odd = (flags[1] & 1) == 1
     lo, hi = received(True, odd, even_in, odd_in)
     field = fields_of(main, windows)
@@ -540,7 +606,7 @@
         for y in INNER:
             for t in range(SPAN):
                 put(f, y, t, tile(stress_in, block_index(f - SXX, y) + t))
-    stress = lambda f: lambda y, t: tile(stress_out, block_index(f - SXX, y) + t)
+    stress = block_reader(stress_out, SXX)
     speeds(
         grid, [inside(stress(f)) for f in range(SXX, SYZ + 1)], speed, field(BUOY), OPEN,
         lambda c, y, t, value: store(partial_out, edge_index(c, y) + t, value),
@@ -559,33 +625,33 @@
     send(False, odd, rows_of, line_out, even_way, odd_way)
 
 
-def middle_rest_kernel(main, windows, around, speed_in, stress_in, speed_out, stress_out):
-    grid = Grid()
+def middle_rest_kernel(flags, before, after, main, windows, around, speed_in, stress_in, speed_out, stress_out):
+    grid = Grid(flags[2], before, after)
     field = fields_of(main, windows)
-    stress = lambda f: lambda y, t: tile(stress_in, block_index(f - SXX, y) + t)
+    stress = block_reader(stress_in, SXX)
     speeds(
         grid, [inside(stress(f)) for f in range(SXX, SYZ + 1)], speed_reader(around, speed_in), field(BUOY), CLOSED,
         lambda c, y, t, value: store(speed_out, block_index(c, y) + t, value),
     )
     stresses(
-        grid, INNER, TILES, lambda c: lambda y, t: tile(speed_out, block_index(c, y) + t), stress,
+        grid, INNER, TILES, block_reader(speed_out, VX), stress,
         field(LAME), field(SHEAR),
         lambda f, y, t, value: store(stress_out, block_index(f - SXX, y) + t, value),
     )
 
 
 def last_kernel(
-    flags, main, windows, flat, flat_windows, stress_in, ocean_in, partial, level, speed_in, inner_in,
+    flags, before, after, main, windows, flat, flat_windows, stress_in, ocean_in, partial, level, speed_in, inner_in,
     even_first, odd_first, even_in, odd_in,
     wave_hbm, ocean_out,
     sums, pressure, around, wave, sem,
 ):
-    grid = Grid()
+    grid = Grid(flags[2], before, after)
     odd = (flags[1] & 1) == 1
     lo, hi = received(False, odd, even_in, odd_in)
     lo_buoy, hi_buoy = received(True, odd, even_first, odd_first)
     field = fields_of(main, windows)
-    stress = lambda f: lambda y, t: tile(stress_in, block_index(f - SXX, y) + t)
+    stress = block_reader(stress_in, SXX)
     finish(
         grid, TILES, lambda c, y, t: tile(partial, edge_index(c, y) + t), stress, field(BUOY),
         lo, hi, lo_buoy, hi_buoy, around,
@@ -642,10 +708,10 @@
     specs = [place] * len(arguments)
     if flags is not None:
         arguments, specs = (flags, *arguments), [IN_SMEM] + specs
-    moved = sum(x.size for x in arguments) + sum(tiles) * SUB * LANES
+    moved = sum(x.size for x in arguments) + sum(n for n in tiles if isinstance(n, int)) * SUB * LANES
     return pl.pallas_call(
         kernel,
-        out_shape=[jax.ShapeDtypeStruct((n * SUB, LANES), jnp.float32) for n in tiles],
+        out_shape=[n if hasattr(n, "dtype") else jax.ShapeDtypeStruct((n * SUB, LANES), jnp.float32) for n in tiles],
         in_specs=specs,
         out_specs=out_places or [IN_VMEM] * len(tiles),
         scratch_shapes=scratch,
@@ -671,11 +737,12 @@
 def local(*arguments):
     wave_fields, ocean_state = arguments[0], arguments[4]
     inputs = [pltpu.with_memory_space_constraint(x.reshape(-1, LANES), pltpu.HBM) for x in arguments]
-    flags = jnp.stack([lax.axis_index("gx"), lax.axis_index("gy")])
+    flags = jnp.stack([lax.axis_index("gx"), lax.axis_index("gy"), 0])
+    matrix = jax.ShapeDtypeStruct((2 * LANES, SPAN * LANES), jnp.bfloat16)
 
     message = FIELDS * ROWS // 4 + 2
-    main, flat, own, own_flat, even_way, odd_way = call(
-        edges_kernel, [FIELDS * ROWS * TILES, 6, FIELDS * ROWS, 6, message, message],
+    before, after, main, flat, own, own_flat, even_way, odd_way = call(
+        edges_kernel, [matrix, matrix, FIELDS * ROWS * TILES, 6, FIELDS * ROWS, 6, message, message],
         [pltpu.VMEM(x.shape, x.dtype) for x in inputs] + [pltpu.SemaphoreType.DMA((16,))],
         *inputs, flags=flags, place=IN_HBM,
     )
@@ -684,22 +751,22 @@
     edges, block = len(OPEN) * SPAN, ROWS * SPAN
     windows, flat_windows, partial, level, even_way, odd_way = call(
         start_kernel, [FIELDS * ROWS, 6, edges, 2, first, first], [],
-        main, flat, own, own_flat, *x_in, flags=flags,
+        before, after, main, flat, own, own_flat, *x_in, flags=flags,
     )
     y_in = exchange("gy", even_way, odd_way)
-    speed, inner = call(start_rest_kernel, [3 * block, 6 * block], [], main, windows, work=4)
+    speed, inner = call(start_rest_kernel, [3 * block, 6 * block], [], before, after, main, windows, flags=flags, work=4)
     around, stress, ocean, partial, level, even_way, odd_way = call(
         middle_kernel, [3 * AROUND * SPAN, 6 * block, 6, edges, 2, later, later], [planes(4), planes(2)],
-        main, windows, flat, flat_windows, partial, level, speed, inner, *y_in, flags=flags,
+        before, after, main, windows, flat, flat_windows, partial, level, speed, inner, *y_in, flags=flags,
     )
     y_in2 = exchange("gy", even_way, odd_way)
     speed, inner = call(
-        middle_rest_kernel, [3 * block, 6 * block], [], main, windows, around, speed, stress, work=4
+        middle_rest_kernel, [3 * block, 6 * block], [], before, after, main, windows, around, speed, stress, flags=flags, work=4
     )
     wave_out, ocean_out = call(
         last_kernel, [9 * ROWS * TILES, 3],
         [planes(4), planes(2), planes(3 * AROUND * SPAN), planes(9 * ROWS * TILES), pltpu.SemaphoreType.DMA((9,))],
-        main, windows, flat, flat_windows, stress, ocean, partial, level, speed, inner, *y_in, *y_in2,
+        before, after, main, windows, flat, flat_windows, stress, ocean, partial, level, speed, inner, *y_in, *y_in2,
         flags=flags, out_places=[IN_HBM, IN_VMEM],
     )
     return wave_out.reshape(wave_fields.shape), ocean_out.reshape(ocean_state.shape)

time: 40.6 us -> 36.4 us (0.90)
  Pallas kernels: 19.9 us -> 11.3 us
  waiting for transfers between devices: 7.55 us -> 11.9 us
    pallas_call x6, Pallas kernels: 19.9 us -> 11.3 us  [call(): pl.pallas_call(kernel, out_shape=[n if hasattr(n, 'dtype') else jax.Shape...]
    ppermute x6, waiting for transfers between devices: 7.55 us -> 11.9 us  [swap(): return lax.ppermute(x, axis, pairs + [(j, i) for i, j in pairs])]
  transfers between devices with their start and end apart: 6 -> 6, of which waited for: 3 -> 5; matrix products, arithmetic and copies ran while one was open for 0% -> 0% of each run, Pallas kernels for 16% -> 6%
where the time goes in v4:
time: 36.4 us; the launch traced here: 36 us
  starting transfers between devices  12 us (33%)
  waiting for transfers between devices  11.9 us (33%)
  Pallas kernels  11.3 us (31%)
  between operations  0.71 us (2%)
    ppermute x6, starting transfers between devices, swap(): return lax.ppermute(x, axis, pairs + [(j, i) for i, j in pairs])  12 us
    ppermute x6, waiting for transfers between devices, swap(): return lax.ppermute(x, axis, pairs + [(j, i) for i, j in pairs])  11.9 us
    pallas_call x6, Pallas kernels, call(): pl.pallas_call(kernel, out_shape=[n if hasattr(n, 'dtype') else jax.Shape...  11.3 us
  transfers between devices with their start and end apart: 6, of which 5 were waited for; matrix products, arithmetic and copies ran while one was open for 0% of the time, Pallas kernels for 6%

profile of v4, /device:TPU:10, one launch (start us, length us, event | category | flops | bytes accessed | tf_op | source)
XLA Modules:
  0.0 36.0 jit_solution(2060775248919779376)
XLA Ops:
  0.6 0.1 pad_add_fusion.flags
  0.7 4.0 %shard_map.95 = (bf16[256,640]{1,0:T(8,128)(2,1)S(1)}, bf16[256,640]{1,0:T(8,128)(2,1)S(1)}, f32[3072,128]{1,0:T(8,128)S(1)}, f32[48,128]{1,0:T(8,128)S(1)}, f32...) custom-call(s32[3]{0:T(128)S(1)} %pad_add_fusion.flags, ...), custom_call_target="tpu_custom_call" | custom-call | flops 1000000 | bytes 3825676 | tf_op jit(solution)/shard_map/pallas_call | solution.py:712
  4.7 0.1 collective-permute-start
  4.8 2.5 %collective-permute-start.1 = (f32[208,128]{1,0:T(8,128)S(1)}, f32[208,128]{1,0:T(8,128)S(1)}, u32[]{:S(2)}, u32[]{:S(2)}) collective-permute-start(f32[208,128]{1,0:T(8,128)S(1)} %get-tuple-element.36), channel_id=1, source_target_pairs={{4,8},{12,16},{20,24},{8,4},{16,12},{24,20},{5,9},{13,17},{21,25},... | collective-permute-start | bytes 319496 | tf_op jit(solution)/shard_map/ppermute | solution.py:732
  7.3 0.0 collective-permute-done.even_in
  7.3 3.5 %collective-permute-done.1.odd_in = f32[208,128]{1,0:T(8,128)S(1)} collective-permute-done((f32[208,128]{1,0:T(8,128)S(1)}, f32[208,128]{1,0:T(8,128)S(1)}, u32[]{:S(2)}, u32[]{:S(2)}) %collective-permute-start.1) | collective-permute-done | bytes 106528 | tf_op jit(solution)/shard_map/ppermute | solution.py:732
  10.8 0.9 %shard_map.96 = (f32[768,128]{1,0:T(8,128)S(1)}, f32[48,128]{1,0:T(8,128)S(1)}, f32[360,128]{1,0:T(8,128)S(1)}, f32[16,128]{1,0:T(8,128)S(1)}, f32[456,128]{1,0:T(8,128)S(1)}, /*index=5*/f32[456,128]{1,0:T(8,128)S(1)}) custom-call(s32[3]{0:T(128)S(1)} %pad_add_fusion.flags, bf16[256,640]{1,0:T(8,128)(2,1)S(1)} %get-tuple-element.29.before, ...), custom_call_target="tpu_custom_call" | custom-call | flops 1000000 | bytes 4616204 | tf_op jit(solution)/shard_map/pallas_call | solution.py:712
  11.8 0.5 %collective-permute-start.2 = (f32[456,128]{1,0:T(8,128)S(1)}, f32[456,128]{1,0:T(8,128)S(1)}, u32[]{:S(2)}, u32[]{:S(2)}) collective-permute-start(f32[456,128]{1,0:T(8,128)S(1)} %get-tuple-element.43), channel_id=1, source_target_pairs={{0,1},{2,3},{1,0},{3,2},{4,5},{6,7},{5,4},{7,6},{8,9},{10,11},{9,8... | collective-permute-start | bytes 700424 | tf_op jit(solution)/shard_map/ppermute | solution.py:732
  12.3 4.6 %collective-permute-start.3 = (f32[456,128]{1,0:T(8,128)S(1)}, f32[456,128]{1,0:T(8,128)S(1)}, u32[]{:S(2)}, u32[]{:S(2)}) collective-permute-start(f32[456,128]{1,0:T(8,128)S(1)} %get-tuple-element.44), channel_id=1, source_target_pairs={{1,2},{2,1},{5,6},{6,5},{9,10},{10,9},{13,14},{14,13},{17,18},{18,... | collective-permute-start | bytes 700424 | tf_op jit(solution)/shard_map/ppermute | solution.py:732
  16.9 1.1 %shard_map.97 = (f32[960,128]{1,0:T(8,128)S(1)}, f32[1920,128]{1,0:T(8,128)S(1)}) custom-call(s32[3]{0:T(128)S(1)} %pad_add_fusion.flags, bf16[256,640]{1,0:T(8,128)(2,1)S(1)} %get-tuple-element.29.before, bf16[256,640]{1,0:T(8,128)(2,1)S(1)} %get-tuple-element.30.after, f32[3072,128]{1,0:T(8,128)S(1)} %get-tuple-element.31.main, ...), custom_call_target="tpu_custom_call" | custom-call | flops 4000000 | bytes 4751372 | tf_op jit(solution)/shard_map/pallas_call | solution.py:712
  18.0 1.5 %collective-permute-done.2.even_in.even_first = f32[456,128]{1,0:T(8,128)S(1)} collective-permute-done((f32[456,128]{1,0:T(8,128)S(1)}, f32[456,128]{1,0:T(8,128)S(1)}, u32[]{:S(2)}, u32[]{:S(2)}) %collective-permute-start.2) | collective-permute-done | bytes 233504 | tf_op jit(solution)/shard_map/ppermute | solution.py:732
  19.5 3.0 %collective-permute-done.3.odd_in.odd_first = f32[456,128]{1,0:T(8,128)S(1)} collective-permute-done((f32[456,128]{1,0:T(8,128)S(1)}, f32[456,128]{1,0:T(8,128)S(1)}, u32[]{:S(2)}, u32[]{:S(2)}) %collective-permute-start.3) | collective-permute-done | bytes 233504 | tf_op jit(solution)/shard_map/ppermute | solution.py:732
  22.5 1.4 %shard_map.98 = (f32[1440,128]{1,0:T(8,128)S(1)}, f32[1920,128]{1,0:T(8,128)S(1)}, f32[48,128]{1,0:T(8,128)S(1)}, f32[360,128]{1,0:T(8,128)S(1)}, f32[16,128]{1,...) custom-call(s32[3]{0:T(128)S(1)} %pad_add_fusion.flags, bf16[256,640]{1,0:T(8,128)(2,1)S(1)} %get-tuple-element.29.before, ...), custom_call_target="tpu_custom_call" | custom-call | flops 1000000 | bytes 7749644 | tf_op jit(solution)/shard_map/pallas_call | solution.py:712
  23.9 0.1 collective-permute-start.4
  24.0 4.2 %collective-permute-start.5 = (f32[344,128]{1,0:T(8,128)S(1)}, f32[344,128]{1,0:T(8,128)S(1)}, u32[]{:S(2)}, u32[]{:S(2)}) collective-permute-start(f32[344,128]{1,0:T(8,128)S(1)} %get-tuple-element.53), channel_id=1, source_target_pairs={{1,2},{2,1},{5,6},{6,5},{9,10},{10,9},{13,14},{14,13},{17,18},{18,... | collective-permute-start | bytes 528392 | tf_op jit(solution)/shard_map/ppermute | solution.py:732
  28.2 1.1 %shard_map.99 = (f32[960,128]{1,0:T(8,128)S(1)}, f32[1920,128]{1,0:T(8,128)S(1)}) custom-call(s32[3]{0:T(128)S(1)} %pad_add_fusion.flags, bf16[256,640]{1,0:T(8,128)(2,1)S(1)} %get-tuple-element.29.before, bf16[256,640]{1,0:T(8,128)(2,1)S(1)} %get-tuple-element.30.after, f32[3072,128]{1,0:T(8,128)S(1)} %get-tuple-element.31.main, ...), custom_call_target="tpu_custom_call" | custom-call | flops 4000000 | bytes 6963212 | tf_op jit(solution)/shard_map/pallas_call | solution.py:712
  29.3 1.8 %collective-permute-done.4.even_in = f32[344,128]{1,0:T(8,128)S(1)} collective-permute-done((f32[344,128]{1,0:T(8,128)S(1)}, f32[344,128]{1,0:T(8,128)S(1)}, u32[]{:S(2)}, u32[]{:S(2)}) %collective-permute-start.4) | collective-permute-done | bytes 176160 | tf_op jit(solution)/shard_map/ppermute | solution.py:732
  31.1 2.2 %collective-permute-done.5.odd_in = f32[344,128]{1,0:T(8,128)S(1)} collective-permute-done((f32[344,128]{1,0:T(8,128)S(1)}, f32[344,128]{1,0:T(8,128)S(1)}, u32[]{:S(2)}, u32[]{:S(2)}) %collective-permute-start.5) | collective-permute-done | bytes 176160 | tf_op jit(solution)/shard_map/ppermute | solution.py:732
  33.3 2.7 %shard_map.100 = (f32[2304,128]{1,0:T(8,128)}, f32[24,128]{1,0:T(8,128)}) custom-call(s32[3]{0:T(128)S(1)} %pad_add_fusion.flags, bf16[256,640]{1,0:T(8,128)(2,1)S(1)} %get-tuple-element.29.before, bf16[256,640]{1,0:T(8,128)(2,1)S(1)} %get-tuple-element.30.after, f32[3072,128]{1,0:T(8,128)S(1)} %get-tuple-element.31.main, ...), custom_call_target="tpu_custom_call" | custom-call | flops 1000000 | bytes 8011788 | tf_op jit(solution)/shard_map/pallas_call | solution.py:712
Async XLA Ops:
  4.7 2.6 %collective-permute-start = (f32[208,128]{1,0:T(8,128)S(1)}, f32[208,128]{1,0:T(8,128)S(1)}, u32[]{:S(2)}, u32[]{:S(2)}) collective-permute-start(f32[208,128]{1,0:T(8,128)S(1)} %get-tuple-element.35), channel_id=1, source_target_pairs={{0,4},{8,12},{16,20},{24,28},{4,0},{12,8},{20,16},{28,24},{1,5},{9... | collective-permute-start | bytes 319496 | tf_op jit(solution)/shard_map/ppermute | solution.py:732
  4.8 6.0 %collective-permute-start.1 = (f32[208,128]{1,0:T(8,128)S(1)}, f32[208,128]{1,0:T(8,128)S(1)}, u32[]{:S(2)}, u32[]{:S(2)}) collective-permute-start(f32[208,128]{1,0:T(8,128)S(1)} %get-tuple-element.36), channel_id=1, source_target_pairs={{4,8},{12,16},{20,24},{8,4},{16,12},{24,20},{5,9},{13,17},{21,25},... | collective-permute-start | bytes 319496 | tf_op jit(solution)/shard_map/ppermute | solution.py:732
  11.8 7.7 %collective-permute-start.2 = (f32[456,128]{1,0:T(8,128)S(1)}, f32[456,128]{1,0:T(8,128)S(1)}, u32[]{:S(2)}, u32[]{:S(2)}) collective-permute-start(f32[456,128]{1,0:T(8,128)S(1)} %get-tuple-element.43), channel_id=1, source_target_pairs={{0,1},{2,3},{1,0},{3,2},{4,5},{6,7},{5,4},{7,6},{8,9},{10,11},{9,8... | collective-permute-start | bytes 700424 | tf_op jit(solution)/shard_map/ppermute | solution.py:732
  12.3 10.2 %collective-permute-start.3 = (f32[456,128]{1,0:T(8,128)S(1)}, f32[456,128]{1,0:T(8,128)S(1)}, u32[]{:S(2)}, u32[]{:S(2)}) collective-permute-start(f32[456,128]{1,0:T(8,128)S(1)} %get-tuple-element.44), channel_id=1, source_target_pairs={{1,2},{2,1},{5,6},{6,5},{9,10},{10,9},{13,14},{14,13},{17,18},{18,... | collective-permute-start | bytes 700424 | tf_op jit(solution)/shard_map/ppermute | solution.py:732
  23.9 7.2 %collective-permute-start.4 = (f32[344,128]{1,0:T(8,128)S(1)}, f32[344,128]{1,0:T(8,128)S(1)}, u32[]{:S(2)}, u32[]{:S(2)}) collective-permute-start(f32[344,128]{1,0:T(8,128)S(1)} %get-tuple-element.52), channel_id=1, source_target_pairs={{0,1},{2,3},{1,0},{3,2},{4,5},{6,7},{5,4},{7,6},{8,9},{10,11},{9,8... | collective-permute-start | bytes 528392 | tf_op jit(solution)/shard_map/ppermute | solution.py:732
  24.0 9.3 %collective-permute-start.5 = (f32[344,128]{1,0:T(8,128)S(1)}, f32[344,128]{1,0:T(8,128)S(1)}, u32[]{:S(2)}, u32[]{:S(2)}) collective-permute-start(f32[344,128]{1,0:T(8,128)S(1)} %get-tuple-element.53), channel_id=1, source_target_pairs={{1,2},{2,1},{5,6},{6,5},{9,10},{10,9},{13,14},{14,13},{17,18},{18,... | collective-permute-start | bytes 528392 | tf_op jit(solution)/shard_map/ppermute | solution.py:732

commit v5 on v4

--- a/solution.py
+++ b/solution.py
@@ -177,17 +177,33 @@
     return field
 
 
-def pack(grid, items, odd, even_way, odd_way, index):
-    a, b, c, d = items
-    first, left = grid.first, grid.left
-    right_way = jnp.where(
-        left, jnp.where(first, a, rolled(b, EDGE, 1)), jnp.where(first, c, rolled(d, EDGE, 1))
-    )
-    left_way = jnp.where(
-        left, jnp.where(first, rolled(b, -EDGE, 1), a), jnp.where(first, rolled(d, -EDGE, 1), c)
-    )
-    store(even_way, index, jnp.where(odd, left_way, right_way))
-    store(odd_way, index, jnp.where(odd, right_way, left_way))
+def pack(grid, groups, to_right, out):
+    for index, (a, b, c, d) in enumerate(groups):
+        if to_right:
+            one, two = jnp.where(grid.first, a, rolled(b, EDGE, 1)), jnp.where(grid.first, c, rolled(d, EDGE, 1))
+        else:
+            one, two = jnp.where(grid.first, rolled(b, -EDGE, 1), a), jnp.where(grid.first, rolled(d, -EDGE, 1), c)
+        store(out, index, jnp.where(grid.left, one, two))
+
+
+def pack_edges(grid, own, own_flat, to_right, out):
+    @pl.when(to_right)
+    def _():
+        pack(grid, edge_groups(own, own_flat), True, out)
+
+    @pl.when(jnp.logical_not(to_right))
+    def _():
+        pack(grid, edge_groups(own, own_flat), False, out)
+
+
+def edge_groups(own, own_flat):
+    groups = [
+        [tile(own, h * ROWS + y) for y in (q, q + 1) for h in (f, f + 1)]
+        for f in range(0, FIELDS, 2)
+        for q in range(0, ROWS, 2)
+    ]
+    flat = [tile(own_flat, k) for k in range(6)]
+    return groups + [flat[:4], flat[4:] * 2]
 
 
 def unpack(grid, items, odd, even_in, odd_in, index):
@@ -228,58 +244,51 @@
 
 def edges_kernel(flags, *refs):
     hbm, refs = refs[:8], refs[8:]
-    (before, after, main, flat, own, own_flat, even_way, odd_way), refs = refs[:8], refs[8:]
-    (wave, lame, shear, buoy, ocean, deep, floor, wet), sem = refs[:8], refs[8]
-    size = wave.shape[0] // 9
-    copies = []
-    for f in range(9):
-        part = slice(f * size, (f + 1) * size)
-        copies.append(pltpu.make_async_copy(hbm[0].at[part, :], wave.at[part, :], sem.at[f]))
-    for k, target in enumerate((lame, shear, buoy, ocean, deep, floor, wet)):
-        copies.append(pltpu.make_async_copy(hbm[1 + k], target, sem.at[9 + k]))
-    for copy in copies:
-        copy.start()
+    (before, after, main, flat, own, own_flat, odd_way), (ocean, deep, floor, wet, sem) = refs[:7], refs[7:]
+    ready = {}
+    at = 0
+    for source, first, count in ((0, 0, 3), (0, 3, 3), (0, 6, 3), (1, LAME, 1), (2, SHEAR, 1), (3, BUOY, 1)):
+        copies = []
+        for y in range(ROWS):
+            if source:
+                pair = hbm[source].at[:, y, :], main.at[first, y]
+            else:
+                pair = hbm[0].at[first : first + count, :, y, :], main.at[first : first + count, y]
+            copies.append(pltpu.make_async_copy(*pair, sem.at[at]))
+            at += 1
+        ready[first] = copies
+    flats = [pltpu.make_async_copy(hbm[4 + k], target, sem.at[at + k]) for k, target in enumerate((ocean, deep, floor, wet))]
+    for copies in list(ready.values()) + [flats]:
+        for copy in copies:
+            copy.start()
     difference_matrix(before, (27.0, -27.0, -1.0, 1.0), (0, 1, -1, 2))
     difference_matrix(after, (27.0, -27.0, -1.0, 1.0), (-1, 0, -2, 1))
     pickers = [picker(t) for t in range(TILES)]
     grid = Grid()
-    odd = (flags[0] & 1) == 1
-    sources = [(wave, f) for f in range(9)] + [(lame, 0), (shear, 0), (buoy, 0)]
-    for f in range(0, FIELDS, 2):
-        copies[f].wait()
-        copies[f + 1].wait()
-        totals = []
-        for h in (f, f + 1):
-            ref, base = sources[h]
-            total = None
-            for t in range(TILES):
-                tiles = []
-                for y in range(ROWS):
-                    x = ref[pl.ds(base * size + t * SUB * ROWS + y, SUB, stride=ROWS), :]
-                    store(main, (h * ROWS + y) * TILES + t, x)
-                    tiles.append(x)
-                part = split(jnp.concatenate(tiles, axis=0), 3)
-                part = jnp.dot(part, pickers[t], preferred_element_type=jnp.float32)
-                total = part if total is None else total + part
-            own[h * ROWS * SUB : (h + 1) * ROWS * SUB, :] = total
-            totals.append(total)
-        for q in range(0, ROWS, 2):
-            items = [total[y * SUB : (y + 1) * SUB, :] for y in (q, q + 1) for total in totals]
-            pack(grid, items, odd, even_way, odd_way, (f * ROWS // 2 + q) // 2)
-    for copy in copies[FIELDS:]:
+    for f in range(FIELDS):
+        for copy in ready.get(f, ()):
+            copy.wait()
+        total = None
+        for t in range(TILES):
+            tiles = [main[f, y, t * SUB : (t + 1) * SUB, :] for y in range(ROWS)]
+            part = jnp.dot(split(jnp.concatenate(tiles, axis=0), 3), pickers[t], preferred_element_type=jnp.float32)
+            total = part if total is None else total + part
+        own[f * ROWS * SUB : (f + 1) * ROWS * SUB, :] = total
+    for copy in flats:
         copy.wait()
-    planes = [tile(ocean, k) for k in range(3)] + [deep[...]]
+    planes = [ocean[k] for k in range(3)] + [deep[...]]
     planes += [floor[...].astype(jnp.float32), wet[...].astype(jnp.float32)]
-    items = []
     for k, x in enumerate(planes):
         store(flat, k, x)
         out = grid.zero
         for g in range(LANES // GROUP):
             out = jnp.where(grid.group == g, rolled(x, EDGE + GROUP * g, 1), out)
         store(own_flat, k, out)
-        items.append(out)
-    pack(grid, items[:4], odd, even_way, odd_way, FIELDS * ROWS // 4)
-    pack(grid, items[4:] * 2, odd, even_way, odd_way, FIELDS * ROWS // 4 + 1)
+    pack_edges(grid, own, own_flat, (flags[0] & 1) == 1, odd_way)
+
+
+def edges_rest_kernel(flags, own, own_flat, even_way):
+    pack_edges(Grid(), own, own_flat, (flags[0] & 1) == 0, even_way)
 
 
 def speeds(grid, stress, speed, buoy, todo, put):
@@ -338,36 +347,38 @@
         put(k, flat(LEVEL, k) - OCEAN_RATE * (flat(WET, k) * spread))
 
 
+def cells(rows, tiles):
+    return [(f, y, t) for f, y in rows for t in tiles]
+
+
 class Message:
-    def __init__(self, rows, thin):
-        self.at, size = [], 0
-        for f, _ in rows:
-            self.at.append(size)
-            size += TILES if thin and f < 3 else SPAN
-        self.tiles = self.at[1:] + [size]
-        self.tiles = [b - a for a, b in zip(self.at, self.tiles)]
-        self.rows = rows
-        self.base = size * SUB
+    def __init__(self, tiles):
+        self.at = {which: i for i, which in enumerate(tiles)}
+        self.base = len(tiles) * SUB
         self.size = self.base + 2 * SUB
 
 
-def messages(first):
-    high = SPEED_HIGH + STRESS_HIGH + (BUOY_HIGH if first else ())
-    low = SPEED_LOW + STRESS_LOW + (BUOY_LOW if first else ())
-    return Message(high, not first), Message(low, not first)
-
-
-def message_size(first):
-    return max(m.size for m in messages(first))
-
-
-def send(first, odd, field, line, even_way, odd_way):
-    high, low = messages(first)
+ALL, INSIDE = range(SPAN), range(TILES)
+FIRST = [
+    Message(cells(rows, ALL))
+    for rows in (SPEED_HIGH + STRESS_HIGH + BUOY_HIGH, SPEED_LOW + STRESS_LOW + BUOY_LOW)
+]
+LATER = [
+    Message(cells(speed, INSIDE) + cells(rest, ALL))
+    for speed, rest in ((SPEED_HIGH, STRESS_HIGH), (SPEED_LOW, STRESS_LOW))
+]
+
+
+def message_tiles(kind):
+    return max(m.size for m in kind) // SUB
+
+
+def send(kind, odd, field, line, even_way, odd_way):
+    high, low = kind
 
     def fill(message, edge, out):
-        for (f, y), at, tiles in zip(message.rows, message.at, message.tiles):
-            for t in range(tiles):
-                store(out, at + t, field(f)(y, t))
+        for (f, y, t), at in message.at.items():
+            store(out, at, field(f)(y, t))
         at = message.base
         for which in LINES:
             for k in range(2):
@@ -391,22 +402,19 @@
 
 class Received:
     def __init__(self, message, odd, if_odd, if_even):
-        self.message, self.odd, self.refs = message, odd, (if_odd, if_even)
-
-    def pick(self, take):
-        return jnp.where(self.odd, take(self.refs[0]), take(self.refs[1]))
-
-    def __call__(self, index, t):
-        return self.pick(lambda ref: tile(ref, self.message.at[index] + t))
+        self.message, self.odd, self.if_odd, self.if_even = message, odd, if_odd, if_even
+
+    def __call__(self, f, y, t):
+        at = self.message.at[f, y, t]
+        return jnp.where(self.odd, tile(self.if_odd, at), tile(self.if_even, at))
 
     def line(self, which, k):
         at = self.message.base + 2 * LINES.index(which) + k
-        return self.pick(lambda ref: row(ref, at))
-
-
-def received(first, odd, even_in, odd_in):
-    high, low = messages(first)
-    return Received(high, odd, even_in, odd_in), Received(low, odd, odd_in, even_in)
+        return jnp.where(self.odd, row(self.if_odd, at), row(self.if_even, at))
+
+
+def received(kind, odd, odd_in, even_in):
+    return Received(kind[0], odd, even_in, odd_in), Received(kind[1], odd, odd_in, even_in)
 
 
 AROUND = ROWS + 4
@@ -419,29 +427,28 @@
         store(speed, (c * AROUND + y + 2) * SPAN + t, value)
 
     for t in range(SPAN):
-        sends = {"xy": (4, 5), "yz": (7, 8)}
-        for c, key, at in ((VX, "xy", 5), (VZ, "yz", 8)):
-            two, one = lo(sends[key][0], t), lo(sends[key][1], t)
+        for c, f in ((VX, SXY), (VZ, SYZ)):
+            two, one = lo(f, 6, t), lo(f, 7, t)
             rate = [RATE * buoy(y, t) for y in (0, 1, 7)]
             put(c, 0, t, partial(c, 0, t) + rate[0] * (two - 27.0 * one))
             put(c, 1, t, partial(c, 1, t) + rate[1] * one)
-            put(c, 7, t, partial(c, 7, t) - rate[2] * hi(at, t))
-        h8, h9 = hi(6, t), hi(7, t)
-        put(VY, 0, t, partial(VY, 0, t) + (RATE * buoy(0, t)) * lo(6, t))
+            put(c, 7, t, partial(c, 7, t) - rate[2] * hi(f, 0, t))
+        h8, h9 = hi(SYY, 0, t), hi(SYY, 1, t)
+        put(VY, 0, t, partial(VY, 0, t) + (RATE * buoy(0, t)) * lo(SYY, 7, t))
         put(VY, 6, t, partial(VY, 6, t) - (RATE * buoy(6, t)) * h8)
         put(VY, 7, t, partial(VY, 7, t) + (RATE * buoy(7, t)) * (27.0 * h8 - h9))
     for t in range(tiles):
-        b2, b1 = RATE * lo_buoy(9, t), RATE * lo_buoy(10, t)
-        b8, b9 = RATE * hi_buoy(9, t), RATE * hi_buoy(10, t)
-        put(VX, -1, t, lo(0, t) - b1 * sxy(0, t))
-        put(VY, -2, t, lo(1, t) - b2 * syy(0, t))
-        put(VY, -1, t, lo(2, t) + b1 * (27.0 * syy(0, t) - syy(1, t)))
-        put(VZ, -1, t, lo(3, t) - b1 * syz(0, t))
-        put(VX, 8, t, hi(0, t) + b8 * (sxy(6, t) - 27.0 * sxy(7, t)))
-        put(VX, 9, t, hi(1, t) + b9 * sxy(7, t))
-        put(VY, 8, t, hi(2, t) + b8 * syy(7, t))
-        put(VZ, 8, t, hi(3, t) + b8 * (syz(6, t) - 27.0 * syz(7, t)))
-        put(VZ, 9, t, hi(4, t) + b9 * syz(7, t))
+        b2, b1 = RATE * lo_buoy(BUOY, 6, t), RATE * lo_buoy(BUOY, 7, t)
+        b8, b9 = RATE * hi_buoy(BUOY, 0, t), RATE * hi_buoy(BUOY, 1, t)
+        put(VX, -1, t, lo(VX, 7, t) - b1 * sxy(0, t))
+        put(VY, -2, t, lo(VY, 6, t) - b2 * syy(0, t))
+        put(VY, -1, t, lo(VY, 7, t) + b1 * (27.0 * syy(0, t) - syy(1, t)))
+        put(VZ, -1, t, lo(VZ, 7, t) - b1 * syz(0, t))
+        put(VX, 8, t, hi(VX, 0, t) + b8 * (sxy(6, t) - 27.0 * sxy(7, t)))
+        put(VX, 9, t, hi(VX, 1, t) + b9 * sxy(7, t))
+        put(VY, 8, t, hi(VY, 0, t) + b8 * syy(7, t))
+        put(VZ, 8, t, hi(VZ, 0, t) + b8 * (syz(6, t) - 27.0 * syz(7, t)))
+        put(VZ, 9, t, hi(VZ, 1, t) + b9 * syz(7, t))
 
 
 def seafloor(grid, vz, y, floors, out, index):
@@ -510,7 +517,7 @@
 
 
 def start_kernel(
-    flags, before, after, main, flat, own, own_flat, even_in, odd_in,
+    flags, before, after, main, flat, own, own_flat, odd_in, even_in,
     windows, flat_windows, partial, level, even_way, odd_way,
 ):
     grid = Grid(flags[2], before, after)
@@ -542,7 +549,7 @@
     def line(which, k, y):
         return row(level, k * ROWS + y) if which is None else row(flats[k], which * ROWS + y)
 
-    send(True, (flags[1] & 1) == 1, rows_of, line, even_way, odd_way)
+    send(FIRST, (flags[1] & 1) == 1, rows_of, line, even_way, odd_way)
 
 
 def start_rest_kernel(flags, before, after, main, windows, speed_out, stress_out):
@@ -576,13 +583,14 @@
 
 
 def middle_kernel(
-    flags, before, after, main, windows, flat, flat_windows, partial, level, speed_in, stress_in, even_in, odd_in,
+    flags, before, after, main, windows, flat, flat_windows, partial, level, speed_in, stress_in,
+    odd_in, even_in,
     speed_out, stress_out, ocean, partial_out, level_out, even_way, odd_way,
     sums, pressure,
 ):
     grid = Grid(flags[2], before, after)
     odd = (flags[1] & 1) == 1
-    lo, hi = received(True, odd, even_in, odd_in)
+    lo, hi = received(FIRST, odd, odd_in, even_in)
     field = fields_of(main, windows)
     finish(
         grid, SPAN, lambda c, y, t: tile(partial, edge_index(c, y) + t), field, field(BUOY), lo, hi, lo, hi, speed_out
@@ -622,7 +630,7 @@
             return row(level_out, k * ROWS + y)
         return line(which, k, y) if which >= DEPTH else row(ocean, (3 * k + which) * ROWS + y)
 
-    send(False, odd, rows_of, line_out, even_way, odd_way)
+    send(LATER, odd, rows_of, line_out, even_way, odd_way)
 
 
 def middle_rest_kernel(flags, before, after, main, windows, around, speed_in, stress_in, speed_out, stress_out):
@@ -642,14 +650,14 @@
 
 def last_kernel(
     flags, before, after, main, windows, flat, flat_windows, stress_in, ocean_in, partial, level, speed_in, inner_in,
-    even_first, odd_first, even_in, odd_in,
+    odd_first, even_first, odd_in, even_in,
     wave_hbm, ocean_out,
     sums, pressure, around, wave, sem,
 ):
     grid = Grid(flags[2], before, after)
     odd = (flags[1] & 1) == 1
-    lo, hi = received(False, odd, even_in, odd_in)
-    lo_buoy, hi_buoy = received(True, odd, even_first, odd_first)
+    lo, hi = received(LATER, odd, odd_in, even_in)
+    lo_buoy, hi_buoy = received(FIRST, odd, odd_first, even_first)
     field = fields_of(main, windows)
     stress = block_reader(stress_in, SXX)
     finish(
@@ -657,20 +665,22 @@
         lo, hi, lo_buoy, hi_buoy, around,
     )
     speed = speed_reader(around, speed_in)
-    size = wave.shape[0] // 9
-
-    def put_out(f, y, t, value):
-        wave[pl.ds(f * size + t * SUB * ROWS + y, SUB, stride=ROWS), :] = value
-
-    def copy(f):
-        part = slice(f * size, (f + 1) * size)
-        return pltpu.make_async_copy(wave.at[part, :], wave_hbm.at[part, :], sem.at[f])
-
-    for c in (VX, VY, VZ):
-        for y in range(ROWS):
-            for t in range(TILES):
-                put_out(c, y, t, speed(c)(y, t))
-        copy(c).start()
+    sent = []
+
+    def copy(source, target):
+        sent.append(pltpu.make_async_copy(source, target, sem.at[len(sent)]))
+        sent[-1].start()
+
+    def copy_row(ref, index, f, y):
+        copy(ref.at[index * SUB : (index + TILES) * SUB, :], wave_hbm.at[f, :, y, :])
+
+    for c, y in CLOSED:
+        copy_row(speed_in, block_index(c, y), c, y)
+    for f in (SXX, SYY, SXY, SXZ, SYZ):
+        for y in INNER:
+            copy_row(inner_in, block_index(f - SXX, y), f, y)
+    for c, y in OPEN:
+        copy_row(around, (c * AROUND + y + 2) * SPAN, c, y)
     flats = (flat, flat_windows)
     fixed = lambda f, k: tile(flats[k], f)
 
@@ -687,16 +697,17 @@
     load = press(grid, levels, fixed, line, pressure)
 
     def put(f, y, t, value):
-        put_out(f, y, t, value - load(y, t) if f == SZZ else value)
-
-    stresses(grid, OUTER, TILES, speed, stress, field(LAME), field(SHEAR), put)
-    for f in range(SXX, SYZ + 1):
-        for y in INNER:
-            for t in range(TILES):
-                put(f, y, t, tile(inner_in, block_index(f - SXX, y) + t))
-        copy(f).start()
-    for f in range(9):
-        copy(f).wait()
+        wave[f - SXX, y, t * SUB : (t + 1) * SUB, :] = value - load(y, t) if f == SZZ else value
+
+    for y in INNER:
+        for t in range(TILES):
+            put(SZZ, y, t, tile(inner_in, block_index(SZZ - SXX, y) + t))
+        copy(wave.at[SZZ - SXX, y], wave_hbm.at[SZZ, :, y, :])
+    for y in OUTER:
+        stresses(grid, (y,), TILES, speed, stress, field(LAME), field(SHEAR), put)
+        copy(wave.at[:, y], wave_hbm.at[SXX : SYZ + 1, :, y, :])
+    for one in sent:
+        one.wait()
 
 
 IN_VMEM = pl.BlockSpec(memory_space=pltpu.VMEM)
@@ -724,52 +735,55 @@
     return pltpu.VMEM((n * SUB, LANES), jnp.float32)
 
 
-def exchange(axis, even_way, odd_way):
-    count = lax.axis_size(axis)
-
-    def swap(x, start):
-        pairs = [(i, i + 1) for i in range(start, count - 1, 2)]
-        return lax.ppermute(x, axis, pairs + [(j, i) for i, j in pairs])
-
-    return swap(even_way, 0), swap(odd_way, 1)
+def swap(x, axis, start):
+    pairs = [(i, i + 1) for i in range(start, lax.axis_size(axis) - 1, 2)]
+    return lax.ppermute(x, axis, pairs + [(j, i) for i, j in pairs])
 
 
 def local(*arguments):
-    wave_fields, ocean_state = arguments[0], arguments[4]
-    inputs = [pltpu.with_memory_space_constraint(x.reshape(-1, LANES), pltpu.HBM) for x in arguments]
+    ocean_state = arguments[4]
+    inputs = [pltpu.with_memory_space_constraint(x, pltpu.HBM) for x in arguments]
     flags = jnp.stack([lax.axis_index("gx"), lax.axis_index("gy"), 0])
     matrix = jax.ShapeDtypeStruct((2 * LANES, SPAN * LANES), jnp.bfloat16)
-
-    message = FIELDS * ROWS // 4 + 2
-    before, after, main, flat, own, own_flat, even_way, odd_way = call(
-        edges_kernel, [matrix, matrix, FIELDS * ROWS * TILES, 6, FIELDS * ROWS, 6, message, message],
-        [pltpu.VMEM(x.shape, x.dtype) for x in inputs] + [pltpu.SemaphoreType.DMA((16,))],
+    cells4 = jax.ShapeDtypeStruct((FIELDS, ROWS, TILES * SUB, LANES), jnp.float32)
+
+    edge = FIELDS * ROWS // 4 + 2
+    before, after, main, flat, own, own_flat, odd_way = call(
+        edges_kernel, [matrix, matrix, cells4, 6, FIELDS * ROWS, 6, edge],
+        [pltpu.VMEM(x.shape, x.dtype) for x in inputs[4:]] + [pltpu.SemaphoreType.DMA((6 * ROWS + 4,))],
         *inputs, flags=flags, place=IN_HBM,
     )
-    x_in = exchange("gx", even_way, odd_way)
-    first, later = [message_size(which) // SUB for which in (True, False)]
+    main = main.reshape(-1, LANES)
+    odd_in = swap(odd_way, "gx", 1)
+    first, later = [message_tiles(kind) for kind in (FIRST, LATER)]
+    (even_way,) = call(edges_rest_kernel, [edge], [], own, own_flat, flags=flags, work=400)
+    even_in = swap(even_way, "gx", 0)
     edges, block = len(OPEN) * SPAN, ROWS * SPAN
     windows, flat_windows, partial, level, even_way, odd_way = call(
         start_kernel, [FIELDS * ROWS, 6, edges, 2, first, first], [],
-        before, after, main, flat, own, own_flat, *x_in, flags=flags,
-    )
-    y_in = exchange("gy", even_way, odd_way)
+        before, after, main, flat, own, own_flat, odd_in, even_in, flags=flags,
+    )
+    y_first = swap(odd_way, "gy", 1), swap(even_way, "gy", 0)
     speed, inner = call(start_rest_kernel, [3 * block, 6 * block], [], before, after, main, windows, flags=flags, work=4)
     around, stress, ocean, partial, level, even_way, odd_way = call(
         middle_kernel, [3 * AROUND * SPAN, 6 * block, 6, edges, 2, later, later], [planes(4), planes(2)],
-        before, after, main, windows, flat, flat_windows, partial, level, speed, inner, *y_in, flags=flags,
-    )
-    y_in2 = exchange("gy", even_way, odd_way)
+        before, after, main, windows, flat, flat_windows, partial, level, speed, inner, *y_first, flags=flags,
+    )
+    y_in = swap(odd_way, "gy", 1), swap(even_way, "gy", 0)
     speed, inner = call(
         middle_rest_kernel, [3 * block, 6 * block], [], before, after, main, windows, around, speed, stress, flags=flags, work=4
     )
+    copies = len(CLOSED) + len(OPEN) + 5 * len(INNER) + len(INNER) + len(OUTER)
     wave_out, ocean_out = call(
-        last_kernel, [9 * ROWS * TILES, 3],
-        [planes(4), planes(2), planes(3 * AROUND * SPAN), planes(9 * ROWS * TILES), pltpu.SemaphoreType.DMA((9,))],
-        before, after, main, windows, flat, flat_windows, stress, ocean, partial, level, speed, inner, *y_in, *y_in2,
+        last_kernel, [jax.ShapeDtypeStruct(arguments[0].shape, jnp.float32), 3],
+        [
+            planes(4), planes(2), planes(3 * AROUND * SPAN), pltpu.VMEM((6, *cells4.shape[1:]), jnp.float32),
+            pltpu.SemaphoreType.DMA((copies,)),
+        ],
+        before, after, main, windows, flat, flat_windows, stress, ocean, partial, level, speed, inner, *y_first, *y_in,
         flags=flags, out_places=[IN_HBM, IN_VMEM],
     )
-    return wave_out.reshape(wave_fields.shape), ocean_out.reshape(ocean_state.shape)
+    return wave_out, ocean_out.reshape(ocean_state.shape)
 
 
 def solution(mesh):

time: 36.4 us -> 38.3 us (1.052)
  waiting for transfers between devices: 11.9 us -> 15.7 us
  starting transfers between devices: 12 us -> 8.59 us
  Pallas kernels: 11.3 us -> 12.9 us
    ppermute x6, waiting for transfers between devices: 11.9 us -> 15.7 us  [swap(): return lax.ppermute(x, axis, pairs + [(j, i) for i, j in pairs])]
    ppermute x6, starting transfers between devices: 12 us -> 8.59 us  [swap(): return lax.ppermute(x, axis, pairs + [(j, i) for i, j in pairs])]
    pallas_call x6 -> x7, Pallas kernels: 11.3 us -> 12.9 us  [call(): pl.pallas_call(kernel, out_shape=[n if hasattr(n, 'dtype') else jax.Shape...]
where the time goes in v5:
time: 38.3 us; the launch traced here: 38 us
  waiting for transfers between devices  15.7 us (41%)
  Pallas kernels  12.9 us (34%)
  starting transfers between devices  8.59 us (22%)
  between operations  0.72 us (2%)
    ppermute x6, waiting for transfers between devices, swap(): return lax.ppermute(x, axis, pairs + [(j, i) for i, j in pairs])  15.7 us
    pallas_call x7, Pallas kernels, call(): pl.pallas_call(kernel, out_shape=[n if hasattr(n, 'dtype') else jax.Shape...  12.9 us
    ppermute x6, starting transfers between devices, swap(): return lax.ppermute(x, axis, pairs + [(j, i) for i, j in pairs])  8.59 us
  transfers between devices with their start and end apart: 6, of which 5 were waited for; matrix products, arithmetic and copies ran while one was open for 0% of the time, Pallas kernels for 6%

profile of v5, /device:TPU:10, one launch (start us, length us, event | category | flops | bytes accessed | tf_op | source)
XLA Modules:
  0.0 38.0 jit_solution(14840204667143433101)
XLA Ops:
  0.6 0.1 pad_add_fusion.flags
  0.7 4.0 %shard_map.95 = (bf16[256,640]{1,0:T(8,128)(2,1)S(1)}, bf16[256,640]{1,0:T(8,128)(2,1)S(1)}, f32[12,8,32,128]{3,2,1,0:T(8,128)S(1)}, f32[48,128]{1,0:T(8,128)S(1...) custom-call(s32[3]{0:T(128)S(1)} %pad_add_fusion.flags, f32[9,32,8,128]{3,2,1,0:T(8,128)} %refs_0_.1, ...), custom_call_target="tpu_custom_call" | custom-call | flops 1000000 | bytes 2146316 | tf_op jit(solution)/shard_map/pallas_call | solution.py:723
  4.7 0.7 %shard_map.96 = f32[208,128]{1,0:T(8,128)S(1)} custom-call(s32[3]{0:T(128)S(1)} %pad_add_fusion.flags, f32[768,128]{1,0:T(8,128)S(1)} %get-tuple-element.32.own, f32[48,128]{1,0:T(8,128)S(1)} %get-tuple-element.33.own_flat), custom_call_target="tpu_custom_call" | custom-call | flops 400000000 | bytes 524300 | tf_op jit(solution)/shard_map/pallas_call | solution.py:723
  5.4 0.1 collective-permute-start.1
  5.5 2.5 %collective-permute-start = (f32[208,128]{1,0:T(8,128)S(1)}, f32[208,128]{1,0:T(8,128)S(1)}, u32[]{:S(2)}, u32[]{:S(2)}) collective-permute-start(f32[208,128]{1,0:T(8,128)S(1)} %get-tuple-element.34), channel_id=1, source_target_pairs={{4,8},{12,16},{20,24},{8,4},{16,12},{24,20},{5,9},{13,17},{21,25},... | collective-permute-start | bytes 319496 | tf_op jit(solution)/shard_map/ppermute | solution.py:740
  8.0 0.0 collective-permute-done.1.even_in
  8.0 3.5 %collective-permute-done.odd_in = f32[208,128]{1,0:T(8,128)S(1)} collective-permute-done((f32[208,128]{1,0:T(8,128)S(1)}, f32[208,128]{1,0:T(8,128)S(1)}, u32[]{:S(2)}, u32[]{:S(2)}) %collective-permute-start) | collective-permute-done | bytes 106528 | tf_op jit(solution)/shard_map/ppermute | solution.py:740
  11.5 0.9 %shard_map.97 = (f32[768,128]{1,0:T(8,128)S(1)}, f32[48,128]{1,0:T(8,128)S(1)}, f32[360,128]{1,0:T(8,128)S(1)}, f32[16,128]{1,0:T(8,128)S(1)}, f32[456,128]{1,0:T(8,128)S(1)}, /*index=5*/f32[456,128]{1,0:T(8,128)S(1)}) custom-call(s32[3]{0:T(128)S(1)} %pad_add_fusion.flags, bf16[256,640]{1,0:T(8,128)(2,1)S(1)} %get-tuple-element.28.before, ...), custom_call_target="tpu_custom_call" | custom-call | flops 1000000 | bytes 4616204 | tf_op jit(solution)/shard_map/pallas_call | solution.py:723
  12.4 3.5 %collective-permute-start.2 = (f32[456,128]{1,0:T(8,128)S(1)}, f32[456,128]{1,0:T(8,128)S(1)}, u32[]{:S(2)}, u32[]{:S(2)}) collective-permute-start(f32[456,128]{1,0:T(8,128)S(1)} %get-tuple-element.41), channel_id=1, source_target_pairs={{1,2},{2,1},{5,6},{6,5},{9,10},{10,9},{13,14},{14,13},{17,18},{18,... | collective-permute-start | bytes 700424 | tf_op jit(solution)/shard_map/ppermute | solution.py:740
  15.9 0.1 collective-permute-start.3
  16.0 1.1 %shard_map.98 = (f32[960,128]{1,0:T(8,128)S(1)}, f32[1920,128]{1,0:T(8,128)S(1)}) custom-call(s32[3]{0:T(128)S(1)} %pad_add_fusion.flags, bf16[256,640]{1,0:T(8,128)(2,1)S(1)} %get-tuple-element.28.before, bf16[256,640]{1,0:T(8,128)(2,1)S(1)} %get-tuple-element.29.after, f32[3072,128]{1,0:T(8,128)S(1)} %bitcast.5, f32[768,128]{1,0:T(8,128)S(1)} %get-tuple-element.35.windows), custom_call_target="tpu_custom_call" | custom-call | flops 4000000 | bytes 4751372 | tf_op jit(solution)/shard_map/pallas_call | solution.py:723
  17.1 4.8 %collective-permute-done.2.odd_in.odd_first = f32[456,128]{1,0:T(8,128)S(1)} collective-permute-done((f32[456,128]{1,0:T(8,128)S(1)}, f32[456,128]{1,0:T(8,128)S(1)}, u32[]{:S(2)}, u32[]{:S(2)}) %collective-permute-start.2) | collective-permute-done | bytes 233504 | tf_op jit(solution)/shard_map/ppermute | solution.py:740
  22.0 2.0 %collective-permute-done.3.even_in.even_first = f32[456,128]{1,0:T(8,128)S(1)} collective-permute-done((f32[456,128]{1,0:T(8,128)S(1)}, f32[456,128]{1,0:T(8,128)S(1)}, u32[]{:S(2)}, u32[]{:S(2)}) %collective-permute-start.3) | collective-permute-done | bytes 233504 | tf_op jit(solution)/shard_map/ppermute | solution.py:740
  24.0 1.4 %shard_map.99 = (f32[1440,128]{1,0:T(8,128)S(1)}, f32[1920,128]{1,0:T(8,128)S(1)}, f32[48,128]{1,0:T(8,128)S(1)}, f32[360,128]{1,0:T(8,128)S(1)}, f32[16,128]{1,...) custom-call(s32[3]{0:T(128)S(1)} %pad_add_fusion.flags, bf16[256,640]{1,0:T(8,128)(2,1)S(1)} %get-tuple-element.28.before, ...), custom_call_target="tpu_custom_call" | custom-call | flops 1000000 | bytes 7749644 | tf_op jit(solution)/shard_map/pallas_call | solution.py:723
  25.4 2.4 %collective-permute-start.4 = (f32[344,128]{1,0:T(8,128)S(1)}, f32[344,128]{1,0:T(8,128)S(1)}, u32[]{:S(2)}, u32[]{:S(2)}) collective-permute-start(f32[344,128]{1,0:T(8,128)S(1)} %get-tuple-element.50), channel_id=1, source_target_pairs={{1,2},{2,1},{5,6},{6,5},{9,10},{10,9},{13,14},{14,13},{17,18},{18,... | collective-permute-start | bytes 528392 | tf_op jit(solution)/shard_map/ppermute | solution.py:740
  27.7 0.1 collective-permute-start.5
  27.8 1.1 %shard_map.100 = (f32[960,128]{1,0:T(8,128)S(1)}, f32[1920,128]{1,0:T(8,128)S(1)}) custom-call(s32[3]{0:T(128)S(1)} %pad_add_fusion.flags, bf16[256,640]{1,0:T(8,128)(2,1)S(1)} %get-tuple-element.28.before, bf16[256,640]{1,0:T(8,128)(2,1)S(1)} %get-tuple-element.29.after, f32[3072,128]{1,0:T(8,128)S(1)} %bitcast.7, ...), custom_call_target="tpu_custom_call" | custom-call | flops 4000000 | bytes 6963212 | tf_op jit(solution)/shard_map/pallas_call | solution.py:723
  28.9 5.2 %collective-permute-done.4.odd_in = f32[344,128]{1,0:T(8,128)S(1)} collective-permute-done((f32[344,128]{1,0:T(8,128)S(1)}, f32[344,128]{1,0:T(8,128)S(1)}, u32[]{:S(2)}, u32[]{:S(2)}) %collective-permute-start.4) | collective-permute-done | bytes 176160 | tf_op jit(solution)/shard_map/ppermute | solution.py:740
  34.1 0.2 collective-permute-done.5.even_in
  34.3 3.7 %shard_map.101 = (f32[9,32,8,128]{3,2,1,0:T(8,128)}, f32[24,128]{1,0:T(8,128)}) custom-call(s32[3]{0:T(128)S(1)} %pad_add_fusion.flags, bf16[256,640]{1,0:T(8,128)(2,1)S(1)} %get-tuple-element.28.before, bf16[256,640]{1,0:T(8,128)(2,1)S(1)} %get-tuple-element.29.after, f32[3072,128]{1,0:T(8,128)S(1)} %bitcast.8, f32[768,128]{1,0:T(8,128)S(1)} %get-tuple-element.35.windows, ...), custom_call_target="tpu_custom_call" | custom-call | flops 1000000 | bytes 6832140 | tf_op jit(solution)/shard_map/pallas_call | solution.py:723
Async XLA Ops:
  5.4 2.6 %collective-permute-start.1 = (f32[208,128]{1,0:T(8,128)S(1)}, f32[208,128]{1,0:T(8,128)S(1)}, u32[]{:S(2)}, u32[]{:S(2)}) collective-permute-start(f32[208,128]{1,0:T(8,128)S(1)} %shard_map.96), channel_id=1, source_target_pairs={{0,4},{8,12},{16,20},{24,28},{4,0},{12,8},{20,16},{28,24},{1,5},{9... | collective-permute-start | bytes 319496 | tf_op jit(solution)/shard_map/ppermute | solution.py:740
  5.5 6.0 %collective-permute-start = (f32[208,128]{1,0:T(8,128)S(1)}, f32[208,128]{1,0:T(8,128)S(1)}, u32[]{:S(2)}, u32[]{:S(2)}) collective-permute-start(f32[208,128]{1,0:T(8,128)S(1)} %get-tuple-element.34), channel_id=1, source_target_pairs={{4,8},{12,16},{20,24},{8,4},{16,12},{24,20},{5,9},{13,17},{21,25},... | collective-permute-start | bytes 319496 | tf_op jit(solution)/shard_map/ppermute | solution.py:740
  12.4 9.5 %collective-permute-start.2 = (f32[456,128]{1,0:T(8,128)S(1)}, f32[456,128]{1,0:T(8,128)S(1)}, u32[]{:S(2)}, u32[]{:S(2)}) collective-permute-start(f32[456,128]{1,0:T(8,128)S(1)} %get-tuple-element.41), channel_id=1, source_target_pairs={{1,2},{2,1},{5,6},{6,5},{9,10},{10,9},{13,14},{14,13},{17,18},{18,... | collective-permute-start | bytes 700424 | tf_op jit(solution)/shard_map/ppermute | solution.py:740
  15.9 8.0 %collective-permute-start.3 = (f32[456,128]{1,0:T(8,128)S(1)}, f32[456,128]{1,0:T(8,128)S(1)}, u32[]{:S(2)}, u32[]{:S(2)}) collective-permute-start(f32[456,128]{1,0:T(8,128)S(1)} %get-tuple-element.42), channel_id=1, source_target_pairs={{0,1},{2,3},{1,0},{3,2},{4,5},{6,7},{5,4},{7,6},{8,9},{10,11},{9,8... | collective-permute-start | bytes 700424 | tf_op jit(solution)/shard_map/ppermute | solution.py:740
  25.4 8.7 %collective-permute-start.4 = (f32[344,128]{1,0:T(8,128)S(1)}, f32[344,128]{1,0:T(8,128)S(1)}, u32[]{:S(2)}, u32[]{:S(2)}) collective-permute-start(f32[344,128]{1,0:T(8,128)S(1)} %get-tuple-element.50), channel_id=1, source_target_pairs={{1,2},{2,1},{5,6},{6,5},{9,10},{10,9},{13,14},{14,13},{17,18},{18,... | collective-permute-start | bytes 528392 | tf_op jit(solution)/shard_map/ppermute | solution.py:740
  27.7 6.6 %collective-permute-start.5 = (f32[344,128]{1,0:T(8,128)S(1)}, f32[344,128]{1,0:T(8,128)S(1)}, u32[]{:S(2)}, u32[]{:S(2)}) collective-permute-start(f32[344,128]{1,0:T(8,128)S(1)} %get-tuple-element.51), channel_id=1, source_target_pairs={{0,1},{2,3},{1,0},{3,2},{4,5},{6,7},{5,4},{7,6},{8,9},{10,11},{9,8... | collective-permute-start | bytes 528392 | tf_op jit(solution)/shard_map/ppermute | solution.py:740

commit v6 on v5

--- a/solution.py
+++ b/solution.py
@@ -186,16 +186,6 @@
         store(out, index, jnp.where(grid.left, one, two))
 
 
-def pack_edges(grid, own, own_flat, to_right, out):
-    @pl.when(to_right)
-    def _():
-        pack(grid, edge_groups(own, own_flat), True, out)
-
-    @pl.when(jnp.logical_not(to_right))
-    def _():
-        pack(grid, edge_groups(own, own_flat), False, out)
-
-
 def edge_groups(own, own_flat):
     groups = [
         [tile(own, h * ROWS + y) for y in (q, q + 1) for h in (f, f + 1)]
@@ -239,42 +229,35 @@
     k, n = [lax.broadcasted_iota(jnp.int32, (LANES, LANES), axis) for axis in range(2)]
     column = (n % GROUP - EDGE) % LANES
     one = jnp.where((n % HALF // GROUP == t) & (k == column), 1.0, 0.0).astype(jnp.bfloat16)
-    return jnp.concatenate([one] * 3, axis=0)
+    return jnp.concatenate([one] * 2, axis=0)
 
 
 def edges_kernel(flags, *refs):
-    hbm, refs = refs[:8], refs[8:]
-    (before, after, main, flat, own, own_flat, odd_way), (ocean, deep, floor, wet, sem) = refs[:7], refs[7:]
-    ready = {}
-    at = 0
-    for source, first, count in ((0, 0, 3), (0, 3, 3), (0, 6, 3), (1, LAME, 1), (2, SHEAR, 1), (3, BUOY, 1)):
-        copies = []
-        for y in range(ROWS):
-            if source:
-                pair = hbm[source].at[:, y, :], main.at[first, y]
-            else:
-                pair = hbm[0].at[first : first + count, :, y, :], main.at[first : first + count, y]
-            copies.append(pltpu.make_async_copy(*pair, sem.at[at]))
-            at += 1
-        ready[first] = copies
-    flats = [pltpu.make_async_copy(hbm[4 + k], target, sem.at[at + k]) for k, target in enumerate((ocean, deep, floor, wet))]
-    for copies in list(ready.values()) + [flats]:
-        for copy in copies:
-            copy.start()
+    hbm, (before, after, flat, own, own_flat, even_way, odd_way), refs = refs[:8], refs[8:15], refs[15:]
+    fields, picked, ocean, deep, floor, wet, sem = refs
+    sources = [hbm[0].at[f] for f in range(9)] + [hbm[1], hbm[2], hbm[3]]
+    copies = [pltpu.make_async_copy(x, fields.at[f], sem.at[f]) for f, x in enumerate(sources)]
+    copies += [
+        pltpu.make_async_copy(hbm[4 + k], x, sem.at[FIELDS + k]) for k, x in enumerate((ocean, deep, floor, wet))
+    ]
+    for copy in copies:
+        copy.start()
     difference_matrix(before, (27.0, -27.0, -1.0, 1.0), (0, 1, -1, 2))
     difference_matrix(after, (27.0, -27.0, -1.0, 1.0), (-1, 0, -2, 1))
     pickers = [picker(t) for t in range(TILES)]
     grid = Grid()
     for f in range(FIELDS):
-        for copy in ready.get(f, ()):
-            copy.wait()
+        copies[f].wait()
         total = None
         for t in range(TILES):
-            tiles = [main[f, y, t * SUB : (t + 1) * SUB, :] for y in range(ROWS)]
-            part = jnp.dot(split(jnp.concatenate(tiles, axis=0), 3), pickers[t], preferred_element_type=jnp.float32)
+            x = fields[f, t * SUB : (t + 1) * SUB].reshape(SUB * ROWS, LANES)
+            part = jnp.dot(split(x, 2), pickers[t], preferred_element_type=jnp.float32)
             total = part if total is None else total + part
-        own[f * ROWS * SUB : (f + 1) * ROWS * SUB, :] = total
-    for copy in flats:
+        size = SUB * ROWS
+        picked[f * size : (f + 1) * size, :] = total
+        for y in range(ROWS):
+            store(own, f * ROWS + y, picked[pl.ds(f * size + y, SUB, stride=ROWS), :])
+    for copy in copies[FIELDS:]:
         copy.wait()
     planes = [ocean[k] for k in range(3)] + [deep[...]]
     planes += [floor[...].astype(jnp.float32), wet[...].astype(jnp.float32)]
@@ -284,11 +267,29 @@
         for g in range(LANES // GROUP):
             out = jnp.where(grid.group == g, rolled(x, EDGE + GROUP * g, 1), out)
         store(own_flat, k, out)
-    pack_edges(grid, own, own_flat, (flags[0] & 1) == 1, odd_way)
-
-
-def edges_rest_kernel(flags, own, own_flat, even_way):
-    pack_edges(Grid(), own, own_flat, (flags[0] & 1) == 0, even_way)
+
+    @pl.when((flags[0] & 1) == 1)
+    def _():
+        pack(grid, edge_groups(own, own_flat), True, odd_way)
+        pack(grid, edge_groups(own, own_flat), False, even_way)
+
+    @pl.when((flags[0] & 1) == 0)
+    def _():
+        pack(grid, edge_groups(own, own_flat), False, odd_way)
+        pack(grid, edge_groups(own, own_flat), True, even_way)
+
+
+def turn_kernel(flat, *refs):
+    hbm, main, sem = refs[:4], refs[4], refs[5]
+    copies = []
+    for y in range(ROWS):
+        for source, target in [(hbm[0].at[:, :, y, :], main.at[:LAME, y])] + [
+            (hbm[1 + k].at[:, y, :], main.at[LAME + k, y]) for k in range(3)
+        ]:
+            copies.append(pltpu.make_async_copy(source, target, sem.at[len(copies)]))
+            copies[-1].start()
+    for copy in copies:
+        copy.wait()
 
 
 def speeds(grid, stress, speed, buoy, todo, put):
@@ -413,7 +414,7 @@
         return jnp.where(self.odd, row(self.if_odd, at), row(self.if_even, at))
 
 
-def received(kind, odd, odd_in, even_in):
+def received(kind, odd, even_in, odd_in):
     return Received(kind[0], odd, even_in, odd_in), Received(kind[1], odd, odd_in, even_in)
 
 
@@ -517,7 +518,7 @@
 
 
 def start_kernel(
-    flags, before, after, main, flat, own, own_flat, odd_in, even_in,
+    flags, before, after, main, flat, own, own_flat, even_in, odd_in,
     windows, flat_windows, partial, level, even_way, odd_way,
 ):
     grid = Grid(flags[2], before, after)
@@ -584,13 +585,13 @@
 
 def middle_kernel(
     flags, before, after, main, windows, flat, flat_windows, partial, level, speed_in, stress_in,
-    odd_in, even_in,
+    even_in, odd_in,
     speed_out, stress_out, ocean, partial_out, level_out, even_way, odd_way,
     sums, pressure,
 ):
     grid = Grid(flags[2], before, after)
     odd = (flags[1] & 1) == 1
-    lo, hi = received(FIRST, odd, odd_in, even_in)
+    lo, hi = received(FIRST, odd, even_in, odd_in)
     field = fields_of(main, windows)
     finish(
         grid, SPAN, lambda c, y, t: tile(partial, edge_index(c, y) + t), field, field(BUOY), lo, hi, lo, hi, speed_out
@@ -650,14 +651,14 @@
 
 def last_kernel(
     flags, before, after, main, windows, flat, flat_windows, stress_in, ocean_in, partial, level, speed_in, inner_in,
-    odd_first, even_first, odd_in, even_in,
+    even_first, odd_first, even_in, odd_in,
     wave_hbm, ocean_out,
     sums, pressure, around, wave, sem,
 ):
     grid = Grid(flags[2], before, after)
     odd = (flags[1] & 1) == 1
-    lo, hi = received(LATER, odd, odd_in, even_in)
-    lo_buoy, hi_buoy = received(FIRST, odd, odd_first, even_first)
+    lo, hi = received(LATER, odd, even_in, odd_in)
+    lo_buoy, hi_buoy = received(FIRST, odd, even_first, odd_first)
     field = fields_of(main, windows)
     stress = block_reader(stress_in, SXX)
     finish(
@@ -676,9 +677,6 @@
 
     for c, y in CLOSED:
         copy_row(speed_in, block_index(c, y), c, y)
-    for f in (SXX, SYY, SXY, SXZ, SYZ):
-        for y in INNER:
-            copy_row(inner_in, block_index(f - SXX, y), f, y)
     for c, y in OPEN:
         copy_row(around, (c * AROUND + y + 2) * SPAN, c, y)
     flats = (flat, flat_windows)
@@ -697,15 +695,22 @@
     load = press(grid, levels, fixed, line, pressure)
 
     def put(f, y, t, value):
-        wave[f - SXX, y, t * SUB : (t + 1) * SUB, :] = value - load(y, t) if f == SZZ else value
-
-    for y in INNER:
-        for t in range(TILES):
-            put(SZZ, y, t, tile(inner_in, block_index(SZZ - SXX, y) + t))
-        copy(wave.at[SZZ - SXX, y], wave_hbm.at[SZZ, :, y, :])
-    for y in OUTER:
-        stresses(grid, (y,), TILES, speed, stress, field(LAME), field(SHEAR), put)
-        copy(wave.at[:, y], wave_hbm.at[SXX : SYZ + 1, :, y, :])
+        size = TILES * SUB * ROWS
+        if f == SZZ:
+            value = value - load(y, t)
+        wave[pl.ds((f - SXX) * size + t * SUB * ROWS + y, SUB, stride=ROWS), :] = value
+
+    for f in range(SXX, SYZ + 1):
+        for y in INNER:
+            for t in range(TILES):
+                put(f, y, t, tile(inner_in, block_index(f - SXX, y) + t))
+    stresses(grid, OUTER, TILES, speed, stress, field(LAME), field(SHEAR), put)
+    for f in range(SXX, SYZ + 1):
+        size = TILES * SUB
+        for z in range(0, size, size // 2):
+            at = ((f - SXX) * size + z) * ROWS
+            target = wave_hbm.at[f, z : z + size // 2].reshape(size // 2 * ROWS, LANES)
+            copy(wave.at[at : at + size // 2 * ROWS, :], target)
     for one in sent:
         one.wait()
 
@@ -716,7 +721,7 @@
 
 
 def call(kernel, tiles, scratch, *arguments, flags=None, place=IN_VMEM, out_places=None, work=1):
-    specs = [place] * len(arguments)
+    specs = place if isinstance(place, list) else [place] * len(arguments)
     if flags is not None:
         arguments, specs = (flags, *arguments), [IN_SMEM] + specs
     moved = sum(x.size for x in arguments) + sum(n for n in tiles if isinstance(n, int)) * SUB * LANES
@@ -748,36 +753,39 @@
     cells4 = jax.ShapeDtypeStruct((FIELDS, ROWS, TILES * SUB, LANES), jnp.float32)
 
     edge = FIELDS * ROWS // 4 + 2
-    before, after, main, flat, own, own_flat, odd_way = call(
-        edges_kernel, [matrix, matrix, cells4, 6, FIELDS * ROWS, 6, edge],
-        [pltpu.VMEM(x.shape, x.dtype) for x in inputs[4:]] + [pltpu.SemaphoreType.DMA((6 * ROWS + 4,))],
+    before, after, flat, own, own_flat, even_way, odd_way = call(
+        edges_kernel, [matrix, matrix, 6, FIELDS * ROWS, 6, edge, edge],
+        [pltpu.VMEM((FIELDS, *arguments[1].shape), jnp.float32), planes(FIELDS * SUB)]
+        + [pltpu.VMEM(x.shape, x.dtype) for x in inputs[4:]] + [pltpu.SemaphoreType.DMA((FIELDS + 4,))],
         *inputs, flags=flags, place=IN_HBM,
     )
+    even_in, odd_in = swap(even_way, "gx", 0), swap(odd_way, "gx", 1)
+    (main,) = call(
+        turn_kernel, [cells4], [pltpu.SemaphoreType.DMA((4 * ROWS,))], flat, *inputs[:4],
+        place=[IN_VMEM] + [IN_HBM] * 4, work=4,
+    )
     main = main.reshape(-1, LANES)
-    odd_in = swap(odd_way, "gx", 1)
     first, later = [message_tiles(kind) for kind in (FIRST, LATER)]
-    (even_way,) = call(edges_rest_kernel, [edge], [], own, own_flat, flags=flags, work=400)
-    even_in = swap(even_way, "gx", 0)
     edges, block = len(OPEN) * SPAN, ROWS * SPAN
     windows, flat_windows, partial, level, even_way, odd_way = call(
         start_kernel, [FIELDS * ROWS, 6, edges, 2, first, first], [],
-        before, after, main, flat, own, own_flat, odd_in, even_in, flags=flags,
-    )
-    y_first = swap(odd_way, "gy", 1), swap(even_way, "gy", 0)
+        before, after, main, flat, own, own_flat, even_in, odd_in, flags=flags,
+    )
+    y_first = swap(even_way, "gy", 0), swap(odd_way, "gy", 1)
     speed, inner = call(start_rest_kernel, [3 * block, 6 * block], [], before, after, main, windows, flags=flags, work=4)
     around, stress, ocean, partial, level, even_way, odd_way = call(
         middle_kernel, [3 * AROUND * SPAN, 6 * block, 6, edges, 2, later, later], [planes(4), planes(2)],
         before, after, main, windows, flat, flat_windows, partial, level, speed, inner, *y_first, flags=flags,
     )
-    y_in = swap(odd_way, "gy", 1), swap(even_way, "gy", 0)
+    y_in = swap(even_way, "gy", 0), swap(odd_way, "gy", 1)
     speed, inner = call(
         middle_rest_kernel, [3 * block, 6 * block], [], before, after, main, windows, around, speed, stress, flags=flags, work=4
     )
-    copies = len(CLOSED) + len(OPEN) + 5 * len(INNER) + len(INNER) + len(OUTER)
+    copies = len(CLOSED) + len(OPEN) + 2 * 6
     wave_out, ocean_out = call(
         last_kernel, [jax.ShapeDtypeStruct(arguments[0].shape, jnp.float32), 3],
         [
-            planes(4), planes(2), planes(3 * AROUND * SPAN), pltpu.VMEM((6, *cells4.shape[1:]), jnp.float32),
+            planes(4), planes(2), planes(3 * AROUND * SPAN), planes(6 * ROWS * TILES),
             pltpu.SemaphoreType.DMA((copies,)),
         ],
         before, after, main, windows, flat, flat_windows, stress, ocean, partial, level, speed, inner, *y_first, *y_in,

time: 38.3 us -> 36.7 us (0.958)
  waiting for transfers between devices: 15.7 us -> 10.1 us
  starting transfers between devices: 8.59 us -> 12 us
  Pallas kernels: 12.9 us -> 13.4 us
    ppermute x6, waiting for transfers between devices: 15.7 us -> 10.1 us  [swap(): return lax.ppermute(x, axis, pairs + [(j, i) for i, j in pairs])]
    ppermute x6, starting transfers between devices: 8.59 us -> 12 us  [swap(): return lax.ppermute(x, axis, pairs + [(j, i) for i, j in pairs])]
    pallas_call x7, Pallas kernels: 12.9 us -> 13.4 us  [call(): pl.pallas_call(kernel, out_shape=[n if hasattr(n, 'dtype') else jax.Shape...]
  transfers between devices with their start and end apart: 6 -> 6, of which waited for: 5 -> 5; matrix products, arithmetic and copies ran while one was open for 0% -> 0% of each run, Pallas kernels for 6% -> 11%
where the time goes in v6:
time: 36.7 us; the launch traced here: 36.3 us
  Pallas kernels  13.4 us (37%)
  starting transfers between devices  12 us (33%)
  waiting for transfers between devices  10.1 us (28%)
  between operations  0.72 us (2%)
    pallas_call x7, Pallas kernels, call(): pl.pallas_call(kernel, out_shape=[n if hasattr(n, 'dtype') else jax.Shape...  13.4 us
    ppermute x6, starting transfers between devices, swap(): return lax.ppermute(x, axis, pairs + [(j, i) for i, j in pairs])  12 us
    ppermute x6, waiting for transfers between devices, swap(): return lax.ppermute(x, axis, pairs + [(j, i) for i, j in pairs])  10.1 us
  transfers between devices with their start and end apart: 6, of which 5 were waited for; matrix products, arithmetic and copies ran while one was open for 0% of the time, Pallas kernels for 11%

profile of v6, /device:TPU:10, one launch (start us, length us, event | category | flops | bytes accessed | tf_op | source)
XLA Modules:
  0.0 36.3 jit_solution(17337910592440546500)
XLA Ops:
  0.6 0.1 pad_add_fusion.flags
  0.7 4.1 %shard_map.95 = (bf16[256,640]{1,0:T(8,128)(2,1)S(1)}, bf16[256,640]{1,0:T(8,128)(2,1)S(1)}, f32[48,128]{1,0:T(8,128)S(1)}, f32[768,128]{1,0:T(8,128)S(1)}, f32[...) custom-call(s32[3]{0:T(128)S(1)} %pad_add_fusion.flags, f32[9,32,8,128]{3,2,1,0:T(8,128)} %refs_0_.3, ...), custom_call_target="tpu_custom_call" | custom-call | flops 1000000 | bytes 2252812 | tf_op jit(solution)/shard_map/pallas_call | solution.py:728
  4.9 0.1 collective-permute-start
  4.9 2.5 %collective-permute-start.1 = (f32[208,128]{1,0:T(8,128)S(1)}, f32[208,128]{1,0:T(8,128)S(1)}, u32[]{:S(2)}, u32[]{:S(2)}) collective-permute-start(f32[208,128]{1,0:T(8,128)S(1)} %get-tuple-element.34), channel_id=1, source_target_pairs={{4,8},{12,16},{20,24},{8,4},{16,12},{24,20},{5,9},{13,17},{21,25},... | collective-permute-start | bytes 319496 | tf_op jit(solution)/shard_map/ppermute | solution.py:745
  7.5 1.8 %shard_map.96 = f32[12,8,32,128]{3,2,1,0:T(8,128)S(1)} custom-call(f32[48,128]{1,0:T(8,128)S(1)} %get-tuple-element.30.flat, f32[9,32,8,128]{3,2,1,0:T(8,128)} %refs_0_.3, f32[32,8,128]{2,1,0:T(8,128)} %refs_1_.3, f32[32,8,128]{2,1,0:T(8,128)} %refs_2_.3, f32[32,8,128]{2,1,0:T(8,128)} %refs_3_.3), custom_call_target="tpu_custom_call" | custom-call | flops 4000000 | bytes 1597440 | tf_op jit(solution)/shard_map/pallas_call | solution.py:728
  9.3 0.0 collective-permute-done.even_in
  9.3 1.7 %collective-permute-done.1.odd_in = f32[208,128]{1,0:T(8,128)S(1)} collective-permute-done((f32[208,128]{1,0:T(8,128)S(1)}, f32[208,128]{1,0:T(8,128)S(1)}, u32[]{:S(2)}, u32[]{:S(2)}) %collective-permute-start.1) | collective-permute-done | bytes 106528 | tf_op jit(solution)/shard_map/ppermute | solution.py:745
  11.0 0.9 %shard_map.97 = (f32[768,128]{1,0:T(8,128)S(1)}, f32[48,128]{1,0:T(8,128)S(1)}, f32[360,128]{1,0:T(8,128)S(1)}, f32[16,128]{1,0:T(8,128)S(1)}, f32[456,128]{1,0:T(8,128)S(1)}, /*index=5*/f32[456,128]{1,0:T(8,128)S(1)}) custom-call(s32[3]{0:T(128)S(1)} %pad_add_fusion.flags, bf16[256,640]{1,0:T(8,128)(2,1)S(1)} %get-tuple-element.28.before, ...), custom_call_target="tpu_custom_call" | custom-call | flops 1000000 | bytes 4616204 | tf_op jit(solution)/shard_map/pallas_call | solution.py:728
  11.9 0.5 %collective-permute-start.2 = (f32[456,128]{1,0:T(8,128)S(1)}, f32[456,128]{1,0:T(8,128)S(1)}, u32[]{:S(2)}, u32[]{:S(2)}) collective-permute-start(f32[456,128]{1,0:T(8,128)S(1)} %get-tuple-element.41), channel_id=1, source_target_pairs={{0,1},{2,3},{1,0},{3,2},{4,5},{6,7},{5,4},{7,6},{8,9},{10,11},{9,8... | collective-permute-start | bytes 700424 | tf_op jit(solution)/shard_map/ppermute | solution.py:745
  12.4 4.6 %collective-permute-start.3 = (f32[456,128]{1,0:T(8,128)S(1)}, f32[456,128]{1,0:T(8,128)S(1)}, u32[]{:S(2)}, u32[]{:S(2)}) collective-permute-start(f32[456,128]{1,0:T(8,128)S(1)} %get-tuple-element.42), channel_id=1, source_target_pairs={{1,2},{2,1},{5,6},{6,5},{9,10},{10,9},{13,14},{14,13},{17,18},{18,... | collective-permute-start | bytes 700424 | tf_op jit(solution)/shard_map/ppermute | solution.py:745
  17.0 1.1 %shard_map.98 = (f32[960,128]{1,0:T(8,128)S(1)}, f32[1920,128]{1,0:T(8,128)S(1)}) custom-call(s32[3]{0:T(128)S(1)} %pad_add_fusion.flags, bf16[256,640]{1,0:T(8,128)(2,1)S(1)} %get-tuple-element.28.before, bf16[256,640]{1,0:T(8,128)(2,1)S(1)} %get-tuple-element.29.after, f32[3072,128]{1,0:T(8,128)S(1)} %bitcast.5, f32[768,128]{1,0:T(8,128)S(1)} %get-tuple-element.35.windows), custom_call_target="tpu_custom_call" | custom-call | flops 4000000 | bytes 4751372 | tf_op jit(solution)/shard_map/pallas_call | solution.py:728
  18.1 1.4 %collective-permute-done.2.even_in.even_first = f32[456,128]{1,0:T(8,128)S(1)} collective-permute-done((f32[456,128]{1,0:T(8,128)S(1)}, f32[456,128]{1,0:T(8,128)S(1)}, u32[]{:S(2)}, u32[]{:S(2)}) %collective-permute-start.2) | collective-permute-done | bytes 233504 | tf_op jit(solution)/shard_map/ppermute | solution.py:745
  19.6 3.0 %collective-permute-done.3.odd_in.odd_first = f32[456,128]{1,0:T(8,128)S(1)} collective-permute-done((f32[456,128]{1,0:T(8,128)S(1)}, f32[456,128]{1,0:T(8,128)S(1)}, u32[]{:S(2)}, u32[]{:S(2)}) %collective-permute-start.3) | collective-permute-done | bytes 233504 | tf_op jit(solution)/shard_map/ppermute | solution.py:745
  22.6 1.4 %shard_map.99 = (f32[1440,128]{1,0:T(8,128)S(1)}, f32[1920,128]{1,0:T(8,128)S(1)}, f32[48,128]{1,0:T(8,128)S(1)}, f32[360,128]{1,0:T(8,128)S(1)}, f32[16,128]{1,...) custom-call(s32[3]{0:T(128)S(1)} %pad_add_fusion.flags, bf16[256,640]{1,0:T(8,128)(2,1)S(1)} %get-tuple-element.28.before, ...), custom_call_target="tpu_custom_call" | custom-call | flops 1000000 | bytes 7749644 | tf_op jit(solution)/shard_map/pallas_call | solution.py:728
  24.1 0.1 collective-permute-start.4
  24.1 4.2 %collective-permute-start.5 = (f32[344,128]{1,0:T(8,128)S(1)}, f32[344,128]{1,0:T(8,128)S(1)}, u32[]{:S(2)}, u32[]{:S(2)}) collective-permute-start(f32[344,128]{1,0:T(8,128)S(1)} %get-tuple-element.51), channel_id=1, source_target_pairs={{1,2},{2,1},{5,6},{6,5},{9,10},{10,9},{13,14},{14,13},{17,18},{18,... | collective-permute-start | bytes 528392 | tf_op jit(solution)/shard_map/ppermute | solution.py:745
  28.4 1.1 %shard_map.100 = (f32[960,128]{1,0:T(8,128)S(1)}, f32[1920,128]{1,0:T(8,128)S(1)}) custom-call(s32[3]{0:T(128)S(1)} %pad_add_fusion.flags, bf16[256,640]{1,0:T(8,128)(2,1)S(1)} %get-tuple-element.28.before, bf16[256,640]{1,0:T(8,128)(2,1)S(1)} %get-tuple-element.29.after, f32[3072,128]{1,0:T(8,128)S(1)} %bitcast.7, ...), custom_call_target="tpu_custom_call" | custom-call | flops 4000000 | bytes 6963212 | tf_op jit(solution)/shard_map/pallas_call | solution.py:728
  29.5 1.7 %collective-permute-done.4.even_in = f32[344,128]{1,0:T(8,128)S(1)} collective-permute-done((f32[344,128]{1,0:T(8,128)S(1)}, f32[344,128]{1,0:T(8,128)S(1)}, u32[]{:S(2)}, u32[]{:S(2)}) %collective-permute-start.4) | collective-permute-done | bytes 176160 | tf_op jit(solution)/shard_map/ppermute | solution.py:745
  31.2 2.2 %collective-permute-done.5.odd_in = f32[344,128]{1,0:T(8,128)S(1)} collective-permute-done((f32[344,128]{1,0:T(8,128)S(1)}, f32[344,128]{1,0:T(8,128)S(1)}, u32[]{:S(2)}, u32[]{:S(2)}) %collective-permute-start.5) | collective-permute-done | bytes 176160 | tf_op jit(solution)/shard_map/ppermute | solution.py:745
  33.4 2.9 %shard_map.101 = (f32[9,32,8,128]{3,2,1,0:T(8,128)}, f32[24,128]{1,0:T(8,128)}) custom-call(s32[3]{0:T(128)S(1)} %pad_add_fusion.flags, bf16[256,640]{1,0:T(8,128)(2,1)S(1)} %get-tuple-element.28.before, bf16[256,640]{1,0:T(8,128)(2,1)S(1)} %get-tuple-element.29.after, f32[3072,128]{1,0:T(8,128)S(1)} %bitcast.8, f32[768,128]{1,0:T(8,128)S(1)} %get-tuple-element.35.windows, ...), custom_call_target="tpu_custom_call" | custom-call | flops 1000000 | bytes 6832140 | tf_op jit(solution)/shard_map/pallas_call | solution.py:728
Async XLA Ops:
  4.9 4.4 %collective-permute-start = (f32[208,128]{1,0:T(8,128)S(1)}, f32[208,128]{1,0:T(8,128)S(1)}, u32[]{:S(2)}, u32[]{:S(2)}) collective-permute-start(f32[208,128]{1,0:T(8,128)S(1)} %get-tuple-element.33), channel_id=1, source_target_pairs={{0,4},{8,12},{16,20},{24,28},{4,0},{12,8},{20,16},{28,24},{1,5},{9... | collective-permute-start | bytes 319496 | tf_op jit(solution)/shard_map/ppermute | solution.py:745
  4.9 6.0 %collective-permute-start.1 = (f32[208,128]{1,0:T(8,128)S(1)}, f32[208,128]{1,0:T(8,128)S(1)}, u32[]{:S(2)}, u32[]{:S(2)}) collective-permute-start(f32[208,128]{1,0:T(8,128)S(1)} %get-tuple-element.34), channel_id=1, source_target_pairs={{4,8},{12,16},{20,24},{8,4},{16,12},{24,20},{5,9},{13,17},{21,25},... | collective-permute-start | bytes 319496 | tf_op jit(solution)/shard_map/ppermute | solution.py:745
  11.9 7.7 %collective-permute-start.2 = (f32[456,128]{1,0:T(8,128)S(1)}, f32[456,128]{1,0:T(8,128)S(1)}, u32[]{:S(2)}, u32[]{:S(2)}) collective-permute-start(f32[456,128]{1,0:T(8,128)S(1)} %get-tuple-element.41), channel_id=1, source_target_pairs={{0,1},{2,3},{1,0},{3,2},{4,5},{6,7},{5,4},{7,6},{8,9},{10,11},{9,8... | collective-permute-start | bytes 700424 | tf_op jit(solution)/shard_map/ppermute | solution.py:745
  12.4 10.2 %collective-permute-start.3 = (f32[456,128]{1,0:T(8,128)S(1)}, f32[456,128]{1,0:T(8,128)S(1)}, u32[]{:S(2)}, u32[]{:S(2)}) collective-permute-start(f32[456,128]{1,0:T(8,128)S(1)} %get-tuple-element.42), channel_id=1, source_target_pairs={{1,2},{2,1},{5,6},{6,5},{9,10},{10,9},{13,14},{14,13},{17,18},{18,... | collective-permute-start | bytes 700424 | tf_op jit(solution)/shard_map/ppermute | solution.py:745
  24.1 7.2 %collective-permute-start.4 = (f32[344,128]{1,0:T(8,128)S(1)}, f32[344,128]{1,0:T(8,128)S(1)}, u32[]{:S(2)}, u32[]{:S(2)}) collective-permute-start(f32[344,128]{1,0:T(8,128)S(1)} %get-tuple-element.50), channel_id=1, source_target_pairs={{0,1},{2,3},{1,0},{3,2},{4,5},{6,7},{5,4},{7,6},{8,9},{10,11},{9,8... | collective-permute-start | bytes 528392 | tf_op jit(solution)/shard_map/ppermute | solution.py:745
  24.1 9.3 %collective-permute-start.5 = (f32[344,128]{1,0:T(8,128)S(1)}, f32[344,128]{1,0:T(8,128)S(1)}, u32[]{:S(2)}, u32[]{:S(2)}) collective-permute-start(f32[344,128]{1,0:T(8,128)S(1)} %get-tuple-element.51), channel_id=1, source_target_pairs={{1,2},{2,1},{5,6},{6,5},{9,10},{10,9},{13,14},{14,13},{17,18},{18,... | collective-permute-start | bytes 528392 | tf_op jit(solution)/shard_map/ppermute | solution.py:745

commit v7 on v6

--- a/solution.py
+++ b/solution.py
@@ -233,32 +233,45 @@
 
 
 def edges_kernel(flags, *refs):
-    hbm, (before, after, flat, own, own_flat, even_way, odd_way), refs = refs[:8], refs[8:15], refs[15:]
-    fields, picked, ocean, deep, floor, wet, sem = refs
-    sources = [hbm[0].at[f] for f in range(9)] + [hbm[1], hbm[2], hbm[3]]
-    copies = [pltpu.make_async_copy(x, fields.at[f], sem.at[f]) for f, x in enumerate(sources)]
-    copies += [
-        pltpu.make_async_copy(hbm[4 + k], x, sem.at[FIELDS + k]) for k, x in enumerate((ocean, deep, floor, wet))
-    ]
-    for copy in copies:
-        copy.start()
+    hbm, refs = refs[:8], refs[8:]
+    (before, after, main, flat, own, own_flat, even_way, odd_way, early_even, early_odd), refs = refs[:10], refs[10:]
+    fields, picked, low, high, ocean, deep, floor, wet, sem = refs
+    sent = []
+
+    def copy(source, target):
+        sent.append(pltpu.make_async_copy(source, target, sem.at[len(sent)]))
+        sent[-1].start()
+        return sent[-1]
+
+    whole = [copy(x, fields.at[f]) for f, x in enumerate([hbm[0].at[f] for f in range(9)] + list(hbm[1:4]))]
+    rest = [copy(hbm[4 + k], x) for k, x in enumerate((ocean, deep, floor, wet))]
+    for rows, out in ((BUOY_LOW, low), (BUOY_HIGH, high)):
+        for k, (f, y) in enumerate(rows):
+            rest.append(copy(hbm[f - SHEAR + 2].at[:, y, :], out.at[k * TILES * SUB : (k + 1) * TILES * SUB, :]))
+    turned = []
+    for y in range(ROWS):
+        turned.append(copy(hbm[0].at[:, :, y, :], main.at[:LAME, y]))
+        turned += [copy(hbm[1 + k].at[:, y, :], main.at[LAME + k, y]) for k in range(3)]
     difference_matrix(before, (27.0, -27.0, -1.0, 1.0), (0, 1, -1, 2))
     difference_matrix(after, (27.0, -27.0, -1.0, 1.0), (-1, 0, -2, 1))
     pickers = [picker(t) for t in range(TILES)]
     grid = Grid()
-    for f in range(FIELDS):
-        copies[f].wait()
+    for one in whole:
+        one.wait()
+    size = SUB * ROWS
+    for half in range(2):
+        mine = range(half * FIELDS // 2, (half + 1) * FIELDS // 2)
         total = None
         for t in range(TILES):
-            x = fields[f, t * SUB : (t + 1) * SUB].reshape(SUB * ROWS, LANES)
-            part = jnp.dot(split(x, 2), pickers[t], preferred_element_type=jnp.float32)
+            x = [fields[f, t * SUB : (t + 1) * SUB].reshape(size, LANES) for f in mine]
+            part = jnp.dot(split(jnp.concatenate(x, axis=0), 2), pickers[t], preferred_element_type=jnp.float32)
             total = part if total is None else total + part
-        size = SUB * ROWS
-        picked[f * size : (f + 1) * size, :] = total
-        for y in range(ROWS):
-            store(own, f * ROWS + y, picked[pl.ds(f * size + y, SUB, stride=ROWS), :])
-    for copy in copies[FIELDS:]:
-        copy.wait()
+        picked[mine[0] * size : (mine[-1] + 1) * size, :] = total
+        for f in mine:
+            for y in range(ROWS):
+                store(own, f * ROWS + y, picked[pl.ds(f * size + y, SUB, stride=ROWS), :])
+    for one in rest:
+        one.wait()
     planes = [ocean[k] for k in range(3)] + [deep[...]]
     planes += [floor[...].astype(jnp.float32), wet[...].astype(jnp.float32)]
     for k, x in enumerate(planes):
@@ -278,18 +291,13 @@
         pack(grid, edge_groups(own, own_flat), False, odd_way)
         pack(grid, edge_groups(own, own_flat), True, even_way)
 
-
-def turn_kernel(flat, *refs):
-    hbm, main, sem = refs[:4], refs[4], refs[5]
-    copies = []
-    for y in range(ROWS):
-        for source, target in [(hbm[0].at[:, :, y, :], main.at[:LAME, y])] + [
-            (hbm[1 + k].at[:, y, :], main.at[LAME + k, y]) for k in range(3)
-        ]:
-            copies.append(pltpu.make_async_copy(source, target, sem.at[len(copies)]))
-            copies[-1].start()
-    for copy in copies:
-        copy.wait()
+    odd = (flags[1] & 1) == 1
+    for index in range(2 * TILES):
+        a, b = tile(low, index), tile(high, index)
+        store(early_even, index, jnp.where(odd, a, b))
+        store(early_odd, index, jnp.where(odd, b, a))
+    for one in turned:
+        one.wait()
 
 
 def speeds(grid, stress, speed, buoy, todo, put):
@@ -315,12 +323,12 @@
                 put(c, y, t, speed(c)(y, t) + rate * a)
 
 
-def stresses(grid, rows, tiles, speed, stress, lame, shear, put):
+def stresses(grid, rows, tiles, speed, stress, lame, shear, put, done=lambda t: None):
     vx, vy, vz = [speed(c) for c in (VX, VY, VZ)]
     back = grid.along_rows(grid.before, [(vx, y) for y in rows])
     forth = grid.along_rows(grid.after, [(v, y) for v in (vy, vz) for y in rows])
-    for i, y in enumerate(rows):
-        for t in range(tiles):
+    for t in range(tiles):
+        for i, y in enumerate(rows):
             strain_x = back[i][t]
             strain_y = grid.by(vy, y, t)
             strain_z = grid.bz(vz, y, t)
@@ -333,6 +341,7 @@
             put(SXY, y, t, stress(SXY)(y, t) + mu * (grid.fy(vx, y, t) + forth[i][t]))
             put(SXZ, y, t, stress(SXZ)(y, t) + mu * (grid.fz(vx, y, t) + forth[len(rows) + i][t]))
             put(SYZ, y, t, stress(SYZ)(y, t) + mu * (grid.fz(vy, y, t) + grid.fy(vz, y, t)))
+        done(t)
 
 
 def flat_edge(grid, at, k):
@@ -360,9 +369,11 @@
 
 
 ALL, INSIDE = range(SPAN), range(TILES)
+SIDES = (WINDOW,)
+EARLY = [{which: i for i, which in enumerate(cells(rows, INSIDE))} for rows in (BUOY_HIGH, BUOY_LOW)]
 FIRST = [
-    Message(cells(rows, ALL))
-    for rows in (SPEED_HIGH + STRESS_HIGH + BUOY_HIGH, SPEED_LOW + STRESS_LOW + BUOY_LOW)
+    Message(cells(rows, ALL) + cells(buoy, SIDES))
+    for rows, buoy in ((SPEED_HIGH + STRESS_HIGH, BUOY_HIGH), (SPEED_LOW + STRESS_LOW, BUOY_LOW))
 ]
 LATER = [
     Message(cells(speed, INSIDE) + cells(rest, ALL))
@@ -416,6 +427,18 @@
 
 def received(kind, odd, even_in, odd_in):
     return Received(kind[0], odd, even_in, odd_in), Received(kind[1], odd, odd_in, even_in)
+
+
+def early(odd, even_in, odd_in, later):
+    def reader(at, if_odd, if_even, rest):
+        def read(f, y, t):
+            if (f, y, t) not in at:
+                return rest(f, y, t)
+            return jnp.where(odd, tile(if_odd, at[f, y, t]), tile(if_even, at[f, y, t]))
+
+        return read
+
+    return reader(EARLY[0], even_in, odd_in, later[0]), reader(EARLY[1], odd_in, even_in, later[1])
 
 
 AROUND = ROWS + 4
@@ -518,7 +541,7 @@
 
 
 def start_kernel(
-    flags, before, after, main, flat, own, own_flat, even_in, odd_in,
+    flags, before, after, main, flat, own, own_flat, even_in, odd_in, early_even, early_odd,
     windows, flat_windows, partial, level, even_way, odd_way,
 ):
     grid = Grid(flags[2], before, after)
@@ -585,7 +608,7 @@
 
 def middle_kernel(
     flags, before, after, main, windows, flat, flat_windows, partial, level, speed_in, stress_in,
-    even_in, odd_in,
+    early_even, early_odd, even_in, odd_in,
     speed_out, stress_out, ocean, partial_out, level_out, even_way, odd_way,
     sums, pressure,
 ):
@@ -594,7 +617,8 @@
     lo, hi = received(FIRST, odd, even_in, odd_in)
     field = fields_of(main, windows)
     finish(
-        grid, SPAN, lambda c, y, t: tile(partial, edge_index(c, y) + t), field, field(BUOY), lo, hi, lo, hi, speed_out
+        grid, SPAN, lambda c, y, t: tile(partial, edge_index(c, y) + t), field, field(BUOY), lo, hi, *early(odd, early_even, early_odd, (lo, hi)),
+        speed_out,
     )
     speed = speed_reader(speed_out, speed_in)
     flats = (flat, flat_windows)
@@ -651,14 +675,14 @@
 
 def last_kernel(
     flags, before, after, main, windows, flat, flat_windows, stress_in, ocean_in, partial, level, speed_in, inner_in,
-    even_first, odd_first, even_in, odd_in,
+    early_even, early_odd, even_in, odd_in,
     wave_hbm, ocean_out,
     sums, pressure, around, wave, sem,
 ):
     grid = Grid(flags[2], before, after)
     odd = (flags[1] & 1) == 1
     lo, hi = received(LATER, odd, even_in, odd_in)
-    lo_buoy, hi_buoy = received(FIRST, odd, even_first, odd_first)
+    lo_buoy, hi_buoy = early(odd, early_even, early_odd, (lo, hi))
     field = fields_of(main, windows)
     stress = block_reader(stress_in, SXX)
     finish(
@@ -704,13 +728,13 @@
         for y in INNER:
             for t in range(TILES):
                 put(f, y, t, tile(inner_in, block_index(f - SXX, y) + t))
-    stresses(grid, OUTER, TILES, speed, stress, field(LAME), field(SHEAR), put)
-    for f in range(SXX, SYZ + 1):
-        size = TILES * SUB
-        for z in range(0, size, size // 2):
-            at = ((f - SXX) * size + z) * ROWS
-            target = wave_hbm.at[f, z : z + size // 2].reshape(size // 2 * ROWS, LANES)
-            copy(wave.at[at : at + size // 2 * ROWS, :], target)
+    def done(t):
+        for f in range(SXX, SYZ + 1):
+            at = ((f - SXX) * TILES + t) * SUB * ROWS
+            target = wave_hbm.at[f, t * SUB : (t + 1) * SUB].reshape(SUB * ROWS, LANES)
+            copy(wave.at[at : at + SUB * ROWS, :], target)
+
+    stresses(grid, OUTER, TILES, speed, stress, field(LAME), field(SHEAR), put, done)
     for one in sent:
         one.wait()
 
@@ -753,42 +777,39 @@
     cells4 = jax.ShapeDtypeStruct((FIELDS, ROWS, TILES * SUB, LANES), jnp.float32)
 
     edge = FIELDS * ROWS // 4 + 2
-    before, after, flat, own, own_flat, even_way, odd_way = call(
-        edges_kernel, [matrix, matrix, 6, FIELDS * ROWS, 6, edge, edge],
-        [pltpu.VMEM((FIELDS, *arguments[1].shape), jnp.float32), planes(FIELDS * SUB)]
-        + [pltpu.VMEM(x.shape, x.dtype) for x in inputs[4:]] + [pltpu.SemaphoreType.DMA((FIELDS + 4,))],
+    before, after, main, flat, own, own_flat, even_way, odd_way, early_even, early_odd = call(
+        edges_kernel, [matrix, matrix, cells4, 6, FIELDS * ROWS, 6, edge, edge, 2 * TILES, 2 * TILES],
+        [pltpu.VMEM((FIELDS, *arguments[1].shape), jnp.float32), planes(FIELDS * SUB), planes(2 * TILES), planes(2 * TILES)]
+        + [pltpu.VMEM(x.shape, x.dtype) for x in inputs[4:]] + [pltpu.SemaphoreType.DMA((FIELDS + 8 + 4 * ROWS,))],
         *inputs, flags=flags, place=IN_HBM,
     )
-    even_in, odd_in = swap(even_way, "gx", 0), swap(odd_way, "gx", 1)
-    (main,) = call(
-        turn_kernel, [cells4], [pltpu.SemaphoreType.DMA((4 * ROWS,))], flat, *inputs[:4],
-        place=[IN_VMEM] + [IN_HBM] * 4, work=4,
-    )
+    x_in = swap(even_way, "gx", 0), swap(odd_way, "gx", 1)
+    early_in = swap(early_even, "gy", 0), swap(early_odd, "gy", 1)
     main = main.reshape(-1, LANES)
     first, later = [message_tiles(kind) for kind in (FIRST, LATER)]
     edges, block = len(OPEN) * SPAN, ROWS * SPAN
     windows, flat_windows, partial, level, even_way, odd_way = call(
         start_kernel, [FIELDS * ROWS, 6, edges, 2, first, first], [],
-        before, after, main, flat, own, own_flat, even_in, odd_in, flags=flags,
-    )
-    y_first = swap(even_way, "gy", 0), swap(odd_way, "gy", 1)
+        before, after, main, flat, own, own_flat, *x_in, *early_in, flags=flags,
+    )
+    y_in = swap(even_way, "gy", 0), swap(odd_way, "gy", 1)
     speed, inner = call(start_rest_kernel, [3 * block, 6 * block], [], before, after, main, windows, flags=flags, work=4)
     around, stress, ocean, partial, level, even_way, odd_way = call(
         middle_kernel, [3 * AROUND * SPAN, 6 * block, 6, edges, 2, later, later], [planes(4), planes(2)],
-        before, after, main, windows, flat, flat_windows, partial, level, speed, inner, *y_first, flags=flags,
+        before, after, main, windows, flat, flat_windows, partial, level, speed, inner, *early_in, *y_in, flags=flags,
     )
     y_in = swap(even_way, "gy", 0), swap(odd_way, "gy", 1)
     speed, inner = call(
         middle_rest_kernel, [3 * block, 6 * block], [], before, after, main, windows, around, speed, stress, flags=flags, work=4
     )
-    copies = len(CLOSED) + len(OPEN) + 2 * 6
+    copies = len(CLOSED) + len(OPEN) + 6 * TILES
     wave_out, ocean_out = call(
         last_kernel, [jax.ShapeDtypeStruct(arguments[0].shape, jnp.float32), 3],
         [
             planes(4), planes(2), planes(3 * AROUND * SPAN), planes(6 * ROWS * TILES),
             pltpu.SemaphoreType.DMA((copies,)),
         ],
-        before, after, main, windows, flat, flat_windows, stress, ocean, partial, level, speed, inner, *y_first, *y_in,
+        before, after, main, windows, flat, flat_windows, stress, ocean, partial, level, speed, inner, *early_in, *y_in,
         flags=flags, out_places=[IN_HBM, IN_VMEM],
     )
     return wave_out, ocean_out.reshape(ocean_state.shape)

time: 36.7 us -> 36.2 us (0.986)
  starting transfers between devices: 12 us -> 15 us
  Pallas kernels: 13.4 us -> 10.9 us
  waiting for transfers between devices: 10.1 us -> 9.32 us
    ppermute x6 -> x8, starting transfers between devices: 12 us -> 15 us  [swap(): return lax.ppermute(x, axis, pairs + [(j, i) for i, j in pairs])]
    pallas_call x7 -> x6, Pallas kernels: 13.4 us -> 10.9 us  [call(): pl.pallas_call(kernel, out_shape=[n if hasattr(n, 'dtype') else jax.Shape...]
    ppermute x6 -> x8, waiting for transfers between devices: 10.1 us -> 9.32 us  [swap(): return lax.ppermute(x, axis, pairs + [(j, i) for i, j in pairs])]
  transfers between devices with their start and end apart: 6 -> 8, of which waited for: 5 -> 5; matrix products, arithmetic and copies ran while one was open for 0% -> 0% of each run, Pallas kernels for 11% -> 6%
where the time goes in v7:
time: 36.2 us; the launch traced here: 36 us
  starting transfers between devices  15 us (41%)
  Pallas kernels  10.9 us (30%)
  waiting for transfers between devices  9.32 us (26%)
  between operations  0.73 us (2%)
    ppermute x8, starting transfers between devices, swap(): return lax.ppermute(x, axis, pairs + [(j, i) for i, j in pairs])  15 us
    pallas_call x6, Pallas kernels, call(): pl.pallas_call(kernel, out_shape=[n if hasattr(n, 'dtype') else jax.Shape...  10.9 us
    ppermute x8, waiting for transfers between devices, swap(): return lax.ppermute(x, axis, pairs + [(j, i) for i, j in pairs])  9.32 us
  transfers between devices with their start and end apart: 8, of which 5 were waited for; matrix products, arithmetic and copies ran while one was open for 0% of the time, Pallas kernels for 6%

profile of v7, /device:TPU:10, one launch (start us, length us, event | category | flops | bytes accessed | tf_op | source)
XLA Modules:
  0.0 36.0 jit_solution(16736804426510782472)
XLA Ops:
  0.6 0.1 pad_add_fusion.flags
  0.7 3.4 %shard_map.95 = (bf16[256,640]{1,0:T(8,128)(2,1)S(1)}, bf16[256,640]{1,0:T(8,128)(2,1)S(1)}, f32[12,8,32,128]{3,2,1,0:T(8,128)S(1)}, f32[48,128]{1,0:T(8,128)S(1...) custom-call(s32[3]{0:T(128)S(1)} %pad_add_fusion.flags, ...), custom_call_target="tpu_custom_call" | custom-call | flops 1000000 | bytes 2318348 | tf_op jit(solution)/shard_map/pallas_call | solution.py:752
  4.1 0.1 collective-permute-start
  4.2 2.5 %collective-permute-start.1 = (f32[208,128]{1,0:T(8,128)S(1)}, f32[208,128]{1,0:T(8,128)S(1)}, u32[]{:S(2)}, u32[]{:S(2)}) collective-permute-start(f32[208,128]{1,0:T(8,128)S(1)} %get-tuple-element.38), channel_id=1, source_target_pairs={{4,8},{12,16},{20,24},{8,4},{16,12},{24,20},{5,9},{13,17},{21,25},... | collective-permute-start | bytes 319496 | tf_op jit(solution)/shard_map/ppermute | solution.py:769
  6.7 0.1 collective-permute-start.2
  6.8 5.0 %collective-permute-start.3 = (f32[64,128]{1,0:T(8,128)S(1)}, f32[64,128]{1,0:T(8,128)S(1)}, u32[]{:S(2)}, u32[]{:S(2)}) collective-permute-start(f32[64,128]{1,0:T(8,128)S(1)} %get-tuple-element.40), channel_id=1, source_target_pairs={{1,2},{2,1},{5,6},{6,5},{9,10},{10,9},{13,14},{14,13},{17,18},{18,... | collective-permute-start | bytes 98312 | tf_op jit(solution)/shard_map/ppermute | solution.py:769
  11.9 0.0 collective-permute-done.2.early_even
  11.9 2.2 %collective-permute-done.3.early_odd = f32[64,128]{1,0:T(8,128)S(1)} collective-permute-done((f32[64,128]{1,0:T(8,128)S(1)}, f32[64,128]{1,0:T(8,128)S(1)}, u32[]{:S(2)}, u32[]{:S(2)}) %collective-permute-start.3) | collective-permute-done | bytes 32800 | tf_op jit(solution)/shard_map/ppermute | solution.py:769
  14.1 0.0 collective-permute-done.even_in
  14.1 0.0 collective-permute-done.1.odd_in
  14.1 0.9 %shard_map.96 = (f32[768,128]{1,0:T(8,128)S(1)}, f32[48,128]{1,0:T(8,128)S(1)}, f32[360,128]{1,0:T(8,128)S(1)}, f32[16,128]{1,0:T(8,128)S(1)}, f32[392,128]{1,0:T(8,128)S(1)}, /*index=5*/f32[392,128]{1,0:T(8,128)S(1)}) custom-call(s32[3]{0:T(128)S(1)} %pad_add_fusion.flags, bf16[256,640]{1,0:T(8,128)(2,1)S(1)} %get-tuple-element.31.before, ...), custom_call_target="tpu_custom_call" | custom-call | flops 1000000 | bytes 4616204 | tf_op jit(solution)/shard_map/pallas_call | solution.py:752
  15.0 0.1 collective-permute-start.4
  15.1 3.7 %collective-permute-start.5 = (f32[392,128]{1,0:T(8,128)S(1)}, f32[392,128]{1,0:T(8,128)S(1)}, u32[]{:S(2)}, u32[]{:S(2)}) collective-permute-start(f32[392,128]{1,0:T(8,128)S(1)} %get-tuple-element.48), channel_id=1, source_target_pairs={{1,2},{2,1},{5,6},{6,5},{9,10},{10,9},{13,14},{14,13},{17,18},{18,... | collective-permute-start | bytes 602120 | tf_op jit(solution)/shard_map/ppermute | solution.py:769
  18.8 1.1 %shard_map.97 = (f32[960,128]{1,0:T(8,128)S(1)}, f32[1920,128]{1,0:T(8,128)S(1)}) custom-call(s32[3]{0:T(128)S(1)} %pad_add_fusion.flags, bf16[256,640]{1,0:T(8,128)(2,1)S(1)} %get-tuple-element.31.before, bf16[256,640]{1,0:T(8,128)(2,1)S(1)} %get-tuple-element.32.after, f32[3072,128]{1,0:T(8,128)S(1)} %bitcast.5, f32[768,128]{1,0:T(8,128)S(1)} %get-tuple-element.41.windows), custom_call_target="tpu_custom_call" | custom-call | flops 4000000 | bytes 4751372 | tf_op jit(solution)/shard_map/pallas_call | solution.py:752
  19.9 2.2 %collective-permute-done.4.even_in = f32[392,128]{1,0:T(8,128)S(1)} collective-permute-done((f32[392,128]{1,0:T(8,128)S(1)}, f32[392,128]{1,0:T(8,128)S(1)}, u32[]{:S(2)}, u32[]{:S(2)}) %collective-permute-start.4) | collective-permute-done | bytes 200736 | tf_op jit(solution)/shard_map/ppermute | solution.py:769
  22.1 1.9 %collective-permute-done.5.odd_in = f32[392,128]{1,0:T(8,128)S(1)} collective-permute-done((f32[392,128]{1,0:T(8,128)S(1)}, f32[392,128]{1,0:T(8,128)S(1)}, u32[]{:S(2)}, u32[]{:S(2)}) %collective-permute-start.5) | collective-permute-done | bytes 200736 | tf_op jit(solution)/shard_map/ppermute | solution.py:769
  24.0 1.4 %shard_map.98 = (f32[1440,128]{1,0:T(8,128)S(1)}, f32[1920,128]{1,0:T(8,128)S(1)}, f32[48,128]{1,0:T(8,128)S(1)}, f32[360,128]{1,0:T(8,128)S(1)}, f32[16,128]{1,...) custom-call(s32[3]{0:T(128)S(1)} %pad_add_fusion.flags, bf16[256,640]{1,0:T(8,128)(2,1)S(1)} %get-tuple-element.31.before, ...), custom_call_target="tpu_custom_call" | custom-call | flops 1000000 | bytes 7749644 | tf_op jit(solution)/shard_map/pallas_call | solution.py:752
  25.4 0.1 collective-permute-start.6
  25.5 3.4 %collective-permute-start.7 = (f32[344,128]{1,0:T(8,128)S(1)}, f32[344,128]{1,0:T(8,128)S(1)}, u32[]{:S(2)}, u32[]{:S(2)}) collective-permute-start(f32[344,128]{1,0:T(8,128)S(1)} %get-tuple-element.57), channel_id=1, source_target_pairs={{1,2},{2,1},{5,6},{6,5},{9,10},{10,9},{13,14},{14,13},{17,18},{18,... | collective-permute-start | bytes 528392 | tf_op jit(solution)/shard_map/ppermute | solution.py:769
  28.9 1.1 %shard_map.99 = (f32[960,128]{1,0:T(8,128)S(1)}, f32[1920,128]{1,0:T(8,128)S(1)}) custom-call(s32[3]{0:T(128)S(1)} %pad_add_fusion.flags, bf16[256,640]{1,0:T(8,128)(2,1)S(1)} %get-tuple-element.31.before, bf16[256,640]{1,0:T(8,128)(2,1)S(1)} %get-tuple-element.32.after, f32[3072,128]{1,0:T(8,128)S(1)} %bitcast.7, f32[768,128]{1,0:T(8,128)S(1)} %get-tuple-element.41.windows, ...), custom_call_target="tpu_custom_call" | custom-call | flops 4000000 | bytes 6963212 | tf_op jit(solution)/shard_map/pallas_call | solution.py:752
  30.0 1.1 %collective-permute-done.6.even_in = f32[344,128]{1,0:T(8,128)S(1)} collective-permute-done((f32[344,128]{1,0:T(8,128)S(1)}, f32[344,128]{1,0:T(8,128)S(1)}, u32[]{:S(2)}, u32[]{:S(2)}) %collective-permute-start.6) | collective-permute-done | bytes 176160 | tf_op jit(solution)/shard_map/ppermute | solution.py:769
  31.2 1.9 %collective-permute-done.7.odd_in = f32[344,128]{1,0:T(8,128)S(1)} collective-permute-done((f32[344,128]{1,0:T(8,128)S(1)}, f32[344,128]{1,0:T(8,128)S(1)}, u32[]{:S(2)}, u32[]{:S(2)}) %collective-permute-start.7) | collective-permute-done | bytes 176160 | tf_op jit(solution)/shard_map/ppermute | solution.py:769
  33.1 3.0 %shard_map.100 = (f32[9,32,8,128]{3,2,1,0:T(8,128)}, f32[24,128]{1,0:T(8,128)}) custom-call(s32[3]{0:T(128)S(1)} %pad_add_fusion.flags, bf16[256,640]{1,0:T(8,128)(2,1)S(1)} %get-tuple-element.31.before, bf16[256,640]{1,0:T(8,128)(2,1)S(1)} %get-tuple-element.32.after, f32[3072,128]{1,0:T(8,128)S(1)} %bitcast.8, f32[768,128]{1,0:T(8,128)S(1)} %get-tuple-element.41.windows, ...), custom_call_target="tpu_custom_call" | custom-call | flops 1000000 | bytes 6430732 | tf_op jit(solution)/shard_map/pallas_call | solution.py:752
Async XLA Ops:
  4.1 10.0 %collective-permute-start = (f32[208,128]{1,0:T(8,128)S(1)}, f32[208,128]{1,0:T(8,128)S(1)}, u32[]{:S(2)}, u32[]{:S(2)}) collective-permute-start(f32[208,128]{1,0:T(8,128)S(1)} %get-tuple-element.37), channel_id=1, source_target_pairs={{0,4},{8,12},{16,20},{24,28},{4,0},{12,8},{20,16},{28,24},{1,5},{9... | collective-permute-start | bytes 319496 | tf_op jit(solution)/shard_map/ppermute | solution.py:769
  4.2 9.9 %collective-permute-start.1 = (f32[208,128]{1,0:T(8,128)S(1)}, f32[208,128]{1,0:T(8,128)S(1)}, u32[]{:S(2)}, u32[]{:S(2)}) collective-permute-start(f32[208,128]{1,0:T(8,128)S(1)} %get-tuple-element.38), channel_id=1, source_target_pairs={{4,8},{12,16},{20,24},{8,4},{16,12},{24,20},{5,9},{13,17},{21,25},... | collective-permute-start | bytes 319496 | tf_op jit(solution)/shard_map/ppermute | solution.py:769
  6.7 5.1 %collective-permute-start.2 = (f32[64,128]{1,0:T(8,128)S(1)}, f32[64,128]{1,0:T(8,128)S(1)}, u32[]{:S(2)}, u32[]{:S(2)}) collective-permute-start(f32[64,128]{1,0:T(8,128)S(1)} %get-tuple-element.39), channel_id=1, source_target_pairs={{0,1},{2,3},{1,0},{3,2},{4,5},{6,7},{5,4},{7,6},{8,9},{10,11},{9,8... | collective-permute-start | bytes 98312 | tf_op jit(solution)/shard_map/ppermute | solution.py:769
  6.8 7.3 %collective-permute-start.3 = (f32[64,128]{1,0:T(8,128)S(1)}, f32[64,128]{1,0:T(8,128)S(1)}, u32[]{:S(2)}, u32[]{:S(2)}) collective-permute-start(f32[64,128]{1,0:T(8,128)S(1)} %get-tuple-element.40), channel_id=1, source_target_pairs={{1,2},{2,1},{5,6},{6,5},{9,10},{10,9},{13,14},{14,13},{17,18},{18,... | collective-permute-start | bytes 98312 | tf_op jit(solution)/shard_map/ppermute | solution.py:769
  15.0 7.1 %collective-permute-start.4 = (f32[392,128]{1,0:T(8,128)S(1)}, f32[392,128]{1,0:T(8,128)S(1)}, u32[]{:S(2)}, u32[]{:S(2)}) collective-permute-start(f32[392,128]{1,0:T(8,128)S(1)} %get-tuple-element.47), channel_id=1, source_target_pairs={{0,1},{2,3},{1,0},{3,2},{4,5},{6,7},{5,4},{7,6},{8,9},{10,11},{9,8... | collective-permute-start | bytes 602120 | tf_op jit(solution)/shard_map/ppermute | solution.py:769
  15.1 8.9 %collective-permute-start.5 = (f32[392,128]{1,0:T(8,128)S(1)}, f32[392,128]{1,0:T(8,128)S(1)}, u32[]{:S(2)}, u32[]{:S(2)}) collective-permute-start(f32[392,128]{1,0:T(8,128)S(1)} %get-tuple-element.48), channel_id=1, source_target_pairs={{1,2},{2,1},{5,6},{6,5},{9,10},{10,9},{13,14},{14,13},{17,18},{18,... | collective-permute-start | bytes 602120 | tf_op jit(solution)/shard_map/ppermute | solution.py:769
  25.4 5.7 %collective-permute-start.6 = (f32[344,128]{1,0:T(8,128)S(1)}, f32[344,128]{1,0:T(8,128)S(1)}, u32[]{:S(2)}, u32[]{:S(2)}) collective-permute-start(f32[344,128]{1,0:T(8,128)S(1)} %get-tuple-element.56), channel_id=1, source_target_pairs={{0,1},{2,3},{1,0},{3,2},{4,5},{6,7},{5,4},{7,6},{8,9},{10,11},{9,8... | collective-permute-start | bytes 528392 | tf_op jit(solution)/shard_map/ppermute | solution.py:769
  25.5 7.5 %collective-permute-start.7 = (f32[344,128]{1,0:T(8,128)S(1)}, f32[344,128]{1,0:T(8,128)S(1)}, u32[]{:S(2)}, u32[]{:S(2)}) collective-permute-start(f32[344,128]{1,0:T(8,128)S(1)} %get-tuple-element.57), channel_id=1, source_target_pairs={{1,2},{2,1},{5,6},{6,5},{9,10},{10,9},{13,14},{14,13},{17,18},{18,... | collective-permute-start | bytes 528392 | tf_op jit(solution)/shard_map/ppermute | solution.py:769

commit v8 on v7

--- a/solution.py
+++ b/solution.py
@@ -235,7 +235,7 @@
 def edges_kernel(flags, *refs):
     hbm, refs = refs[:8], refs[8:]
     (before, after, main, flat, own, own_flat, even_way, odd_way, early_even, early_odd), refs = refs[:10], refs[10:]
-    fields, picked, low, high, ocean, deep, floor, wet, sem = refs
+    ocean, deep, floor, wet, sem = refs
     sent = []
 
     def copy(source, target):
@@ -243,33 +243,29 @@
         sent[-1].start()
         return sent[-1]
 
-    whole = [copy(x, fields.at[f]) for f, x in enumerate([hbm[0].at[f] for f in range(9)] + list(hbm[1:4]))]
+    ready = [[], []]
+    cut = FIELDS // 2
+    for y in range(ROWS):
+        ready[0].append(copy(hbm[0].at[:cut, :, y, :], main.at[:cut, y]))
+    for y in range(ROWS):
+        ready[1].append(copy(hbm[0].at[cut:, :, y, :], main.at[cut:LAME, y]))
+        ready[1] += [copy(hbm[1 + k].at[:, y, :], main.at[LAME + k, y]) for k in range(3)]
     rest = [copy(hbm[4 + k], x) for k, x in enumerate((ocean, deep, floor, wet))]
-    for rows, out in ((BUOY_LOW, low), (BUOY_HIGH, high)):
-        for k, (f, y) in enumerate(rows):
-            rest.append(copy(hbm[f - SHEAR + 2].at[:, y, :], out.at[k * TILES * SUB : (k + 1) * TILES * SUB, :]))
-    turned = []
-    for y in range(ROWS):
-        turned.append(copy(hbm[0].at[:, :, y, :], main.at[:LAME, y]))
-        turned += [copy(hbm[1 + k].at[:, y, :], main.at[LAME + k, y]) for k in range(3)]
     difference_matrix(before, (27.0, -27.0, -1.0, 1.0), (0, 1, -1, 2))
     difference_matrix(after, (27.0, -27.0, -1.0, 1.0), (-1, 0, -2, 1))
     pickers = [picker(t) for t in range(TILES)]
     grid = Grid()
-    for one in whole:
-        one.wait()
     size = SUB * ROWS
     for half in range(2):
-        mine = range(half * FIELDS // 2, (half + 1) * FIELDS // 2)
+        for one in ready[half]:
+            one.wait()
+        mine = range(half * cut, (half + 1) * cut)
         total = None
         for t in range(TILES):
-            x = [fields[f, t * SUB : (t + 1) * SUB].reshape(size, LANES) for f in mine]
+            x = [main[f, y, t * SUB : (t + 1) * SUB, :] for f in mine for y in range(ROWS)]
             part = jnp.dot(split(jnp.concatenate(x, axis=0), 2), pickers[t], preferred_element_type=jnp.float32)
             total = part if total is None else total + part
-        picked[mine[0] * size : (mine[-1] + 1) * size, :] = total
-        for f in mine:
-            for y in range(ROWS):
-                store(own, f * ROWS + y, picked[pl.ds(f * size + y, SUB, stride=ROWS), :])
+        own[mine[0] * size : (mine[-1] + 1) * size, :] = total
     for one in rest:
         one.wait()
     planes = [ocean[k] for k in range(3)] + [deep[...]]
@@ -292,12 +288,11 @@
         pack(grid, edge_groups(own, own_flat), True, even_way)
 
     odd = (flags[1] & 1) == 1
-    for index in range(2 * TILES):
-        a, b = tile(low, index), tile(high, index)
-        store(early_even, index, jnp.where(odd, a, b))
-        store(early_odd, index, jnp.where(odd, b, a))
-    for one in turned:
-        one.wait()
+    for k, ((_, below), (_, above)) in enumerate(zip(BUOY_LOW, BUOY_HIGH)):
+        for t in range(TILES):
+            a, b = [main[BUOY, y, t * SUB : (t + 1) * SUB, :] for y in (below, above)]
+            store(early_even, k * TILES + t, jnp.where(odd, a, b))
+            store(early_odd, k * TILES + t, jnp.where(odd, b, a))
 
 
 def speeds(grid, stress, speed, buoy, todo, put):
@@ -323,12 +318,12 @@
                 put(c, y, t, speed(c)(y, t) + rate * a)
 
 
-def stresses(grid, rows, tiles, speed, stress, lame, shear, put, done=lambda t: None):
+def stresses(grid, rows, tiles, speed, stress, lame, shear, put, done=lambda y: None):
     vx, vy, vz = [speed(c) for c in (VX, VY, VZ)]
     back = grid.along_rows(grid.before, [(vx, y) for y in rows])
     forth = grid.along_rows(grid.after, [(v, y) for v in (vy, vz) for y in rows])
-    for t in range(tiles):
-        for i, y in enumerate(rows):
+    for i, y in enumerate(rows):
+        for t in range(tiles):
             strain_x = back[i][t]
             strain_y = grid.by(vy, y, t)
             strain_z = grid.bz(vz, y, t)
@@ -341,7 +336,7 @@
             put(SXY, y, t, stress(SXY)(y, t) + mu * (grid.fy(vx, y, t) + forth[i][t]))
             put(SXZ, y, t, stress(SXZ)(y, t) + mu * (grid.fz(vx, y, t) + forth[len(rows) + i][t]))
             put(SYZ, y, t, stress(SYZ)(y, t) + mu * (grid.fz(vy, y, t) + grid.fy(vz, y, t)))
-        done(t)
+        done(y)
 
 
 def flat_edge(grid, at, k):
@@ -658,7 +653,15 @@
     send(LATER, odd, rows_of, line_out, even_way, odd_way)
 
 
-def middle_rest_kernel(flags, before, after, main, windows, around, speed_in, stress_in, speed_out, stress_out):
+def copy_rows(ref, index, hbm, f, y, sem):
+    return pltpu.make_async_copy(ref.at[index * SUB : (index + TILES) * SUB, :], hbm.at[f, :, y, :], sem)
+
+
+BY_ROWS = (SXX, SYY)
+BY_FIELD = (SZZ, SXY, SXZ, SYZ)
+
+
+def middle_rest_kernel(flags, before, after, main, windows, around, speed_in, stress_in, speed_out, stress_out, wave_hbm, sem):
     grid = Grid(flags[2], before, after)
     field = fields_of(main, windows)
     stress = block_reader(stress_in, SXX)
@@ -666,18 +669,27 @@
         grid, [inside(stress(f)) for f in range(SXX, SYZ + 1)], speed_reader(around, speed_in), field(BUOY), CLOSED,
         lambda c, y, t, value: store(speed_out, block_index(c, y) + t, value),
     )
+    sent = [copy_rows(speed_out, block_index(c, y), wave_hbm, c, y, sem.at[i]) for i, (c, y) in enumerate(CLOSED)]
+    for one in sent:
+        one.start()
     stresses(
         grid, INNER, TILES, block_reader(speed_out, VX), stress,
         field(LAME), field(SHEAR),
         lambda f, y, t, value: store(stress_out, block_index(f - SXX, y) + t, value),
     )
+    for f in BY_ROWS:
+        for y in INNER:
+            sent.append(copy_rows(stress_out, block_index(f - SXX, y), wave_hbm, f, y, sem.at[len(sent)]))
+            sent[-1].start()
+    for one in sent:
+        one.wait()
 
 
 def last_kernel(
     flags, before, after, main, windows, flat, flat_windows, stress_in, ocean_in, partial, level, speed_in, inner_in,
-    early_even, early_odd, even_in, odd_in,
+    early_even, early_odd, even_in, odd_in, wave_in,
     wave_hbm, ocean_out,
-    sums, pressure, around, wave, sem,
+    sums, pressure, around, turned, wave, sem,
 ):
     grid = Grid(flags[2], before, after)
     odd = (flags[1] & 1) == 1
@@ -696,13 +708,9 @@
         sent.append(pltpu.make_async_copy(source, target, sem.at[len(sent)]))
         sent[-1].start()
 
-    def copy_row(ref, index, f, y):
-        copy(ref.at[index * SUB : (index + TILES) * SUB, :], wave_hbm.at[f, :, y, :])
-
-    for c, y in CLOSED:
-        copy_row(speed_in, block_index(c, y), c, y)
     for c, y in OPEN:
-        copy_row(around, (c * AROUND + y + 2) * SPAN, c, y)
+        sent.append(copy_rows(around, (c * AROUND + y + 2) * SPAN, wave_hbm, c, y, sem.at[len(sent)]))
+        sent[-1].start()
     flats = (flat, flat_windows)
     fixed = lambda f, k: tile(flats[k], f)
 
@@ -718,23 +726,25 @@
     )
     load = press(grid, levels, fixed, line, pressure)
 
+    size = TILES * SUB * ROWS
+
     def put(f, y, t, value):
-        size = TILES * SUB * ROWS
+        if f in BY_ROWS:
+            turned[f - SXX, y, t * SUB : (t + 1) * SUB, :] = value
+            return
         if f == SZZ:
             value = value - load(y, t)
-        wave[pl.ds((f - SXX) * size + t * SUB * ROWS + y, SUB, stride=ROWS), :] = value
-
-    for f in range(SXX, SYZ + 1):
+        wave[pl.ds(BY_FIELD.index(f) * size + t * SUB * ROWS + y, SUB, stride=ROWS), :] = value
+
+    def done(y):
+        copy(turned.at[:, y], wave_hbm.at[SXX : SYY + 1, :, y, :])
+
+    stresses(grid, OUTER, TILES, speed, stress, field(LAME), field(SHEAR), put, done)
+    for f in BY_FIELD:
         for y in INNER:
             for t in range(TILES):
                 put(f, y, t, tile(inner_in, block_index(f - SXX, y) + t))
-    def done(t):
-        for f in range(SXX, SYZ + 1):
-            at = ((f - SXX) * TILES + t) * SUB * ROWS
-            target = wave_hbm.at[f, t * SUB : (t + 1) * SUB].reshape(SUB * ROWS, LANES)
-            copy(wave.at[at : at + SUB * ROWS, :], target)
-
-    stresses(grid, OUTER, TILES, speed, stress, field(LAME), field(SHEAR), put, done)
+    copy(wave, wave_hbm.at[SZZ : SYZ + 1].reshape(len(BY_FIELD) * size, LANES))
     for one in sent:
         one.wait()
 
@@ -744,7 +754,7 @@
 IN_HBM = pl.BlockSpec(memory_space=pltpu.HBM)
 
 
-def call(kernel, tiles, scratch, *arguments, flags=None, place=IN_VMEM, out_places=None, work=1):
+def call(kernel, tiles, scratch, *arguments, flags=None, place=IN_VMEM, out_places=None, work=1, aliases={}):
     specs = place if isinstance(place, list) else [place] * len(arguments)
     if flags is not None:
         arguments, specs = (flags, *arguments), [IN_SMEM] + specs
@@ -755,6 +765,7 @@
         in_specs=specs,
         out_specs=out_places or [IN_VMEM] * len(tiles),
         scratch_shapes=scratch,
+        input_output_aliases=aliases,
         cost_estimate=pl.CostEstimate(flops=work * 1000000, bytes_accessed=4 * moved, transcendentals=0),
         compiler_params=pltpu.CompilerParams(vmem_limit_bytes=24 * 1024 * 1024),
     )(*arguments)
@@ -779,8 +790,7 @@
     edge = FIELDS * ROWS // 4 + 2
     before, after, main, flat, own, own_flat, even_way, odd_way, early_even, early_odd = call(
         edges_kernel, [matrix, matrix, cells4, 6, FIELDS * ROWS, 6, edge, edge, 2 * TILES, 2 * TILES],
-        [pltpu.VMEM((FIELDS, *arguments[1].shape), jnp.float32), planes(FIELDS * SUB), planes(2 * TILES), planes(2 * TILES)]
-        + [pltpu.VMEM(x.shape, x.dtype) for x in inputs[4:]] + [pltpu.SemaphoreType.DMA((FIELDS + 8 + 4 * ROWS,))],
+        [pltpu.VMEM(x.shape, x.dtype) for x in inputs[4:]] + [pltpu.SemaphoreType.DMA((4 + 5 * ROWS,))],
         *inputs, flags=flags, place=IN_HBM,
     )
     x_in = swap(even_way, "gx", 0), swap(odd_way, "gx", 1)
@@ -799,18 +809,24 @@
         before, after, main, windows, flat, flat_windows, partial, level, speed, inner, *early_in, *y_in, flags=flags,
     )
     y_in = swap(even_way, "gy", 0), swap(odd_way, "gy", 1)
-    speed, inner = call(
-        middle_rest_kernel, [3 * block, 6 * block], [], before, after, main, windows, around, speed, stress, flags=flags, work=4
-    )
-    copies = len(CLOSED) + len(OPEN) + 6 * TILES
+    wave = jax.ShapeDtypeStruct(arguments[0].shape, jnp.float32)
+    speed, inner, wave_part = call(
+        middle_rest_kernel, [3 * block, 6 * block, wave],
+        [pltpu.SemaphoreType.DMA((len(CLOSED) + len(BY_ROWS) * len(INNER),))],
+        before, after, main, windows, around, speed, stress, flags=flags, out_places=[IN_VMEM, IN_VMEM, IN_HBM], work=4,
+    )
+    operands = (
+        before, after, main, windows, flat, flat_windows, stress, ocean, partial, level, speed, inner, *early_in, *y_in, wave_part
+    )
     wave_out, ocean_out = call(
-        last_kernel, [jax.ShapeDtypeStruct(arguments[0].shape, jnp.float32), 3],
+        last_kernel, [wave, 3],
         [
-            planes(4), planes(2), planes(3 * AROUND * SPAN), planes(6 * ROWS * TILES),
-            pltpu.SemaphoreType.DMA((copies,)),
+            planes(4), planes(2), planes(3 * AROUND * SPAN),
+            pltpu.VMEM((len(BY_ROWS), *cells4.shape[1:]), jnp.float32), planes(len(BY_FIELD) * ROWS * TILES),
+            pltpu.SemaphoreType.DMA((len(OPEN) + len(OUTER) + 1,)),
         ],
-        before, after, main, windows, flat, flat_windows, stress, ocean, partial, level, speed, inner, *early_in, *y_in,
-        flags=flags, out_places=[IN_HBM, IN_VMEM],
+        *operands, flags=flags, place=[IN_VMEM] * (len(operands) - 1) + [IN_HBM], out_places=[IN_HBM, IN_VMEM],
+        aliases={len(operands): 0},
     )
     return wave_out, ocean_out.reshape(ocean_state.shape)
 

time: 36.2 us -> 36.3 us (level)
  Pallas kernels: 10.9 us -> 11.8 us
  waiting for transfers between devices: 9.32 us -> 8.51 us
    pallas_call x6, Pallas kernels: 10.9 us -> 11.8 us  [call(): pl.pallas_call(kernel, out_shape=[n if hasattr(n, 'dtype') else jax.Shape...]
    ppermute x8, waiting for transfers between devices: 9.32 us -> 8.51 us  [swap(): return lax.ppermute(x, axis, pairs + [(j, i) for i, j in pairs])]
  transfers between devices with their start and end apart: 8 -> 8, of which waited for: 5 -> 5; matrix products, arithmetic and copies ran while one was open for 0% -> 0% of each run, Pallas kernels for 6% -> 8%
where the time goes in v8:
time: 36.3 us; the launch traced here: 36.1 us
  starting transfers between devices  15 us (41%)
  Pallas kernels  11.8 us (33%)
  waiting for transfers between devices  8.51 us (23%)
  between operations  0.74 us (2%)
    ppermute x8, starting transfers between devices, swap(): return lax.ppermute(x, axis, pairs + [(j, i) for i, j in pairs])  15 us
    pallas_call x6, Pallas kernels, call(): pl.pallas_call(kernel, out_shape=[n if hasattr(n, 'dtype') else jax.Shape...  11.8 us
    ppermute x8, waiting for transfers between devices, swap(): return lax.ppermute(x, axis, pairs + [(j, i) for i, j in pairs])  8.51 us
  transfers between devices with their start and end apart: 8, of which 5 were waited for; matrix products, arithmetic and copies ran while one was open for 0% of the time, Pallas kernels for 8%

profile of v8, /device:TPU:10, one launch (start us, length us, event | category | flops | bytes accessed | tf_op | source)
XLA Modules:
  0.0 36.1 jit_solution(9811316277728805858)
XLA Ops:
  0.6 0.1 pad_add_fusion.flags
  0.7 3.6 %shard_map.95 = (bf16[256,640]{1,0:T(8,128)(2,1)S(1)}, bf16[256,640]{1,0:T(8,128)(2,1)S(1)}, f32[12,8,32,128]{3,2,1,0:T(8,128)S(1)}, f32[48,128]{1,0:T(8,128)S(1...) custom-call(s32[3]{0:T(128)S(1)} %pad_add_fusion.flags, ...), custom_call_target="tpu_custom_call" | custom-call | flops 1000000 | bytes 2318348 | tf_op jit(solution)/shard_map/pallas_call | solution.py:762
  4.3 0.1 collective-permute-start
  4.4 2.5 %collective-permute-start.1 = (f32[208,128]{1,0:T(8,128)S(1)}, f32[208,128]{1,0:T(8,128)S(1)}, u32[]{:S(2)}, u32[]{:S(2)}) collective-permute-start(f32[208,128]{1,0:T(8,128)S(1)} %get-tuple-element.39), channel_id=1, source_target_pairs={{4,8},{12,16},{20,24},{8,4},{16,12},{24,20},{5,9},{13,17},{21,25},... | collective-permute-start | bytes 319496 | tf_op jit(solution)/shard_map/ppermute | solution.py:780
  7.0 0.1 collective-permute-start.2
  7.0 5.0 %collective-permute-start.3 = (f32[64,128]{1,0:T(8,128)S(1)}, f32[64,128]{1,0:T(8,128)S(1)}, u32[]{:S(2)}, u32[]{:S(2)}) collective-permute-start(f32[64,128]{1,0:T(8,128)S(1)} %get-tuple-element.41), channel_id=1, source_target_pairs={{1,2},{2,1},{5,6},{6,5},{9,10},{10,9},{13,14},{14,13},{17,18},{18,... | collective-permute-start | bytes 98312 | tf_op jit(solution)/shard_map/ppermute | solution.py:780
  12.1 0.0 collective-permute-done.2.early_even
  12.1 2.2 %collective-permute-done.3.early_odd = f32[64,128]{1,0:T(8,128)S(1)} collective-permute-done((f32[64,128]{1,0:T(8,128)S(1)}, f32[64,128]{1,0:T(8,128)S(1)}, u32[]{:S(2)}, u32[]{:S(2)}) %collective-permute-start.3) | collective-permute-done | bytes 32800 | tf_op jit(solution)/shard_map/ppermute | solution.py:780
  14.3 0.0 collective-permute-done.even_in
  14.3 0.0 collective-permute-done.1.odd_in
  14.3 0.9 %shard_map.96 = (f32[768,128]{1,0:T(8,128)S(1)}, f32[48,128]{1,0:T(8,128)S(1)}, f32[360,128]{1,0:T(8,128)S(1)}, f32[16,128]{1,0:T(8,128)S(1)}, f32[392,128]{1,0:T(8,128)S(1)}, /*index=5*/f32[392,128]{1,0:T(8,128)S(1)}) custom-call(s32[3]{0:T(128)S(1)} %pad_add_fusion.flags, bf16[256,640]{1,0:T(8,128)(2,1)S(1)} %get-tuple-element.32.before, ...), custom_call_target="tpu_custom_call" | custom-call | flops 1000000 | bytes 4616204 | tf_op jit(solution)/shard_map/pallas_call | solution.py:762
  15.2 0.1 collective-permute-start.4
  15.3 3.7 %collective-permute-start.5 = (f32[392,128]{1,0:T(8,128)S(1)}, f32[392,128]{1,0:T(8,128)S(1)}, u32[]{:S(2)}, u32[]{:S(2)}) collective-permute-start(f32[392,128]{1,0:T(8,128)S(1)} %get-tuple-element.49), channel_id=1, source_target_pairs={{1,2},{2,1},{5,6},{6,5},{9,10},{10,9},{13,14},{14,13},{17,18},{18,... | collective-permute-start | bytes 602120 | tf_op jit(solution)/shard_map/ppermute | solution.py:780
  19.0 1.1 %shard_map.97 = (f32[960,128]{1,0:T(8,128)S(1)}, f32[1920,128]{1,0:T(8,128)S(1)}) custom-call(s32[3]{0:T(128)S(1)} %pad_add_fusion.flags, bf16[256,640]{1,0:T(8,128)(2,1)S(1)} %get-tuple-element.32.before, bf16[256,640]{1,0:T(8,128)(2,1)S(1)} %get-tuple-element.33.after, f32[3072,128]{1,0:T(8,128)S(1)} %bitcast.5, f32[768,128]{1,0:T(8,128)S(1)} %get-tuple-element.42.windows), custom_call_target="tpu_custom_call" | custom-call | flops 4000000 | bytes 4751372 | tf_op jit(solution)/shard_map/pallas_call | solution.py:762
  20.1 2.2 %collective-permute-done.4.even_in = f32[392,128]{1,0:T(8,128)S(1)} collective-permute-done((f32[392,128]{1,0:T(8,128)S(1)}, f32[392,128]{1,0:T(8,128)S(1)}, u32[]{:S(2)}, u32[]{:S(2)}) %collective-permute-start.4) | collective-permute-done | bytes 200736 | tf_op jit(solution)/shard_map/ppermute | solution.py:780
  22.3 1.9 %collective-permute-done.5.odd_in = f32[392,128]{1,0:T(8,128)S(1)} collective-permute-done((f32[392,128]{1,0:T(8,128)S(1)}, f32[392,128]{1,0:T(8,128)S(1)}, u32[]{:S(2)}, u32[]{:S(2)}) %collective-permute-start.5) | collective-permute-done | bytes 200736 | tf_op jit(solution)/shard_map/ppermute | solution.py:780
  24.2 1.4 %shard_map.98 = (f32[1440,128]{1,0:T(8,128)S(1)}, f32[1920,128]{1,0:T(8,128)S(1)}, f32[48,128]{1,0:T(8,128)S(1)}, f32[360,128]{1,0:T(8,128)S(1)}, f32[16,128]{1,...) custom-call(s32[3]{0:T(128)S(1)} %pad_add_fusion.flags, bf16[256,640]{1,0:T(8,128)(2,1)S(1)} %get-tuple-element.32.before, ...), custom_call_target="tpu_custom_call" | custom-call | flops 1000000 | bytes 7749644 | tf_op jit(solution)/shard_map/pallas_call | solution.py:762
  25.7 0.1 collective-permute-start.6
  25.7 3.4 %collective-permute-start.7 = (f32[344,128]{1,0:T(8,128)S(1)}, f32[344,128]{1,0:T(8,128)S(1)}, u32[]{:S(2)}, u32[]{:S(2)}) collective-permute-start(f32[344,128]{1,0:T(8,128)S(1)} %get-tuple-element.58), channel_id=1, source_target_pairs={{1,2},{2,1},{5,6},{6,5},{9,10},{10,9},{13,14},{14,13},{17,18},{18,... | collective-permute-start | bytes 528392 | tf_op jit(solution)/shard_map/ppermute | solution.py:780
  29.2 1.9 %shard_map.99 = (f32[960,128]{1,0:T(8,128)S(1)}, f32[1920,128]{1,0:T(8,128)S(1)}, f32[9,32,8,128]{3,2,1,0:T(8,128)}) custom-call(s32[3]{0:T(128)S(1)} %pad_add_fusion.flags, bf16[256,640]{1,0:T(8,128)(2,1)S(1)} %get-tuple-element.32.before, bf16[256,640]{1,0:T(8,128)(2,1)S(1)} %get-tuple-element.33.after, f32[3072,128]{1,0:T(8,128)S(1)} %bitcast.7, ...), custom_call_target="tpu_custom_call" | custom-call | flops 4000000 | bytes 6963212 | tf_op jit(solution)/shard_map/pallas_call | solution.py:762
  31.1 0.3 collective-permute-done.6.even_in
  31.4 1.9 %collective-permute-done.7.odd_in = f32[344,128]{1,0:T(8,128)S(1)} collective-permute-done((f32[344,128]{1,0:T(8,128)S(1)}, f32[344,128]{1,0:T(8,128)S(1)}, u32[]{:S(2)}, u32[]{:S(2)}) %collective-permute-start.7) | collective-permute-done | bytes 176160 | tf_op jit(solution)/shard_map/ppermute | solution.py:780
  33.3 2.8 %shard_map.100 = (f32[9,32,8,128]{3,2,1,0:T(8,128)}, f32[24,128]{1,0:T(8,128)}) custom-call(s32[3]{0:T(128)S(1)} %pad_add_fusion.flags, bf16[256,640]{1,0:T(8,128)(2,1)S(1)} %get-tuple-element.32.before, bf16[256,640]{1,0:T(8,128)(2,1)S(1)} %get-tuple-element.33.after, f32[3072,128]{1,0:T(8,128)S(1)} %bitcast.8, ...), custom_call_target="tpu_custom_call", output_to_operand_aliasing={{0}: (17, {})} | custom-call | flops 1000000 | bytes 7610380 | tf_op jit(solution)/shard_map/pallas_call | solution.py:762
Async XLA Ops:
  4.3 10.0 %collective-permute-start = (f32[208,128]{1,0:T(8,128)S(1)}, f32[208,128]{1,0:T(8,128)S(1)}, u32[]{:S(2)}, u32[]{:S(2)}) collective-permute-start(f32[208,128]{1,0:T(8,128)S(1)} %get-tuple-element.38), channel_id=1, source_target_pairs={{0,4},{8,12},{16,20},{24,28},{4,0},{12,8},{20,16},{28,24},{1,5},{9... | collective-permute-start | bytes 319496 | tf_op jit(solution)/shard_map/ppermute | solution.py:780
  4.4 9.9 %collective-permute-start.1 = (f32[208,128]{1,0:T(8,128)S(1)}, f32[208,128]{1,0:T(8,128)S(1)}, u32[]{:S(2)}, u32[]{:S(2)}) collective-permute-start(f32[208,128]{1,0:T(8,128)S(1)} %get-tuple-element.39), channel_id=1, source_target_pairs={{4,8},{12,16},{20,24},{8,4},{16,12},{24,20},{5,9},{13,17},{21,25},... | collective-permute-start | bytes 319496 | tf_op jit(solution)/shard_map/ppermute | solution.py:780
  7.0 5.1 %collective-permute-start.2 = (f32[64,128]{1,0:T(8,128)S(1)}, f32[64,128]{1,0:T(8,128)S(1)}, u32[]{:S(2)}, u32[]{:S(2)}) collective-permute-start(f32[64,128]{1,0:T(8,128)S(1)} %get-tuple-element.40), channel_id=1, source_target_pairs={{0,1},{2,3},{1,0},{3,2},{4,5},{6,7},{5,4},{7,6},{8,9},{10,11},{9,8... | collective-permute-start | bytes 98312 | tf_op jit(solution)/shard_map/ppermute | solution.py:780
  7.0 7.3 %collective-permute-start.3 = (f32[64,128]{1,0:T(8,128)S(1)}, f32[64,128]{1,0:T(8,128)S(1)}, u32[]{:S(2)}, u32[]{:S(2)}) collective-permute-start(f32[64,128]{1,0:T(8,128)S(1)} %get-tuple-element.41), channel_id=1, source_target_pairs={{1,2},{2,1},{5,6},{6,5},{9,10},{10,9},{13,14},{14,13},{17,18},{18,... | collective-permute-start | bytes 98312 | tf_op jit(solution)/shard_map/ppermute | solution.py:780
  15.2 7.1 %collective-permute-start.4 = (f32[392,128]{1,0:T(8,128)S(1)}, f32[392,128]{1,0:T(8,128)S(1)}, u32[]{:S(2)}, u32[]{:S(2)}) collective-permute-start(f32[392,128]{1,0:T(8,128)S(1)} %get-tuple-element.48), channel_id=1, source_target_pairs={{0,1},{2,3},{1,0},{3,2},{4,5},{6,7},{5,4},{7,6},{8,9},{10,11},{9,8... | collective-permute-start | bytes 602120 | tf_op jit(solution)/shard_map/ppermute | solution.py:780
  15.3 8.9 %collective-permute-start.5 = (f32[392,128]{1,0:T(8,128)S(1)}, f32[392,128]{1,0:T(8,128)S(1)}, u32[]{:S(2)}, u32[]{:S(2)}) collective-permute-start(f32[392,128]{1,0:T(8,128)S(1)} %get-tuple-element.49), channel_id=1, source_target_pairs={{1,2},{2,1},{5,6},{6,5},{9,10},{10,9},{13,14},{14,13},{17,18},{18,... | collective-permute-start | bytes 602120 | tf_op jit(solution)/shard_map/ppermute | solution.py:780
  25.7 5.7 %collective-permute-start.6 = (f32[344,128]{1,0:T(8,128)S(1)}, f32[344,128]{1,0:T(8,128)S(1)}, u32[]{:S(2)}, u32[]{:S(2)}) collective-permute-start(f32[344,128]{1,0:T(8,128)S(1)} %get-tuple-element.57), channel_id=1, source_target_pairs={{0,1},{2,3},{1,0},{3,2},{4,5},{6,7},{5,4},{7,6},{8,9},{10,11},{9,8... | collective-permute-start | bytes 528392 | tf_op jit(solution)/shard_map/ppermute | solution.py:780
  25.7 7.5 %collective-permute-start.7 = (f32[344,128]{1,0:T(8,128)S(1)}, f32[344,128]{1,0:T(8,128)S(1)}, u32[]{:S(2)}, u32[]{:S(2)}) collective-permute-start(f32[344,128]{1,0:T(8,128)S(1)} %get-tuple-element.58), channel_id=1, source_target_pairs={{1,2},{2,1},{5,6},{6,5},{9,10},{10,9},{13,14},{14,13},{17,18},{18,... | collective-permute-start | bytes 528392 | tf_op jit(solution)/shard_map/ppermute | solution.py:780

commit v9 on v8

--- a/solution.py
+++ b/solution.py
@@ -177,13 +177,12 @@
     return field
 
 
-def pack(grid, groups, to_right, out):
-    for index, (a, b, c, d) in enumerate(groups):
-        if to_right:
-            one, two = jnp.where(grid.first, a, rolled(b, EDGE, 1)), jnp.where(grid.first, c, rolled(d, EDGE, 1))
-        else:
-            one, two = jnp.where(grid.first, rolled(b, -EDGE, 1), a), jnp.where(grid.first, rolled(d, -EDGE, 1), c)
-        store(out, index, jnp.where(grid.left, one, two))
+def pack(grid, own, other, flat, other_flat, to_right, out):
+    for index, (near, far) in enumerate(zip(edge_groups(own, flat), edge_groups(other, other_flat))):
+        a, b, c, d = near[0], far[1], near[2], far[3]
+        if not to_right:
+            a, b, c, d = b, a, d, c
+        store(out, index, jnp.where(grid.left, jnp.where(grid.first, a, b), jnp.where(grid.first, c, d)))
 
 
 def edge_groups(own, own_flat):
@@ -227,15 +226,19 @@
 
 def picker(t):
     k, n = [lax.broadcasted_iota(jnp.int32, (LANES, LANES), axis) for axis in range(2)]
-    column = (n % GROUP - EDGE) % LANES
-    one = jnp.where((n % HALF // GROUP == t) & (k == column), 1.0, 0.0).astype(jnp.bfloat16)
-    return jnp.concatenate([one] * 2, axis=0)
+    inner, mine = n % GROUP, n % HALF // GROUP == t
+    both = []
+    for swapped in (False, True):
+        last = inner >= EDGE if swapped else inner < EDGE
+        column = jnp.where(last, LANES - EDGE, 0) + inner % EDGE
+        both.append(jnp.where(mine & (k == column), 1.0, 0.0).astype(jnp.bfloat16))
+    return jnp.concatenate([jnp.concatenate(both, axis=1)] * 2, axis=0)
 
 
 def edges_kernel(flags, *refs):
     hbm, refs = refs[:8], refs[8:]
     (before, after, main, flat, own, own_flat, even_way, odd_way, early_even, early_odd), refs = refs[:10], refs[10:]
-    ocean, deep, floor, wet, sem = refs
+    other, other_flat, ocean, deep, floor, wet, sem = refs
     sent = []
 
     def copy(source, target):
@@ -254,7 +257,12 @@
     difference_matrix(before, (27.0, -27.0, -1.0, 1.0), (0, 1, -1, 2))
     difference_matrix(after, (27.0, -27.0, -1.0, 1.0), (-1, 0, -2, 1))
     pickers = [picker(t) for t in range(TILES)]
-    grid = Grid()
+    for one in rest:
+        one.wait()
+    planes = [ocean[k] for k in range(3)] + [deep[...]]
+    planes += [floor[...].astype(jnp.float32), wet[...].astype(jnp.float32)]
+    for k, x in enumerate(planes):
+        store(flat, k, x)
     size = SUB * ROWS
     for half in range(2):
         for one in ready[half]:
@@ -263,29 +271,25 @@
         total = None
         for t in range(TILES):
             x = [main[f, y, t * SUB : (t + 1) * SUB, :] for f in mine for y in range(ROWS)]
+            x = x if half else x + planes
             part = jnp.dot(split(jnp.concatenate(x, axis=0), 2), pickers[t], preferred_element_type=jnp.float32)
             total = part if total is None else total + part
-        own[mine[0] * size : (mine[-1] + 1) * size, :] = total
-    for one in rest:
-        one.wait()
-    planes = [ocean[k] for k in range(3)] + [deep[...]]
-    planes += [floor[...].astype(jnp.float32), wet[...].astype(jnp.float32)]
-    for k, x in enumerate(planes):
-        store(flat, k, x)
-        out = grid.zero
-        for g in range(LANES // GROUP):
-            out = jnp.where(grid.group == g, rolled(x, EDGE + GROUP * g, 1), out)
-        store(own_flat, k, out)
+        for ref, ref_flat, x in ((own, own_flat, total[:, :LANES]), (other, other_flat, total[:, LANES:])):
+            ref[mine[0] * size : (mine[-1] + 1) * size, :] = x[: cut * size, :]
+            if not half:
+                ref_flat[...] = x[cut * size :, :]
+    grid = Grid()
+    edges = own, other, own_flat, other_flat
 
     @pl.when((flags[0] & 1) == 1)
     def _():
-        pack(grid, edge_groups(own, own_flat), True, odd_way)
-        pack(grid, edge_groups(own, own_flat), False, even_way)
+        pack(grid, *edges, True, odd_way)
+        pack(grid, *edges, False, even_way)
 
     @pl.when((flags[0] & 1) == 0)
     def _():
-        pack(grid, edge_groups(own, own_flat), False, odd_way)
-        pack(grid, edge_groups(own, own_flat), True, even_way)
+        pack(grid, *edges, False, odd_way)
+        pack(grid, *edges, True, even_way)
 
     odd = (flags[1] & 1) == 1
     for k, ((_, below), (_, above)) in enumerate(zip(BUOY_LOW, BUOY_HIGH)):
@@ -536,7 +540,7 @@
 
 
 def start_kernel(
-    flags, before, after, main, flat, own, own_flat, even_in, odd_in, early_even, early_odd,
+    flags, before, after, main, flat, own, own_flat, even_in, odd_in, early_odd, early_even,
     windows, flat_windows, partial, level, even_way, odd_way,
 ):
     grid = Grid(flags[2], before, after)
@@ -790,7 +794,8 @@
     edge = FIELDS * ROWS // 4 + 2
     before, after, main, flat, own, own_flat, even_way, odd_way, early_even, early_odd = call(
         edges_kernel, [matrix, matrix, cells4, 6, FIELDS * ROWS, 6, edge, edge, 2 * TILES, 2 * TILES],
-        [pltpu.VMEM(x.shape, x.dtype) for x in inputs[4:]] + [pltpu.SemaphoreType.DMA((4 + 5 * ROWS,))],
+        [planes(FIELDS * ROWS), planes(6)] + [pltpu.VMEM(x.shape, x.dtype) for x in inputs[4:]]
+        + [pltpu.SemaphoreType.DMA((4 + 5 * ROWS,))],
         *inputs, flags=flags, place=IN_HBM,
     )
     x_in = swap(even_way, "gx", 0), swap(odd_way, "gx", 1)
@@ -800,7 +805,7 @@
     edges, block = len(OPEN) * SPAN, ROWS * SPAN
     windows, flat_windows, partial, level, even_way, odd_way = call(
         start_kernel, [FIELDS * ROWS, 6, edges, 2, first, first], [],
-        before, after, main, flat, own, own_flat, *x_in, *early_in, flags=flags,
+        before, after, main, flat, own, own_flat, *x_in, *early_in[::-1], flags=flags,
     )
     y_in = swap(even_way, "gy", 0), swap(odd_way, "gy", 1)
     speed, inner = call(start_rest_kernel, [3 * block, 6 * block], [], before, after, main, windows, flags=flags, work=4)

time: 36.3 us -> 36.2 us (level)
  starting transfers between devices: 15 us -> 11.4 us
  waiting for transfers between devices: 8.51 us -> 12.1 us
    ppermute x8, waiting for transfers between devices: 8.51 us -> 12.1 us  [swap(): return lax.ppermute(x, axis, pairs + [(j, i) for i, j in pairs])]
    ppermute x8, starting transfers between devices: 15 us -> 11.4 us  [swap(): return lax.ppermute(x, axis, pairs + [(j, i) for i, j in pairs])]
  transfers between devices with their start and end apart: 8 -> 8, of which waited for: 5 -> 6; matrix products, arithmetic and copies ran while one was open for 0% -> 0% of each run, Pallas kernels for 8% -> 8%
where the time goes in v9:
time: 36.2 us; the launch traced here: 36 us
  waiting for transfers between devices  12.1 us (33%)
  Pallas kernels  11.7 us (32%)
  starting transfers between devices  11.4 us (31%)
  between operations  0.73 us (2%)
    ppermute x8, waiting for transfers between devices, swap(): return lax.ppermute(x, axis, pairs + [(j, i) for i, j in pairs])  12.1 us
    pallas_call x6, Pallas kernels, call(): pl.pallas_call(kernel, out_shape=[n if hasattr(n, 'dtype') else jax.Shape...  11.7 us
    ppermute x8, starting transfers between devices, swap(): return lax.ppermute(x, axis, pairs + [(j, i) for i, j in pairs])  11.4 us
  transfers between devices with their start and end apart: 8, of which 6 were waited for; matrix products, arithmetic and copies ran while one was open for 0% of the time, Pallas kernels for 8%

profile of v9, /device:TPU:10, one launch (start us, length us, event | category | flops | bytes accessed | tf_op | source)
XLA Modules:
  0.0 36.0 jit_solution(13570624342441751776)
XLA Ops:
  0.6 0.1 pad_add_fusion.flags
  0.7 3.6 %shard_map.95 = (bf16[256,640]{1,0:T(8,128)(2,1)S(1)}, bf16[256,640]{1,0:T(8,128)(2,1)S(1)}, f32[12,8,32,128]{3,2,1,0:T(8,128)S(1)}, f32[48,128]{1,0:T(8,128)S(1...) custom-call(s32[3]{0:T(128)S(1)} %pad_add_fusion.flags, ...), custom_call_target="tpu_custom_call" | custom-call | flops 1000000 | bytes 2318348 | tf_op jit(solution)/shard_map/pallas_call | solution.py:766
  4.3 0.1 collective-permute-start
  4.3 2.5 %collective-permute-start.1 = (f32[208,128]{1,0:T(8,128)S(1)}, f32[208,128]{1,0:T(8,128)S(1)}, u32[]{:S(2)}, u32[]{:S(2)}) collective-permute-start(f32[208,128]{1,0:T(8,128)S(1)} %get-tuple-element.39), channel_id=1, source_target_pairs={{4,8},{12,16},{20,24},{8,4},{16,12},{24,20},{5,9},{13,17},{21,25},... | collective-permute-start | bytes 319496 | tf_op jit(solution)/shard_map/ppermute | solution.py:784
  6.9 3.5 %collective-permute-start.2 = (f32[64,128]{1,0:T(8,128)S(1)}, f32[64,128]{1,0:T(8,128)S(1)}, u32[]{:S(2)}, u32[]{:S(2)}) collective-permute-start(f32[64,128]{1,0:T(8,128)S(1)} %get-tuple-element.40), channel_id=1, source_target_pairs={{1,2},{2,1},{5,6},{6,5},{9,10},{10,9},{13,14},{14,13},{17,18},{18,... | collective-permute-start | bytes 98312 | tf_op jit(solution)/shard_map/ppermute | solution.py:784
  10.4 0.1 collective-permute-start.3
  10.5 2.6 %collective-permute-done.2.early_odd = f32[64,128]{1,0:T(8,128)S(1)} collective-permute-done((f32[64,128]{1,0:T(8,128)S(1)}, f32[64,128]{1,0:T(8,128)S(1)}, u32[]{:S(2)}, u32[]{:S(2)}) %collective-permute-start.2) | collective-permute-done | bytes 32800 | tf_op jit(solution)/shard_map/ppermute | solution.py:784
  13.0 1.4 %collective-permute-done.3.early_even = f32[64,128]{1,0:T(8,128)S(1)} collective-permute-done((f32[64,128]{1,0:T(8,128)S(1)}, f32[64,128]{1,0:T(8,128)S(1)}, u32[]{:S(2)}, u32[]{:S(2)}) %collective-permute-start.3) | collective-permute-done | bytes 32800 | tf_op jit(solution)/shard_map/ppermute | solution.py:784
  14.4 0.0 collective-permute-done.even_in
  14.4 0.0 collective-permute-done.1.odd_in
  14.5 0.9 %shard_map.96 = (f32[768,128]{1,0:T(8,128)S(1)}, f32[48,128]{1,0:T(8,128)S(1)}, f32[360,128]{1,0:T(8,128)S(1)}, f32[16,128]{1,0:T(8,128)S(1)}, f32[392,128]{1,0:T(8,128)S(1)}, /*index=5*/f32[392,128]{1,0:T(8,128)S(1)}) custom-call(s32[3]{0:T(128)S(1)} %pad_add_fusion.flags, bf16[256,640]{1,0:T(8,128)(2,1)S(1)} %get-tuple-element.32.before, ...), custom_call_target="tpu_custom_call" | custom-call | flops 1000000 | bytes 4616204 | tf_op jit(solution)/shard_map/pallas_call | solution.py:766
  15.4 0.3 collective-permute-start.4
  15.7 2.3 %collective-permute-start.5 = (f32[392,128]{1,0:T(8,128)S(1)}, f32[392,128]{1,0:T(8,128)S(1)}, u32[]{:S(2)}, u32[]{:S(2)}) collective-permute-start(f32[392,128]{1,0:T(8,128)S(1)} %get-tuple-element.49), channel_id=1, source_target_pairs={{1,2},{2,1},{5,6},{6,5},{9,10},{10,9},{13,14},{14,13},{17,18},{18,... | collective-permute-start | bytes 602120 | tf_op jit(solution)/shard_map/ppermute | solution.py:784
  18.1 1.1 %shard_map.97 = (f32[960,128]{1,0:T(8,128)S(1)}, f32[1920,128]{1,0:T(8,128)S(1)}) custom-call(s32[3]{0:T(128)S(1)} %pad_add_fusion.flags, bf16[256,640]{1,0:T(8,128)(2,1)S(1)} %get-tuple-element.32.before, bf16[256,640]{1,0:T(8,128)(2,1)S(1)} %get-tuple-element.33.after, f32[3072,128]{1,0:T(8,128)S(1)} %bitcast.5, f32[768,128]{1,0:T(8,128)S(1)} %get-tuple-element.42.windows), custom_call_target="tpu_custom_call" | custom-call | flops 4000000 | bytes 4751372 | tf_op jit(solution)/shard_map/pallas_call | solution.py:766
  19.2 3.0 %collective-permute-done.4.even_in = f32[392,128]{1,0:T(8,128)S(1)} collective-permute-done((f32[392,128]{1,0:T(8,128)S(1)}, f32[392,128]{1,0:T(8,128)S(1)}, u32[]{:S(2)}, u32[]{:S(2)}) %collective-permute-start.4) | collective-permute-done | bytes 200736 | tf_op jit(solution)/shard_map/ppermute | solution.py:784
  22.2 2.1 %collective-permute-done.5.odd_in = f32[392,128]{1,0:T(8,128)S(1)} collective-permute-done((f32[392,128]{1,0:T(8,128)S(1)}, f32[392,128]{1,0:T(8,128)S(1)}, u32[]{:S(2)}, u32[]{:S(2)}) %collective-permute-start.5) | collective-permute-done | bytes 200736 | tf_op jit(solution)/shard_map/ppermute | solution.py:784
  24.4 1.4 %shard_map.98 = (f32[1440,128]{1,0:T(8,128)S(1)}, f32[1920,128]{1,0:T(8,128)S(1)}, f32[48,128]{1,0:T(8,128)S(1)}, f32[360,128]{1,0:T(8,128)S(1)}, f32[16,128]{1,...) custom-call(s32[3]{0:T(128)S(1)} %pad_add_fusion.flags, bf16[256,640]{1,0:T(8,128)(2,1)S(1)} %get-tuple-element.32.before, ...), custom_call_target="tpu_custom_call" | custom-call | flops 1000000 | bytes 7749644 | tf_op jit(solution)/shard_map/pallas_call | solution.py:766
  25.8 0.1 collective-permute-start.6
  25.9 2.5 %collective-permute-start.7 = (f32[344,128]{1,0:T(8,128)S(1)}, f32[344,128]{1,0:T(8,128)S(1)}, u32[]{:S(2)}, u32[]{:S(2)}) collective-permute-start(f32[344,128]{1,0:T(8,128)S(1)} %get-tuple-element.58), channel_id=1, source_target_pairs={{1,2},{2,1},{5,6},{6,5},{9,10},{10,9},{13,14},{14,13},{17,18},{18,... | collective-permute-start | bytes 528392 | tf_op jit(solution)/shard_map/ppermute | solution.py:784
  28.4 1.9 %shard_map.99 = (f32[960,128]{1,0:T(8,128)S(1)}, f32[1920,128]{1,0:T(8,128)S(1)}, f32[9,32,8,128]{3,2,1,0:T(8,128)}) custom-call(s32[3]{0:T(128)S(1)} %pad_add_fusion.flags, bf16[256,640]{1,0:T(8,128)(2,1)S(1)} %get-tuple-element.32.before, bf16[256,640]{1,0:T(8,128)(2,1)S(1)} %get-tuple-element.33.after, f32[3072,128]{1,0:T(8,128)S(1)} %bitcast.7, ...), custom_call_target="tpu_custom_call" | custom-call | flops 4000000 | bytes 6963212 | tf_op jit(solution)/shard_map/pallas_call | solution.py:766
  30.3 1.0 %collective-permute-done.6.even_in = f32[344,128]{1,0:T(8,128)S(1)} collective-permute-done((f32[344,128]{1,0:T(8,128)S(1)}, f32[344,128]{1,0:T(8,128)S(1)}, u32[]{:S(2)}, u32[]{:S(2)}) %collective-permute-start.6) | collective-permute-done | bytes 176160 | tf_op jit(solution)/shard_map/ppermute | solution.py:784
  31.3 1.9 %collective-permute-done.7.odd_in = f32[344,128]{1,0:T(8,128)S(1)} collective-permute-done((f32[344,128]{1,0:T(8,128)S(1)}, f32[344,128]{1,0:T(8,128)S(1)}, u32[]{:S(2)}, u32[]{:S(2)}) %collective-permute-start.7) | collective-permute-done | bytes 176160 | tf_op jit(solution)/shard_map/ppermute | solution.py:784
  33.2 2.8 %shard_map.100 = (f32[9,32,8,128]{3,2,1,0:T(8,128)}, f32[24,128]{1,0:T(8,128)}) custom-call(s32[3]{0:T(128)S(1)} %pad_add_fusion.flags, bf16[256,640]{1,0:T(8,128)(2,1)S(1)} %get-tuple-element.32.before, bf16[256,640]{1,0:T(8,128)(2,1)S(1)} %get-tuple-element.33.after, f32[3072,128]{1,0:T(8,128)S(1)} %bitcast.8, ...), custom_call_target="tpu_custom_call", output_to_operand_aliasing={{0}: (17, {})} | custom-call | flops 1000000 | bytes 7610380 | tf_op jit(solution)/shard_map/pallas_call | solution.py:766
Async XLA Ops:
  4.3 10.2 %collective-permute-start = (f32[208,128]{1,0:T(8,128)S(1)}, f32[208,128]{1,0:T(8,128)S(1)}, u32[]{:S(2)}, u32[]{:S(2)}) collective-permute-start(f32[208,128]{1,0:T(8,128)S(1)} %get-tuple-element.38), channel_id=1, source_target_pairs={{0,4},{8,12},{16,20},{24,28},{4,0},{12,8},{20,16},{28,24},{1,5},{9... | collective-permute-start | bytes 319496 | tf_op jit(solution)/shard_map/ppermute | solution.py:784
  4.3 10.1 %collective-permute-start.1 = (f32[208,128]{1,0:T(8,128)S(1)}, f32[208,128]{1,0:T(8,128)S(1)}, u32[]{:S(2)}, u32[]{:S(2)}) collective-permute-start(f32[208,128]{1,0:T(8,128)S(1)} %get-tuple-element.39), channel_id=1, source_target_pairs={{4,8},{12,16},{20,24},{8,4},{16,12},{24,20},{5,9},{13,17},{21,25},... | collective-permute-start | bytes 319496 | tf_op jit(solution)/shard_map/ppermute | solution.py:784
  6.9 6.1 %collective-permute-start.2 = (f32[64,128]{1,0:T(8,128)S(1)}, f32[64,128]{1,0:T(8,128)S(1)}, u32[]{:S(2)}, u32[]{:S(2)}) collective-permute-start(f32[64,128]{1,0:T(8,128)S(1)} %get-tuple-element.40), channel_id=1, source_target_pairs={{1,2},{2,1},{5,6},{6,5},{9,10},{10,9},{13,14},{14,13},{17,18},{18,... | collective-permute-start | bytes 98312 | tf_op jit(solution)/shard_map/ppermute | solution.py:784
  10.4 4.1 %collective-permute-start.3 = (f32[64,128]{1,0:T(8,128)S(1)}, f32[64,128]{1,0:T(8,128)S(1)}, u32[]{:S(2)}, u32[]{:S(2)}) collective-permute-start(f32[64,128]{1,0:T(8,128)S(1)} %get-tuple-element.41), channel_id=1, source_target_pairs={{0,1},{2,3},{1,0},{3,2},{4,5},{6,7},{5,4},{7,6},{8,9},{10,11},{9,8... | collective-permute-start | bytes 98312 | tf_op jit(solution)/shard_map/ppermute | solution.py:784
  15.4 6.8 %collective-permute-start.4 = (f32[392,128]{1,0:T(8,128)S(1)}, f32[392,128]{1,0:T(8,128)S(1)}, u32[]{:S(2)}, u32[]{:S(2)}) collective-permute-start(f32[392,128]{1,0:T(8,128)S(1)} %get-tuple-element.48), channel_id=1, source_target_pairs={{0,1},{2,3},{1,0},{3,2},{4,5},{6,7},{5,4},{7,6},{8,9},{10,11},{9,8... | collective-permute-start | bytes 602120 | tf_op jit(solution)/shard_map/ppermute | solution.py:784
  15.7 8.6 %collective-permute-start.5 = (f32[392,128]{1,0:T(8,128)S(1)}, f32[392,128]{1,0:T(8,128)S(1)}, u32[]{:S(2)}, u32[]{:S(2)}) collective-permute-start(f32[392,128]{1,0:T(8,128)S(1)} %get-tuple-element.49), channel_id=1, source_target_pairs={{1,2},{2,1},{5,6},{6,5},{9,10},{10,9},{13,14},{14,13},{17,18},{18,... | collective-permute-start | bytes 602120 | tf_op jit(solution)/shard_map/ppermute | solution.py:784
  25.8 5.5 %collective-permute-start.6 = (f32[344,128]{1,0:T(8,128)S(1)}, f32[344,128]{1,0:T(8,128)S(1)}, u32[]{:S(2)}, u32[]{:S(2)}) collective-permute-start(f32[344,128]{1,0:T(8,128)S(1)} %get-tuple-element.57), channel_id=1, source_target_pairs={{0,1},{2,3},{1,0},{3,2},{4,5},{6,7},{5,4},{7,6},{8,9},{10,11},{9,8... | collective-permute-start | bytes 528392 | tf_op jit(solution)/shard_map/ppermute | solution.py:784
  25.9 7.3 %collective-permute-start.7 = (f32[344,128]{1,0:T(8,128)S(1)}, f32[344,128]{1,0:T(8,128)S(1)}, u32[]{:S(2)}, u32[]{:S(2)}) collective-permute-start(f32[344,128]{1,0:T(8,128)S(1)} %get-tuple-element.58), channel_id=1, source_target_pairs={{1,2},{2,1},{5,6},{6,5},{9,10},{10,9},{13,14},{14,13},{17,18},{18,... | collective-permute-start | bytes 528392 | tf_op jit(solution)/shard_map/ppermute | solution.py:784

commit v10 on v9

--- a/solution.py
+++ b/solution.py
@@ -39,6 +39,14 @@
 LINES = (None, WET, FLOOR, FLUX_X, FLUX_Y)
 
 
+def rest(x, size):
+    return x & (size - 1)
+
+
+def count(x, size):
+    return x >> (size.bit_length() - 1)
+
+
 def rolled(x, shift, axis):
     shift %= x.shape[axis]
     return x if shift == 0 else pltpu.roll(x, shift, axis)
@@ -83,11 +91,11 @@
         self.origin, self.before, self.after = origin, before, after
         self.sub = lax.broadcasted_iota(jnp.int32, (SUB, LANES), 0)
         self.lane = lax.broadcasted_iota(jnp.int32, (SUB, LANES), 1)
-        self.first = self.lane % GROUP < EDGE
+        self.first = rest(self.lane, GROUP) < EDGE
         self.left = self.lane < HALF
-        self.group = self.lane // GROUP
+        self.group = count(self.lane, GROUP)
         self.zero = jnp.zeros((SUB, LANES), jnp.float32)
-        depth = [self.sub + SUB * t for t in range(TILES)] + [self.sub + SUB * (self.group % TILES)]
+        depth = [self.sub + SUB * t for t in range(TILES)] + [self.sub + SUB * rest(self.group, TILES)]
         self.depth = [d.astype(jnp.float32) for d in depth]
 
     def beside(self, window):
@@ -111,7 +119,7 @@
             if t == TILES - 1 and offset > 0:
                 return jnp.where(self.sub < SUB - offset, x, 0.0)
             return x
-        x, at = field(y, t), self.lane % HALF
+        x, at = field(y, t), rest(self.lane, HALF)
         if offset < 0:
             beyond, far = jnp.where(at >= GROUP, rolled(x, GROUP, 1), 0.0), self.sub >= SUB + offset
         else:
@@ -155,7 +163,7 @@
 
     def every_group(self, x):
         for shift in (GROUP, 2 * GROUP):
-            x = x + jnp.where(self.lane % HALF >= shift, rolled(x, shift, 1), rolled(x, shift - HALF, 1))
+            x = x + jnp.where(rest(self.lane, HALF) >= shift, rolled(x, shift, 1), rolled(x, shift - HALF, 1))
         return x
 
     def across(self, x, offset, beside):
@@ -213,12 +221,12 @@
             total = jnp.where(apart == offset, w, total)
         return total
 
-    inner, left = k % GROUP, k < HALF
+    inner, left = rest(k, GROUP), k < HALF
     column = jnp.where(left, inner - EDGE, LANES - EDGE + inner)
     outside = (left & (inner < EDGE)) | (jnp.logical_not(left) & (inner >= EDGE))
     beside = jnp.where(outside, weight(n - column), 0.0)
     parts = [weight(n - k)]
-    parts += [jnp.where(k % HALF // GROUP == t, beside, 0.0) for t in range(TILES)]
+    parts += [jnp.where(count(rest(k, HALF), GROUP) == t, beside, 0.0) for t in range(TILES)]
     for p, x in enumerate(parts):
         for half in range(2):
             out[half * LANES : (half + 1) * LANES, p * LANES : (p + 1) * LANES] = x.astype(jnp.bfloat16)
@@ -226,11 +234,11 @@
 
 def picker(t):
     k, n = [lax.broadcasted_iota(jnp.int32, (LANES, LANES), axis) for axis in range(2)]
-    inner, mine = n % GROUP, n % HALF // GROUP == t
+    inner, mine = rest(n, GROUP), count(rest(n, HALF), GROUP) == t
     both = []
     for swapped in (False, True):
         last = inner >= EDGE if swapped else inner < EDGE
-        column = jnp.where(last, LANES - EDGE, 0) + inner % EDGE
+        column = jnp.where(last, LANES - EDGE, 0) + rest(inner, EDGE)
         both.append(jnp.where(mine & (k == column), 1.0, 0.0).astype(jnp.bfloat16))
     return jnp.concatenate([jnp.concatenate(both, axis=1)] * 2, axis=0)
 
@@ -253,11 +261,11 @@
     for y in range(ROWS):
         ready[1].append(copy(hbm[0].at[cut:, :, y, :], main.at[cut:LAME, y]))
         ready[1] += [copy(hbm[1 + k].at[:, y, :], main.at[LAME + k, y]) for k in range(3)]
-    rest = [copy(hbm[4 + k], x) for k, x in enumerate((ocean, deep, floor, wet))]
+    flats = [copy(hbm[4 + k], x) for k, x in enumerate((ocean, deep, floor, wet))]
     difference_matrix(before, (27.0, -27.0, -1.0, 1.0), (0, 1, -1, 2))
     difference_matrix(after, (27.0, -27.0, -1.0, 1.0), (-1, 0, -2, 1))
     pickers = [picker(t) for t in range(TILES)]
-    for one in rest:
+    for one in flats:
         one.wait()
     planes = [ocean[k] for k in range(3)] + [deep[...]]
     planes += [floor[...].astype(jnp.float32), wet[...].astype(jnp.float32)]

time: 36.2 us -> 36.2 us (level)
  no operation moved by 1% of the time
where the time goes in v10:
time: 36.2 us; the launch traced here: 36 us
  waiting for transfers between devices  12.1 us (33%)
  Pallas kernels  11.7 us (32%)
  starting transfers between devices  11.4 us (31%)
  between operations  0.73 us (2%)
    ppermute x8, waiting for transfers between devices, swap(): return lax.ppermute(x, axis, pairs + [(j, i) for i, j in pairs])  12.1 us
    pallas_call x6, Pallas kernels, call(): pl.pallas_call(kernel, out_shape=[n if hasattr(n, 'dtype') else jax.Shape...  11.7 us
    ppermute x8, starting transfers between devices, swap(): return lax.ppermute(x, axis, pairs + [(j, i) for i, j in pairs])  11.4 us
  transfers between devices with their start and end apart: 8, of which 6 were waited for; matrix products, arithmetic and copies ran while one was open for 0% of the time, Pallas kernels for 8%

profile of v10, /device:TPU:10, one launch (start us, length us, event | category | flops | bytes accessed | tf_op | source)
XLA Modules:
  0.0 36.0 jit_solution(8122044291129242299)
XLA Ops:
  0.6 0.1 pad_add_fusion.flags
  0.7 3.5 %shard_map.95 = (bf16[256,640]{1,0:T(8,128)(2,1)S(1)}, bf16[256,640]{1,0:T(8,128)(2,1)S(1)}, f32[12,8,32,128]{3,2,1,0:T(8,128)S(1)}, f32[48,128]{1,0:T(8,128)S(1...) custom-call(s32[3]{0:T(128)S(1)} %pad_add_fusion.flags, ...), custom_call_target="tpu_custom_call" | custom-call | flops 1000000 | bytes 2318348 | tf_op jit(solution)/shard_map/pallas_call | solution.py:774
  4.3 0.1 collective-permute-start
  4.3 2.5 %collective-permute-start.1 = (f32[208,128]{1,0:T(8,128)S(1)}, f32[208,128]{1,0:T(8,128)S(1)}, u32[]{:S(2)}, u32[]{:S(2)}) collective-permute-start(f32[208,128]{1,0:T(8,128)S(1)} %get-tuple-element.39), channel_id=1, source_target_pairs={{4,8},{12,16},{20,24},{8,4},{16,12},{24,20},{5,9},{13,17},{21,25},... | collective-permute-start | bytes 319496 | tf_op jit(solution)/shard_map/ppermute | solution.py:792
  6.9 3.5 %collective-permute-start.2 = (f32[64,128]{1,0:T(8,128)S(1)}, f32[64,128]{1,0:T(8,128)S(1)}, u32[]{:S(2)}, u32[]{:S(2)}) collective-permute-start(f32[64,128]{1,0:T(8,128)S(1)} %get-tuple-element.40), channel_id=1, source_target_pairs={{1,2},{2,1},{5,6},{6,5},{9,10},{10,9},{13,14},{14,13},{17,18},{18,... | collective-permute-start | bytes 98312 | tf_op jit(solution)/shard_map/ppermute | solution.py:792
  10.4 0.1 collective-permute-start.3
  10.5 2.6 %collective-permute-done.2.early_odd = f32[64,128]{1,0:T(8,128)S(1)} collective-permute-done((f32[64,128]{1,0:T(8,128)S(1)}, f32[64,128]{1,0:T(8,128)S(1)}, u32[]{:S(2)}, u32[]{:S(2)}) %collective-permute-start.2) | collective-permute-done | bytes 32800 | tf_op jit(solution)/shard_map/ppermute | solution.py:792
  13.0 1.4 %collective-permute-done.3.early_even = f32[64,128]{1,0:T(8,128)S(1)} collective-permute-done((f32[64,128]{1,0:T(8,128)S(1)}, f32[64,128]{1,0:T(8,128)S(1)}, u32[]{:S(2)}, u32[]{:S(2)}) %collective-permute-start.3) | collective-permute-done | bytes 32800 | tf_op jit(solution)/shard_map/ppermute | solution.py:792
  14.4 0.0 collective-permute-done.even_in
  14.4 0.0 collective-permute-done.1.odd_in
  14.4 0.9 %shard_map.96 = (f32[768,128]{1,0:T(8,128)S(1)}, f32[48,128]{1,0:T(8,128)S(1)}, f32[360,128]{1,0:T(8,128)S(1)}, f32[16,128]{1,0:T(8,128)S(1)}, f32[392,128]{1,0:T(8,128)S(1)}, /*index=5*/f32[392,128]{1,0:T(8,128)S(1)}) custom-call(s32[3]{0:T(128)S(1)} %pad_add_fusion.flags, bf16[256,640]{1,0:T(8,128)(2,1)S(1)} %get-tuple-element.32.before, ...), custom_call_target="tpu_custom_call" | custom-call | flops 1000000 | bytes 4616204 | tf_op jit(solution)/shard_map/pallas_call | solution.py:774
  15.4 0.3 collective-permute-start.4
  15.7 2.3 %collective-permute-start.5 = (f32[392,128]{1,0:T(8,128)S(1)}, f32[392,128]{1,0:T(8,128)S(1)}, u32[]{:S(2)}, u32[]{:S(2)}) collective-permute-start(f32[392,128]{1,0:T(8,128)S(1)} %get-tuple-element.49), channel_id=1, source_target_pairs={{1,2},{2,1},{5,6},{6,5},{9,10},{10,9},{13,14},{14,13},{17,18},{18,... | collective-permute-start | bytes 602120 | tf_op jit(solution)/shard_map/ppermute | solution.py:792
  18.1 1.1 %shard_map.97 = (f32[960,128]{1,0:T(8,128)S(1)}, f32[1920,128]{1,0:T(8,128)S(1)}) custom-call(s32[3]{0:T(128)S(1)} %pad_add_fusion.flags, bf16[256,640]{1,0:T(8,128)(2,1)S(1)} %get-tuple-element.32.before, bf16[256,640]{1,0:T(8,128)(2,1)S(1)} %get-tuple-element.33.after, f32[3072,128]{1,0:T(8,128)S(1)} %bitcast.5, f32[768,128]{1,0:T(8,128)S(1)} %get-tuple-element.42.windows), custom_call_target="tpu_custom_call" | custom-call | flops 4000000 | bytes 4751372 | tf_op jit(solution)/shard_map/pallas_call | solution.py:774
  19.2 3.0 %collective-permute-done.4.even_in = f32[392,128]{1,0:T(8,128)S(1)} collective-permute-done((f32[392,128]{1,0:T(8,128)S(1)}, f32[392,128]{1,0:T(8,128)S(1)}, u32[]{:S(2)}, u32[]{:S(2)}) %collective-permute-start.4) | collective-permute-done | bytes 200736 | tf_op jit(solution)/shard_map/ppermute | solution.py:792
  22.2 2.1 %collective-permute-done.5.odd_in = f32[392,128]{1,0:T(8,128)S(1)} collective-permute-done((f32[392,128]{1,0:T(8,128)S(1)}, f32[392,128]{1,0:T(8,128)S(1)}, u32[]{:S(2)}, u32[]{:S(2)}) %collective-permute-start.5) | collective-permute-done | bytes 200736 | tf_op jit(solution)/shard_map/ppermute | solution.py:792
  24.4 1.4 %shard_map.98 = (f32[1440,128]{1,0:T(8,128)S(1)}, f32[1920,128]{1,0:T(8,128)S(1)}, f32[48,128]{1,0:T(8,128)S(1)}, f32[360,128]{1,0:T(8,128)S(1)}, f32[16,128]{1,...) custom-call(s32[3]{0:T(128)S(1)} %pad_add_fusion.flags, bf16[256,640]{1,0:T(8,128)(2,1)S(1)} %get-tuple-element.32.before, ...), custom_call_target="tpu_custom_call" | custom-call | flops 1000000 | bytes 7749644 | tf_op jit(solution)/shard_map/pallas_call | solution.py:774
  25.8 0.1 collective-permute-start.6
  25.9 2.5 %collective-permute-start.7 = (f32[344,128]{1,0:T(8,128)S(1)}, f32[344,128]{1,0:T(8,128)S(1)}, u32[]{:S(2)}, u32[]{:S(2)}) collective-permute-start(f32[344,128]{1,0:T(8,128)S(1)} %get-tuple-element.58), channel_id=1, source_target_pairs={{1,2},{2,1},{5,6},{6,5},{9,10},{10,9},{13,14},{14,13},{17,18},{18,... | collective-permute-start | bytes 528392 | tf_op jit(solution)/shard_map/ppermute | solution.py:792
  28.4 1.9 %shard_map.99 = (f32[960,128]{1,0:T(8,128)S(1)}, f32[1920,128]{1,0:T(8,128)S(1)}, f32[9,32,8,128]{3,2,1,0:T(8,128)}) custom-call(s32[3]{0:T(128)S(1)} %pad_add_fusion.flags, bf16[256,640]{1,0:T(8,128)(2,1)S(1)} %get-tuple-element.32.before, bf16[256,640]{1,0:T(8,128)(2,1)S(1)} %get-tuple-element.33.after, f32[3072,128]{1,0:T(8,128)S(1)} %bitcast.7, ...), custom_call_target="tpu_custom_call" | custom-call | flops 4000000 | bytes 6963212 | tf_op jit(solution)/shard_map/pallas_call | solution.py:774
  30.3 1.0 %collective-permute-done.6.even_in = f32[344,128]{1,0:T(8,128)S(1)} collective-permute-done((f32[344,128]{1,0:T(8,128)S(1)}, f32[344,128]{1,0:T(8,128)S(1)}, u32[]{:S(2)}, u32[]{:S(2)}) %collective-permute-start.6) | collective-permute-done | bytes 176160 | tf_op jit(solution)/shard_map/ppermute | solution.py:792
  31.3 1.9 %collective-permute-done.7.odd_in = f32[344,128]{1,0:T(8,128)S(1)} collective-permute-done((f32[344,128]{1,0:T(8,128)S(1)}, f32[344,128]{1,0:T(8,128)S(1)}, u32[]{:S(2)}, u32[]{:S(2)}) %collective-permute-start.7) | collective-permute-done | bytes 176160 | tf_op jit(solution)/shard_map/ppermute | solution.py:792
  33.2 2.8 %shard_map.100 = (f32[9,32,8,128]{3,2,1,0:T(8,128)}, f32[24,128]{1,0:T(8,128)}) custom-call(s32[3]{0:T(128)S(1)} %pad_add_fusion.flags, bf16[256,640]{1,0:T(8,128)(2,1)S(1)} %get-tuple-element.32.before, bf16[256,640]{1,0:T(8,128)(2,1)S(1)} %get-tuple-element.33.after, f32[3072,128]{1,0:T(8,128)S(1)} %bitcast.8, ...), custom_call_target="tpu_custom_call", output_to_operand_aliasing={{0}: (17, {})} | custom-call | flops 1000000 | bytes 7610380 | tf_op jit(solution)/shard_map/pallas_call | solution.py:774
Async XLA Ops:
  4.3 10.2 %collective-permute-start = (f32[208,128]{1,0:T(8,128)S(1)}, f32[208,128]{1,0:T(8,128)S(1)}, u32[]{:S(2)}, u32[]{:S(2)}) collective-permute-start(f32[208,128]{1,0:T(8,128)S(1)} %get-tuple-element.38), channel_id=1, source_target_pairs={{0,4},{8,12},{16,20},{24,28},{4,0},{12,8},{20,16},{28,24},{1,5},{9... | collective-permute-start | bytes 319496 | tf_op jit(solution)/shard_map/ppermute | solution.py:792
  4.3 10.1 %collective-permute-start.1 = (f32[208,128]{1,0:T(8,128)S(1)}, f32[208,128]{1,0:T(8,128)S(1)}, u32[]{:S(2)}, u32[]{:S(2)}) collective-permute-start(f32[208,128]{1,0:T(8,128)S(1)} %get-tuple-element.39), channel_id=1, source_target_pairs={{4,8},{12,16},{20,24},{8,4},{16,12},{24,20},{5,9},{13,17},{21,25},... | collective-permute-start | bytes 319496 | tf_op jit(solution)/shard_map/ppermute | solution.py:792
  6.9 6.1 %collective-permute-start.2 = (f32[64,128]{1,0:T(8,128)S(1)}, f32[64,128]{1,0:T(8,128)S(1)}, u32[]{:S(2)}, u32[]{:S(2)}) collective-permute-start(f32[64,128]{1,0:T(8,128)S(1)} %get-tuple-element.40), channel_id=1, source_target_pairs={{1,2},{2,1},{5,6},{6,5},{9,10},{10,9},{13,14},{14,13},{17,18},{18,... | collective-permute-start | bytes 98312 | tf_op jit(solution)/shard_map/ppermute | solution.py:792
  10.4 4.1 %collective-permute-start.3 = (f32[64,128]{1,0:T(8,128)S(1)}, f32[64,128]{1,0:T(8,128)S(1)}, u32[]{:S(2)}, u32[]{:S(2)}) collective-permute-start(f32[64,128]{1,0:T(8,128)S(1)} %get-tuple-element.41), channel_id=1, source_target_pairs={{0,1},{2,3},{1,0},{3,2},{4,5},{6,7},{5,4},{7,6},{8,9},{10,11},{9,8... | collective-permute-start | bytes 98312 | tf_op jit(solution)/shard_map/ppermute | solution.py:792
  15.4 6.8 %collective-permute-start.4 = (f32[392,128]{1,0:T(8,128)S(1)}, f32[392,128]{1,0:T(8,128)S(1)}, u32[]{:S(2)}, u32[]{:S(2)}) collective-permute-start(f32[392,128]{1,0:T(8,128)S(1)} %get-tuple-element.48), channel_id=1, source_target_pairs={{0,1},{2,3},{1,0},{3,2},{4,5},{6,7},{5,4},{7,6},{8,9},{10,11},{9,8... | collective-permute-start | bytes 602120 | tf_op jit(solution)/shard_map/ppermute | solution.py:792
  15.7 8.6 %collective-permute-start.5 = (f32[392,128]{1,0:T(8,128)S(1)}, f32[392,128]{1,0:T(8,128)S(1)}, u32[]{:S(2)}, u32[]{:S(2)}) collective-permute-start(f32[392,128]{1,0:T(8,128)S(1)} %get-tuple-element.49), channel_id=1, source_target_pairs={{1,2},{2,1},{5,6},{6,5},{9,10},{10,9},{13,14},{14,13},{17,18},{18,... | collective-permute-start | bytes 602120 | tf_op jit(solution)/shard_map/ppermute | solution.py:792
  25.8 5.5 %collective-permute-start.6 = (f32[344,128]{1,0:T(8,128)S(1)}, f32[344,128]{1,0:T(8,128)S(1)}, u32[]{:S(2)}, u32[]{:S(2)}) collective-permute-start(f32[344,128]{1,0:T(8,128)S(1)} %get-tuple-element.57), channel_id=1, source_target_pairs={{0,1},{2,3},{1,0},{3,2},{4,5},{6,7},{5,4},{7,6},{8,9},{10,11},{9,8... | collective-permute-start | bytes 528392 | tf_op jit(solution)/shard_map/ppermute | solution.py:792
  25.9 7.3 %collective-permute-start.7 = (f32[344,128]{1,0:T(8,128)S(1)}, f32[344,128]{1,0:T(8,128)S(1)}, u32[]{:S(2)}, u32[]{:S(2)}) collective-permute-start(f32[344,128]{1,0:T(8,128)S(1)} %get-tuple-element.58), channel_id=1, source_target_pairs={{1,2},{2,1},{5,6},{6,5},{9,10},{10,9},{13,14},{14,13},{17,18},{18,... | collective-permute-start | bytes 528392 | tf_op jit(solution)/shard_map/ppermute | solution.py:792

commit v11 on v10

--- a/solution.py
+++ b/solution.py
@@ -615,7 +615,7 @@
 
 def middle_kernel(
     flags, before, after, main, windows, flat, flat_windows, partial, level, speed_in, stress_in,
-    early_even, early_odd, even_in, odd_in,
+    early_even, early_odd, odd_in, even_in,
     speed_out, stress_out, ocean, partial_out, level_out, even_way, odd_way,
     sums, pressure,
 ):
@@ -819,7 +819,7 @@
     speed, inner = call(start_rest_kernel, [3 * block, 6 * block], [], before, after, main, windows, flags=flags, work=4)
     around, stress, ocean, partial, level, even_way, odd_way = call(
         middle_kernel, [3 * AROUND * SPAN, 6 * block, 6, edges, 2, later, later], [planes(4), planes(2)],
-        before, after, main, windows, flat, flat_windows, partial, level, speed, inner, *early_in, *y_in, flags=flags,
+        before, after, main, windows, flat, flat_windows, partial, level, speed, inner, *early_in, *y_in[::-1], flags=flags,
     )
     y_in = swap(even_way, "gy", 0), swap(odd_way, "gy", 1)
     wave = jax.ShapeDtypeStruct(arguments[0].shape, jnp.float32)

time: 36.2 us -> 36.5 us (level)
  starting transfers between devices: 11.4 us -> 12.4 us
  waiting for transfers between devices: 12.1 us -> 11.3 us
    ppermute x8, starting transfers between devices: 11.4 us -> 12.4 us  [swap(): return lax.ppermute(x, axis, pairs + [(j, i) for i, j in pairs])]
    ppermute x8, waiting for transfers between devices: 12.1 us -> 11.3 us  [swap(): return lax.ppermute(x, axis, pairs + [(j, i) for i, j in pairs])]
  transfers between devices with their start and end apart: 8 -> 8, of which waited for: 6 -> 5; matrix products, arithmetic and copies ran while one was open for 0% -> 0% of each run, Pallas kernels for 8% -> 8%
where the time goes in v11:
time: 36.5 us; the launch traced here: 36.2 us
  starting transfers between devices  12.4 us (34%)
  Pallas kernels  11.7 us (32%)
  waiting for transfers between devices  11.3 us (31%)
  between operations  0.73 us (2%)
    ppermute x8, starting transfers between devices, swap(): return lax.ppermute(x, axis, pairs + [(j, i) for i, j in pairs])  12.4 us
    pallas_call x6, Pallas kernels, call(): pl.pallas_call(kernel, out_shape=[n if hasattr(n, 'dtype') else jax.Shape...  11.7 us
    ppermute x8, waiting for transfers between devices, swap(): return lax.ppermute(x, axis, pairs + [(j, i) for i, j in pairs])  11.3 us
  transfers between devices with their start and end apart: 8, of which 5 were waited for; matrix products, arithmetic and copies ran while one was open for 0% of the time, Pallas kernels for 8%

profile of v11, /device:TPU:10, one launch (start us, length us, event | category | flops | bytes accessed | tf_op | source)
XLA Modules:
  0.0 36.2 jit_solution(16744562208348481023)
XLA Ops:
  0.6 0.1 pad_add_fusion.flags
  0.7 3.5 %shard_map.95 = (bf16[256,640]{1,0:T(8,128)(2,1)S(1)}, bf16[256,640]{1,0:T(8,128)(2,1)S(1)}, f32[12,8,32,128]{3,2,1,0:T(8,128)S(1)}, f32[48,128]{1,0:T(8,128)S(1...) custom-call(s32[3]{0:T(128)S(1)} %pad_add_fusion.flags, ...), custom_call_target="tpu_custom_call" | custom-call | flops 1000000 | bytes 2318348 | tf_op jit(solution)/shard_map/pallas_call | solution.py:774
  4.3 0.1 collective-permute-start
  4.3 2.5 %collective-permute-start.1 = (f32[208,128]{1,0:T(8,128)S(1)}, f32[208,128]{1,0:T(8,128)S(1)}, u32[]{:S(2)}, u32[]{:S(2)}) collective-permute-start(f32[208,128]{1,0:T(8,128)S(1)} %get-tuple-element.39), channel_id=1, source_target_pairs={{4,8},{12,16},{20,24},{8,4},{16,12},{24,20},{5,9},{13,17},{21,25},... | collective-permute-start | bytes 319496 | tf_op jit(solution)/shard_map/ppermute | solution.py:792
  6.9 3.5 %collective-permute-start.2 = (f32[64,128]{1,0:T(8,128)S(1)}, f32[64,128]{1,0:T(8,128)S(1)}, u32[]{:S(2)}, u32[]{:S(2)}) collective-permute-start(f32[64,128]{1,0:T(8,128)S(1)} %get-tuple-element.40), channel_id=1, source_target_pairs={{1,2},{2,1},{5,6},{6,5},{9,10},{10,9},{13,14},{14,13},{17,18},{18,... | collective-permute-start | bytes 98312 | tf_op jit(solution)/shard_map/ppermute | solution.py:792
  10.4 0.1 collective-permute-start.3
  10.5 2.6 %collective-permute-done.2.early_odd = f32[64,128]{1,0:T(8,128)S(1)} collective-permute-done((f32[64,128]{1,0:T(8,128)S(1)}, f32[64,128]{1,0:T(8,128)S(1)}, u32[]{:S(2)}, u32[]{:S(2)}) %collective-permute-start.2) | collective-permute-done | bytes 32800 | tf_op jit(solution)/shard_map/ppermute | solution.py:792
  13.0 1.4 %collective-permute-done.3.early_even = f32[64,128]{1,0:T(8,128)S(1)} collective-permute-done((f32[64,128]{1,0:T(8,128)S(1)}, f32[64,128]{1,0:T(8,128)S(1)}, u32[]{:S(2)}, u32[]{:S(2)}) %collective-permute-start.3) | collective-permute-done | bytes 32800 | tf_op jit(solution)/shard_map/ppermute | solution.py:792
  14.4 0.0 collective-permute-done.even_in
  14.4 0.0 collective-permute-done.1.odd_in
  14.4 0.9 %shard_map.96 = (f32[768,128]{1,0:T(8,128)S(1)}, f32[48,128]{1,0:T(8,128)S(1)}, f32[360,128]{1,0:T(8,128)S(1)}, f32[16,128]{1,0:T(8,128)S(1)}, f32[392,128]{1,0:T(8,128)S(1)}, /*index=5*/f32[392,128]{1,0:T(8,128)S(1)}) custom-call(s32[3]{0:T(128)S(1)} %pad_add_fusion.flags, bf16[256,640]{1,0:T(8,128)(2,1)S(1)} %get-tuple-element.32.before, ...), custom_call_target="tpu_custom_call" | custom-call | flops 1000000 | bytes 4616204 | tf_op jit(solution)/shard_map/pallas_call | solution.py:774
  15.4 2.4 %collective-permute-start.4 = (f32[392,128]{1,0:T(8,128)S(1)}, f32[392,128]{1,0:T(8,128)S(1)}, u32[]{:S(2)}, u32[]{:S(2)}) collective-permute-start(f32[392,128]{1,0:T(8,128)S(1)} %get-tuple-element.48), channel_id=1, source_target_pairs={{1,2},{2,1},{5,6},{6,5},{9,10},{10,9},{13,14},{14,13},{17,18},{18,... | collective-permute-start | bytes 602120 | tf_op jit(solution)/shard_map/ppermute | solution.py:792
  17.8 0.1 collective-permute-start.5
  17.9 1.1 %shard_map.97 = (f32[960,128]{1,0:T(8,128)S(1)}, f32[1920,128]{1,0:T(8,128)S(1)}) custom-call(s32[3]{0:T(128)S(1)} %pad_add_fusion.flags, bf16[256,640]{1,0:T(8,128)(2,1)S(1)} %get-tuple-element.32.before, bf16[256,640]{1,0:T(8,128)(2,1)S(1)} %get-tuple-element.33.after, f32[3072,128]{1,0:T(8,128)S(1)} %bitcast.5, f32[768,128]{1,0:T(8,128)S(1)} %get-tuple-element.42.windows), custom_call_target="tpu_custom_call" | custom-call | flops 4000000 | bytes 4751372 | tf_op jit(solution)/shard_map/pallas_call | solution.py:774
  19.0 5.1 %collective-permute-done.4.odd_in = f32[392,128]{1,0:T(8,128)S(1)} collective-permute-done((f32[392,128]{1,0:T(8,128)S(1)}, f32[392,128]{1,0:T(8,128)S(1)}, u32[]{:S(2)}, u32[]{:S(2)}) %collective-permute-start.4) | collective-permute-done | bytes 200736 | tf_op jit(solution)/shard_map/ppermute | solution.py:792
  24.0 0.3 collective-permute-done.5.even_in
  24.3 1.4 %shard_map.98 = (f32[1440,128]{1,0:T(8,128)S(1)}, f32[1920,128]{1,0:T(8,128)S(1)}, f32[48,128]{1,0:T(8,128)S(1)}, f32[360,128]{1,0:T(8,128)S(1)}, f32[16,128]{1,...) custom-call(s32[3]{0:T(128)S(1)} %pad_add_fusion.flags, bf16[256,640]{1,0:T(8,128)(2,1)S(1)} %get-tuple-element.32.before, ...), custom_call_target="tpu_custom_call" | custom-call | flops 1000000 | bytes 7749644 | tf_op jit(solution)/shard_map/pallas_call | solution.py:774
  25.7 0.4 collective-permute-start.6
  26.1 3.4 %collective-permute-start.7 = (f32[344,128]{1,0:T(8,128)S(1)}, f32[344,128]{1,0:T(8,128)S(1)}, u32[]{:S(2)}, u32[]{:S(2)}) collective-permute-start(f32[344,128]{1,0:T(8,128)S(1)} %get-tuple-element.58), channel_id=1, source_target_pairs={{1,2},{2,1},{5,6},{6,5},{9,10},{10,9},{13,14},{14,13},{17,18},{18,... | collective-permute-start | bytes 528392 | tf_op jit(solution)/shard_map/ppermute | solution.py:792
  29.6 1.9 %shard_map.99 = (f32[960,128]{1,0:T(8,128)S(1)}, f32[1920,128]{1,0:T(8,128)S(1)}, f32[9,32,8,128]{3,2,1,0:T(8,128)}) custom-call(s32[3]{0:T(128)S(1)} %pad_add_fusion.flags, bf16[256,640]{1,0:T(8,128)(2,1)S(1)} %get-tuple-element.32.before, bf16[256,640]{1,0:T(8,128)(2,1)S(1)} %get-tuple-element.33.after, f32[3072,128]{1,0:T(8,128)S(1)} %bitcast.7, ...), custom_call_target="tpu_custom_call" | custom-call | flops 4000000 | bytes 6963212 | tf_op jit(solution)/shard_map/pallas_call | solution.py:774
  31.5 0.0 collective-permute-done.6.even_in
  31.5 2.0 %collective-permute-done.7.odd_in = f32[344,128]{1,0:T(8,128)S(1)} collective-permute-done((f32[344,128]{1,0:T(8,128)S(1)}, f32[344,128]{1,0:T(8,128)S(1)}, u32[]{:S(2)}, u32[]{:S(2)}) %collective-permute-start.7) | collective-permute-done | bytes 176160 | tf_op jit(solution)/shard_map/ppermute | solution.py:792
  33.4 2.8 %shard_map.100 = (f32[9,32,8,128]{3,2,1,0:T(8,128)}, f32[24,128]{1,0:T(8,128)}) custom-call(s32[3]{0:T(128)S(1)} %pad_add_fusion.flags, bf16[256,640]{1,0:T(8,128)(2,1)S(1)} %get-tuple-element.32.before, bf16[256,640]{1,0:T(8,128)(2,1)S(1)} %get-tuple-element.33.after, f32[3072,128]{1,0:T(8,128)S(1)} %bitcast.8, ...), custom_call_target="tpu_custom_call", output_to_operand_aliasing={{0}: (17, {})} | custom-call | flops 1000000 | bytes 7610380 | tf_op jit(solution)/shard_map/pallas_call | solution.py:774
Async XLA Ops:
  4.3 10.2 %collective-permute-start = (f32[208,128]{1,0:T(8,128)S(1)}, f32[208,128]{1,0:T(8,128)S(1)}, u32[]{:S(2)}, u32[]{:S(2)}) collective-permute-start(f32[208,128]{1,0:T(8,128)S(1)} %get-tuple-element.38), channel_id=1, source_target_pairs={{0,4},{8,12},{16,20},{24,28},{4,0},{12,8},{20,16},{28,24},{1,5},{9... | collective-permute-start | bytes 319496 | tf_op jit(solution)/shard_map/ppermute | solution.py:792
  4.3 10.1 %collective-permute-start.1 = (f32[208,128]{1,0:T(8,128)S(1)}, f32[208,128]{1,0:T(8,128)S(1)}, u32[]{:S(2)}, u32[]{:S(2)}) collective-permute-start(f32[208,128]{1,0:T(8,128)S(1)} %get-tuple-element.39), channel_id=1, source_target_pairs={{4,8},{12,16},{20,24},{8,4},{16,12},{24,20},{5,9},{13,17},{21,25},... | collective-permute-start | bytes 319496 | tf_op jit(solution)/shard_map/ppermute | solution.py:792
  6.9 6.1 %collective-permute-start.2 = (f32[64,128]{1,0:T(8,128)S(1)}, f32[64,128]{1,0:T(8,128)S(1)}, u32[]{:S(2)}, u32[]{:S(2)}) collective-permute-start(f32[64,128]{1,0:T(8,128)S(1)} %get-tuple-element.40), channel_id=1, source_target_pairs={{1,2},{2,1},{5,6},{6,5},{9,10},{10,9},{13,14},{14,13},{17,18},{18,... | collective-permute-start | bytes 98312 | tf_op jit(solution)/shard_map/ppermute | solution.py:792
  10.4 4.1 %collective-permute-start.3 = (f32[64,128]{1,0:T(8,128)S(1)}, f32[64,128]{1,0:T(8,128)S(1)}, u32[]{:S(2)}, u32[]{:S(2)}) collective-permute-start(f32[64,128]{1,0:T(8,128)S(1)} %get-tuple-element.41), channel_id=1, source_target_pairs={{0,1},{2,3},{1,0},{3,2},{4,5},{6,7},{5,4},{7,6},{8,9},{10,11},{9,8... | collective-permute-start | bytes 98312 | tf_op jit(solution)/shard_map/ppermute | solution.py:792
  15.4 8.6 %collective-permute-start.4 = (f32[392,128]{1,0:T(8,128)S(1)}, f32[392,128]{1,0:T(8,128)S(1)}, u32[]{:S(2)}, u32[]{:S(2)}) collective-permute-start(f32[392,128]{1,0:T(8,128)S(1)} %get-tuple-element.48), channel_id=1, source_target_pairs={{1,2},{2,1},{5,6},{6,5},{9,10},{10,9},{13,14},{14,13},{17,18},{18,... | collective-permute-start | bytes 602120 | tf_op jit(solution)/shard_map/ppermute | solution.py:792
  17.8 6.5 %collective-permute-start.5 = (f32[392,128]{1,0:T(8,128)S(1)}, f32[392,128]{1,0:T(8,128)S(1)}, u32[]{:S(2)}, u32[]{:S(2)}) collective-permute-start(f32[392,128]{1,0:T(8,128)S(1)} %get-tuple-element.49), channel_id=1, source_target_pairs={{0,1},{2,3},{1,0},{3,2},{4,5},{6,7},{5,4},{7,6},{8,9},{10,11},{9,8... | collective-permute-start | bytes 602120 | tf_op jit(solution)/shard_map/ppermute | solution.py:792
  25.7 5.7 %collective-permute-start.6 = (f32[344,128]{1,0:T(8,128)S(1)}, f32[344,128]{1,0:T(8,128)S(1)}, u32[]{:S(2)}, u32[]{:S(2)}) collective-permute-start(f32[344,128]{1,0:T(8,128)S(1)} %get-tuple-element.57), channel_id=1, source_target_pairs={{0,1},{2,3},{1,0},{3,2},{4,5},{6,7},{5,4},{7,6},{8,9},{10,11},{9,8... | collective-permute-start | bytes 528392 | tf_op jit(solution)/shard_map/ppermute | solution.py:792
  26.1 7.3 %collective-permute-start.7 = (f32[344,128]{1,0:T(8,128)S(1)}, f32[344,128]{1,0:T(8,128)S(1)}, u32[]{:S(2)}, u32[]{:S(2)}) collective-permute-start(f32[344,128]{1,0:T(8,128)S(1)} %get-tuple-element.58), channel_id=1, source_target_pairs={{1,2},{2,1},{5,6},{6,5},{9,10},{10,9},{13,14},{14,13},{17,18},{18,... | collective-permute-start | bytes 528392 | tf_op jit(solution)/shard_map/ppermute | solution.py:792
